TPU v7x, 32 devices: a whole 2x2x4 slice. The times are simulated.
32 devices in a mesh: section: 4 (over y, x), shard: 8 (over z, core).
Axes of the slice: x: 2, y: 2, z: 4, core: 2. Of those that a mesh axis runs over, the one named last changes fastest.
Arguments:
- features: bfloat16 [512, 768], P('shard'), may hold values from -6 to 6
- tile_cols: int32 [4, 4, 16], P('section'), may hold values from 0 to 3
- live_tiles: int32 [4, 4], P('section'), may hold values from 1 to 16, 32 in all within a row
- tile_values: bfloat16 [4, 512, 16, 128], P('section', 'shard'), may hold values from -0.375 to 0.375
- degrees: int32 [4, 512], P('section', 'shard'), may hold values from 1 to 8
Outputs:
- hops: bfloat16 [4, 512, 768], P('section', 'shard')
Inputs may be any that keep to these rules, and one draw needn't show every extreme that they name: `live_tiles`: every row block has at least one live tile slot; the live counts of one relation sum to 32.
All inputs are finite; a program needn't handle non-finite values.
Results may differ from a plain program's by a relative error of at most 0.0056.
Values may be sent and summed in bfloat16 or wider, within the bound.
No kernel may reach another device: no remote copies, remote signals or barrier semaphores. Data moves between devices by JAX's collectives and lax.ppermute only.
A program may use at most 64 MiB of HBM per device.

v0:
```python
import jax
import jax.numpy as jnp
from jax import lax
from jax.sharding import PartitionSpec as P


def from_behind(value, axis, by):
    peers = lax.axis_size(axis)
    pairs = [(i, i + by) for i in range(peers) if 0 <= i + by < peers]
    return lax.ppermute(value, axis, pairs)


def propagate(gathered, block_ids, live_count, tile_rows, row_scale):
    tile_size = tile_rows.shape[2]
    width = gathered.shape[1]
    blocks = gathered.reshape(gathered.shape[0] // tile_size, tile_size, width)
    source = blocks[block_ids]
    live_mask = (jnp.arange(tile_rows.shape[1], dtype=jnp.int32) < live_count).astype(jnp.bfloat16)
    masked = tile_rows * live_mask[None, :, None]
    summed = jnp.einsum("rkc,kcw->rw", masked, source, preferred_element_type=jnp.float32)
    return (summed * row_scale[:, None]).astype(jnp.bfloat16)


def per_device(features, tile_cols, live_tiles, tile_values, degrees):
    section_index = lax.axis_index("section")
    section_count = lax.axis_size("section")
    tile_rows = tile_values[0]
    row_count = tile_rows.shape[0]
    tile_size = tile_rows.shape[2]
    block_row = lax.axis_index("shard") * row_count // tile_size
    block_ids = lax.dynamic_index_in_dim(tile_cols[0], block_row, 0, keepdims=False)
    live_count = lax.dynamic_index_in_dim(live_tiles[0], block_row, 0, keepdims=False)
    row_scale = lax.rsqrt(degrees[0].astype(jnp.float32))
    width = features.shape[1]
    result = jnp.zeros((row_count, width), jnp.bfloat16)
    arrived = jnp.zeros((row_count, width), jnp.bfloat16)
    for hop_num in range(section_count):
        slab_in = jnp.where(section_index == 0, features, arrived)
        gathered = lax.all_gather(slab_in, "shard", axis=0, tiled=True)
        output = propagate(gathered, block_ids, live_count, tile_rows, row_scale)
        result = jnp.where(section_index == hop_num, output, result)
        arrived = from_behind(output, "section", 1)
    return result[None]


def solution(mesh):
    in_specs = (
        P("shard", None),
        P("section", None, None),
        P("section", None),
        P("section", "shard", None, None),
        P("section", "shard"),
    )
    out_specs = P("section", "shard", None)
    return jax.shard_map(
        per_device, mesh=mesh, in_specs=in_specs, out_specs=out_specs, check_vma=False
    )
```

profile of v0, /device:TPU:13, one launch (start us, length us, event | category | flops | bytes accessed | tf_op | source)
XLA Modules:
  0.0 110.6 jit_solution(15229078297644260339)
XLA Ops:
  0.0 0.0 copy-start
  0.0 0.7 fusion.14
  0.7 16.3 %all_gather.12 = bf16[512,768]{1,0:T(8,128)(2,1)S(1)} all-gather(bf16[64,768]{1,0:T(8,128)(2,1)S(1)} %broadcast_select_fusion.3), channel_id=1, replica_groups=mesh['section'=4,'shard'=8] {'shard'}, dimensions={0}, use_global_device_ids=true | all-gather | bytes 884736 | tf_op jit(solution)/shard_map/all_gather | solution.py:39
  17.1 0.6 constant_dynamic-slice_fusion
  17.6 0.6 compare_convert_fusion
  18.3 0.7 rsqrt_bitcast_fusion
  19.0 2.4 %gather_fusion = bf16[16,128,768]{2,1,0:T(8,128)(2,1)} fusion(bf16[4,128,768]{2,1,0:T(8,128)(2,1)S(1)} %bitcast.47, s32[1024]{0:T(1024)S(1)} %pad_clamp_fusion), kind=kCustom, calls=%fused_computation | custom fusion | bytes 6291520 | tf_op jit(solution)/shard_map/gather | solution.py:17
  21.4 0.1 bitcast_multiply_fusion
  21.5 2.6 %fusion.4 = bf16[64,768]{1,0:T(8,128)(2,1)S(1)} fusion(bf16[16,128,768]{2,1,0:T(8,128)(2,1)} %gather_fusion, bf16[64,16,128]{2,1,0:T(8,128)(2,1)S(1)} %bitcast_multiply_fusion, f32[64]{0:T(128)S(1)} %rsqrt_bitcast_fusion), kind=kOutput, calls=%fused_computation.12 | convolution fusion | flops 201424896 | bytes 3506432 | tf_op jit(solution)/shard_map/rkc,kcw->rw/dot_general | solution.py:20
  24.0 3.1 %collective-permute-start = (bf16[64,768]{1,0:T(8,128)(2,1)S(1)}, bf16[64,768]{1,0:T(8,128)(2,1)S(1)}, u32[]{:S(2)}, u32[]{:S(2)}) collective-permute-start(bf16[64,768]{1,0:T(8,128)(2,1)S(1)} %fusion.4), channel_id=1, source_target_pairs={{0,8},{8,16},{16,24},{1,9},{9,17},{17,25},{2,10},{10,18},{18,26},{... | collective-permute-start | bytes 294920 | tf_op jit(solution)/shard_map/ppermute | solution.py:10
  27.1 3.9 %collective-permute-done = bf16[64,768]{1,0:T(8,128)(2,1)S(1)} collective-permute-done((bf16[64,768]{1,0:T(8,128)(2,1)S(1)}, bf16[64,768]{1,0:T(8,128)(2,1)S(1)}, u32[]{:S(2)}, u32[]{:S(2)}) %collective-permute-start) | collective-permute-done | bytes 98336 | tf_op jit(solution)/shard_map/ppermute | solution.py:10
  31.1 16.6 %all_gather.13 = bf16[512,768]{1,0:T(8,128)(2,1)S(1)} all-gather(bf16[64,768]{1,0:T(8,128)(2,1)S(1)} %broadcast_select_fusion.2), channel_id=1, replica_groups=mesh['section'=4,'shard'=8] {'shard'}, dimensions={0}, use_global_device_ids=true | all-gather | bytes 884736 | tf_op jit(solution)/shard_map/all_gather | solution.py:39
  47.7 2.4 %gather_fusion.1 = bf16[16,128,768]{2,1,0:T(8,128)(2,1)} fusion(bf16[4,128,768]{2,1,0:T(8,128)(2,1)S(1)} %bitcast.49, s32[1024]{0:T(1024)S(1)} %pad_clamp_fusion), kind=kCustom, calls=%fused_computation.1 | custom fusion | bytes 6291520 | tf_op jit(solution)/shard_map/gather | solution.py:17
  50.1 2.5 %fusion.5 = bf16[64,768]{1,0:T(8,128)(2,1)S(1)} fusion(bf16[16,128,768]{2,1,0:T(8,128)(2,1)} %gather_fusion.1, bf16[64,16,128]{2,1,0:T(8,128)(2,1)S(1)} %bitcast_multiply_fusion, f32[64]{0:T(128)S(1)} %rsqrt_bitcast_fusion), kind=kOutput, calls=%fused_computation.13 | convolution fusion | flops 201424896 | bytes 3506432 | tf_op jit(solution)/shard_map/rkc,kcw->rw/dot_general | solution.py:20
  52.7 2.2 %collective-permute-start.1 = (bf16[64,768]{1,0:T(8,128)(2,1)S(1)}, bf16[64,768]{1,0:T(8,128)(2,1)S(1)}, u32[]{:S(2)}, u32[]{:S(2)}) collective-permute-start(bf16[64,768]{1,0:T(8,128)(2,1)S(1)} %fusion.5), channel_id=1, source_target_pairs={{0,8},{8,16},{16,24},{1,9},{9,17},{17,25},{2,10},{10,18},{18,26},{... | collective-permute-start | bytes 294920 | tf_op jit(solution)/shard_map/ppermute | solution.py:10
  54.9 4.8 %collective-permute-done.1 = bf16[64,768]{1,0:T(8,128)(2,1)S(1)} collective-permute-done((bf16[64,768]{1,0:T(8,128)(2,1)S(1)}, bf16[64,768]{1,0:T(8,128)(2,1)S(1)}, u32[]{:S(2)}, u32[]{:S(2)}) %collective-permute-start.1) | collective-permute-done | bytes 98336 | tf_op jit(solution)/shard_map/ppermute | solution.py:10
  59.7 16.6 %all_gather.14 = bf16[512,768]{1,0:T(8,128)(2,1)S(1)} all-gather(bf16[64,768]{1,0:T(8,128)(2,1)S(1)} %broadcast_select_fusion.1), channel_id=1, replica_groups=mesh['section'=4,'shard'=8] {'shard'}, dimensions={0}, use_global_device_ids=true | all-gather | bytes 884736 | tf_op jit(solution)/shard_map/all_gather | solution.py:39
  76.4 2.4 %gather_fusion.2 = bf16[16,128,768]{2,1,0:T(8,128)(2,1)} fusion(bf16[4,128,768]{2,1,0:T(8,128)(2,1)S(1)} %bitcast.50, s32[1024]{0:T(1024)S(1)} %pad_clamp_fusion), kind=kCustom, calls=%fused_computation.2 | custom fusion | bytes 6291520 | tf_op jit(solution)/shard_map/gather | solution.py:17
  78.8 2.5 %fusion.6 = bf16[64,768]{1,0:T(8,128)(2,1)S(1)} fusion(bf16[16,128,768]{2,1,0:T(8,128)(2,1)} %gather_fusion.2, bf16[64,16,128]{2,1,0:T(8,128)(2,1)S(1)} %bitcast_multiply_fusion, f32[64]{0:T(128)S(1)} %rsqrt_bitcast_fusion), kind=kOutput, calls=%fused_computation.14 | convolution fusion | flops 201424896 | bytes 3506432 | tf_op jit(solution)/shard_map/rkc,kcw->rw/dot_general | solution.py:20
  81.3 1.9 %collective-permute-start.2 = (bf16[64,768]{1,0:T(8,128)(2,1)S(1)}, bf16[64,768]{1,0:T(8,128)(2,1)S(1)}, u32[]{:S(2)}, u32[]{:S(2)}) collective-permute-start(bf16[64,768]{1,0:T(8,128)(2,1)S(1)} %fusion.6), channel_id=1, source_target_pairs={{0,8},{8,16},{16,24},{1,9},{9,17},{17,25},{2,10},{10,18},{18,26},{... | collective-permute-start | bytes 294920 | tf_op jit(solution)/shard_map/ppermute | solution.py:10
  83.2 5.1 %collective-permute-done.2 = bf16[64,768]{1,0:T(8,128)(2,1)S(1)} collective-permute-done((bf16[64,768]{1,0:T(8,128)(2,1)S(1)}, bf16[64,768]{1,0:T(8,128)(2,1)S(1)}, u32[]{:S(2)}, u32[]{:S(2)}) %collective-permute-start.2) | collective-permute-done | bytes 98336 | tf_op jit(solution)/shard_map/ppermute | solution.py:10
  88.4 16.6 %all_gather.15 = bf16[512,768]{1,0:T(8,128)(2,1)S(1)} all-gather(bf16[64,768]{1,0:T(8,128)(2,1)S(1)} %broadcast_select_fusion), channel_id=1, replica_groups=mesh['section'=4,'shard'=8] {'shard'}, dimensions={0}, use_global_device_ids=true | all-gather | bytes 884736 | tf_op jit(solution)/shard_map/all_gather | solution.py:39
  105.0 2.4 %gather_fusion.3 = bf16[16,128,768]{2,1,0:T(8,128)(2,1)} fusion(bf16[4,128,768]{2,1,0:T(8,128)(2,1)S(1)} %bitcast.48, s32[1024]{0:T(1024)S(1)} %pad_clamp_fusion), kind=kCustom, calls=%fused_computation.3 | custom fusion | bytes 6291520 | tf_op jit(solution)/shard_map/gather | solution.py:17
  107.4 3.2 %fusion.9 = bf16[1,64,768]{2,1,0:T(8,128)(2,1)} fusion(bf16[16,128,768]{2,1,0:T(8,128)(2,1)} %gather_fusion.3, bf16[64,16,128]{2,1,0:T(8,128)(2,1)S(1)} %bitcast_multiply_fusion, bf16[64,768]{1,0:T(8,128)(2,1)S(1)} %fusion.6, bf16[64,768]{1,0:T(8,128)(2,1)S(1)} %fusion.5, bf16[64,768]{1,0:T(8,128)(2,1)S(1)} %fusion.4, f32[64]{0:T(128)S(1)} %rsqrt_bitcast_fusion, ...), kind=kOutput, calls=%fused_computation.17 | convolution fusion | flops 201621504 | bytes 3801348 | tf_op jit(solution)/shard_map/rkc,kcw->rw/dot_general | solution.py:20
  (10 shorter events, 0.1 us)
Async XLA Ops:
  0.0 17.1 %copy-start = (s32[1,4]{1,0:T(1,128)S(1)}, s32[1,4]{1,0:T(1,128)}, u32[]{:S(2)}) copy-start(s32[1,4]{1,0:T(1,128)} %param.7) | copy-start | bytes 52
  19.0 2.4 %copy-start.2 = (bf16[1,64,16,128]{3,2,1,0:T(8,128)(2,1)S(1)}, bf16[1,64,16,128]{3,2,1,0:T(8,128)(2,1)}, u32[]{:S(2)}) copy-start(bf16[1,64,16,128]{3,2,1,0:T(8,128)(2,1)} %param.8) | copy-start | bytes 786436
  21.4 9.7 %copy-start.1 = (bf16[64,768]{1,0:T(8,128)(2,1)S(1)}, bf16[64,768]{1,0:T(8,128)(2,1)}, u32[]{:S(2)}) copy-start(bf16[64,768]{1,0:T(8,128)(2,1)} %param.5) | copy-start | bytes 294916
  24.0 7.0 %collective-permute-start = (bf16[64,768]{1,0:T(8,128)(2,1)S(1)}, bf16[64,768]{1,0:T(8,128)(2,1)S(1)}, u32[]{:S(2)}, u32[]{:S(2)}) collective-permute-start(bf16[64,768]{1,0:T(8,128)(2,1)S(1)} %fusion.4), channel_id=1, source_target_pairs={{0,8},{8,16},{16,24},{1,9},{9,17},{17,25},{2,10},{10,18},{18,26},{... | collective-permute-start | bytes 294920 | tf_op jit(solution)/shard_map/ppermute | solution.py:10
  52.7 7.0 %collective-permute-start.1 = (bf16[64,768]{1,0:T(8,128)(2,1)S(1)}, bf16[64,768]{1,0:T(8,128)(2,1)S(1)}, u32[]{:S(2)}, u32[]{:S(2)}) collective-permute-start(bf16[64,768]{1,0:T(8,128)(2,1)S(1)} %fusion.5), channel_id=1, source_target_pairs={{0,8},{8,16},{16,24},{1,9},{9,17},{17,25},{2,10},{10,18},{18,26},{... | collective-permute-start | bytes 294920 | tf_op jit(solution)/shard_map/ppermute | solution.py:10
  81.3 7.0 %collective-permute-start.2 = (bf16[64,768]{1,0:T(8,128)(2,1)S(1)}, bf16[64,768]{1,0:T(8,128)(2,1)S(1)}, u32[]{:S(2)}, u32[]{:S(2)}) collective-permute-start(bf16[64,768]{1,0:T(8,128)(2,1)S(1)} %fusion.6), channel_id=1, source_target_pairs={{0,8},{8,16},{16,24},{1,9},{9,17},{17,25},{2,10},{10,18},{18,26},{... | collective-permute-start | bytes 294920 | tf_op jit(solution)/shard_map/ppermute | solution.py:10
where the time goes:
time: 111 us
  blocking collectives  66.2 us (60%)
  waiting for transfers between devices  13.8 us (12%)
  matrix products  10.8 us (10%)
  local copies, waits for them, and re-layouts  10.2 us (9%)
  starting transfers between devices  7.25 us (7%)
  other arithmetic  2.17 us (2%)
    all_gather x4, blocking collectives, per_device(): gathered = lax.all_gather(slab_in, 'shard', axis=0, tiled=True)  66.2 us
    ppermute x3, waiting for transfers between devices, from_behind(): return lax.ppermute(value, axis, pairs)  13.8 us
    dot_general x4, matrix products, propagate(): jnp.einsum('rkc,kcw->rw', masked, source, preferred_element_type=jnp.floa...  10.8 us
    gather x4, local copies, waits for them, and re-layouts, propagate(): source = blocks[block_ids]  9.61 us
    ppermute x3, starting transfers between devices, from_behind(): return lax.ppermute(value, axis, pairs)  7.25 us
  transfers between devices with their start and end apart: 3, of which 3 were waited for; matrix products, arithmetic and copies ran while one was open for 0% of the time, Pallas kernels for 0%

commit v1 on v0

v1 whole, which is shorter than its diff:
```python
import jax
import jax.numpy as jnp
from jax import lax
from jax.experimental import pallas as pl
from jax.experimental.pallas import tpu as pltpu
from jax.sharding import PartitionSpec as P


def dense_rows_kernel(cols_ref, live_ref, tiles_ref, degrees_ref, rows_ref):
    row_count, slots, tile_size = tiles_ref.shape
    blocks = rows_ref.shape[1] // tile_size
    block_row = lax.axis_index("shard") * row_count // tile_size
    live = live_ref[0, block_row]
    wide = row_count * slots
    place = lax.broadcasted_iota(jnp.int32, (row_count, wide), 1)
    slot = lax.rem(place, slots)
    mine = lax.broadcasted_iota(jnp.int32, (row_count, wide), 0) == lax.div(place, slots)
    column = jnp.full((row_count, wide), -1, jnp.int32)
    for k in range(slots):
        column = jnp.where((slot == k) & mine & (k < live), cols_ref[0, block_row, k], column)
    tiles = tiles_ref[...].reshape(wide, tile_size)
    degree = jnp.broadcast_to(degrees_ref[...].astype(jnp.float32), (row_count, row_count))
    diagonal = lax.broadcasted_iota(jnp.int32, (row_count, row_count), 0) == lax.broadcasted_iota(
        jnp.int32, (row_count, row_count), 1
    )
    scale = lax.rsqrt(jnp.sum(jnp.where(diagonal, degree, 0.0), axis=1, keepdims=True))
    for b in range(blocks):
        pick = (column == b).astype(jnp.bfloat16)
        summed = jnp.dot(pick, tiles, preferred_element_type=jnp.float32)
        rows_ref[:, b * tile_size : (b + 1) * tile_size] = (summed * scale).astype(jnp.bfloat16)


def dense_rows(tile_cols, live_tiles, tile_rows, degrees, nodes):
    row_count = tile_rows.shape[0]
    return pl.pallas_call(
        dense_rows_kernel,
        out_shape=jax.ShapeDtypeStruct((row_count, nodes), jnp.bfloat16),
        in_specs=[
            pl.BlockSpec(memory_space=pltpu.SMEM),
            pl.BlockSpec(memory_space=pltpu.SMEM),
            pl.BlockSpec(memory_space=pltpu.VMEM),
            pl.BlockSpec(memory_space=pltpu.VMEM),
        ],
        out_specs=pl.BlockSpec(memory_space=pltpu.VMEM),
        name="dense_rows",
    )(tile_cols, live_tiles, tile_rows, degrees)


def chain_kernel(own_ref, relations_ref, slab_ref, out_ref, halves):
    row_count = own_ref.shape[0]
    section = lax.axis_index("section")
    halves[:row_count] = own_ref[...]
    halves[row_count:] = jnp.zeros_like(own_ref)

    def times(i, carry):
        both = jnp.dot(halves[...], relations_ref[section - 1 - i], preferred_element_type=jnp.float32)
        product = both[:row_count] + both[row_count:]
        high = product.astype(jnp.bfloat16)
        halves[:row_count] = high
        halves[row_count:] = (product - high.astype(jnp.float32)).astype(jnp.bfloat16)
        return carry

    lax.fori_loop(0, section, times, 0)
    both = jnp.dot(halves[...], slab_ref[...], preferred_element_type=jnp.float32)
    out_ref[...] = (both[:row_count] + both[row_count:]).astype(jnp.bfloat16)


def chain(own, relations, slab):
    row_count, nodes = own.shape
    return pl.pallas_call(
        chain_kernel,
        out_shape=jax.ShapeDtypeStruct((row_count, slab.shape[1]), jnp.bfloat16),
        in_specs=[pl.BlockSpec(memory_space=pltpu.VMEM)] * 3,
        out_specs=pl.BlockSpec(memory_space=pltpu.VMEM),
        scratch_shapes=[pltpu.VMEM((2 * row_count, nodes), jnp.bfloat16)],
        compiler_params=pltpu.CompilerParams(vmem_limit_bytes=32 * 1024 * 1024),
        name="chain",
    )(own, relations, slab)


def by_products(features, own):
    sections = lax.axis_size("section")
    nodes = own.shape[1]
    slab = lax.all_gather(features, "shard", axis=0, tiled=True)
    relations = lax.all_gather(own, ("section", "shard"), axis=0, tiled=True)
    return chain(own, relations.reshape(sections, nodes, nodes), slab)


def by_hops(features, own):
    sections = lax.axis_size("section")
    section = lax.axis_index("section")
    step = [(i, i + 1) for i in range(sections - 1)]
    result = jnp.zeros_like(features)
    arrived = features
    for hop in range(sections):
        slab = lax.all_gather(arrived, "shard", axis=0, tiled=True)
        output = jnp.dot(own, slab, preferred_element_type=jnp.float32).astype(jnp.bfloat16)
        result = jnp.where(section == hop, output, result)
        arrived = lax.ppermute(output, "section", step)
    return result


def per_device(features, tile_cols, live_tiles, tile_values, degrees):
    nodes = features.shape[0] * lax.axis_size("shard")
    own = dense_rows(tile_cols, live_tiles, tile_values[0], degrees, nodes)
    plan = by_products if nodes <= features.shape[1] else by_hops
    return plan(features, own)[None]


def solution(mesh):
    in_specs = (
        P("shard", None),
        P("section", None, None),
        P("section", None),
        P("section", "shard", None, None),
        P("section", "shard"),
    )
    out_specs = P("section", "shard", None)
    return jax.shard_map(
        per_device, mesh=mesh, in_specs=in_specs, out_specs=out_specs, check_vma=False
    )
```

time: 111 us -> 80 us (0.72)
  the two profiles are of different devices: /device:TPU:13 before, /device:TPU:0 now
where the time goes in v1:
time: 80 us; the launch traced here: 79.8 us
  waiting for transfers between devices  43.7 us (55%)
  blocking collectives  17.4 us (22%)
  between operations  13.4 us (17%)
  Pallas kernels  2.87 us (4%)
  local copies, waits for them, and re-layouts  2.43 us (3%)
    all_gather x1, waiting for transfers between devices, by_products(): relations = lax.all_gather(own, ('section', 'shard'), axis=0, tiled=True)  43.6 us
    all_gather x1, blocking collectives, by_products(): slab = lax.all_gather(features, 'shard', axis=0, tiled=True)  17.4 us
    unnamed x4, local copies, waits for them, and re-layouts  2.43 us
    pallas_call x1, Pallas kernels, dense_rows(): pl.pallas_call(dense_rows_kernel, out_shape=jax.ShapeDtypeStruct((row_cou...  1.94 us
  transfers between devices with their start and end apart: 1, of which 1 were waited for; matrix products, arithmetic and copies ran while one was open for 0% of the time, Pallas kernels for 0%

profile of v1, /device:TPU:0, one launch (start us, length us, event | category | flops | bytes accessed | tf_op | source)
XLA Modules:
  0.0 79.8 jit_solution(1156265178192066561)
XLA Ops:
  6.5 0.0 all-gather.2.cloned.1.call-start
  6.5 1.9 %dense_rows.1.own_ref = bf16[64,512]{1,0:T(8,128)(2,1)} custom-call(s32[1,4,16]{2,1,0:T(4,128)} %cols_ref.1, s32[1,4]{1,0:T(1,128)} %live_ref.1, bf16[64,16,128]{2,1,0:T(8,128)(2,1)} %bitcast.4, s32[1,64]{1,0:T(1,128)} %degrees_ref.1), custom_call_target="tpu_custom_call" | custom-call | tf_op jit(solution)/shard_map/dense_rows/pallas_call | solution.py:35
  8.5 0.0 all-gather.2.cloned.1.call-update
  8.5 17.4 %all_gather.7.slab_ref = bf16[512,768]{1,0:T(8,128)(2,1)S(1)} all-gather(bf16[64,768]{1,0:T(8,128)(2,1)} %param.5), channel_id=1, replica_groups=mesh['section'=4,'shard'=8] {'shard'}, dimensions={0}, use_global_device_ids=true | all-gather | bytes 884736 | tf_op jit(solution)/shard_map/all_gather | solution.py:84
  25.9 43.6 %all-gather.2.cloned.1.call-done = bf16[2048,512]{1,0:T(8,128)(2,1)} async-done(((bf16[64,512]{1,0:T(8,128)(2,1)}), bf16[2048,512]{1,0:T(8,128)(2,1)}) %all-gather.2.cloned.1.call-update) | async-done | bytes 2097168 | tf_op jit(solution)/shard_map/all_gather | solution.py:85
  69.6 0.0 copy-start
  69.6 1.6 %copy-done = bf16[2048,512]{1,0:T(8,128)(2,1)S(1)} copy-done((bf16[2048,512]{1,0:T(8,128)(2,1)S(1)}, bf16[2048,512]{1,0:T(8,128)(2,1)}, u32[]{:S(2)}) %copy-start) | copy-done | bytes 2097176
  71.2 0.0 copy-start.1
  71.2 0.8 %copy-done.1 = bf16[64,512]{1,0:T(8,128)(2,1)S(1)} copy-done((bf16[64,512]{1,0:T(8,128)(2,1)S(1)}, bf16[64,512]{1,0:T(8,128)(2,1)}, u32[]{:S(2)}) %copy-start.1) | copy-done | bytes 65560
  72.0 0.9 %chain.1 = bf16[64,768]{1,0:T(8,128)(2,1)} custom-call(bf16[64,512]{1,0:T(8,128)(2,1)S(1)} %copy-done.1, bf16[4,512,512]{2,1,0:T(8,128)(2,1)S(1)} %bitcast.3, bf16[512,768]{1,0:T(8,128)(2,1)S(1)} %all_gather.7.slab_ref), custom_call_target="tpu_custom_call" | custom-call | tf_op jit(solution)/shard_map/chain/pallas_call | solution.py:70
Async XLA Ops:
  6.5 63.1 %all-gather.2.cloned.1.call-start = ((), (), s32[]{:S(2)}) async-start(), calls=%async_computation | async-start | bytes 2162688 | tf_op jit(solution)/shard_map/all_gather | solution.py:85
  69.6 1.6 %copy-start = (bf16[2048,512]{1,0:T(8,128)(2,1)S(1)}, bf16[2048,512]{1,0:T(8,128)(2,1)}, u32[]{:S(2)}) copy-start(bf16[2048,512]{1,0:T(8,128)(2,1)} %all-gather.2.cloned.1.call-done) | copy-start | bytes 6291460
  71.2 0.8 %copy-start.1 = (bf16[64,512]{1,0:T(8,128)(2,1)S(1)}, bf16[64,512]{1,0:T(8,128)(2,1)}, u32[]{:S(2)}) copy-start(bf16[64,512]{1,0:T(8,128)(2,1)} %dense_rows.1.own_ref) | copy-start | bytes 196612
Sparse Core Ops, SparseCore 0:
  10.3 59.2 all-gather.1

commit v2 on v1

v2 whole, which is shorter than its diff:
```python
import jax
import jax.numpy as jnp
from jax import lax
from jax.experimental import pallas as pl
from jax.experimental.pallas import tpu as pltpu
from jax.sharding import PartitionSpec as P


def dense_rows_kernel(cols_ref, live_ref, tiles_ref, degrees_ref, rows_ref):
    row_count, slots, tile_size = tiles_ref.shape
    blocks = rows_ref.shape[1] // tile_size
    block_row = lax.axis_index("shard") * row_count // tile_size
    live = live_ref[0, block_row]
    wide = row_count * slots
    place = lax.broadcasted_iota(jnp.int32, (row_count, wide), 1)
    slot = lax.rem(place, slots)
    mine = lax.broadcasted_iota(jnp.int32, (row_count, wide), 0) == lax.div(place, slots)
    column = jnp.full((row_count, wide), -1, jnp.int32)
    for k in range(slots):
        column = jnp.where((slot == k) & mine & (k < live), cols_ref[0, block_row, k], column)
    tiles = tiles_ref[...].reshape(wide, tile_size)
    degree = jnp.broadcast_to(degrees_ref[...].astype(jnp.float32), (row_count, row_count))
    diagonal = lax.broadcasted_iota(jnp.int32, (row_count, row_count), 0) == lax.broadcasted_iota(
        jnp.int32, (row_count, row_count), 1
    )
    scale = lax.rsqrt(jnp.sum(jnp.where(diagonal, degree, 0.0), axis=1, keepdims=True))
    for b in range(blocks):
        pick = (column == b).astype(jnp.bfloat16)
        summed = jnp.dot(pick, tiles, preferred_element_type=jnp.float32)
        rows_ref[:, b * tile_size : (b + 1) * tile_size] = (summed * scale).astype(jnp.bfloat16)


def dense_rows(tile_cols, live_tiles, tile_rows, degrees, nodes):
    row_count = tile_rows.shape[0]
    return pl.pallas_call(
        dense_rows_kernel,
        out_shape=jax.ShapeDtypeStruct((row_count, nodes), jnp.bfloat16),
        in_specs=[
            pl.BlockSpec(memory_space=pltpu.SMEM),
            pl.BlockSpec(memory_space=pltpu.SMEM),
            pl.BlockSpec(memory_space=pltpu.VMEM),
            pl.BlockSpec(memory_space=pltpu.VMEM),
        ],
        out_specs=pl.BlockSpec(memory_space=pltpu.VMEM),
        name="dense_rows",
    )(tile_cols, live_tiles, tile_rows, degrees)


def per_device(features, tile_cols, live_tiles, tile_values, degrees):
    sections = lax.axis_size("section")
    part = features.shape[1] // sections
    row_count = features.shape[0]
    nodes = row_count * lax.axis_size("shard")
    piece = lax.dynamic_slice_in_dim(features, lax.axis_index("section") * part, part, axis=1)
    own = dense_rows(tile_cols, live_tiles, tile_values[0], degrees, nodes)
    relations = lax.all_gather(own, "section", axis=0, tiled=False)
    pieces = []
    for hop in range(sections):
        slab = lax.all_gather(piece, "shard", axis=0, tiled=True)
        piece = jnp.dot(relations[hop], slab, preferred_element_type=jnp.float32).astype(jnp.bfloat16)
        pieces.append(piece)
    mine = lax.all_to_all(jnp.stack(pieces), "section", split_axis=0, concat_axis=0, tiled=True)
    return jnp.swapaxes(mine, 0, 1).reshape(row_count, sections * part)[None]


def solution(mesh):
    in_specs = (
        P("shard", None),
        P("section", None, None),
        P("section", None),
        P("section", "shard", None, None),
        P("section", "shard"),
    )
    out_specs = P("section", "shard", None)
    return jax.shard_map(
        per_device, mesh=mesh, in_specs=in_specs, out_specs=out_specs, check_vma=False
    )
```

time: 80 us -> 79.3 us (level)
  blocking collectives: 17.4 us -> 75.3 us
  waiting for transfers between devices: 43.7 us -> 0 us
  between operations: 13.4 us -> 0.02 us
  local copies, waits for them, and re-layouts: 2.43 us -> 0.98 us
  Pallas kernels: 2.87 us -> 1.98 us
    all_gather x1 -> x5, blocking collectives: 17.4 us -> 67.8 us  [the longest x4 57.1 us: per_device(): slab = lax.all_gather(piece, 'shard', axis=0, tiled=True)]
    all_gather x1 -> x0, waiting for transfers between devices: 43.6 us -> none  [by_products(): relations = lax.all_gather(own, ('section', 'shard'), axis=0, tiled=True)]
    all_to_all x0 -> x1, blocking collectives: none -> 7.55 us  [per_device(): lax.all_to_all(jnp.stack(pieces), 'section', split_axis=0, concat_axis=0,...]
    unnamed x4 -> x2, local copies, waits for them, and re-layouts: 2.43 us -> 0.01 us
    pallas_call x1 -> x0, Pallas kernels: 0.92 us -> none  [chain(): pl.pallas_call(chain_kernel, out_shape=jax.ShapeDtypeStruct((row_count, s...]
  transfers between devices with their start and end apart: 1 -> 0, of which waited for: 1 -> 0; matrix products, arithmetic and copies ran while one was open for 0% -> 0% of each run, Pallas kernels for 0% -> 0%
where the time goes in v2:
time: 79.3 us; the launch traced here: 79 us
  blocking collectives  75.3 us (95%)
  Pallas kernels  1.98 us (2%)
  local copies, waits for them, and re-layouts  0.98 us (1%)
    all_gather x4, blocking collectives, per_device(): slab = lax.all_gather(piece, 'shard', axis=0, tiled=True)  57.1 us
    all_gather x1, blocking collectives, per_device(): relations = lax.all_gather(own, 'section', axis=0, tiled=False)  10.7 us
    all_to_all x1, blocking collectives, per_device(): lax.all_to_all(jnp.stack(pieces), 'section', split_axis=0, concat_axis=0,...  7.55 us
    pallas_call x1, Pallas kernels, dense_rows(): pl.pallas_call(dense_rows_kernel, out_shape=jax.ShapeDtypeStruct((row_cou...  1.98 us

profile of v2, /device:TPU:0, one launch (start us, length us, event | category | flops | bytes accessed | tf_op | source)
XLA Modules:
  0.0 79.0 jit_solution(2773647658376031690)
XLA Ops:
  0.0 0.0 copy-start
  0.0 2.0 %dense_rows.1 = bf16[64,512]{1,0:T(8,128)(2,1)} custom-call(s32[1,4,16]{2,1,0:T(4,128)} %cols_ref.1, s32[1,4]{1,0:T(1,128)} %live_ref.1, bf16[64,16,128]{2,1,0:T(8,128)(2,1)} %bitcast.15, s32[1,64]{1,0:T(1,128)} %degrees_ref.1), custom_call_target="tpu_custom_call" | custom-call | tf_op jit(solution)/shard_map/dense_rows/pallas_call | solution.py:35
  2.0 10.7 %all-gather = bf16[256,512]{1,0:T(8,128)(2,1)S(1)} all-gather(bf16[64,512]{1,0:T(8,128)(2,1)} %dense_rows.1), channel_id=2, replica_groups=mesh['section'=4,'shard'=8] {'section'}, dimensions={0}, use_global_device_ids=true | all-gather | bytes 327680 | tf_op jit(solution)/shard_map/all_gather | solution.py:56
  12.7 0.0 copy-done
  12.7 0.1 constant_dynamic-slice_fusion
  12.8 14.4 %all_gather.20 = bf16[512,192]{1,0:T(8,128)(2,1)S(1)} all-gather(bf16[64,192]{1,0:T(8,128)(2,1)S(1)} %constant_dynamic-slice_fusion), channel_id=1, replica_groups=mesh['section'=4,'shard'=8] {'shard'}, dimensions={0}, use_global_device_ids=true | all-gather | bytes 221184 | tf_op jit(solution)/shard_map/all_gather | solution.py:59
  27.2 0.2 convolution_convert_fusion.3
  27.4 14.2 %all_gather.21 = bf16[512,192]{1,0:T(8,128)(2,1)S(1)} all-gather(bf16[64,192]{1,0:T(8,128)(2,1)S(1)} %convolution_convert_fusion.3), channel_id=1, replica_groups=mesh['section'=4,'shard'=8] {'shard'}, dimensions={0}, use_global_device_ids=true | all-gather | bytes 221184 | tf_op jit(solution)/shard_map/all_gather | solution.py:59
  41.6 0.2 convolution_convert_fusion.2
  41.7 14.2 %all_gather.22 = bf16[512,192]{1,0:T(8,128)(2,1)S(1)} all-gather(bf16[64,192]{1,0:T(8,128)(2,1)S(1)} %convolution_convert_fusion.2), channel_id=1, replica_groups=mesh['section'=4,'shard'=8] {'shard'}, dimensions={0}, use_global_device_ids=true | all-gather | bytes 221184 | tf_op jit(solution)/shard_map/all_gather | solution.py:59
  56.0 0.2 convolution_convert_fusion.1
  56.1 14.2 %all_gather.23 = bf16[512,192]{1,0:T(8,128)(2,1)S(1)} all-gather(bf16[64,192]{1,0:T(8,128)(2,1)S(1)} %convolution_convert_fusion.1), channel_id=1, replica_groups=mesh['section'=4,'shard'=8] {'shard'}, dimensions={0}, use_global_device_ids=true | all-gather | bytes 221184 | tf_op jit(solution)/shard_map/all_gather | solution.py:59
  70.4 0.2 fusion
  70.6 7.6 %all_to_all.5 = bf16[4,64,192]{2,1,0:T(8,128)(2,1)S(1)} all-to-all(bf16[4,64,192]{2,1,0:T(8,128)(2,1)S(1)} %pad_maximum_fusion), channel_id=1, replica_groups=mesh['section'=4,'shard'=8] {'section'}, dimensions={0} | all-to-all | bytes 196608 | tf_op jit(solution)/shard_map/all_to_all | solution.py:62
  78.1 0.1 copy.6
  78.2 0.8 broadcast_in_dim_reshape.3
  (1 shorter events, 0.0 us)
Async XLA Ops:
  0.0 12.7 %copy-start = (bf16[64,768]{1,0:T(8,128)(2,1)S(1)}, bf16[64,768]{1,0:T(8,128)(2,1)}, u32[]{:S(2)}) copy-start(bf16[64,768]{1,0:T(8,128)(2,1)} %param.5) | copy-start | bytes 294916

commit v3 on v1

--- a/solution.py
+++ b/solution.py
@@ -46,14 +46,16 @@
     )(tile_cols, live_tiles, tile_rows, degrees)
 
 
-def chain_kernel(own_ref, relations_ref, slab_ref, out_ref, halves):
-    row_count = own_ref.shape[0]
+def chain_kernel(own_ref, gathered_ref, out_ref, halves):
+    row_count, nodes = own_ref.shape
+    width = out_ref.shape[1]
     section = lax.axis_index("section")
     halves[:row_count] = own_ref[...]
     halves[row_count:] = jnp.zeros_like(own_ref)
 
     def times(i, carry):
-        both = jnp.dot(halves[...], relations_ref[section - 1 - i], preferred_element_type=jnp.float32)
+        columns = pl.ds(pl.multiple_of((section - 1 - i) * nodes, 128), nodes)
+        both = jnp.dot(halves[...], gathered_ref[:, columns], preferred_element_type=jnp.float32)
         product = both[:row_count] + both[row_count:]
         high = product.astype(jnp.bfloat16)
         halves[:row_count] = high
@@ -61,43 +63,44 @@
         return carry
 
     lax.fori_loop(0, section, times, 0)
-    both = jnp.dot(halves[...], slab_ref[...], preferred_element_type=jnp.float32)
+    slab = gathered_ref[:, gathered_ref.shape[1] - width :]
+    both = jnp.dot(halves[...], slab, preferred_element_type=jnp.float32)
     out_ref[...] = (both[:row_count] + both[row_count:]).astype(jnp.bfloat16)
 
 
-def chain(own, relations, slab):
+def chain(own, gathered, width):
     row_count, nodes = own.shape
     return pl.pallas_call(
         chain_kernel,
-        out_shape=jax.ShapeDtypeStruct((row_count, slab.shape[1]), jnp.bfloat16),
-        in_specs=[pl.BlockSpec(memory_space=pltpu.VMEM)] * 3,
+        out_shape=jax.ShapeDtypeStruct((row_count, width), jnp.bfloat16),
+        in_specs=[pl.BlockSpec(memory_space=pltpu.VMEM)] * 2,
         out_specs=pl.BlockSpec(memory_space=pltpu.VMEM),
         scratch_shapes=[pltpu.VMEM((2 * row_count, nodes), jnp.bfloat16)],
         compiler_params=pltpu.CompilerParams(vmem_limit_bytes=32 * 1024 * 1024),
         name="chain",
-    )(own, relations, slab)
+    )(own, gathered)
 
 
 def by_products(features, own):
     sections = lax.axis_size("section")
-    nodes = own.shape[1]
-    slab = lax.all_gather(features, "shard", axis=0, tiled=True)
-    relations = lax.all_gather(own, ("section", "shard"), axis=0, tiled=True)
-    return chain(own, relations.reshape(sections, nodes, nodes), slab)
+    relations = lax.all_gather(own, "section", axis=0, tiled=False)
+    payload = jnp.concatenate([relations[s] for s in range(sections - 1)] + [features], axis=1)
+    gathered = lax.all_gather(payload, "shard", axis=0, tiled=True)
+    return chain(own, gathered, features.shape[1])
 
 
 def by_hops(features, own):
     sections = lax.axis_size("section")
-    section = lax.axis_index("section")
-    step = [(i, i + 1) for i in range(sections - 1)]
-    result = jnp.zeros_like(features)
-    arrived = features
+    part = features.shape[1] // sections
+    piece = lax.dynamic_slice_in_dim(features, lax.axis_index("section") * part, part, axis=1)
+    relations = lax.all_gather(own, "section", axis=0, tiled=False)
+    pieces = []
     for hop in range(sections):
-        slab = lax.all_gather(arrived, "shard", axis=0, tiled=True)
-        output = jnp.dot(own, slab, preferred_element_type=jnp.float32).astype(jnp.bfloat16)
-        result = jnp.where(section == hop, output, result)
-        arrived = lax.ppermute(output, "section", step)
-    return result
+        slab = lax.all_gather(piece, "shard", axis=0, tiled=True)
+        piece = jnp.dot(relations[hop], slab, preferred_element_type=jnp.float32).astype(jnp.bfloat16)
+        pieces.append(piece)
+    mine = lax.all_to_all(jnp.stack(pieces), "section", split_axis=0, concat_axis=0, tiled=True)
+    return jnp.swapaxes(mine, 0, 1).reshape(features.shape)
 
 
 def per_device(features, tile_cols, live_tiles, tile_values, degrees):

time: 80 us -> 63.5 us (0.79)
  waiting for transfers between devices: 43.7 us -> 32.1 us
  blocking collectives: 17.4 us -> 10.7 us
  other arithmetic: 0 us -> 1.63 us
    all_gather x1, waiting for transfers between devices: 43.6 us -> 32 us  [by_products(): gathered = lax.all_gather(payload, 'shard', axis=0, tiled=True)]
    all_gather x1, blocking collectives: 17.4 us -> 10.7 us  [by_products(): relations = lax.all_gather(own, 'section', axis=0, tiled=False)]
    concatenate x0 -> x1, other arithmetic: none -> 1.63 us  [by_products(): jnp.concatenate([relations[s] for s in range(sections - 1)] + [features],...]
where the time goes in v3:
time: 63.5 us; the launch traced here: 63.2 us
  waiting for transfers between devices  32.1 us (51%)
  between operations  13.4 us (21%)
  blocking collectives  10.7 us (17%)
  Pallas kernels  2.87 us (5%)
  local copies, waits for them, and re-layouts  2.52 us (4%)
  other arithmetic  1.63 us (3%)
    all_gather x1, waiting for transfers between devices, by_products(): gathered = lax.all_gather(payload, 'shard', axis=0, tiled=True)  32 us
    all_gather x1, blocking collectives, by_products(): relations = lax.all_gather(own, 'section', axis=0, tiled=False)  10.7 us
    unnamed x4, local copies, waits for them, and re-layouts  2.5 us
    pallas_call x1, Pallas kernels, dense_rows(): pl.pallas_call(dense_rows_kernel, out_shape=jax.ShapeDtypeStruct((row_cou...  1.94 us
    concatenate x1, other arithmetic, by_products(): jnp.concatenate([relations[s] for s in range(sections - 1)] + [features],...  1.63 us
  transfers between devices with their start and end apart: 1, of which 1 were waited for; matrix products, arithmetic and copies ran while one was open for 0% of the time, Pallas kernels for 0%

profile of v3, /device:TPU:0, one launch (start us, length us, event | category | flops | bytes accessed | tf_op | source)
XLA Modules:
  0.0 63.2 jit_solution(11823041902243144488)
XLA Ops:
  6.5 0.0 all-gather.3.cloned.1.call-start
  6.5 1.9 %dense_rows.1.own_ref = bf16[64,512]{1,0:T(8,128)(2,1)} custom-call(s32[1,4,16]{2,1,0:T(4,128)} %cols_ref.1, s32[1,4]{1,0:T(1,128)} %live_ref.1, bf16[64,16,128]{2,1,0:T(8,128)(2,1)} %bitcast.2, s32[1,64]{1,0:T(1,128)} %degrees_ref.1), custom_call_target="tpu_custom_call" | custom-call | tf_op jit(solution)/shard_map/dense_rows/pallas_call | solution.py:35
  8.5 10.7 %all-gather = bf16[256,512]{1,0:T(8,128)(2,1)S(1)} all-gather(bf16[64,512]{1,0:T(8,128)(2,1)} %dense_rows.1.own_ref), channel_id=2, replica_groups=mesh['section'=4,'shard'=8] {'section'}, dimensions={0}, use_global_device_ids=true | all-gather | bytes 327680 | tf_op jit(solution)/shard_map/all_gather | solution.py:86
  19.2 1.6 %pad_maximum_fusion = bf16[64,2304]{1,0:T(8,128)(2,1)} fusion(bf16[64,768]{1,0:T(8,128)(2,1)} %param.5, bf16[64,512]{1,0:T(8,128)(2,1)S(1)} %get-tuple-element.7, bf16[64,512]{1,0:T(8,128)(2,1)S(1)} %get-tuple-element.6, bf16[64,512]{1,0:T(8,128)(2,1)S(1)} %get-tuple-element.5), kind=kLoop, calls=%fused_computation | loop fusion | flops 1179648 | bytes 589824 | tf_op jit(solution)/shard_map/concatenate | solution.py:87
  20.8 0.0 all-gather.3.cloned.1.call-update
  20.9 32.0 %all-gather.3.cloned.1.call-done.gathered_ref = bf16[512,2304]{1,0:T(8,128)(2,1)} async-done(((bf16[64,2304]{1,0:T(8,128)(2,1)}), bf16[512,2304]{1,0:T(8,128)(2,1)}) %all-gather.3.cloned.1.call-update) | async-done | bytes 2359312 | tf_op jit(solution)/shard_map/all_gather | solution.py:88
  52.9 0.0 copy-start
  52.9 1.7 %copy-done = bf16[512,2304]{1,0:T(8,128)(2,1)S(1)} copy-done((bf16[512,2304]{1,0:T(8,128)(2,1)S(1)}, bf16[512,2304]{1,0:T(8,128)(2,1)}, u32[]{:S(2)}) %copy-start) | copy-done | bytes 2359320
  54.6 0.0 copy-start.1
  54.6 0.8 %copy-done.1 = bf16[64,512]{1,0:T(8,128)(2,1)S(1)} copy-done((bf16[64,512]{1,0:T(8,128)(2,1)S(1)}, bf16[64,512]{1,0:T(8,128)(2,1)}, u32[]{:S(2)}) %copy-start.1) | copy-done | bytes 65560
  55.4 0.9 %chain.1 = bf16[64,768]{1,0:T(8,128)(2,1)} custom-call(bf16[64,512]{1,0:T(8,128)(2,1)S(1)} %copy-done.1, bf16[512,2304]{1,0:T(8,128)(2,1)S(1)} %copy-done), custom_call_target="tpu_custom_call" | custom-call | tf_op jit(solution)/shard_map/chain/pallas_call | solution.py:73
  (1 shorter events, 0.0 us)
Async XLA Ops:
  6.5 46.4 %all-gather.3.cloned.1.call-start = ((), (), s32[]{:S(2)}) async-start(), calls=%async_computation | async-start | bytes 2654208 | tf_op jit(solution)/shard_map/all_gather | solution.py:88
  52.9 1.7 %copy-start = (bf16[512,2304]{1,0:T(8,128)(2,1)S(1)}, bf16[512,2304]{1,0:T(8,128)(2,1)}, u32[]{:S(2)}) copy-start(bf16[512,2304]{1,0:T(8,128)(2,1)} %all-gather.3.cloned.1.call-done.gathered_ref) | copy-start | bytes 7077892
  54.6 0.8 %copy-start.1 = (bf16[64,512]{1,0:T(8,128)(2,1)S(1)}, bf16[64,512]{1,0:T(8,128)(2,1)}, u32[]{:S(2)}) copy-start(bf16[64,512]{1,0:T(8,128)(2,1)} %dense_rows.1.own_ref) | copy-start | bytes 196612
Sparse Core Ops, SparseCore 0:
  21.0 31.8 all-gather.2

commit v4 on v2

--- a/solution.py
+++ b/solution.py
@@ -6,9 +6,11 @@
 from jax.sharding import PartitionSpec as P
 
 
-def dense_rows_kernel(cols_ref, live_ref, tiles_ref, degrees_ref, rows_ref):
+def dense_rows_kernel(cols_ref, live_ref, tiles_ref, degrees_ref, features_ref, rows_ref):
     row_count, slots, tile_size = tiles_ref.shape
-    blocks = rows_ref.shape[1] // tile_size
+    nodes = row_count * lax.axis_size("shard")
+    blocks = nodes // tile_size
+    share = rows_ref.shape[1] - nodes
     block_row = lax.axis_index("shard") * row_count // tile_size
     live = live_ref[0, block_row]
     wide = row_count * slots
@@ -28,31 +30,87 @@
         pick = (column == b).astype(jnp.bfloat16)
         summed = jnp.dot(pick, tiles, preferred_element_type=jnp.float32)
         rows_ref[:, b * tile_size : (b + 1) * tile_size] = (summed * scale).astype(jnp.bfloat16)
+    if share:
+        shares = features_ref.shape[1] // share
+        first = pl.multiple_of(lax.rem(lax.axis_index("section"), shares) * share, 128)
+        rows_ref[:, nodes:] = features_ref[:, pl.ds(first, share)]
 
 
-def dense_rows(tile_cols, live_tiles, tile_rows, degrees, nodes):
+def dense_rows(tile_cols, live_tiles, tile_rows, degrees, features, share):
     row_count = tile_rows.shape[0]
+    nodes = row_count * lax.axis_size("shard")
     return pl.pallas_call(
         dense_rows_kernel,
-        out_shape=jax.ShapeDtypeStruct((row_count, nodes), jnp.bfloat16),
-        in_specs=[
-            pl.BlockSpec(memory_space=pltpu.SMEM),
-            pl.BlockSpec(memory_space=pltpu.SMEM),
-            pl.BlockSpec(memory_space=pltpu.VMEM),
-            pl.BlockSpec(memory_space=pltpu.VMEM),
-        ],
+        out_shape=jax.ShapeDtypeStruct((row_count, nodes + share), jnp.bfloat16),
+        in_specs=[pl.BlockSpec(memory_space=pltpu.SMEM)] * 2 + [pl.BlockSpec(memory_space=pltpu.VMEM)] * 3,
         out_specs=pl.BlockSpec(memory_space=pltpu.VMEM),
         name="dense_rows",
-    )(tile_cols, live_tiles, tile_rows, degrees)
+    )(tile_cols, live_tiles, tile_rows, degrees, features)
 
 
-def per_device(features, tile_cols, live_tiles, tile_values, degrees):
+def chain_kernel(own_ref, here_ref, there_ref, out_ref, halves):
+    chips, relations, row_count, both_widths = here_ref.shape
+    nodes = 2 * chips * row_count
+    share = both_widths - nodes
+    section = lax.axis_index("section")
+
+    def run(even_ref, odd_ref):
+        def rows_of(relation, columns):
+            parts = []
+            for chip in range(chips):
+                parts += [even_ref[chip, relation, :, columns], odd_ref[chip, relation, :, columns]]
+            return jnp.concatenate(parts, axis=0)
+
+        halves[:row_count] = own_ref[:, :nodes]
+        halves[row_count:] = jnp.zeros((row_count, nodes), jnp.bfloat16)
+
+        def times(i, carry):
+            matrix = rows_of(section - 1 - i, slice(0, nodes))
+            both = jnp.dot(halves[...], matrix, preferred_element_type=jnp.float32)
+            product = both[:row_count] + both[row_count:]
+            high = product.astype(jnp.bfloat16)
+            halves[:row_count] = high
+            halves[row_count:] = (product - high.astype(jnp.float32)).astype(jnp.bfloat16)
+            return carry
+
+        lax.fori_loop(0, section, times, 0)
+        for part in range(relations):
+            slab = rows_of(part, slice(nodes, both_widths))
+            both = jnp.dot(halves[...], slab, preferred_element_type=jnp.float32)
+            out_ref[:, part * share : (part + 1) * share] = (both[:row_count] + both[row_count:]).astype(jnp.bfloat16)
+
+    core = lax.rem(lax.axis_index("shard"), 2)
+    pl.when(core == 0)(lambda: run(here_ref, there_ref))
+    pl.when(core == 1)(lambda: run(there_ref, here_ref))
+
+
+def chain(own, here, there, width):
+    row_count = own.shape[0]
+    nodes = row_count * lax.axis_size("shard")
+    return pl.pallas_call(
+        chain_kernel,
+        out_shape=jax.ShapeDtypeStruct((row_count, width), jnp.bfloat16),
+        in_specs=[pl.BlockSpec(memory_space=pltpu.VMEM)] * 3,
+        out_specs=pl.BlockSpec(memory_space=pltpu.VMEM),
+        scratch_shapes=[pltpu.VMEM((2 * row_count, nodes), jnp.bfloat16)],
+        compiler_params=pltpu.CompilerParams(vmem_limit_bytes=32 * 1024 * 1024),
+        name="chain",
+    )(own, here, there)
+
+
+def by_products(own, width):
+    sections, shards = lax.axis_size("section"), lax.axis_size("shard")
+    relations = lax.all_gather(own, "section", axis=0, tiled=False)[: sections - 1]
+    same_core = [list(range(core, shards, 2)) for core in range(2)]
+    here = lax.all_gather(relations, "shard", axis=0, tiled=False, axis_index_groups=same_core)
+    there = lax.ppermute(here, "shard", [(i, i ^ 1) for i in range(shards)])
+    return chain(own, here, there, width)
+
+
+def by_hops(features, own):
     sections = lax.axis_size("section")
     part = features.shape[1] // sections
-    row_count = features.shape[0]
-    nodes = row_count * lax.axis_size("shard")
     piece = lax.dynamic_slice_in_dim(features, lax.axis_index("section") * part, part, axis=1)
-    own = dense_rows(tile_cols, live_tiles, tile_values[0], degrees, nodes)
     relations = lax.all_gather(own, "section", axis=0, tiled=False)
     pieces = []
     for hop in range(sections):
@@ -60,7 +118,17 @@
         piece = jnp.dot(relations[hop], slab, preferred_element_type=jnp.float32).astype(jnp.bfloat16)
         pieces.append(piece)
     mine = lax.all_to_all(jnp.stack(pieces), "section", split_axis=0, concat_axis=0, tiled=True)
-    return jnp.swapaxes(mine, 0, 1).reshape(row_count, sections * part)[None]
+    return jnp.swapaxes(mine, 0, 1).reshape(features.shape)
+
+
+def per_device(features, tile_cols, live_tiles, tile_values, degrees):
+    row_count, width = features.shape
+    sections = lax.axis_size("section")
+    products = row_count * lax.axis_size("shard") <= width and width % (sections - 1) == 0
+    share = width // (sections - 1) if products else 0
+    own = dense_rows(tile_cols, live_tiles, tile_values[0], degrees, features, share)
+    out = by_products(own, width) if products else by_hops(features, own)
+    return out[None]
 
 
 def solution(mesh):

time: 79.3 us -> 63.9 us (0.81)
  blocking collectives: 75.3 us -> 11.4 us
  waiting for transfers between devices: 0 us -> 33.9 us
  between operations: 0.02 us -> 13.4 us
  local copies, waits for them, and re-layouts: 0.98 us -> 2.03 us
  Pallas kernels: 1.98 us -> 2.91 us
    all_gather x5 -> x1, blocking collectives: 67.8 us -> 11.4 us  [by_products(): lax.all_gather(own, 'section', axis=0, tiled=False)[:sections - 1]]
    all_gather x0 -> x1, waiting for transfers between devices: none -> 30.9 us  [by_products(): lax.all_gather(relations, 'shard', axis=0, tiled=False, axis_index_groups...]
    all_to_all x1 -> x0, blocking collectives: 7.55 us -> none  [per_device(): lax.all_to_all(jnp.stack(pieces), 'section', split_axis=0, concat_axis=0,...]
    ppermute x0 -> x1, waiting for transfers between devices: none -> 3.06 us  [by_products(): there = lax.ppermute(here, 'shard', [(i, i ^ 1) for i in range(shards)])]
    unnamed x2 -> x4, local copies, waits for them, and re-layouts: 0.01 us -> 1.27 us
    pallas_call x0 -> x1, Pallas kernels: none -> 0.92 us  [chain(): pl.pallas_call(chain_kernel, out_shape=jax.ShapeDtypeStruct((row_count, w...]
  transfers between devices with their start and end apart: 0 -> 2, of which waited for: 0 -> 2; matrix products, arithmetic and copies ran while one was open for 0% -> 0% of each run, Pallas kernels for 0% -> 0%
where the time goes in v4:
time: 63.9 us; the launch traced here: 63.7 us
  waiting for transfers between devices  33.9 us (53%)
  between operations  13.4 us (21%)
  blocking collectives  11.4 us (18%)
  Pallas kernels  2.91 us (5%)
  local copies, waits for them, and re-layouts  2.03 us (3%)
    all_gather x1, waiting for transfers between devices, by_products(): lax.all_gather(relations, 'shard', axis=0, tiled=False, axis_index_groups...  30.9 us
    all_gather x1, blocking collectives, by_products(): lax.all_gather(own, 'section', axis=0, tiled=False)[:sections - 1]  11.4 us
    ppermute x1, waiting for transfers between devices, by_products(): there = lax.ppermute(here, 'shard', [(i, i ^ 1) for i in range(shards)])  3.06 us
    pallas_call x1, Pallas kernels, dense_rows(): pl.pallas_call(dense_rows_kernel, out_shape=jax.ShapeDtypeStruct((row_cou...  1.98 us
  transfers between devices with their start and end apart: 2, of which 2 were waited for; matrix products, arithmetic and copies ran while one was open for 0% of the time, Pallas kernels for 0%

profile of v4, /device:TPU:0, one launch (start us, length us, event | category | flops | bytes accessed | tf_op | source)
XLA Modules:
  0.0 63.7 jit_solution(9083139026826243413)
XLA Ops:
  6.5 0.0 all-gather.4.cloned.1.call-start
  6.5 2.0 %dense_rows.1.own_ref = bf16[64,768]{1,0:T(8,128)(2,1)} custom-call(s32[1,4,16]{2,1,0:T(4,128)} %cols_ref.1, s32[1,4]{1,0:T(1,128)} %live_ref.1, bf16[64,16,128]{2,1,0:T(8,128)(2,1)} %bitcast.7, s32[1,64]{1,0:T(1,128)} %degrees_ref.1, bf16[64,768]{1,0:T(8,128)(2,1)} %features_ref.1), custom_call_target="tpu_custom_call" | custom-call | tf_op jit(solution)/shard_map/dense_rows/pallas_call | solution.py:42
  8.5 0.0 copy-start.1
  8.5 11.4 %all-gather = bf16[256,768]{1,0:T(8,128)(2,1)S(1)} all-gather(bf16[64,768]{1,0:T(8,128)(2,1)} %dense_rows.1.own_ref), channel_id=2, replica_groups=mesh['section'=4,'shard'=8] {'section'}, dimensions={0}, use_global_device_ids=true | all-gather | bytes 491520 | tf_op jit(solution)/shard_map/all_gather | solution.py:103
  19.9 0.8 %slice.5 = bf16[192,768]{1,0:T(8,128)(2,1)} slice(bf16[256,768]{1,0:T(8,128)(2,1)S(1)} %all-gather), slice={[0:192], [0:768]} | slice | bytes 589824 | tf_op jit(solution)/shard_map/slice | solution.py:103
  20.7 0.0 all-gather.4.cloned.1.call-update
  20.7 30.9 %all-gather.4.cloned.1.call-done = bf16[12,64,768]{2,1,0:T(8,128)(2,1)} async-done(((bf16[3,64,768]{2,1,0:T(8,128)(2,1)}), bf16[12,64,768]{2,1,0:T(8,128)(2,1)}) %all-gather.4.cloned.1.call-update) | async-done | bytes 1179664 | tf_op jit(solution)/shard_map/all_gather | solution.py:105
  51.6 0.0 collective-permute-start
  51.6 3.1 %collective-permute-done.there_ref = bf16[4,3,64,768]{3,2,1,0:T(8,128)(2,1)S(1)} collective-permute-done((bf16[4,3,64,768]{3,2,1,0:T(8,128)(2,1)}, bf16[4,3,64,768]{3,2,1,0:T(8,128)(2,1)S(1)}, u32[]{:S(2)}, u32[]{:S(2)}) %collective-permute-start) | collective-permute-done | bytes 1179680 | tf_op jit(solution)/shard_map/ppermute | solution.py:106
  54.7 0.0 copy-done.1
  54.7 0.0 copy-start
  54.7 1.3 %copy-done = bf16[12,64,768]{2,1,0:T(8,128)(2,1)S(1)} copy-done((bf16[12,64,768]{2,1,0:T(8,128)(2,1)S(1)}, bf16[12,64,768]{2,1,0:T(8,128)(2,1)}, u32[]{:S(2)}) %copy-start) | copy-done | bytes 1179672
  55.9 0.9 %chain.1 = bf16[64,768]{1,0:T(8,128)(2,1)} custom-call(bf16[64,768]{1,0:T(8,128)(2,1)S(1)} %copy-done.1, bf16[4,3,64,768]{3,2,1,0:T(8,128)(2,1)S(1)} %bitcast.5, bf16[4,3,64,768]{3,2,1,0:T(8,128)(2,1)S(1)} %collective-permute-done.there_ref), custom_call_target="tpu_custom_call" | custom-call | tf_op jit(solution)/shard_map/chain/pallas_call | solution.py:90
Async XLA Ops:
  6.5 45.1 %all-gather.4.cloned.1.call-start = ((), (), s32[]{:S(2)}) async-start(), calls=%async_computation | async-start | bytes 1474560 | tf_op jit(solution)/shard_map/all_gather | solution.py:105
  8.5 46.1 %copy-start.1 = (bf16[64,768]{1,0:T(8,128)(2,1)S(1)}, bf16[64,768]{1,0:T(8,128)(2,1)}, u32[]{:S(2)}) copy-start(bf16[64,768]{1,0:T(8,128)(2,1)} %dense_rows.1.own_ref) | copy-start | bytes 294916
  51.6 3.1 %collective-permute-start = (bf16[4,3,64,768]{3,2,1,0:T(8,128)(2,1)}, bf16[4,3,64,768]{3,2,1,0:T(8,128)(2,1)S(1)}, u32[]{:S(2)}, u32[]{:S(2)}) collective-permute-start(bf16[4,3,64,768]{3,2,1,0:T(8,128)(2,1)} %bitcast.4), channel_id=1, source_target_pairs={{0,1},{1,0},{2,3},{3,2},{4,5},{5,4},{6,7},{7,6},{8,9},{9,8},{10,11... | collective-permute-start | bytes 3538952 | tf_op jit(solution)/shard_map/ppermute | solution.py:106
  54.7 1.3 %copy-start = (bf16[12,64,768]{2,1,0:T(8,128)(2,1)S(1)}, bf16[12,64,768]{2,1,0:T(8,128)(2,1)}, u32[]{:S(2)}) copy-start(bf16[12,64,768]{2,1,0:T(8,128)(2,1)} %all-gather.4.cloned.1.call-done) | copy-start | bytes 3538948
Sparse Core Ops, SparseCore 0:
  20.9 30.6 all-gather.3

commit v5 on v2

--- a/solution.py
+++ b/solution.py
@@ -46,13 +46,71 @@
     )(tile_cols, live_tiles, tile_rows, degrees)
 
 
-def per_device(features, tile_cols, live_tiles, tile_values, degrees):
+def chain_kernel(own_ref, here_ref, there_ref, slab_here_ref, slab_there_ref, out_ref, halves):
+    chips, _, row_count, nodes = here_ref.shape
+    section, shard = lax.axis_index("section"), lax.axis_index("shard")
+    chip, core = lax.div(shard, 2), lax.rem(shard, 2)
+
+    def run(even_ref, odd_ref, slab_even_ref, slab_odd_ref):
+        halves[:row_count] = own_ref[...]
+        halves[row_count:] = jnp.zeros((row_count, nodes), jnp.bfloat16)
+
+        def times(i, carry):
+            parts = []
+            for at in range(chips):
+                parts += [even_ref[at, section - 1 - i], odd_ref[at, section - 1 - i]]
+            both = jnp.dot(halves[...], jnp.concatenate(parts, axis=0), preferred_element_type=jnp.float32)
+            product = both[:row_count] + both[row_count:]
+            high = product.astype(jnp.bfloat16)
+            halves[:row_count] = high
+            halves[row_count:] = (product - high.astype(jnp.float32)).astype(jnp.bfloat16)
+            return carry
+
+        lax.fori_loop(0, section, times, 0)
+        parts = []
+        for at in range(chips):
+            back = lax.rem(chip - at + chips, chips)
+            parts += [slab_even_ref[back], slab_odd_ref[back]]
+        both = jnp.dot(halves[...], jnp.concatenate(parts, axis=0), preferred_element_type=jnp.float32)
+        out_ref[...] = (both[:row_count] + both[row_count:]).astype(jnp.bfloat16)
+
+    pl.when(core == 0)(lambda: run(here_ref, there_ref, slab_here_ref, slab_there_ref))
+    pl.when(core == 1)(lambda: run(there_ref, here_ref, slab_there_ref, slab_here_ref))
+
+
+def chain(own, here, there, slab_here, slab_there):
+    row_count, nodes = own.shape
+    return pl.pallas_call(
+        chain_kernel,
+        out_shape=jax.ShapeDtypeStruct((row_count, slab_here.shape[2]), jnp.bfloat16),
+        in_specs=[pl.BlockSpec(memory_space=pltpu.VMEM)] * 5,
+        out_specs=pl.BlockSpec(memory_space=pltpu.VMEM),
+        scratch_shapes=[pltpu.VMEM((2 * row_count, nodes), jnp.bfloat16)],
+        compiler_params=pltpu.CompilerParams(vmem_limit_bytes=32 * 1024 * 1024),
+        name="chain",
+    )(own, here, there, slab_here, slab_there)
+
+
+def by_products(features, own):
+    sections, shards = lax.axis_size("section"), lax.axis_size("shard")
+    chips = shards // 2
+    slabs = [features]
+    for back in range(1, chips):
+        slabs.append(lax.ppermute(features, "shard", [(i, (i + 2 * back) % shards) for i in range(shards)]))
+    relations = lax.all_gather(own, "section", axis=0, tiled=False)[: sections - 1]
+    same_core = [list(range(core, shards, 2)) for core in range(2)]
+    here = lax.all_gather(relations, "shard", axis=0, tiled=False, axis_index_groups=same_core)
+    swap = [(i, i ^ 1) for i in range(shards)]
+    slab_here = jnp.stack(slabs)
+    slab_there = lax.ppermute(slab_here, "shard", swap)
+    there = lax.ppermute(here, "shard", swap)
+    return chain(own, here, there, slab_here, slab_there)
+
+
+def by_hops(features, own):
     sections = lax.axis_size("section")
     part = features.shape[1] // sections
-    row_count = features.shape[0]
-    nodes = row_count * lax.axis_size("shard")
     piece = lax.dynamic_slice_in_dim(features, lax.axis_index("section") * part, part, axis=1)
-    own = dense_rows(tile_cols, live_tiles, tile_values[0], degrees, nodes)
     relations = lax.all_gather(own, "section", axis=0, tiled=False)
     pieces = []
     for hop in range(sections):
@@ -60,7 +118,14 @@
         piece = jnp.dot(relations[hop], slab, preferred_element_type=jnp.float32).astype(jnp.bfloat16)
         pieces.append(piece)
     mine = lax.all_to_all(jnp.stack(pieces), "section", split_axis=0, concat_axis=0, tiled=True)
-    return jnp.swapaxes(mine, 0, 1).reshape(row_count, sections * part)[None]
+    return jnp.swapaxes(mine, 0, 1).reshape(features.shape)
+
+
+def per_device(features, tile_cols, live_tiles, tile_values, degrees):
+    nodes = features.shape[0] * lax.axis_size("shard")
+    own = dense_rows(tile_cols, live_tiles, tile_values[0], degrees, nodes)
+    plan = by_products if nodes <= features.shape[1] else by_hops
+    return plan(features, own)[None]
 
 
 def solution(mesh):

time: 79.3 us -> 47 us (0.59)
  blocking collectives: 75.3 us -> 29.9 us
  waiting for transfers between devices: 0 us -> 9.96 us
  starting transfers between devices: 0 us -> 3.89 us
  local copies, waits for them, and re-layouts: 0.98 us -> 0.02 us
  Pallas kernels: 1.98 us -> 2.87 us
    all_gather x5 -> x2, blocking collectives: 67.8 us -> 29.9 us  [the longest x1 19.2 us: by_products(): lax.all_gather(relations, 'shard', axis=0, tiled=False, axis_index_groups...]
    ppermute x0 -> x5, waiting for transfers between devices: none -> 9.96 us  [the longest x3 8.24 us: by_products(): lax.ppermute(features, 'shard', [(i, (i + 2 * back) % shards) for i in ra...]
    all_to_all x1 -> x0, blocking collectives: 7.55 us -> none  [per_device(): lax.all_to_all(jnp.stack(pieces), 'section', split_axis=0, concat_axis=0,...]
    ppermute x0 -> x5, starting transfers between devices: none -> 3.89 us  [the longest x3 3.82 us: by_products(): lax.ppermute(features, 'shard', [(i, (i + 2 * back) % shards) for i in ra...]
    pallas_call x0 -> x1, Pallas kernels: none -> 0.93 us  [chain(): pl.pallas_call(chain_kernel, out_shape=jax.ShapeDtypeStruct((row_count, s...]
  transfers between devices with their start and end apart: 0 -> 5, of which waited for: 0 -> 3; matrix products, arithmetic and copies ran while one was open for 0% -> 0% of each run, Pallas kernels for 0% -> 0%
where the time goes in v5:
time: 47 us; the launch traced here: 46.8 us
  blocking collectives  29.9 us (64%)
  waiting for transfers between devices  9.96 us (21%)
  starting transfers between devices  3.89 us (8%)
  Pallas kernels  2.87 us (6%)
    all_gather x1, blocking collectives, by_products(): lax.all_gather(relations, 'shard', axis=0, tiled=False, axis_index_groups...  19.2 us
    all_gather x1, blocking collectives, by_products(): lax.all_gather(own, 'section', axis=0, tiled=False)[:sections - 1]  10.7 us
    ppermute x3, waiting for transfers between devices, by_products(): lax.ppermute(features, 'shard', [(i, (i + 2 * back) % shards) for i in ra...  8.24 us
    ppermute x3, starting transfers between devices, by_products(): lax.ppermute(features, 'shard', [(i, (i + 2 * back) % shards) for i in ra...  3.82 us
    pallas_call x1, Pallas kernels, dense_rows(): pl.pallas_call(dense_rows_kernel, out_shape=jax.ShapeDtypeStruct((row_cou...  1.94 us
    ppermute x1, waiting for transfers between devices, by_products(): slab_there = lax.ppermute(slab_here, 'shard', swap)  1.71 us
  transfers between devices with their start and end apart: 5, of which 3 were waited for; matrix products, arithmetic and copies ran while one was open for 0% of the time, Pallas kernels for 0%

profile of v5, /device:TPU:0, one launch (start us, length us, event | category | flops | bytes accessed | tf_op | source)
XLA Modules:
  0.0 46.8 jit_solution(18251386518036772598)
XLA Ops:
  0.0 1.9 %dense_rows.1.own_ref = bf16[64,512]{1,0:T(8,128)(2,1)} custom-call(s32[1,4,16]{2,1,0:T(4,128)} %cols_ref.1, s32[1,4]{1,0:T(1,128)} %live_ref.1, bf16[64,16,128]{2,1,0:T(8,128)(2,1)} %bitcast.11, s32[1,64]{1,0:T(1,128)} %degrees_ref.1), custom_call_target="tpu_custom_call" | custom-call | tf_op jit(solution)/shard_map/dense_rows/pallas_call | solution.py:35
  1.9 10.7 %all-gather = bf16[256,512]{1,0:T(8,128)(2,1)S(1)} all-gather(bf16[64,512]{1,0:T(8,128)(2,1)} %dense_rows.1.own_ref), channel_id=2, replica_groups=mesh['section'=4,'shard'=8] {'section'}, dimensions={0}, use_global_device_ids=true | all-gather | bytes 327680 | tf_op jit(solution)/shard_map/all_gather | solution.py:100
  12.7 0.0 copy-start.1
  12.7 19.2 %all-gather.1 = bf16[12,64,512]{2,1,0:T(8,128)(2,1)S(1)} all-gather(bf16[3,64,512]{2,1,0:T(8,128)(2,1)S(1)} %bitcast.10), channel_id=3, replica_groups={{0,2,4,6},{1,3,5,7},{8,10,12,14},{9,11,13,15},{16,18,20,22},{17,19,21,2..., dimensions={0}, use_global_device_ids=true | all-gather | bytes 983040 | tf_op jit(solution)/shard_map/all_gather | solution.py:102
  31.9 0.0 collective-permute-start
  31.9 0.0 copy-done.1
  31.9 0.0 collective-permute-start.1
  31.9 3.8 %collective-permute-start.3 = (bf16[64,768]{1,0:T(8,128)(2,1)S(1)}, bf16[64,768]{1,0:T(8,128)(2,1)S(1)}, u32[]{:S(2)}, u32[]{:S(2)}) collective-permute-start(bf16[64,768]{1,0:T(8,128)(2,1)S(1)} %copy-done.1), channel_id=1, source_target_pairs={{0,6},{1,7},{2,0},{3,1},{4,2},{5,3},{6,4},{7,5},{8,14},{9,15},{10,... | collective-permute-start | bytes 294920 | tf_op jit(solution)/shard_map/ppermute | solution.py:99
  35.7 0.0 collective-permute-start.2
  35.7 3.6 %collective-permute-done.1 = bf16[64,768]{1,0:T(8,128)(2,1)S(1)} collective-permute-done((bf16[64,768]{1,0:T(8,128)(2,1)S(1)}, bf16[64,768]{1,0:T(8,128)(2,1)S(1)}, u32[]{:S(2)}, u32[]{:S(2)}) %collective-permute-start.1) | collective-permute-done | bytes 98336 | tf_op jit(solution)/shard_map/ppermute | solution.py:99
  39.3 0.0 collective-permute-done.3
  39.3 4.6 %collective-permute-done.2 = bf16[64,768]{1,0:T(8,128)(2,1)S(1)} collective-permute-done((bf16[64,768]{1,0:T(8,128)(2,1)S(1)}, bf16[64,768]{1,0:T(8,128)(2,1)S(1)}, u32[]{:S(2)}, u32[]{:S(2)}) %collective-permute-start.2) | collective-permute-done | bytes 98336 | tf_op jit(solution)/shard_map/ppermute | solution.py:99
  44.0 0.0 copy-start
  44.0 0.1 pad_maximum_fusion.slab_here_ref
  44.0 0.1 collective-permute-start.4
  44.1 1.7 %collective-permute-done.4.slab_there_ref = bf16[4,64,768]{2,1,0:T(8,128)(2,1)S(1)} collective-permute-done((bf16[4,64,768]{2,1,0:T(8,128)(2,1)S(1)}, bf16[4,64,768]{2,1,0:T(8,128)(2,1)S(1)}, u32[]{:S(2)}, u32[]{:S(2)}) %collective-permute-start.4) | collective-permute-done | bytes 393248 | tf_op jit(solution)/shard_map/ppermute | solution.py:105
  45.8 0.0 collective-permute-done.there_ref
  45.8 0.0 copy-done
  45.8 0.9 %chain.1 = bf16[64,768]{1,0:T(8,128)(2,1)} custom-call(bf16[64,512]{1,0:T(8,128)(2,1)S(1)} %copy-done, bf16[4,3,64,512]{3,2,1,0:T(8,128)(2,1)S(1)} %bitcast.9, bf16[4,3,64,512]{3,2,1,0:T(8,128)(2,1)S(1)} %collective-permute-done.there_ref, bf16[4,64,768]{2,1,0:T(8,128)(2,1)S(1)} %pad_maximum_fusion.slab_here_ref, ...), custom_call_target="tpu_custom_call" | custom-call | tf_op jit(solution)/shard_map/chain/pallas_call | solution.py:83
  (1 shorter events, 0.0 us)
Async XLA Ops:
  12.7 19.2 %copy-start.1 = (bf16[64,768]{1,0:T(8,128)(2,1)S(1)}, bf16[64,768]{1,0:T(8,128)(2,1)}, u32[]{:S(2)}) copy-start(bf16[64,768]{1,0:T(8,128)(2,1)} %param.5) | copy-start | bytes 294916
  31.9 13.9 %collective-permute-start = (bf16[4,3,64,512]{3,2,1,0:T(8,128)(2,1)S(1)}, bf16[4,3,64,512]{3,2,1,0:T(8,128)(2,1)S(1)}, u32[]{:S(2)}, u32[]{:S(2)}) collective-permute-start(bf16[4,3,64,512]{3,2,1,0:T(8,128)(2,1)S(1)} %bitcast.8), channel_id=1, source_target_pairs={{0,1},{1,0},{2,3},{3,2},{4,5},{5,4},{6,7},{7,6},{8,9},{9,8},{10,11... | collective-permute-start | bytes 2359304 | tf_op jit(solution)/shard_map/ppermute | solution.py:106
  31.9 7.4 %collective-permute-start.1 = (bf16[64,768]{1,0:T(8,128)(2,1)S(1)}, bf16[64,768]{1,0:T(8,128)(2,1)S(1)}, u32[]{:S(2)}, u32[]{:S(2)}) collective-permute-start(bf16[64,768]{1,0:T(8,128)(2,1)S(1)} %copy-done.1), channel_id=1, source_target_pairs={{0,2},{1,3},{2,4},{3,5},{4,6},{5,7},{6,0},{7,1},{8,10},{9,11},{10,... | collective-permute-start | bytes 294920 | tf_op jit(solution)/shard_map/ppermute | solution.py:99
  31.9 7.4 %collective-permute-start.3 = (bf16[64,768]{1,0:T(8,128)(2,1)S(1)}, bf16[64,768]{1,0:T(8,128)(2,1)S(1)}, u32[]{:S(2)}, u32[]{:S(2)}) collective-permute-start(bf16[64,768]{1,0:T(8,128)(2,1)S(1)} %copy-done.1), channel_id=1, source_target_pairs={{0,6},{1,7},{2,0},{3,1},{4,2},{5,3},{6,4},{7,5},{8,14},{9,15},{10,... | collective-permute-start | bytes 294920 | tf_op jit(solution)/shard_map/ppermute | solution.py:99
  35.7 8.2 %collective-permute-start.2 = (bf16[64,768]{1,0:T(8,128)(2,1)S(1)}, bf16[64,768]{1,0:T(8,128)(2,1)S(1)}, u32[]{:S(2)}, u32[]{:S(2)}) collective-permute-start(bf16[64,768]{1,0:T(8,128)(2,1)S(1)} %copy-done.1), channel_id=1, source_target_pairs={{0,4},{1,5},{2,6},{3,7},{4,0},{5,1},{6,2},{7,3},{8,12},{9,13},{10,... | collective-permute-start | bytes 294920 | tf_op jit(solution)/shard_map/ppermute | solution.py:99
  44.0 1.9 %copy-start = (bf16[64,512]{1,0:T(8,128)(2,1)S(1)}, bf16[64,512]{1,0:T(8,128)(2,1)}, u32[]{:S(2)}) copy-start(bf16[64,512]{1,0:T(8,128)(2,1)} %dense_rows.1.own_ref) | copy-start | bytes 196612
  44.0 1.8 %collective-permute-start.4 = (bf16[4,64,768]{2,1,0:T(8,128)(2,1)S(1)}, bf16[4,64,768]{2,1,0:T(8,128)(2,1)S(1)}, u32[]{:S(2)}, u32[]{:S(2)}) collective-permute-start(bf16[4,64,768]{2,1,0:T(8,128)(2,1)S(1)} %pad_maximum_fusion.slab_here_ref), channel_id=1, source_target_pairs={{0,1},{1,0},{2,3},{3,2},{4,5},{5,4},{6,7},{7,6},{8,9},{9,8},{10,11... | collective-permute-start | bytes 1179656 | tf_op jit(solution)/shard_map/ppermute | solution.py:105

commit v6 on v5

--- a/solution.py
+++ b/solution.py
@@ -98,6 +98,7 @@
     for back in range(1, chips):
         slabs.append(lax.ppermute(features, "shard", [(i, (i + 2 * back) % shards) for i in range(shards)]))
     relations = lax.all_gather(own, "section", axis=0, tiled=False)[: sections - 1]
+    relations, slabs = lax.optimization_barrier((relations, slabs))
     same_core = [list(range(core, shards, 2)) for core in range(2)]
     here = lax.all_gather(relations, "shard", axis=0, tiled=False, axis_index_groups=same_core)
     swap = [(i, i ^ 1) for i in range(shards)]

time: 47 us -> 39.6 us (0.84)
  waiting for transfers between devices: 9.96 us -> 2.22 us
  starting transfers between devices: 3.89 us -> 8.42 us
  blocking collectives: 29.9 us -> 25.7 us
    ppermute x3, waiting for transfers between devices: 8.24 us -> 0.01 us  [by_products(): lax.ppermute(features, 'shard', [(i, (i + 2 * back) % shards) for i in ra...]
    ppermute x3, starting transfers between devices: 3.82 us -> 7.86 us  [by_products(): lax.ppermute(features, 'shard', [(i, (i + 2 * back) % shards) for i in ra...]
    all_gather x1, blocking collectives: 19.2 us -> 16.4 us  [by_products(): lax.all_gather(relations, 'shard', axis=0, tiled=False, axis_index_groups...]
    all_gather x1, blocking collectives: 10.7 us -> 9.26 us  [by_products(): lax.all_gather(own, 'section', axis=0, tiled=False)[:sections - 1]]
    ppermute x1, waiting for transfers between devices: 1.71 us -> 2.21 us  [by_products(): slab_there = lax.ppermute(slab_here, 'shard', swap)]
    ppermute x1, starting transfers between devices: 0.07 us -> 0.56 us  [by_products(): slab_there = lax.ppermute(slab_here, 'shard', swap)]
  transfers between devices with their start and end apart: 5 -> 5, of which waited for: 3 -> 1; matrix products, arithmetic and copies ran while one was open for 0% -> 0% of each run, Pallas kernels for 0% -> 5%
where the time goes in v6:
time: 39.6 us; the launch traced here: 39.4 us
  blocking collectives  25.7 us (65%)
  starting transfers between devices  8.42 us (21%)
  Pallas kernels  2.87 us (7%)
  waiting for transfers between devices  2.22 us (6%)
    all_gather x1, blocking collectives, by_products(): lax.all_gather(relations, 'shard', axis=0, tiled=False, axis_index_groups...  16.4 us
    all_gather x1, blocking collectives, by_products(): lax.all_gather(own, 'section', axis=0, tiled=False)[:sections - 1]  9.26 us
    ppermute x3, starting transfers between devices, by_products(): lax.ppermute(features, 'shard', [(i, (i + 2 * back) % shards) for i in ra...  7.86 us
    ppermute x1, waiting for transfers between devices, by_products(): slab_there = lax.ppermute(slab_here, 'shard', swap)  2.21 us
    pallas_call x1, Pallas kernels, dense_rows(): pl.pallas_call(dense_rows_kernel, out_shape=jax.ShapeDtypeStruct((row_cou...  1.94 us
    pallas_call x1, Pallas kernels, chain(): pl.pallas_call(chain_kernel, out_shape=jax.ShapeDtypeStruct((row_count, s...  0.93 us
  transfers between devices with their start and end apart: 5, of which 1 were waited for; matrix products, arithmetic and copies ran while one was open for 0% of the time, Pallas kernels for 5%

profile of v6, /device:TPU:0, one launch (start us, length us, event | category | flops | bytes accessed | tf_op | source)
XLA Modules:
  0.0 39.4 jit_solution(10608649701229277599)
XLA Ops:
  0.0 4.0 %collective-permute-start.1 = (bf16[64,768]{1,0:T(8,128)(2,1)}, bf16[64,768]{1,0:T(8,128)(2,1)S(1)}, u32[]{:S(2)}, u32[]{:S(2)}) collective-permute-start(bf16[64,768]{1,0:T(8,128)(2,1)} %param.5), channel_id=1, source_target_pairs={{0,4},{1,5},{2,6},{3,7},{4,0},{5,1},{6,2},{7,3},{8,12},{9,13},{10,... | collective-permute-start | bytes 294920 | tf_op jit(solution)/shard_map/ppermute | solution.py:99
  4.0 1.6 %collective-permute-start = (bf16[64,768]{1,0:T(8,128)(2,1)}, bf16[64,768]{1,0:T(8,128)(2,1)S(1)}, u32[]{:S(2)}, u32[]{:S(2)}) collective-permute-start(bf16[64,768]{1,0:T(8,128)(2,1)} %param.5), channel_id=1, source_target_pairs={{0,2},{1,3},{2,4},{3,5},{4,6},{5,7},{6,0},{7,1},{8,10},{9,11},{10,... | collective-permute-start | bytes 294920 | tf_op jit(solution)/shard_map/ppermute | solution.py:99
  5.6 2.2 %collective-permute-start.2 = (bf16[64,768]{1,0:T(8,128)(2,1)}, bf16[64,768]{1,0:T(8,128)(2,1)S(1)}, u32[]{:S(2)}, u32[]{:S(2)}) collective-permute-start(bf16[64,768]{1,0:T(8,128)(2,1)} %param.5), channel_id=1, source_target_pairs={{0,6},{1,7},{2,0},{3,1},{4,2},{5,3},{6,4},{7,5},{8,14},{9,15},{10,... | collective-permute-start | bytes 294920 | tf_op jit(solution)/shard_map/ppermute | solution.py:99
  7.9 1.9 %dense_rows.1.own_ref = bf16[64,512]{1,0:T(8,128)(2,1)} custom-call(s32[1,4,16]{2,1,0:T(4,128)} %cols_ref.1, s32[1,4]{1,0:T(1,128)} %live_ref.1, bf16[64,16,128]{2,1,0:T(8,128)(2,1)} %bitcast.11, s32[1,64]{1,0:T(1,128)} %degrees_ref.1), custom_call_target="tpu_custom_call" | custom-call | tf_op jit(solution)/shard_map/dense_rows/pallas_call | solution.py:35
  9.8 9.3 %all-gather = bf16[256,512]{1,0:T(8,128)(2,1)S(1)} all-gather(bf16[64,512]{1,0:T(8,128)(2,1)} %dense_rows.1.own_ref), channel_id=2, replica_groups=mesh['section'=4,'shard'=8] {'section'}, dimensions={0}, use_global_device_ids=true | all-gather | bytes 327680 | tf_op jit(solution)/shard_map/all_gather | solution.py:100
  19.1 0.0 collective-permute-done.1
  19.1 0.0 collective-permute-done
  19.1 0.0 collective-permute-done.2
  19.1 0.0 copy-start.1
  19.1 16.4 %all-gather.1 = bf16[12,64,512]{2,1,0:T(8,128)(2,1)S(1)} all-gather(bf16[3,64,512]{2,1,0:T(8,128)(2,1)S(1)} %bitcast.10), channel_id=3, replica_groups={{0,2,4,6},{1,3,5,7},{8,10,12,14},{9,11,13,15},{16,18,20,22},{17,19,21,2..., dimensions={0}, use_global_device_ids=true | all-gather | bytes 983040 | tf_op jit(solution)/shard_map/all_gather | solution.py:103
  35.6 0.0 collective-permute-start.3
  35.6 0.0 copy-done.1
  35.6 0.0 copy-start
  35.6 0.1 pad_maximum_fusion.slab_here_ref
  35.7 0.6 %collective-permute-start.4 = (bf16[4,64,768]{2,1,0:T(8,128)(2,1)S(1)}, bf16[4,64,768]{2,1,0:T(8,128)(2,1)S(1)}, u32[]{:S(2)}, u32[]{:S(2)}) collective-permute-start(bf16[4,64,768]{2,1,0:T(8,128)(2,1)S(1)} %pad_maximum_fusion.slab_here_ref), channel_id=1, source_target_pairs={{0,1},{1,0},{2,3},{3,2},{4,5},{5,4},{6,7},{7,6},{8,9},{9,8},{10,11... | collective-permute-start | bytes 1179656 | tf_op jit(solution)/shard_map/ppermute | solution.py:106
  36.2 2.2 %collective-permute-done.4.slab_there_ref = bf16[4,64,768]{2,1,0:T(8,128)(2,1)S(1)} collective-permute-done((bf16[4,64,768]{2,1,0:T(8,128)(2,1)S(1)}, bf16[4,64,768]{2,1,0:T(8,128)(2,1)S(1)}, u32[]{:S(2)}, u32[]{:S(2)}) %collective-permute-start.4) | collective-permute-done | bytes 393248 | tf_op jit(solution)/shard_map/ppermute | solution.py:106
  38.4 0.0 collective-permute-done.3.there_ref
  38.4 0.0 copy-done
  38.4 0.9 %chain.1 = bf16[64,768]{1,0:T(8,128)(2,1)} custom-call(bf16[64,512]{1,0:T(8,128)(2,1)S(1)} %copy-done, bf16[4,3,64,512]{3,2,1,0:T(8,128)(2,1)S(1)} %bitcast.9, bf16[4,3,64,512]{3,2,1,0:T(8,128)(2,1)S(1)} %collective-permute-done.3.there_ref, bf16[4,64,768]{2,1,0:T(8,128)(2,1)S(1)} %pad_maximum_fusion.slab_here_ref, ...), custom_call_target="tpu_custom_call" | custom-call | tf_op jit(solution)/shard_map/chain/pallas_call | solution.py:83
  (1 shorter events, 0.0 us)
Async XLA Ops:
  0.0 19.1 %collective-permute-start.1 = (bf16[64,768]{1,0:T(8,128)(2,1)}, bf16[64,768]{1,0:T(8,128)(2,1)S(1)}, u32[]{:S(2)}, u32[]{:S(2)}) collective-permute-start(bf16[64,768]{1,0:T(8,128)(2,1)} %param.5), channel_id=1, source_target_pairs={{0,4},{1,5},{2,6},{3,7},{4,0},{5,1},{6,2},{7,3},{8,12},{9,13},{10,... | collective-permute-start | bytes 294920 | tf_op jit(solution)/shard_map/ppermute | solution.py:99
  4.0 15.1 %collective-permute-start = (bf16[64,768]{1,0:T(8,128)(2,1)}, bf16[64,768]{1,0:T(8,128)(2,1)S(1)}, u32[]{:S(2)}, u32[]{:S(2)}) collective-permute-start(bf16[64,768]{1,0:T(8,128)(2,1)} %param.5), channel_id=1, source_target_pairs={{0,2},{1,3},{2,4},{3,5},{4,6},{5,7},{6,0},{7,1},{8,10},{9,11},{10,... | collective-permute-start | bytes 294920 | tf_op jit(solution)/shard_map/ppermute | solution.py:99
  5.6 13.5 %collective-permute-start.2 = (bf16[64,768]{1,0:T(8,128)(2,1)}, bf16[64,768]{1,0:T(8,128)(2,1)S(1)}, u32[]{:S(2)}, u32[]{:S(2)}) collective-permute-start(bf16[64,768]{1,0:T(8,128)(2,1)} %param.5), channel_id=1, source_target_pairs={{0,6},{1,7},{2,0},{3,1},{4,2},{5,3},{6,4},{7,5},{8,14},{9,15},{10,... | collective-permute-start | bytes 294920 | tf_op jit(solution)/shard_map/ppermute | solution.py:99
  19.1 16.5 %copy-start.1 = (bf16[64,768]{1,0:T(8,128)(2,1)S(1)}, bf16[64,768]{1,0:T(8,128)(2,1)}, u32[]{:S(2)}) copy-start(bf16[64,768]{1,0:T(8,128)(2,1)} %param.5) | copy-start | bytes 294916
  35.6 2.9 %collective-permute-start.3 = (bf16[4,3,64,512]{3,2,1,0:T(8,128)(2,1)S(1)}, bf16[4,3,64,512]{3,2,1,0:T(8,128)(2,1)S(1)}, u32[]{:S(2)}, u32[]{:S(2)}) collective-permute-start(bf16[4,3,64,512]{3,2,1,0:T(8,128)(2,1)S(1)} %bitcast.8), channel_id=1, source_target_pairs={{0,1},{1,0},{2,3},{3,2},{4,5},{5,4},{6,7},{7,6},{8,9},{9,8},{10,11... | collective-permute-start | bytes 2359304 | tf_op jit(solution)/shard_map/ppermute | solution.py:107
  35.6 2.8 %copy-start = (bf16[64,512]{1,0:T(8,128)(2,1)S(1)}, bf16[64,512]{1,0:T(8,128)(2,1)}, u32[]{:S(2)}) copy-start(bf16[64,512]{1,0:T(8,128)(2,1)} %dense_rows.1.own_ref) | copy-start | bytes 196612
  35.7 2.8 %collective-permute-start.4 = (bf16[4,64,768]{2,1,0:T(8,128)(2,1)S(1)}, bf16[4,64,768]{2,1,0:T(8,128)(2,1)S(1)}, u32[]{:S(2)}, u32[]{:S(2)}) collective-permute-start(bf16[4,64,768]{2,1,0:T(8,128)(2,1)S(1)} %pad_maximum_fusion.slab_here_ref), channel_id=1, source_target_pairs={{0,1},{1,0},{2,3},{3,2},{4,5},{5,4},{6,7},{7,6},{8,9},{9,8},{10,11... | collective-permute-start | bytes 1179656 | tf_op jit(solution)/shard_map/ppermute | solution.py:106

commit v7 on v5

--- a/solution.py
+++ b/solution.py
@@ -46,65 +46,69 @@
     )(tile_cols, live_tiles, tile_rows, degrees)
 
 
-def chain_kernel(own_ref, here_ref, there_ref, slab_here_ref, slab_there_ref, out_ref, halves):
-    chips, _, row_count, nodes = here_ref.shape
+def chain_kernel(own_ref, slab_here_ref, slab_there_ref, *refs):
+    relation_refs, out_ref, halves = refs[:-2], refs[-2], refs[-1]
+    row_count, nodes = own_ref.shape
+    chips = slab_here_ref.shape[0]
     section, shard = lax.axis_index("section"), lax.axis_index("shard")
-    chip, core = lax.div(shard, 2), lax.rem(shard, 2)
+    chip, first_core = lax.div(shard, 2), lax.rem(shard, 2) == 0
 
-    def run(even_ref, odd_ref, slab_even_ref, slab_odd_ref):
-        halves[:row_count] = own_ref[...]
-        halves[row_count:] = jnp.zeros((row_count, nodes), jnp.bfloat16)
+    def in_order(pairs):
+        parts = []
+        for here, there in pairs:
+            parts += [jnp.where(first_core, here, there), jnp.where(first_core, there, here)]
+        return jnp.concatenate(parts, axis=0)
 
-        def times(i, carry):
-            parts = []
-            for at in range(chips):
-                parts += [even_ref[at, section - 1 - i], odd_ref[at, section - 1 - i]]
-            both = jnp.dot(halves[...], jnp.concatenate(parts, axis=0), preferred_element_type=jnp.float32)
+    halves[:row_count] = own_ref[...]
+    halves[row_count:] = jnp.zeros((row_count, nodes), jnp.bfloat16)
+    for back in range(len(relation_refs) // 2):
+
+        @pl.when(section > back)
+        def _(here_ref=relation_refs[2 * back], there_ref=relation_refs[2 * back + 1]):
+            rows = [slice(at * row_count, (at + 1) * row_count) for at in range(chips)]
+            matrix = in_order([(here_ref[at], there_ref[at]) for at in rows])
+            both = jnp.dot(halves[...], matrix, preferred_element_type=jnp.float32)
             product = both[:row_count] + both[row_count:]
             high = product.astype(jnp.bfloat16)
             halves[:row_count] = high
             halves[row_count:] = (product - high.astype(jnp.float32)).astype(jnp.bfloat16)
-            return carry
 
-        lax.fori_loop(0, section, times, 0)
-        parts = []
-        for at in range(chips):
-            back = lax.rem(chip - at + chips, chips)
-            parts += [slab_even_ref[back], slab_odd_ref[back]]
-        both = jnp.dot(halves[...], jnp.concatenate(parts, axis=0), preferred_element_type=jnp.float32)
-        out_ref[...] = (both[:row_count] + both[row_count:]).astype(jnp.bfloat16)
-
-    pl.when(core == 0)(lambda: run(here_ref, there_ref, slab_here_ref, slab_there_ref))
-    pl.when(core == 1)(lambda: run(there_ref, here_ref, slab_there_ref, slab_here_ref))
+    at = [lax.rem(chip - place + chips, chips) for place in range(chips)]
+    slab = in_order([(slab_here_ref[back], slab_there_ref[back]) for back in at])
+    both = jnp.dot(halves[...], slab, preferred_element_type=jnp.float32)
+    out_ref[...] = (both[:row_count] + both[row_count:]).astype(jnp.bfloat16)
 
 
-def chain(own, here, there, slab_here, slab_there):
+def chain(own, slab_here, slab_there, relations):
     row_count, nodes = own.shape
     return pl.pallas_call(
         chain_kernel,
         out_shape=jax.ShapeDtypeStruct((row_count, slab_here.shape[2]), jnp.bfloat16),
-        in_specs=[pl.BlockSpec(memory_space=pltpu.VMEM)] * 5,
+        in_specs=[pl.BlockSpec(memory_space=pltpu.VMEM)] * (3 + len(relations)),
         out_specs=pl.BlockSpec(memory_space=pltpu.VMEM),
         scratch_shapes=[pltpu.VMEM((2 * row_count, nodes), jnp.bfloat16)],
         compiler_params=pltpu.CompilerParams(vmem_limit_bytes=32 * 1024 * 1024),
         name="chain",
-    )(own, here, there, slab_here, slab_there)
+    )(own, slab_here, slab_there, *relations)
 
 
 def by_products(features, own):
     sections, shards = lax.axis_size("section"), lax.axis_size("shard")
     chips = shards // 2
+    swap = [(i, i ^ 1) for i in range(shards)]
+    same_core = [list(range(core, shards, 2)) for core in range(2)]
+    mine = lax.all_gather(own, "shard", axis=0, tiled=True, axis_index_groups=same_core)
+    mine, features = lax.optimization_barrier((mine, features))
+    relations = []
+    for back in range(1, sections):
+        here = lax.ppermute(mine, "section", [(i, i + back) for i in range(sections - back)])
+        relations += [here, lax.ppermute(here, "shard", swap)]
     slabs = [features]
     for back in range(1, chips):
         slabs.append(lax.ppermute(features, "shard", [(i, (i + 2 * back) % shards) for i in range(shards)]))
-    relations = lax.all_gather(own, "section", axis=0, tiled=False)[: sections - 1]
-    same_core = [list(range(core, shards, 2)) for core in range(2)]
-    here = lax.all_gather(relations, "shard", axis=0, tiled=False, axis_index_groups=same_core)
-    swap = [(i, i ^ 1) for i in range(shards)]
     slab_here = jnp.stack(slabs)
     slab_there = lax.ppermute(slab_here, "shard", swap)
-    there = lax.ppermute(here, "shard", swap)
-    return chain(own, here, there, slab_here, slab_there)
+    return chain(own, slab_here, slab_there, relations)
 
 
 def by_hops(features, own):

time: 47 us -> 39.6 us (0.84)
  the two profiles are of different devices: /device:TPU:0 before, /device:TPU:13 now
where the time goes in v7:
time: 39.6 us; the launch traced here: 39.4 us
  starting transfers between devices  21.7 us (55%)
  blocking collectives  11.5 us (29%)
  Pallas kernels  3.38 us (9%)
  waiting for transfers between devices  2.66 us (7%)
    all_gather x1, blocking collectives, by_products(): lax.all_gather(own, 'shard', axis=0, tiled=True, axis_index_groups=same_c...  11.5 us
    ppermute x3, starting transfers between devices, by_products(): relations += [here, lax.ppermute(here, 'shard', swap)]  6.09 us
    ppermute x3, starting transfers between devices, by_products(): lax.ppermute(mine, 'section', [(i, i + back) for i in range(sections - ba...  5.69 us
    ppermute x1, starting transfers between devices, by_products(): slab_there = lax.ppermute(slab_here, 'shard', swap)  5.42 us
    ppermute x3, starting transfers between devices, by_products(): lax.ppermute(features, 'shard', [(i, (i + 2 * back) % shards) for i in ra...  4.54 us
    pallas_call x1, Pallas kernels, dense_rows(): pl.pallas_call(dense_rows_kernel, out_shape=jax.ShapeDtypeStruct((row_cou...  1.94 us
    ppermute x3, waiting for transfers between devices, by_products(): relations += [here, lax.ppermute(here, 'shard', swap)]  1.52 us
    pallas_call x1, Pallas kernels, chain(): pl.pallas_call(chain_kernel, out_shape=jax.ShapeDtypeStruct((row_count, s...  1.43 us
  transfers between devices with their start and end apart: 10, of which 3 were waited for; matrix products, arithmetic and copies ran while one was open for 0% of the time, Pallas kernels for 0%

profile of v7, /device:TPU:13, one launch (start us, length us, event | category | flops | bytes accessed | tf_op | source)
XLA Modules:
  0.0 39.4 jit_solution(12251660433432665284)
XLA Ops:
  0.0 1.9 %dense_rows.1.own_ref = bf16[64,512]{1,0:T(8,128)(2,1)} custom-call(s32[1,4,16]{2,1,0:T(4,128)} %cols_ref.1, s32[1,4]{1,0:T(1,128)} %live_ref.1, bf16[64,16,128]{2,1,0:T(8,128)(2,1)} %bitcast.6, s32[1,64]{1,0:T(1,128)} %degrees_ref.1), custom_call_target="tpu_custom_call" | custom-call | tf_op jit(solution)/shard_map/dense_rows/pallas_call | solution.py:35
  1.9 11.5 %all_gather.3 = bf16[256,512]{1,0:T(8,128)(2,1)S(1)} all-gather(bf16[64,512]{1,0:T(8,128)(2,1)} %dense_rows.1.own_ref), channel_id=1, replica_groups={{0,2,4,6},{1,3,5,7},{8,10,12,14},{9,11,13,15},{16,18,20,22},{17,19,21,2..., dimensions={0}, use_global_device_ids=true | all-gather | bytes 327680 | tf_op jit(solution)/shard_map/all_gather | solution.py:100
  13.4 1.5 %collective-permute-start.2 = (bf16[64,768]{1,0:T(8,128)(2,1)S(1)}, bf16[64,768]{1,0:T(8,128)(2,1)S(1)}, u32[]{:S(2)}, u32[]{:S(2)}) collective-permute-start(bf16[64,768]{1,0:T(8,128)(2,1)S(1)} %copy-done.1), channel_id=1, source_target_pairs={{0,6},{1,7},{2,0},{3,1},{4,2},{5,3},{6,4},{7,5},{8,14},{9,15},{10,... | collective-permute-start | bytes 294920 | tf_op jit(solution)/shard_map/ppermute | solution.py:108
  14.9 0.7 %collective-permute-start.1 = (bf16[64,768]{1,0:T(8,128)(2,1)S(1)}, bf16[64,768]{1,0:T(8,128)(2,1)S(1)}, u32[]{:S(2)}, u32[]{:S(2)}) collective-permute-start(bf16[64,768]{1,0:T(8,128)(2,1)S(1)} %copy-done.1), channel_id=1, source_target_pairs={{0,4},{1,5},{2,6},{3,7},{4,0},{5,1},{6,2},{7,3},{8,12},{9,13},{10,... | collective-permute-start | bytes 294920 | tf_op jit(solution)/shard_map/ppermute | solution.py:108
  15.6 2.3 %collective-permute-start = (bf16[64,768]{1,0:T(8,128)(2,1)S(1)}, bf16[64,768]{1,0:T(8,128)(2,1)S(1)}, u32[]{:S(2)}, u32[]{:S(2)}) collective-permute-start(bf16[64,768]{1,0:T(8,128)(2,1)S(1)} %copy-done.1), channel_id=1, source_target_pairs={{0,2},{1,3},{2,4},{3,5},{4,6},{5,7},{6,0},{7,1},{8,10},{9,11},{10,... | collective-permute-start | bytes 294920 | tf_op jit(solution)/shard_map/ppermute | solution.py:108
  18.0 0.7 %collective-permute-start.8 = (bf16[256,512]{1,0:T(8,128)(2,1)S(1)}, bf16[256,512]{1,0:T(8,128)(2,1)S(1)}, u32[]{:S(2)}, u32[]{:S(2)}) collective-permute-start(bf16[256,512]{1,0:T(8,128)(2,1)S(1)} %all_gather.3), channel_id=1, source_target_pairs={{0,24},{1,25},{2,26},{3,27},{4,28},{5,29},{6,30},{7,31}} | collective-permute-start | bytes 786440 | tf_op jit(solution)/shard_map/ppermute | solution.py:104
  18.6 1.3 %collective-permute-start.6 = (bf16[256,512]{1,0:T(8,128)(2,1)S(1)}, bf16[256,512]{1,0:T(8,128)(2,1)S(1)}, u32[]{:S(2)}, u32[]{:S(2)}) collective-permute-start(bf16[256,512]{1,0:T(8,128)(2,1)S(1)} %all_gather.3), channel_id=1, source_target_pairs={{0,16},{8,24},{1,17},{9,25},{2,18},{10,26},{3,19},{11,27},{4,20},{... | collective-permute-start | bytes 786440 | tf_op jit(solution)/shard_map/ppermute | solution.py:104
  19.9 0.0 collective-permute-done.2
  20.0 3.7 %collective-permute-start.4 = (bf16[256,512]{1,0:T(8,128)(2,1)S(1)}, bf16[256,512]{1,0:T(8,128)(2,1)S(1)}, u32[]{:S(2)}, u32[]{:S(2)}) collective-permute-start(bf16[256,512]{1,0:T(8,128)(2,1)S(1)} %all_gather.3), channel_id=1, source_target_pairs={{0,8},{8,16},{16,24},{1,9},{9,17},{17,25},{2,10},{10,18},{18,26},{... | collective-permute-start | bytes 786440 | tf_op jit(solution)/shard_map/ppermute | solution.py:104
  23.7 0.0 collective-permute-done.1
  23.7 0.0 collective-permute-done
  23.7 0.0 copy-start
  23.7 0.1 pad_maximum_fusion.slab_here_ref
  23.8 5.4 %collective-permute-start.3 = (bf16[4,64,768]{2,1,0:T(8,128)(2,1)S(1)}, bf16[4,64,768]{2,1,0:T(8,128)(2,1)S(1)}, u32[]{:S(2)}, u32[]{:S(2)}) collective-permute-start(bf16[4,64,768]{2,1,0:T(8,128)(2,1)S(1)} %pad_maximum_fusion.slab_here_ref), channel_id=1, source_target_pairs={{0,1},{1,0},{2,3},{3,2},{4,5},{5,4},{6,7},{7,6},{8,9},{9,8},{10,11... | collective-permute-start | bytes 1179656 | tf_op jit(solution)/shard_map/ppermute | solution.py:110
  29.2 0.0 collective-permute-done.8.refs_4_
  29.2 0.1 collective-permute-start.9
  29.3 1.1 %collective-permute-done.6.refs_2_ = bf16[256,512]{1,0:T(8,128)(2,1)S(1)} collective-permute-done((bf16[256,512]{1,0:T(8,128)(2,1)S(1)}, bf16[256,512]{1,0:T(8,128)(2,1)S(1)}, u32[]{:S(2)}, u32[]{:S(2)}) %collective-permute-start.6) | collective-permute-done | bytes 262176 | tf_op jit(solution)/shard_map/ppermute | solution.py:104
  30.4 6.0 %collective-permute-start.7 = (bf16[256,512]{1,0:T(8,128)(2,1)S(1)}, bf16[256,512]{1,0:T(8,128)(2,1)S(1)}, u32[]{:S(2)}, u32[]{:S(2)}) collective-permute-start(bf16[256,512]{1,0:T(8,128)(2,1)S(1)} %collective-permute-done.6.refs_2_), channel_id=1, source_target_pairs={{0,1},{1,0},{2,3},{3,2},{4,5},{5,4},{6,7},{7,6},{8,9},{9,8},{10,11... | collective-permute-start | bytes 786440 | tf_op jit(solution)/shard_map/ppermute | solution.py:105
  36.4 0.0 collective-permute-done.4.refs_0_
  36.4 0.0 collective-permute-start.5
  36.4 0.0 collective-permute-done.3.slab_there_ref
  36.5 1.1 %collective-permute-done.7.refs_3_ = bf16[256,512]{1,0:T(8,128)(2,1)S(1)} collective-permute-done((bf16[256,512]{1,0:T(8,128)(2,1)S(1)}, bf16[256,512]{1,0:T(8,128)(2,1)S(1)}, u32[]{:S(2)}, u32[]{:S(2)}) %collective-permute-start.7) | collective-permute-done | bytes 262176 | tf_op jit(solution)/shard_map/ppermute | solution.py:105
  37.6 0.4 collective-permute-done.5.refs_1_
  38.0 1.4 %chain.1 = bf16[64,768]{1,0:T(8,128)(2,1)} custom-call(bf16[64,512]{1,0:T(8,128)(2,1)S(1)} %copy-done, bf16[4,64,768]{2,1,0:T(8,128)(2,1)S(1)} %pad_maximum_fusion.slab_here_ref, bf16[4,64,768]{2,1,0:T(8,128)(2,1)S(1)} %collective-permute-done.3.slab_there_ref, bf16[256,512]{1,0:T(8,128)(2,1)S(1)} %collective-permute-done.4.refs_0_, ...), custom_call_target="tpu_custom_call" | custom-call | tf_op jit(solution)/shard_map/chain/pallas_call | solution.py:84
  (4 shorter events, 0.0 us)
Async XLA Ops:
  1.9 11.5 %copy-start.1 = (bf16[64,768]{1,0:T(8,128)(2,1)S(1)}, bf16[64,768]{1,0:T(8,128)(2,1)}, u32[]{:S(2)}) copy-start(bf16[64,768]{1,0:T(8,128)(2,1)} %param.5) | copy-start | bytes 294916
  13.4 6.5 %collective-permute-start.2 = (bf16[64,768]{1,0:T(8,128)(2,1)S(1)}, bf16[64,768]{1,0:T(8,128)(2,1)S(1)}, u32[]{:S(2)}, u32[]{:S(2)}) collective-permute-start(bf16[64,768]{1,0:T(8,128)(2,1)S(1)} %copy-done.1), channel_id=1, source_target_pairs={{0,6},{1,7},{2,0},{3,1},{4,2},{5,3},{6,4},{7,5},{8,14},{9,15},{10,... | collective-permute-start | bytes 294920 | tf_op jit(solution)/shard_map/ppermute | solution.py:108
  14.9 8.8 %collective-permute-start.1 = (bf16[64,768]{1,0:T(8,128)(2,1)S(1)}, bf16[64,768]{1,0:T(8,128)(2,1)S(1)}, u32[]{:S(2)}, u32[]{:S(2)}) collective-permute-start(bf16[64,768]{1,0:T(8,128)(2,1)S(1)} %copy-done.1), channel_id=1, source_target_pairs={{0,4},{1,5},{2,6},{3,7},{4,0},{5,1},{6,2},{7,3},{8,12},{9,13},{10,... | collective-permute-start | bytes 294920 | tf_op jit(solution)/shard_map/ppermute | solution.py:108
  15.6 8.1 %collective-permute-start = (bf16[64,768]{1,0:T(8,128)(2,1)S(1)}, bf16[64,768]{1,0:T(8,128)(2,1)S(1)}, u32[]{:S(2)}, u32[]{:S(2)}) collective-permute-start(bf16[64,768]{1,0:T(8,128)(2,1)S(1)} %copy-done.1), channel_id=1, source_target_pairs={{0,2},{1,3},{2,4},{3,5},{4,6},{5,7},{6,0},{7,1},{8,10},{9,11},{10,... | collective-permute-start | bytes 294920 | tf_op jit(solution)/shard_map/ppermute | solution.py:108
  18.0 11.2 %collective-permute-start.8 = (bf16[256,512]{1,0:T(8,128)(2,1)S(1)}, bf16[256,512]{1,0:T(8,128)(2,1)S(1)}, u32[]{:S(2)}, u32[]{:S(2)}) collective-permute-start(bf16[256,512]{1,0:T(8,128)(2,1)S(1)} %all_gather.3), channel_id=1, source_target_pairs={{0,24},{1,25},{2,26},{3,27},{4,28},{5,29},{6,30},{7,31}} | collective-permute-start | bytes 786440 | tf_op jit(solution)/shard_map/ppermute | solution.py:104
  18.6 11.8 %collective-permute-start.6 = (bf16[256,512]{1,0:T(8,128)(2,1)S(1)}, bf16[256,512]{1,0:T(8,128)(2,1)S(1)}, u32[]{:S(2)}, u32[]{:S(2)}) collective-permute-start(bf16[256,512]{1,0:T(8,128)(2,1)S(1)} %all_gather.3), channel_id=1, source_target_pairs={{0,16},{8,24},{1,17},{9,25},{2,18},{10,26},{3,19},{11,27},{4,20},{... | collective-permute-start | bytes 786440 | tf_op jit(solution)/shard_map/ppermute | solution.py:104
  20.0 16.5 %collective-permute-start.4 = (bf16[256,512]{1,0:T(8,128)(2,1)S(1)}, bf16[256,512]{1,0:T(8,128)(2,1)S(1)}, u32[]{:S(2)}, u32[]{:S(2)}) collective-permute-start(bf16[256,512]{1,0:T(8,128)(2,1)S(1)} %all_gather.3), channel_id=1, source_target_pairs={{0,8},{8,16},{16,24},{1,9},{9,17},{17,25},{2,10},{10,18},{18,26},{... | collective-permute-start | bytes 786440 | tf_op jit(solution)/shard_map/ppermute | solution.py:104
  23.7 14.3 %copy-start = (bf16[64,512]{1,0:T(8,128)(2,1)S(1)}, bf16[64,512]{1,0:T(8,128)(2,1)}, u32[]{:S(2)}) copy-start(bf16[64,512]{1,0:T(8,128)(2,1)} %dense_rows.1.own_ref) | copy-start | bytes 196612
  23.8 12.7 %collective-permute-start.3 = (bf16[4,64,768]{2,1,0:T(8,128)(2,1)S(1)}, bf16[4,64,768]{2,1,0:T(8,128)(2,1)S(1)}, u32[]{:S(2)}, u32[]{:S(2)}) collective-permute-start(bf16[4,64,768]{2,1,0:T(8,128)(2,1)S(1)} %pad_maximum_fusion.slab_here_ref), channel_id=1, source_target_pairs={{0,1},{1,0},{2,3},{3,2},{4,5},{5,4},{6,7},{7,6},{8,9},{9,8},{10,11... | collective-permute-start | bytes 1179656 | tf_op jit(solution)/shard_map/ppermute | solution.py:110
  29.2 7.2 %collective-permute-start.9 = (bf16[256,512]{1,0:T(8,128)(2,1)S(1)}, bf16[256,512]{1,0:T(8,128)(2,1)S(1)}, u32[]{:S(2)}, u32[]{:S(2)}) collective-permute-start(bf16[256,512]{1,0:T(8,128)(2,1)S(1)} %collective-permute-done.8.refs_4_), channel_id=1, source_target_pairs={{0,1},{1,0},{2,3},{3,2},{4,5},{5,4},{6,7},{7,6},{8,9},{9,8},{10,11... | collective-permute-start | bytes 786440 | tf_op jit(solution)/shard_map/ppermute | solution.py:105
  30.4 7.2 %collective-permute-start.7 = (bf16[256,512]{1,0:T(8,128)(2,1)S(1)}, bf16[256,512]{1,0:T(8,128)(2,1)S(1)}, u32[]{:S(2)}, u32[]{:S(2)}) collective-permute-start(bf16[256,512]{1,0:T(8,128)(2,1)S(1)} %collective-permute-done.6.refs_2_), channel_id=1, source_target_pairs={{0,1},{1,0},{2,3},{3,2},{4,5},{5,4},{6,7},{7,6},{8,9},{9,8},{10,11... | collective-permute-start | bytes 786440 | tf_op jit(solution)/shard_map/ppermute | solution.py:105
  36.4 1.5 %collective-permute-start.5 = (bf16[256,512]{1,0:T(8,128)(2,1)S(1)}, bf16[256,512]{1,0:T(8,128)(2,1)S(1)}, u32[]{:S(2)}, u32[]{:S(2)}) collective-permute-start(bf16[256,512]{1,0:T(8,128)(2,1)S(1)} %collective-permute-done.4.refs_0_), channel_id=1, source_target_pairs={{0,1},{1,0},{2,3},{3,2},{4,5},{5,4},{6,7},{7,6},{8,9},{9,8},{10,11... | collective-permute-start | bytes 786440 | tf_op jit(solution)/shard_map/ppermute | solution.py:105

commit v8 on v7

--- a/solution.py
+++ b/solution.py
@@ -52,6 +52,7 @@
     chips = slab_here_ref.shape[0]
     section, shard = lax.axis_index("section"), lax.axis_index("shard")
     chip, first_core = lax.div(shard, 2), lax.rem(shard, 2) == 0
+    backs = [lax.rem(chip - place + chips, chips) for place in range(chips)]
 
     def in_order(pairs):
         parts = []
@@ -65,16 +66,14 @@
 
         @pl.when(section > back)
         def _(here_ref=relation_refs[2 * back], there_ref=relation_refs[2 * back + 1]):
-            rows = [slice(at * row_count, (at + 1) * row_count) for at in range(chips)]
-            matrix = in_order([(here_ref[at], there_ref[at]) for at in rows])
+            matrix = in_order([(here_ref[at], there_ref[at]) for at in backs])
             both = jnp.dot(halves[...], matrix, preferred_element_type=jnp.float32)
             product = both[:row_count] + both[row_count:]
             high = product.astype(jnp.bfloat16)
             halves[:row_count] = high
             halves[row_count:] = (product - high.astype(jnp.float32)).astype(jnp.bfloat16)
 
-    at = [lax.rem(chip - place + chips, chips) for place in range(chips)]
-    slab = in_order([(slab_here_ref[back], slab_there_ref[back]) for back in at])
+    slab = in_order([(slab_here_ref[at], slab_there_ref[at]) for at in backs])
     both = jnp.dot(halves[...], slab, preferred_element_type=jnp.float32)
     out_ref[...] = (both[:row_count] + both[row_count:]).astype(jnp.bfloat16)
 
@@ -96,18 +95,19 @@
     sections, shards = lax.axis_size("section"), lax.axis_size("shard")
     chips = shards // 2
     swap = [(i, i ^ 1) for i in range(shards)]
-    same_core = [list(range(core, shards, 2)) for core in range(2)]
-    mine = lax.all_gather(own, "shard", axis=0, tiled=True, axis_index_groups=same_core)
-    mine, features = lax.optimization_barrier((mine, features))
+
+    def along_z(value, back):
+        return lax.ppermute(value, "shard", [(i, (i + 2 * back) % shards) for i in range(shards)])
+
+    rows = [own] + [along_z(own, back) for back in range(1, chips)]
+    rows[1], features = lax.optimization_barrier((rows[1], features))
+    slab_here = jnp.stack([features] + [along_z(features, back) for back in range(1, chips)])
+    slab_there = lax.ppermute(slab_here, "shard", swap)
+    mine = jnp.stack(rows)
     relations = []
     for back in range(1, sections):
         here = lax.ppermute(mine, "section", [(i, i + back) for i in range(sections - back)])
         relations += [here, lax.ppermute(here, "shard", swap)]
-    slabs = [features]
-    for back in range(1, chips):
-        slabs.append(lax.ppermute(features, "shard", [(i, (i + 2 * back) % shards) for i in range(shards)]))
-    slab_here = jnp.stack(slabs)
-    slab_there = lax.ppermute(slab_here, "shard", swap)
     return chain(own, slab_here, slab_there, relations)
 
 

time: 39.6 us -> 36.2 us (0.914)
  the two profiles are of different devices: /device:TPU:13 before, /device:TPU:29 now
where the time goes in v8:
time: 36.2 us; the launch traced here: 36 us
  waiting for transfers between devices  16.2 us (45%)
  starting transfers between devices  15.4 us (43%)
  Pallas kernels  3.41 us (9%)
  other arithmetic  0.93 us (3%)
    ppermute x3, waiting for transfers between devices, by_products(): lax.ppermute(mine, 'section', [(i, i + back) for i in range(sections - ba...  7.75 us
    ppermute x6, waiting for transfers between devices, along_z(): lax.ppermute(value, 'shard', [(i, (i + 2 * back) % shards) for i in range...  6.89 us
    ppermute x3, starting transfers between devices, by_products(): lax.ppermute(mine, 'section', [(i, i + back) for i in range(sections - ba...  5.7 us
    ppermute x6, starting transfers between devices, along_z(): lax.ppermute(value, 'shard', [(i, (i + 2 * back) % shards) for i in range...  4.79 us
    ppermute x3, starting transfers between devices, by_products(): relations += [here, lax.ppermute(here, 'shard', swap)]  2.59 us
    ppermute x1, starting transfers between devices, by_products(): slab_there = lax.ppermute(slab_here, 'shard', swap)  2.3 us
    pallas_call x1, Pallas kernels, dense_rows(): pl.pallas_call(dense_rows_kernel, out_shape=jax.ShapeDtypeStruct((row_cou...  1.98 us
    ppermute x3, waiting for transfers between devices, by_products(): relations += [here, lax.ppermute(here, 'shard', swap)]  1.52 us
  transfers between devices with their start and end apart: 13, of which 5 were waited for; matrix products, arithmetic and copies ran while one was open for 3% of the time, Pallas kernels for 0%

profile of v8, /device:TPU:29, one launch (start us, length us, event | category | flops | bytes accessed | tf_op | source)
XLA Modules:
  0.0 36.0 jit_solution(71737113421500149)
XLA Ops:
  0.0 2.0 %dense_rows.1.own_ref = bf16[64,512]{1,0:T(8,128)(2,1)} custom-call(s32[1,4,16]{2,1,0:T(4,128)} %cols_ref.1, s32[1,4]{1,0:T(1,128)} %live_ref.1, bf16[64,16,128]{2,1,0:T(8,128)(2,1)} %bitcast.11, s32[1,64]{1,0:T(1,128)} %degrees_ref.1), custom_call_target="tpu_custom_call" | custom-call | tf_op jit(solution)/shard_map/dense_rows/pallas_call | solution.py:35
  2.0 1.5 %collective-permute-start.6 = (bf16[64,512]{1,0:T(8,128)(2,1)}, bf16[64,512]{1,0:T(8,128)(2,1)S(1)}, u32[]{:S(2)}, u32[]{:S(2)}) collective-permute-start(bf16[64,512]{1,0:T(8,128)(2,1)} %dense_rows.1.own_ref), channel_id=1, source_target_pairs={{0,6},{1,7},{2,0},{3,1},{4,2},{5,3},{6,4},{7,5},{8,14},{9,15},{10,... | collective-permute-start | bytes 196616 | tf_op jit(solution)/shard_map/ppermute | solution.py:100
  3.4 0.1 collective-permute-start.5
  3.5 1.8 %collective-permute-done = bf16[64,512]{1,0:T(8,128)(2,1)S(1)} collective-permute-done((bf16[64,512]{1,0:T(8,128)(2,1)}, bf16[64,512]{1,0:T(8,128)(2,1)S(1)}, u32[]{:S(2)}, u32[]{:S(2)}) %collective-permute-start) | collective-permute-done | bytes 65568 | tf_op jit(solution)/shard_map/ppermute | solution.py:100
  5.3 0.2 collective-permute-start.3
  5.5 2.0 %collective-permute-start.2 = (bf16[64,768]{1,0:T(8,128)(2,1)S(1)}, bf16[64,768]{1,0:T(8,128)(2,1)S(1)}, u32[]{:S(2)}, u32[]{:S(2)}) collective-permute-start(bf16[64,768]{1,0:T(8,128)(2,1)S(1)} %copy-done.1), channel_id=1, source_target_pairs={{0,4},{1,5},{2,6},{3,7},{4,0},{5,1},{6,2},{7,3},{8,12},{9,13},{10,... | collective-permute-start | bytes 294920 | tf_op jit(solution)/shard_map/ppermute | solution.py:100
  7.5 1.1 %collective-permute-start.1 = (bf16[64,768]{1,0:T(8,128)(2,1)S(1)}, bf16[64,768]{1,0:T(8,128)(2,1)S(1)}, u32[]{:S(2)}, u32[]{:S(2)}) collective-permute-start(bf16[64,768]{1,0:T(8,128)(2,1)S(1)} %copy-done.1), channel_id=1, source_target_pairs={{0,2},{1,3},{2,4},{3,5},{4,6},{5,7},{6,0},{7,1},{8,10},{9,11},{10,... | collective-permute-start | bytes 294920 | tf_op jit(solution)/shard_map/ppermute | solution.py:100
  8.6 0.0 collective-permute-done.6
  8.6 5.1 %collective-permute-done.5 = bf16[64,512]{1,0:T(8,128)(2,1)S(1)} collective-permute-done((bf16[64,512]{1,0:T(8,128)(2,1)}, bf16[64,512]{1,0:T(8,128)(2,1)S(1)}, u32[]{:S(2)}, u32[]{:S(2)}) %collective-permute-start.5) | collective-permute-done | bytes 65568 | tf_op jit(solution)/shard_map/ppermute | solution.py:100
  13.7 0.9 %pad_maximum_fusion.1 = bf16[4,64,512]{2,1,0:T(8,128)(2,1)S(1)} fusion(bf16[1,64,512]{2,1,0:T(8,128)(2,1)S(1)} %bitcast.17, bf16[1,64,512]{2,1,0:T(8,128)(2,1)S(1)} %bitcast.18, bf16[1,64,512]{2,1,0:T(8,128)(2,1)S(1)} %bitcast.16, bf16[1,64,512]{2,1,0:T(8,128)(2,1)} %bitcast.10), kind=kLoop, calls=%fused_computation.1 | loop fusion | flops 393216 | bytes 524288 | tf_op jit(solution)/shard_map/stack | solution.py:106
  14.5 0.7 %collective-permute-start.11 = (bf16[4,64,512]{2,1,0:T(8,128)(2,1)S(1)}, bf16[4,64,512]{2,1,0:T(8,128)(2,1)S(1)}, u32[]{:S(2)}, u32[]{:S(2)}) collective-permute-start(bf16[4,64,512]{2,1,0:T(8,128)(2,1)S(1)} %pad_maximum_fusion.1), channel_id=1, source_target_pairs={{0,24},{1,25},{2,26},{3,27},{4,28},{5,29},{6,30},{7,31}} | collective-permute-start | bytes 786440 | tf_op jit(solution)/shard_map/ppermute | solution.py:109
  15.2 1.3 %collective-permute-start.9 = (bf16[4,64,512]{2,1,0:T(8,128)(2,1)S(1)}, bf16[4,64,512]{2,1,0:T(8,128)(2,1)S(1)}, u32[]{:S(2)}, u32[]{:S(2)}) collective-permute-start(bf16[4,64,512]{2,1,0:T(8,128)(2,1)S(1)} %pad_maximum_fusion.1), channel_id=1, source_target_pairs={{0,16},{8,24},{1,17},{9,25},{2,18},{10,26},{3,19},{11,27},{4,20},{... | collective-permute-start | bytes 786440 | tf_op jit(solution)/shard_map/ppermute | solution.py:109
  16.5 0.0 collective-permute-done.3
  16.5 3.7 %collective-permute-start.7 = (bf16[4,64,512]{2,1,0:T(8,128)(2,1)S(1)}, bf16[4,64,512]{2,1,0:T(8,128)(2,1)S(1)}, u32[]{:S(2)}, u32[]{:S(2)}) collective-permute-start(bf16[4,64,512]{2,1,0:T(8,128)(2,1)S(1)} %pad_maximum_fusion.1), channel_id=1, source_target_pairs={{0,8},{8,16},{16,24},{1,9},{9,17},{17,25},{2,10},{10,18},{18,26},{... | collective-permute-start | bytes 786440 | tf_op jit(solution)/shard_map/ppermute | solution.py:109
  20.3 0.0 copy-start
  20.3 0.1 pad_maximum_fusion.slab_here_ref
  20.4 2.3 %collective-permute-start.4 = (bf16[4,64,768]{2,1,0:T(8,128)(2,1)S(1)}, bf16[4,64,768]{2,1,0:T(8,128)(2,1)S(1)}, u32[]{:S(2)}, u32[]{:S(2)}) collective-permute-start(bf16[4,64,768]{2,1,0:T(8,128)(2,1)S(1)} %pad_maximum_fusion.slab_here_ref), channel_id=1, source_target_pairs={{0,1},{1,0},{2,3},{3,2},{4,5},{5,4},{6,7},{7,6},{8,9},{9,8},{10,11... | collective-permute-start | bytes 1179656 | tf_op jit(solution)/shard_map/ppermute | solution.py:105
  22.7 0.1 collective-permute-start.12
  22.8 7.7 %collective-permute-done.9.refs_2_ = bf16[4,64,512]{2,1,0:T(8,128)(2,1)S(1)} collective-permute-done((bf16[4,64,512]{2,1,0:T(8,128)(2,1)S(1)}, bf16[4,64,512]{2,1,0:T(8,128)(2,1)S(1)}, u32[]{:S(2)}, u32[]{:S(2)}) %collective-permute-start.9) | collective-permute-done | bytes 262176 | tf_op jit(solution)/shard_map/ppermute | solution.py:109
  30.5 2.5 %collective-permute-start.10 = (bf16[4,64,512]{2,1,0:T(8,128)(2,1)S(1)}, bf16[4,64,512]{2,1,0:T(8,128)(2,1)S(1)}, u32[]{:S(2)}, u32[]{:S(2)}) collective-permute-start(bf16[4,64,512]{2,1,0:T(8,128)(2,1)S(1)} %collective-permute-done.9.refs_2_), channel_id=1, source_target_pairs={{0,1},{1,0},{2,3},{3,2},{4,5},{5,4},{6,7},{7,6},{8,9},{9,8},{10,11... | collective-permute-start | bytes 786440 | tf_op jit(solution)/shard_map/ppermute | solution.py:110
  33.0 0.0 collective-permute-start.8
  33.0 1.1 %collective-permute-done.10.refs_3_ = bf16[4,64,512]{2,1,0:T(8,128)(2,1)S(1)} collective-permute-done((bf16[4,64,512]{2,1,0:T(8,128)(2,1)S(1)}, bf16[4,64,512]{2,1,0:T(8,128)(2,1)S(1)}, u32[]{:S(2)}, u32[]{:S(2)}) %collective-permute-start.10) | collective-permute-done | bytes 262176 | tf_op jit(solution)/shard_map/ppermute | solution.py:110
  34.2 0.4 %collective-permute-done.8.refs_1_ = bf16[4,64,512]{2,1,0:T(8,128)(2,1)S(1)} collective-permute-done((bf16[4,64,512]{2,1,0:T(8,128)(2,1)S(1)}, bf16[4,64,512]{2,1,0:T(8,128)(2,1)S(1)}, u32[]{:S(2)}, u32[]{:S(2)}) %collective-permute-start.8) | collective-permute-done | bytes 262176 | tf_op jit(solution)/shard_map/ppermute | solution.py:110
  34.6 1.4 %chain.1 = bf16[64,768]{1,0:T(8,128)(2,1)} custom-call(bf16[64,512]{1,0:T(8,128)(2,1)S(1)} %copy-done, bf16[4,64,768]{2,1,0:T(8,128)(2,1)S(1)} %pad_maximum_fusion.slab_here_ref, bf16[4,64,768]{2,1,0:T(8,128)(2,1)S(1)} %collective-permute-done.4.slab_there_ref, bf16[4,64,512]{2,1,0:T(8,128)(2,1)S(1)} %collective-permute-done.7.refs_0_, ...), custom_call_target="tpu_custom_call" | custom-call | tf_op jit(solution)/shard_map/chain/pallas_call | solution.py:83
  (10 shorter events, 0.0 us)
Async XLA Ops:
  0.0 5.3 %copy-start.1 = (bf16[64,768]{1,0:T(8,128)(2,1)S(1)}, bf16[64,768]{1,0:T(8,128)(2,1)}, u32[]{:S(2)}) copy-start(bf16[64,768]{1,0:T(8,128)(2,1)} %param.5) | copy-start | bytes 294916
  2.0 3.3 %collective-permute-start = (bf16[64,512]{1,0:T(8,128)(2,1)}, bf16[64,512]{1,0:T(8,128)(2,1)S(1)}, u32[]{:S(2)}, u32[]{:S(2)}) collective-permute-start(bf16[64,512]{1,0:T(8,128)(2,1)} %dense_rows.1.own_ref), channel_id=1, source_target_pairs={{0,2},{1,3},{2,4},{3,5},{4,6},{5,7},{6,0},{7,1},{8,10},{9,11},{10,... | collective-permute-start | bytes 196616 | tf_op jit(solution)/shard_map/ppermute | solution.py:100
  2.0 6.6 %collective-permute-start.6 = (bf16[64,512]{1,0:T(8,128)(2,1)}, bf16[64,512]{1,0:T(8,128)(2,1)S(1)}, u32[]{:S(2)}, u32[]{:S(2)}) collective-permute-start(bf16[64,512]{1,0:T(8,128)(2,1)} %dense_rows.1.own_ref), channel_id=1, source_target_pairs={{0,6},{1,7},{2,0},{3,1},{4,2},{5,3},{6,4},{7,5},{8,14},{9,15},{10,... | collective-permute-start | bytes 196616 | tf_op jit(solution)/shard_map/ppermute | solution.py:100
  3.4 10.2 %collective-permute-start.5 = (bf16[64,512]{1,0:T(8,128)(2,1)}, bf16[64,512]{1,0:T(8,128)(2,1)S(1)}, u32[]{:S(2)}, u32[]{:S(2)}) collective-permute-start(bf16[64,512]{1,0:T(8,128)(2,1)} %dense_rows.1.own_ref), channel_id=1, source_target_pairs={{0,4},{1,5},{2,6},{3,7},{4,0},{5,1},{6,2},{7,3},{8,12},{9,13},{10,... | collective-permute-start | bytes 196616 | tf_op jit(solution)/shard_map/ppermute | solution.py:100
  5.3 11.2 %collective-permute-start.3 = (bf16[64,768]{1,0:T(8,128)(2,1)S(1)}, bf16[64,768]{1,0:T(8,128)(2,1)S(1)}, u32[]{:S(2)}, u32[]{:S(2)}) collective-permute-start(bf16[64,768]{1,0:T(8,128)(2,1)S(1)} %copy-done.1), channel_id=1, source_target_pairs={{0,6},{1,7},{2,0},{3,1},{4,2},{5,3},{6,4},{7,5},{8,14},{9,15},{10,... | collective-permute-start | bytes 294920 | tf_op jit(solution)/shard_map/ppermute | solution.py:100
  5.5 14.7 %collective-permute-start.2 = (bf16[64,768]{1,0:T(8,128)(2,1)S(1)}, bf16[64,768]{1,0:T(8,128)(2,1)S(1)}, u32[]{:S(2)}, u32[]{:S(2)}) collective-permute-start(bf16[64,768]{1,0:T(8,128)(2,1)S(1)} %copy-done.1), channel_id=1, source_target_pairs={{0,4},{1,5},{2,6},{3,7},{4,0},{5,1},{6,2},{7,3},{8,12},{9,13},{10,... | collective-permute-start | bytes 294920 | tf_op jit(solution)/shard_map/ppermute | solution.py:100
  7.5 12.8 %collective-permute-start.1 = (bf16[64,768]{1,0:T(8,128)(2,1)S(1)}, bf16[64,768]{1,0:T(8,128)(2,1)S(1)}, u32[]{:S(2)}, u32[]{:S(2)}) collective-permute-start(bf16[64,768]{1,0:T(8,128)(2,1)S(1)} %copy-done.1), channel_id=1, source_target_pairs={{0,2},{1,3},{2,4},{3,5},{4,6},{5,7},{6,0},{7,1},{8,10},{9,11},{10,... | collective-permute-start | bytes 294920 | tf_op jit(solution)/shard_map/ppermute | solution.py:100
  14.5 8.1 %collective-permute-start.11 = (bf16[4,64,512]{2,1,0:T(8,128)(2,1)S(1)}, bf16[4,64,512]{2,1,0:T(8,128)(2,1)S(1)}, u32[]{:S(2)}, u32[]{:S(2)}) collective-permute-start(bf16[4,64,512]{2,1,0:T(8,128)(2,1)S(1)} %pad_maximum_fusion.1), channel_id=1, source_target_pairs={{0,24},{1,25},{2,26},{3,27},{4,28},{5,29},{6,30},{7,31}} | collective-permute-start | bytes 786440 | tf_op jit(solution)/shard_map/ppermute | solution.py:109
  15.2 15.3 %collective-permute-start.9 = (bf16[4,64,512]{2,1,0:T(8,128)(2,1)S(1)}, bf16[4,64,512]{2,1,0:T(8,128)(2,1)S(1)}, u32[]{:S(2)}, u32[]{:S(2)}) collective-permute-start(bf16[4,64,512]{2,1,0:T(8,128)(2,1)S(1)} %pad_maximum_fusion.1), channel_id=1, source_target_pairs={{0,16},{8,24},{1,17},{9,25},{2,18},{10,26},{3,19},{11,27},{4,20},{... | collective-permute-start | bytes 786440 | tf_op jit(solution)/shard_map/ppermute | solution.py:109
  16.5 16.5 %collective-permute-start.7 = (bf16[4,64,512]{2,1,0:T(8,128)(2,1)S(1)}, bf16[4,64,512]{2,1,0:T(8,128)(2,1)S(1)}, u32[]{:S(2)}, u32[]{:S(2)}) collective-permute-start(bf16[4,64,512]{2,1,0:T(8,128)(2,1)S(1)} %pad_maximum_fusion.1), channel_id=1, source_target_pairs={{0,8},{8,16},{16,24},{1,9},{9,17},{17,25},{2,10},{10,18},{18,26},{... | collective-permute-start | bytes 786440 | tf_op jit(solution)/shard_map/ppermute | solution.py:109
  20.3 14.3 %copy-start = (bf16[64,512]{1,0:T(8,128)(2,1)S(1)}, bf16[64,512]{1,0:T(8,128)(2,1)}, u32[]{:S(2)}) copy-start(bf16[64,512]{1,0:T(8,128)(2,1)} %dense_rows.1.own_ref) | copy-start | bytes 196612
  20.4 12.7 %collective-permute-start.4 = (bf16[4,64,768]{2,1,0:T(8,128)(2,1)S(1)}, bf16[4,64,768]{2,1,0:T(8,128)(2,1)S(1)}, u32[]{:S(2)}, u32[]{:S(2)}) collective-permute-start(bf16[4,64,768]{2,1,0:T(8,128)(2,1)S(1)} %pad_maximum_fusion.slab_here_ref), channel_id=1, source_target_pairs={{0,1},{1,0},{2,3},{3,2},{4,5},{5,4},{6,7},{7,6},{8,9},{9,8},{10,11... | collective-permute-start | bytes 1179656 | tf_op jit(solution)/shard_map/ppermute | solution.py:105
  22.7 10.3 %collective-permute-start.12 = (bf16[4,64,512]{2,1,0:T(8,128)(2,1)S(1)}, bf16[4,64,512]{2,1,0:T(8,128)(2,1)S(1)}, u32[]{:S(2)}, u32[]{:S(2)}) collective-permute-start(bf16[4,64,512]{2,1,0:T(8,128)(2,1)S(1)} %collective-permute-done.11.refs_4_), channel_id=1, source_target_pairs={{0,1},{1,0},{2,3},{3,2},{4,5},{5,4},{6,7},{7,6},{8,9},{9,8},{10,11... | collective-permute-start | bytes 786440 | tf_op jit(solution)/shard_map/ppermute | solution.py:110
  30.5 3.7 %collective-permute-start.10 = (bf16[4,64,512]{2,1,0:T(8,128)(2,1)S(1)}, bf16[4,64,512]{2,1,0:T(8,128)(2,1)S(1)}, u32[]{:S(2)}, u32[]{:S(2)}) collective-permute-start(bf16[4,64,512]{2,1,0:T(8,128)(2,1)S(1)} %collective-permute-done.9.refs_2_), channel_id=1, source_target_pairs={{0,1},{1,0},{2,3},{3,2},{4,5},{5,4},{6,7},{7,6},{8,9},{9,8},{10,11... | collective-permute-start | bytes 786440 | tf_op jit(solution)/shard_map/ppermute | solution.py:110
  33.0 1.5 %collective-permute-start.8 = (bf16[4,64,512]{2,1,0:T(8,128)(2,1)S(1)}, bf16[4,64,512]{2,1,0:T(8,128)(2,1)S(1)}, u32[]{:S(2)}, u32[]{:S(2)}) collective-permute-start(bf16[4,64,512]{2,1,0:T(8,128)(2,1)S(1)} %collective-permute-done.7.refs_0_), channel_id=1, source_target_pairs={{0,1},{1,0},{2,3},{3,2},{4,5},{5,4},{6,7},{7,6},{8,9},{9,8},{10,11... | collective-permute-start | bytes 786440 | tf_op jit(solution)/shard_map/ppermute | solution.py:110

commit v9 on v8

v9 whole, which is shorter than its diff:
```python
import jax
import jax.numpy as jnp
from jax import lax
from jax.experimental import pallas as pl
from jax.experimental.pallas import tpu as pltpu
from jax.sharding import PartitionSpec as P


def dense_rows_kernel(cols_ref, live_ref, tiles_ref, degrees_ref, rows_ref):
    row_count, slots, tile_size = tiles_ref.shape
    blocks = rows_ref.shape[1] // tile_size
    block_row = lax.axis_index("shard") * row_count // tile_size
    live = live_ref[0, block_row]
    wide = row_count * slots
    slot = lax.rem(lax.broadcasted_iota(jnp.int32, (1, wide), 1), slots)
    column = jnp.full((1, wide), -1, jnp.int32)
    for k in range(slots):
        column = jnp.where(slot == k, jnp.where(k < live, cols_ref[0, block_row, k], -1), column)
    owner = lax.div(lax.broadcasted_iota(jnp.int32, (row_count, wide), 1), slots)
    mine = lax.broadcasted_iota(jnp.int32, (row_count, wide), 0) == owner
    column = jnp.where(mine, jnp.broadcast_to(column, (row_count, wide)), -1)
    tiles = tiles_ref[...].reshape(wide, tile_size)
    degree = jnp.broadcast_to(degrees_ref[...].astype(jnp.float32), (row_count, row_count))
    diagonal = lax.broadcasted_iota(jnp.int32, (row_count, row_count), 0) == lax.broadcasted_iota(
        jnp.int32, (row_count, row_count), 1
    )
    scale = lax.rsqrt(jnp.sum(jnp.where(diagonal, degree, 0.0), axis=1, keepdims=True))
    for b in range(blocks):
        pick = (column == b).astype(jnp.bfloat16)
        summed = jnp.dot(pick, tiles, preferred_element_type=jnp.float32)
        rows_ref[:, b * tile_size : (b + 1) * tile_size] = (summed * scale).astype(jnp.bfloat16)


def dense_rows(tile_cols, live_tiles, tile_rows, degrees, nodes):
    row_count = tile_rows.shape[0]
    return pl.pallas_call(
        dense_rows_kernel,
        out_shape=pltpu.VMEM((row_count, nodes), jnp.bfloat16),
        in_specs=[
            pl.BlockSpec(memory_space=pltpu.SMEM),
            pl.BlockSpec(memory_space=pltpu.SMEM),
            pl.BlockSpec(memory_space=pltpu.VMEM),
            pl.BlockSpec(memory_space=pltpu.VMEM),
        ],
        out_specs=pl.BlockSpec(memory_space=pltpu.VMEM),
        name="dense_rows",
    )(tile_cols, live_tiles, tile_rows, degrees)


def chain_kernel(own_ref, *refs):
    slab_refs, relation_refs, out_ref, halves = refs[:4], refs[4:-2], refs[-2], refs[-1]
    row_count, nodes = own_ref.shape
    section, shard = lax.axis_index("section"), lax.axis_index("shard")
    chip, first_core = lax.div(shard, 2), lax.rem(shard, 2) == 0

    def times(*matrix_refs):
        left, right = [], []
        for here_ref, there_ref in zip(matrix_refs[::2], matrix_refs[1::2]):
            for piece in range(here_ref.shape[0]):
                source = lax.bitwise_xor(chip, len(left))
                left.append(halves[:, pl.ds(pl.multiple_of(source * 2 * row_count, 128), 2 * row_count)])
                here, there = here_ref[piece], there_ref[piece]
                right += [jnp.where(first_core, here, there), jnp.where(first_core, there, here)]
        left, right = jnp.concatenate(left, axis=1), jnp.concatenate(right, axis=0)
        both = jnp.dot(left, right, preferred_element_type=jnp.float32)
        return both[:row_count] + both[row_count:]

    halves[:row_count] = own_ref[...]
    halves[row_count:] = jnp.zeros((row_count, nodes), jnp.bfloat16)
    for back in range(len(relation_refs) // 2):

        @pl.when(section > back)
        def _(here_ref=relation_refs[2 * back], there_ref=relation_refs[2 * back + 1]):
            product = times(here_ref, there_ref)
            high = product.astype(jnp.bfloat16)
            halves[:row_count] = high
            halves[row_count:] = (product - high.astype(jnp.float32)).astype(jnp.bfloat16)

    out_ref[...] = times(*slab_refs).astype(jnp.bfloat16)


def chain(own, slab, relations):
    row_count, nodes = own.shape
    return pl.pallas_call(
        chain_kernel,
        out_shape=jax.ShapeDtypeStruct((row_count, slab[0].shape[2]), jnp.bfloat16),
        in_specs=[pl.BlockSpec(memory_space=pltpu.VMEM)] * (1 + len(slab) + len(relations)),
        out_specs=pl.BlockSpec(memory_space=pltpu.VMEM),
        scratch_shapes=[pltpu.VMEM((2 * row_count, nodes), jnp.bfloat16)],
        compiler_params=pltpu.CompilerParams(vmem_limit_bytes=32 * 1024 * 1024),
        name="chain",
    )(own, *slab, *relations)


def by_products(features, own):
    sections, shards = lax.axis_size("section"), lax.axis_size("shard")
    chips = shards // 2

    def swap(value, mask):
        return lax.ppermute(value, "shard", [(i, i ^ mask) for i in range(shards)])

    own, features = lax.optimization_barrier((own, features))
    rows = [own] + [swap(own, 2 * step) for step in range(1, chips)]
    held, step = features[None], 1
    while 2 * step < chips:
        held = jnp.concatenate([held, swap(held, 2 * step)])
        step *= 2
    mine = jnp.stack(rows)
    mine, held = lax.optimization_barrier((mine, held))
    came = swap(held, 2 * step)
    slab = [held, swap(held, 1), came, swap(came, 1)]
    relations = []
    for back in range(1, sections):
        here = lax.ppermute(mine, "section", [(i, i + back) for i in range(sections - back)])
        relations += [here, swap(here, 1)]
    return chain(own, slab, relations)


def by_hops(features, own):
    sections = lax.axis_size("section")
    part = features.shape[1] // sections
    piece = lax.dynamic_slice_in_dim(features, lax.axis_index("section") * part, part, axis=1)
    relations = lax.all_gather(own, "section", axis=0, tiled=False)
    pieces = []
    for hop in range(sections):
        slab = lax.all_gather(piece, "shard", axis=0, tiled=True)
        piece = jnp.dot(relations[hop], slab, preferred_element_type=jnp.float32).astype(jnp.bfloat16)
        pieces.append(piece)
    mine = lax.all_to_all(jnp.stack(pieces), "section", split_axis=0, concat_axis=0, tiled=True)
    return jnp.swapaxes(mine, 0, 1).reshape(features.shape)


def per_device(features, tile_cols, live_tiles, tile_values, degrees):
    nodes = features.shape[0] * lax.axis_size("shard")
    own = dense_rows(tile_cols, live_tiles, tile_values[0], degrees, nodes)
    shards = lax.axis_size("shard")
    doubles = shards >= 4 and shards & (shards - 1) == 0
    plan = by_products if doubles and nodes <= features.shape[1] else by_hops
    return plan(features, own)[None]


def solution(mesh):
    in_specs = (
        P("shard", None),
        P("section", None, None),
        P("section", None),
        P("section", "shard", None, None),
        P("section", "shard"),
    )
    out_specs = P("section", "shard", None)
    return jax.shard_map(
        per_device, mesh=mesh, in_specs=in_specs, out_specs=out_specs, check_vma=False
    )
```

time: 36.2 us -> 35.2 us (0.972)
  the two profiles are of different devices: /device:TPU:29 before, /device:TPU:0 now
where the time goes in v9:
time: 35.2 us; the launch traced here: 35 us
  starting transfers between devices  16.9 us (48%)
  waiting for transfers between devices  15.8 us (45%)
  Pallas kernels  2.27 us (6%)
    ppermute x10, waiting for transfers between devices, swap(): return lax.ppermute(value, 'shard', [(i, i ^ mask) for i in range(shards)])  8.72 us
    ppermute x10, starting transfers between devices, swap(): return lax.ppermute(value, 'shard', [(i, i ^ mask) for i in range(shards)])  8.58 us
    ppermute x3, starting transfers between devices, by_products(): lax.ppermute(mine, 'section', [(i, i + back) for i in range(sections - ba...  8.33 us
    ppermute x3, waiting for transfers between devices, by_products(): lax.ppermute(mine, 'section', [(i, i + back) for i in range(sections - ba...  7.04 us
    pallas_call x1, Pallas kernels, dense_rows(): pl.pallas_call(dense_rows_kernel, out_shape=pltpu.VMEM((row_count, nodes)...  1.32 us
    pallas_call x1, Pallas kernels, chain(): pl.pallas_call(chain_kernel, out_shape=jax.ShapeDtypeStruct((row_count, s...  0.94 us
  transfers between devices with their start and end apart: 13, of which 8 were waited for; matrix products, arithmetic and copies ran while one was open for 0% of the time, Pallas kernels for 0%

profile of v9, /device:TPU:0, one launch (start us, length us, event | category | flops | bytes accessed | tf_op | source)
XLA Modules:
  0.0 35.0 jit_solution(10743076884643137853)
XLA Ops:
  0.0 1.3 %dense_rows.1.own_ref = bf16[64,512]{1,0:T(8,128)(2,1)S(1)} custom-call(s32[1,4,16]{2,1,0:T(4,128)} %cols_ref.1, s32[1,4]{1,0:T(1,128)} %live_ref.1, bf16[64,16,128]{2,1,0:T(8,128)(2,1)} %bitcast.8, s32[1,64]{1,0:T(1,128)} %degrees_ref.1), custom_call_target="tpu_custom_call" | custom-call | tf_op jit(solution)/shard_map/dense_rows/pallas_call | solution.py:36
  1.3 5.1 %collective-permute-start.2 = (bf16[64,512]{1,0:T(8,128)(2,1)S(1)}, bf16[64,512]{1,0:T(8,128)(2,1)S(1)}, u32[]{:S(2)}, u32[]{:S(2)}) collective-permute-start(bf16[64,512]{1,0:T(8,128)(2,1)S(1)} %dense_rows.1.own_ref), channel_id=1, source_target_pairs={{0,6},{1,7},{2,4},{3,5},{4,2},{5,3},{6,0},{7,1},{8,14},{9,15},{10,... | collective-permute-start | bytes 196616 | tf_op jit(solution)/shard_map/ppermute | solution.py:100
  6.4 0.0 collective-permute-start.1
  6.4 0.6 %collective-permute-start = (bf16[64,512]{1,0:T(8,128)(2,1)S(1)}, bf16[64,512]{1,0:T(8,128)(2,1)S(1)}, u32[]{:S(2)}, u32[]{:S(2)}) collective-permute-start(bf16[64,512]{1,0:T(8,128)(2,1)S(1)} %dense_rows.1.own_ref), channel_id=1, source_target_pairs={{0,2},{1,3},{2,0},{3,1},{4,6},{5,7},{6,4},{7,5},{8,10},{9,11},{10,... | collective-permute-start | bytes 196616 | tf_op jit(solution)/shard_map/ppermute | solution.py:100
  7.1 1.4 %collective-permute-start.3 = (bf16[1,64,768]{2,1,0:T(8,128)(2,1)S(1)}, bf16[1,64,768]{2,1,0:T(8,128)(2,1)S(1)}, u32[]{:S(2)}, u32[]{:S(2)}) collective-permute-start(bf16[1,64,768]{2,1,0:T(8,128)(2,1)S(1)} %bitcast.9), channel_id=1, source_target_pairs={{0,2},{1,3},{2,0},{3,1},{4,6},{5,7},{6,4},{7,5},{8,10},{9,11},{10,... | collective-permute-start | bytes 294920 | tf_op jit(solution)/shard_map/ppermute | solution.py:100
  8.5 0.6 %collective-permute-done.2 = bf16[64,512]{1,0:T(8,128)(2,1)S(1)} collective-permute-done((bf16[64,512]{1,0:T(8,128)(2,1)S(1)}, bf16[64,512]{1,0:T(8,128)(2,1)S(1)}, u32[]{:S(2)}, u32[]{:S(2)}) %collective-permute-start.2) | collective-permute-done | bytes 65568 | tf_op jit(solution)/shard_map/ppermute | solution.py:100
  9.0 3.1 %collective-permute-done.1 = bf16[64,512]{1,0:T(8,128)(2,1)S(1)} collective-permute-done((bf16[64,512]{1,0:T(8,128)(2,1)S(1)}, bf16[64,512]{1,0:T(8,128)(2,1)S(1)}, u32[]{:S(2)}, u32[]{:S(2)}) %collective-permute-start.1) | collective-permute-done | bytes 65568 | tf_op jit(solution)/shard_map/ppermute | solution.py:100
  12.2 0.5 %collective-permute-done = bf16[64,512]{1,0:T(8,128)(2,1)S(1)} collective-permute-done((bf16[64,512]{1,0:T(8,128)(2,1)S(1)}, bf16[64,512]{1,0:T(8,128)(2,1)S(1)}, u32[]{:S(2)}, u32[]{:S(2)}) %collective-permute-start) | collective-permute-done | bytes 65568 | tf_op jit(solution)/shard_map/ppermute | solution.py:100
  12.7 1.1 %collective-permute-done.3 = bf16[1,64,768]{2,1,0:T(8,128)(2,1)S(1)} collective-permute-done((bf16[1,64,768]{2,1,0:T(8,128)(2,1)S(1)}, bf16[1,64,768]{2,1,0:T(8,128)(2,1)S(1)}, u32[]{:S(2)}, u32[]{:S(2)}) %collective-permute-start.3) | collective-permute-done | bytes 98336 | tf_op jit(solution)/shard_map/ppermute | solution.py:100
  13.7 4.6 %collective-permute-start.11 = (bf16[4,64,512]{2,1,0:T(8,128)(2,1)S(1)}, bf16[4,64,512]{2,1,0:T(8,128)(2,1)S(1)}, u32[]{:S(2)}, u32[]{:S(2)}) collective-permute-start(bf16[4,64,512]{2,1,0:T(8,128)(2,1)S(1)} %pad_maximum_fusion), channel_id=1, source_target_pairs={{0,24},{1,25},{2,26},{3,27},{4,28},{5,29},{6,30},{7,31}} | collective-permute-start | bytes 786440 | tf_op jit(solution)/shard_map/ppermute | solution.py:114
  18.3 1.3 %collective-permute-start.9 = (bf16[4,64,512]{2,1,0:T(8,128)(2,1)S(1)}, bf16[4,64,512]{2,1,0:T(8,128)(2,1)S(1)}, u32[]{:S(2)}, u32[]{:S(2)}) collective-permute-start(bf16[4,64,512]{2,1,0:T(8,128)(2,1)S(1)} %pad_maximum_fusion), channel_id=1, source_target_pairs={{0,16},{8,24},{1,17},{9,25},{2,18},{10,26},{3,19},{11,27},{4,20},{... | collective-permute-start | bytes 786440 | tf_op jit(solution)/shard_map/ppermute | solution.py:114
  19.6 2.5 %collective-permute-start.7 = (bf16[4,64,512]{2,1,0:T(8,128)(2,1)S(1)}, bf16[4,64,512]{2,1,0:T(8,128)(2,1)S(1)}, u32[]{:S(2)}, u32[]{:S(2)}) collective-permute-start(bf16[4,64,512]{2,1,0:T(8,128)(2,1)S(1)} %pad_maximum_fusion), channel_id=1, source_target_pairs={{0,8},{8,16},{16,24},{1,9},{9,17},{17,25},{2,10},{10,18},{18,26},{... | collective-permute-start | bytes 786440 | tf_op jit(solution)/shard_map/ppermute | solution.py:114
  22.1 0.9 %collective-permute-start.5 = (bf16[2,64,768]{2,1,0:T(8,128)(2,1)S(1)}, bf16[2,64,768]{2,1,0:T(8,128)(2,1)S(1)}, u32[]{:S(2)}, u32[]{:S(2)}) collective-permute-start(bf16[2,64,768]{2,1,0:T(8,128)(2,1)S(1)} %pad_maximum_fusion.1.refs_0_), channel_id=1, source_target_pairs={{0,4},{1,5},{2,6},{3,7},{4,0},{5,1},{6,2},{7,3},{8,12},{9,13},{10,... | collective-permute-start | bytes 589832 | tf_op jit(solution)/shard_map/ppermute | solution.py:100
  23.0 2.1 %collective-permute-done.11.refs_8_ = bf16[4,64,512]{2,1,0:T(8,128)(2,1)S(1)} collective-permute-done((bf16[4,64,512]{2,1,0:T(8,128)(2,1)S(1)}, bf16[4,64,512]{2,1,0:T(8,128)(2,1)S(1)}, u32[]{:S(2)}, u32[]{:S(2)}) %collective-permute-start.11) | collective-permute-done | bytes 262176 | tf_op jit(solution)/shard_map/ppermute | solution.py:114
  25.1 5.0 %collective-permute-done.9.refs_6_ = bf16[4,64,512]{2,1,0:T(8,128)(2,1)S(1)} collective-permute-done((bf16[4,64,512]{2,1,0:T(8,128)(2,1)S(1)}, bf16[4,64,512]{2,1,0:T(8,128)(2,1)S(1)}, u32[]{:S(2)}, u32[]{:S(2)}) %collective-permute-start.9) | collective-permute-done | bytes 262176 | tf_op jit(solution)/shard_map/ppermute | solution.py:114
  30.1 0.0 collective-permute-start.10
  30.1 0.0 collective-permute-done.7.refs_4_
  30.1 0.5 %collective-permute-start.8 = (bf16[4,64,512]{2,1,0:T(8,128)(2,1)S(1)}, bf16[4,64,512]{2,1,0:T(8,128)(2,1)S(1)}, u32[]{:S(2)}, u32[]{:S(2)}) collective-permute-start(bf16[4,64,512]{2,1,0:T(8,128)(2,1)S(1)} %collective-permute-done.7.refs_4_), channel_id=1, source_target_pairs={{0,1},{1,0},{2,3},{3,2},{4,5},{5,4},{6,7},{7,6},{8,9},{9,8},{10,11... | collective-permute-start | bytes 786440 | tf_op jit(solution)/shard_map/ppermute | solution.py:100
  30.6 0.0 collective-permute-start.4
  30.6 2.1 %collective-permute-done.5.refs_2_ = bf16[2,64,768]{2,1,0:T(8,128)(2,1)S(1)} collective-permute-done((bf16[2,64,768]{2,1,0:T(8,128)(2,1)S(1)}, bf16[2,64,768]{2,1,0:T(8,128)(2,1)S(1)}, u32[]{:S(2)}, u32[]{:S(2)}) %collective-permute-start.5) | collective-permute-done | bytes 196640 | tf_op jit(solution)/shard_map/ppermute | solution.py:100
  32.6 0.0 collective-permute-start.6
  32.6 0.0 collective-permute-done.4.refs_1_
  32.7 1.4 %collective-permute-done.6.refs_3_ = bf16[2,64,768]{2,1,0:T(8,128)(2,1)S(1)} collective-permute-done((bf16[2,64,768]{2,1,0:T(8,128)(2,1)S(1)}, bf16[2,64,768]{2,1,0:T(8,128)(2,1)S(1)}, u32[]{:S(2)}, u32[]{:S(2)}) %collective-permute-start.6) | collective-permute-done | bytes 196640 | tf_op jit(solution)/shard_map/ppermute | solution.py:100
  34.1 0.9 %chain.1 = bf16[64,768]{1,0:T(8,128)(2,1)} custom-call(bf16[64,512]{1,0:T(8,128)(2,1)S(1)} %dense_rows.1.own_ref, bf16[2,64,768]{2,1,0:T(8,128)(2,1)S(1)} %pad_maximum_fusion.1.refs_0_, bf16[2,64,768]{2,1,0:T(8,128)(2,1)S(1)} %collective-permute-done.4.refs_1_, bf16[2,64,768]{2,1,0:T(8,128)(2,1)S(1)} %collective-permute-done.5.refs_2_, ...), custom_call_target="tpu_custom_call" | custom-call | tf_op jit(solution)/shard_map/chain/pallas_call | solution.py:84
  (8 shorter events, 0.1 us)
Async XLA Ops:
  0.0 7.1 %copy-start = (bf16[64,768]{1,0:T(8,128)(2,1)S(1)}, bf16[64,768]{1,0:T(8,128)(2,1)}, u32[]{:S(2)}) copy-start(bf16[64,768]{1,0:T(8,128)(2,1)} %param.5) | copy-start | bytes 294916
  1.3 7.7 %collective-permute-start.2 = (bf16[64,512]{1,0:T(8,128)(2,1)S(1)}, bf16[64,512]{1,0:T(8,128)(2,1)S(1)}, u32[]{:S(2)}, u32[]{:S(2)}) collective-permute-start(bf16[64,512]{1,0:T(8,128)(2,1)S(1)} %dense_rows.1.own_ref), channel_id=1, source_target_pairs={{0,6},{1,7},{2,4},{3,5},{4,2},{5,3},{6,0},{7,1},{8,14},{9,15},{10,... | collective-permute-start | bytes 196616 | tf_op jit(solution)/shard_map/ppermute | solution.py:100
  6.4 5.7 %collective-permute-start.1 = (bf16[64,512]{1,0:T(8,128)(2,1)S(1)}, bf16[64,512]{1,0:T(8,128)(2,1)S(1)}, u32[]{:S(2)}, u32[]{:S(2)}) collective-permute-start(bf16[64,512]{1,0:T(8,128)(2,1)S(1)} %dense_rows.1.own_ref), channel_id=1, source_target_pairs={{0,4},{1,5},{2,6},{3,7},{4,0},{5,1},{6,2},{7,3},{8,12},{9,13},{10,... | collective-permute-start | bytes 196616 | tf_op jit(solution)/shard_map/ppermute | solution.py:100
  6.4 6.2 %collective-permute-start = (bf16[64,512]{1,0:T(8,128)(2,1)S(1)}, bf16[64,512]{1,0:T(8,128)(2,1)S(1)}, u32[]{:S(2)}, u32[]{:S(2)}) collective-permute-start(bf16[64,512]{1,0:T(8,128)(2,1)S(1)} %dense_rows.1.own_ref), channel_id=1, source_target_pairs={{0,2},{1,3},{2,0},{3,1},{4,6},{5,7},{6,4},{7,5},{8,10},{9,11},{10,... | collective-permute-start | bytes 196616 | tf_op jit(solution)/shard_map/ppermute | solution.py:100
  7.1 6.6 %collective-permute-start.3 = (bf16[1,64,768]{2,1,0:T(8,128)(2,1)S(1)}, bf16[1,64,768]{2,1,0:T(8,128)(2,1)S(1)}, u32[]{:S(2)}, u32[]{:S(2)}) collective-permute-start(bf16[1,64,768]{2,1,0:T(8,128)(2,1)S(1)} %bitcast.9), channel_id=1, source_target_pairs={{0,2},{1,3},{2,0},{3,1},{4,6},{5,7},{6,4},{7,5},{8,10},{9,11},{10,... | collective-permute-start | bytes 294920 | tf_op jit(solution)/shard_map/ppermute | solution.py:100
  13.7 11.3 %collective-permute-start.11 = (bf16[4,64,512]{2,1,0:T(8,128)(2,1)S(1)}, bf16[4,64,512]{2,1,0:T(8,128)(2,1)S(1)}, u32[]{:S(2)}, u32[]{:S(2)}) collective-permute-start(bf16[4,64,512]{2,1,0:T(8,128)(2,1)S(1)} %pad_maximum_fusion), channel_id=1, source_target_pairs={{0,24},{1,25},{2,26},{3,27},{4,28},{5,29},{6,30},{7,31}} | collective-permute-start | bytes 786440 | tf_op jit(solution)/shard_map/ppermute | solution.py:114
  18.3 11.7 %collective-permute-start.9 = (bf16[4,64,512]{2,1,0:T(8,128)(2,1)S(1)}, bf16[4,64,512]{2,1,0:T(8,128)(2,1)S(1)}, u32[]{:S(2)}, u32[]{:S(2)}) collective-permute-start(bf16[4,64,512]{2,1,0:T(8,128)(2,1)S(1)} %pad_maximum_fusion), channel_id=1, source_target_pairs={{0,16},{8,24},{1,17},{9,25},{2,18},{10,26},{3,19},{11,27},{4,20},{... | collective-permute-start | bytes 786440 | tf_op jit(solution)/shard_map/ppermute | solution.py:114
  19.6 10.4 %collective-permute-start.7 = (bf16[4,64,512]{2,1,0:T(8,128)(2,1)S(1)}, bf16[4,64,512]{2,1,0:T(8,128)(2,1)S(1)}, u32[]{:S(2)}, u32[]{:S(2)}) collective-permute-start(bf16[4,64,512]{2,1,0:T(8,128)(2,1)S(1)} %pad_maximum_fusion), channel_id=1, source_target_pairs={{0,8},{8,16},{16,24},{1,9},{9,17},{17,25},{2,10},{10,18},{18,26},{... | collective-permute-start | bytes 786440 | tf_op jit(solution)/shard_map/ppermute | solution.py:114
  22.1 10.5 %collective-permute-start.5 = (bf16[2,64,768]{2,1,0:T(8,128)(2,1)S(1)}, bf16[2,64,768]{2,1,0:T(8,128)(2,1)S(1)}, u32[]{:S(2)}, u32[]{:S(2)}) collective-permute-start(bf16[2,64,768]{2,1,0:T(8,128)(2,1)S(1)} %pad_maximum_fusion.1.refs_0_), channel_id=1, source_target_pairs={{0,4},{1,5},{2,6},{3,7},{4,0},{5,1},{6,2},{7,3},{8,12},{9,13},{10,... | collective-permute-start | bytes 589832 | tf_op jit(solution)/shard_map/ppermute | solution.py:100
  25.1 9.0 %collective-permute-start.12 = (bf16[4,64,512]{2,1,0:T(8,128)(2,1)S(1)}, bf16[4,64,512]{2,1,0:T(8,128)(2,1)S(1)}, u32[]{:S(2)}, u32[]{:S(2)}) collective-permute-start(bf16[4,64,512]{2,1,0:T(8,128)(2,1)S(1)} %collective-permute-done.11.refs_8_), channel_id=1, source_target_pairs={{0,1},{1,0},{2,3},{3,2},{4,5},{5,4},{6,7},{7,6},{8,9},{9,8},{10,11... | collective-permute-start | bytes 786440 | tf_op jit(solution)/shard_map/ppermute | solution.py:100
  30.1 4.0 %collective-permute-start.10 = (bf16[4,64,512]{2,1,0:T(8,128)(2,1)S(1)}, bf16[4,64,512]{2,1,0:T(8,128)(2,1)S(1)}, u32[]{:S(2)}, u32[]{:S(2)}) collective-permute-start(bf16[4,64,512]{2,1,0:T(8,128)(2,1)S(1)} %collective-permute-done.9.refs_6_), channel_id=1, source_target_pairs={{0,1},{1,0},{2,3},{3,2},{4,5},{5,4},{6,7},{7,6},{8,9},{9,8},{10,11... | collective-permute-start | bytes 786440 | tf_op jit(solution)/shard_map/ppermute | solution.py:100
  30.1 4.0 %collective-permute-start.8 = (bf16[4,64,512]{2,1,0:T(8,128)(2,1)S(1)}, bf16[4,64,512]{2,1,0:T(8,128)(2,1)S(1)}, u32[]{:S(2)}, u32[]{:S(2)}) collective-permute-start(bf16[4,64,512]{2,1,0:T(8,128)(2,1)S(1)} %collective-permute-done.7.refs_4_), channel_id=1, source_target_pairs={{0,1},{1,0},{2,3},{3,2},{4,5},{5,4},{6,7},{7,6},{8,9},{9,8},{10,11... | collective-permute-start | bytes 786440 | tf_op jit(solution)/shard_map/ppermute | solution.py:100
  30.6 2.1 %collective-permute-start.4 = (bf16[2,64,768]{2,1,0:T(8,128)(2,1)S(1)}, bf16[2,64,768]{2,1,0:T(8,128)(2,1)S(1)}, u32[]{:S(2)}, u32[]{:S(2)}) collective-permute-start(bf16[2,64,768]{2,1,0:T(8,128)(2,1)S(1)} %pad_maximum_fusion.1.refs_0_), channel_id=1, source_target_pairs={{0,1},{1,0},{2,3},{3,2},{4,5},{5,4},{6,7},{7,6},{8,9},{9,8},{10,11... | collective-permute-start | bytes 589832 | tf_op jit(solution)/shard_map/ppermute | solution.py:100
  32.6 1.4 %collective-permute-start.6 = (bf16[2,64,768]{2,1,0:T(8,128)(2,1)S(1)}, bf16[2,64,768]{2,1,0:T(8,128)(2,1)S(1)}, u32[]{:S(2)}, u32[]{:S(2)}) collective-permute-start(bf16[2,64,768]{2,1,0:T(8,128)(2,1)S(1)} %collective-permute-done.5.refs_2_), channel_id=1, source_target_pairs={{0,1},{1,0},{2,3},{3,2},{4,5},{5,4},{6,7},{7,6},{8,9},{9,8},{10,11... | collective-permute-start | bytes 589832 | tf_op jit(solution)/shard_map/ppermute | solution.py:100

commit v10 on v9

--- a/solution.py
+++ b/solution.py
@@ -1,3 +1,5 @@
+import functools
+
 import jax
 import jax.numpy as jnp
 from jax import lax
@@ -47,17 +49,17 @@
     )(tile_cols, live_tiles, tile_rows, degrees)
 
 
-def chain_kernel(own_ref, *refs):
+def chain_kernel(slab_masks, own_ref, *refs):
     slab_refs, relation_refs, out_ref, halves = refs[:4], refs[4:-2], refs[-2], refs[-1]
     row_count, nodes = own_ref.shape
     section, shard = lax.axis_index("section"), lax.axis_index("shard")
     chip, first_core = lax.div(shard, 2), lax.rem(shard, 2) == 0
 
-    def times(*matrix_refs):
+    def times(pairs):
         left, right = [], []
-        for here_ref, there_ref in zip(matrix_refs[::2], matrix_refs[1::2]):
-            for piece in range(here_ref.shape[0]):
-                source = lax.bitwise_xor(chip, len(left))
+        for here_ref, there_ref, masks in pairs:
+            for piece, mask in enumerate(masks):
+                source = lax.bitwise_xor(chip, mask)
                 left.append(halves[:, pl.ds(pl.multiple_of(source * 2 * row_count, 128), 2 * row_count)])
                 here, there = here_ref[piece], there_ref[piece]
                 right += [jnp.where(first_core, here, there), jnp.where(first_core, there, here)]
@@ -67,22 +69,26 @@
 
     halves[:row_count] = own_ref[...]
     halves[row_count:] = jnp.zeros((row_count, nodes), jnp.bfloat16)
-    for back in range(len(relation_refs) // 2):
+    for at in range(1, len(relation_refs) // 2 + 1):
 
-        @pl.when(section > back)
-        def _(here_ref=relation_refs[2 * back], there_ref=relation_refs[2 * back + 1]):
-            product = times(here_ref, there_ref)
-            high = product.astype(jnp.bfloat16)
-            halves[:row_count] = high
-            halves[row_count:] = (product - high.astype(jnp.float32)).astype(jnp.bfloat16)
+        @pl.when(section == at)
+        def _(at=at):
+            for earlier in reversed(range(at)):
+                other = 2 * ((at ^ earlier) - 1)
+                here_ref, there_ref = relation_refs[other], relation_refs[other + 1]
+                product = times([(here_ref, there_ref, range(here_ref.shape[0]))])
+                high = product.astype(jnp.bfloat16)
+                halves[:row_count] = high
+                halves[row_count:] = (product - high.astype(jnp.float32)).astype(jnp.bfloat16)
 
-    out_ref[...] = times(*slab_refs).astype(jnp.bfloat16)
+    slab = [(slab_refs[0], slab_refs[1], slab_masks[0]), (slab_refs[2], slab_refs[3], slab_masks[1])]
+    out_ref[...] = times(slab).astype(jnp.bfloat16)
 
 
-def chain(own, slab, relations):
+def chain(own, slab, slab_masks, relations):
     row_count, nodes = own.shape
     return pl.pallas_call(
-        chain_kernel,
+        functools.partial(chain_kernel, slab_masks),
         out_shape=jax.ShapeDtypeStruct((row_count, slab[0].shape[2]), jnp.bfloat16),
         in_specs=[pl.BlockSpec(memory_space=pltpu.VMEM)] * (1 + len(slab) + len(relations)),
         out_specs=pl.BlockSpec(memory_space=pltpu.VMEM),
@@ -99,21 +105,25 @@
     def swap(value, mask):
         return lax.ppermute(value, "shard", [(i, i ^ mask) for i in range(shards)])
 
-    own, features = lax.optimization_barrier((own, features))
-    rows = [own] + [swap(own, 2 * step) for step in range(1, chips)]
-    held, step = features[None], 1
-    while 2 * step < chips:
-        held = jnp.concatenate([held, swap(held, 2 * step)])
-        step *= 2
-    mine = jnp.stack(rows)
+    def later(value, mask):
+        return lax.ppermute(value, "section", [(i, i ^ mask) for i in range(sections) if i ^ mask > i])
+
+    def along_z(value):
+        return jnp.stack([value] + [swap(value, 2 * mask) for mask in range(1, chips)])
+
+    held, masks, step = features[None], [0], chips // 2
+    while step > 1:
+        held, masks, step = jnp.concatenate([held, swap(held, 2 * step)]), masks + [m ^ step for m in masks], step // 2
+    crossing = {mask: later(own, mask) for mask in range(1, sections) if mask & (mask - 1)}
+    mine = along_z(own)
     mine, held = lax.optimization_barrier((mine, held))
-    came = swap(held, 2 * step)
+    came = swap(held, 2)
     slab = [held, swap(held, 1), came, swap(came, 1)]
     relations = []
-    for back in range(1, sections):
-        here = lax.ppermute(mine, "section", [(i, i + back) for i in range(sections - back)])
+    for mask in range(1, sections):
+        here = along_z(crossing[mask]) if mask in crossing else later(mine, mask)
         relations += [here, swap(here, 1)]
-    return chain(own, slab, relations)
+    return chain(own, slab, (masks, [m ^ 1 for m in masks]), relations)
 
 
 def by_hops(features, own):
@@ -133,8 +143,8 @@
 def per_device(features, tile_cols, live_tiles, tile_values, degrees):
     nodes = features.shape[0] * lax.axis_size("shard")
     own = dense_rows(tile_cols, live_tiles, tile_values[0], degrees, nodes)
-    shards = lax.axis_size("shard")
-    doubles = shards >= 4 and shards & (shards - 1) == 0
+    sections, shards = lax.axis_size("section"), lax.axis_size("shard")
+    doubles = shards >= 4 and shards & (shards - 1) == 0 and sections & (sections - 1) == 0
     plan = by_products if doubles and nodes <= features.shape[1] else by_hops
     return plan(features, own)[None]
 

time: 35.2 us -> 38.3 us (1.088)
  starting transfers between devices: 16.9 us -> 22.9 us
  waiting for transfers between devices: 15.8 us -> 12.7 us
    ppermute x3, waiting for transfers between devices: 7.04 us -> 0.01 us  [later(): lax.ppermute(value, 'section', [(i, i ^ mask) for i in range(sections) if...]
    ppermute x10 -> x13, starting transfers between devices: 8.58 us -> 13.5 us  [swap(): return lax.ppermute(value, 'shard', [(i, i ^ mask) for i in range(shards)])]
    ppermute x10 -> x13, waiting for transfers between devices: 8.72 us -> 12.7 us  [swap(): return lax.ppermute(value, 'shard', [(i, i ^ mask) for i in range(shards)])]
    ppermute x3, starting transfers between devices: 8.33 us -> 9.38 us  [later(): lax.ppermute(value, 'section', [(i, i ^ mask) for i in range(sections) if...]
  transfers between devices with their start and end apart: 13 -> 16, of which waited for: 8 -> 6; matrix products, arithmetic and copies ran while one was open for 0% -> 0% of each run, Pallas kernels for 0% -> 0%
where the time goes in v10:
time: 38.3 us; the launch traced here: 38.1 us
  starting transfers between devices  22.9 us (60%)
  waiting for transfers between devices  12.7 us (33%)
  Pallas kernels  2.27 us (6%)
    ppermute x13, starting transfers between devices, swap(): return lax.ppermute(value, 'shard', [(i, i ^ mask) for i in range(shards)])  13.5 us
    ppermute x13, waiting for transfers between devices, swap(): return lax.ppermute(value, 'shard', [(i, i ^ mask) for i in range(shards)])  12.7 us
    ppermute x3, starting transfers between devices, later(): lax.ppermute(value, 'section', [(i, i ^ mask) for i in range(sections) if...  9.38 us
    pallas_call x1, Pallas kernels, dense_rows(): pl.pallas_call(dense_rows_kernel, out_shape=pltpu.VMEM((row_count, nodes)...  1.32 us
    pallas_call x1, Pallas kernels, chain(): pl.pallas_call(functools.partial(chain_kernel, slab_masks), out_shape=jax...  0.94 us
  transfers between devices with their start and end apart: 16, of which 6 were waited for; matrix products, arithmetic and copies ran while one was open for 0% of the time, Pallas kernels for 0%

profile of v10, /device:TPU:0, one launch (start us, length us, event | category | flops | bytes accessed | tf_op | source)
XLA Modules:
  0.0 38.1 jit_solution(12233441971440719733)
XLA Ops:
  0.0 1.3 %dense_rows.1.own_ref = bf16[64,512]{1,0:T(8,128)(2,1)S(1)} custom-call(s32[1,4,16]{2,1,0:T(4,128)} %cols_ref.1, s32[1,4]{1,0:T(1,128)} %live_ref.1, bf16[64,16,128]{2,1,0:T(8,128)(2,1)} %bitcast.12, s32[1,64]{1,0:T(1,128)} %degrees_ref.1), custom_call_target="tpu_custom_call" | custom-call | tf_op jit(solution)/shard_map/dense_rows/pallas_call | solution.py:38
  1.3 5.1 %collective-permute-start.2 = (bf16[64,512]{1,0:T(8,128)(2,1)S(1)}, bf16[64,512]{1,0:T(8,128)(2,1)S(1)}, u32[]{:S(2)}, u32[]{:S(2)}) collective-permute-start(bf16[64,512]{1,0:T(8,128)(2,1)S(1)} %dense_rows.1.own_ref), channel_id=1, source_target_pairs={{0,6},{1,7},{2,4},{3,5},{4,2},{5,3},{6,0},{7,1},{8,14},{9,15},{10,... | collective-permute-start | bytes 196616 | tf_op jit(solution)/shard_map/ppermute | solution.py:106
  6.4 0.0 collective-permute-start.1
  6.4 0.6 %collective-permute-start = (bf16[64,512]{1,0:T(8,128)(2,1)S(1)}, bf16[64,512]{1,0:T(8,128)(2,1)S(1)}, u32[]{:S(2)}, u32[]{:S(2)}) collective-permute-start(bf16[64,512]{1,0:T(8,128)(2,1)S(1)} %dense_rows.1.own_ref), channel_id=1, source_target_pairs={{0,2},{1,3},{2,0},{3,1},{4,6},{5,7},{6,4},{7,5},{8,10},{9,11},{10,... | collective-permute-start | bytes 196616 | tf_op jit(solution)/shard_map/ppermute | solution.py:106
  7.1 4.5 %collective-permute-start.11 = (bf16[64,512]{1,0:T(8,128)(2,1)S(1)}, bf16[64,512]{1,0:T(8,128)(2,1)S(1)}, u32[]{:S(2)}, u32[]{:S(2)}) collective-permute-start(bf16[64,512]{1,0:T(8,128)(2,1)S(1)} %dense_rows.1.own_ref), channel_id=1, source_target_pairs={{0,24},{8,16},{1,25},{9,17},{2,26},{10,18},{3,27},{11,19},{4,28},{... | collective-permute-start | bytes 196616 | tf_op jit(solution)/shard_map/ppermute | solution.py:109
  11.6 2.2 %collective-permute-start.3 = (bf16[1,64,768]{2,1,0:T(8,128)(2,1)S(1)}, bf16[1,64,768]{2,1,0:T(8,128)(2,1)S(1)}, u32[]{:S(2)}, u32[]{:S(2)}) collective-permute-start(bf16[1,64,768]{2,1,0:T(8,128)(2,1)S(1)} %bitcast.13), channel_id=1, source_target_pairs={{0,4},{1,5},{2,6},{3,7},{4,0},{5,1},{6,2},{7,3},{8,12},{9,13},{10,... | collective-permute-start | bytes 294920 | tf_op jit(solution)/shard_map/ppermute | solution.py:106
  13.8 0.0 collective-permute-done.2
  13.8 0.0 collective-permute-done.1
  13.8 0.0 collective-permute-done
  13.9 4.4 %collective-permute-done.3 = bf16[1,64,768]{2,1,0:T(8,128)(2,1)S(1)} collective-permute-done((bf16[1,64,768]{2,1,0:T(8,128)(2,1)S(1)}, bf16[1,64,768]{2,1,0:T(8,128)(2,1)S(1)}, u32[]{:S(2)}, u32[]{:S(2)}) %collective-permute-start.3) | collective-permute-done | bytes 98336 | tf_op jit(solution)/shard_map/ppermute | solution.py:106
  18.3 1.5 %collective-permute-start.9 = (bf16[4,64,512]{2,1,0:T(8,128)(2,1)S(1)}, bf16[4,64,512]{2,1,0:T(8,128)(2,1)S(1)}, u32[]{:S(2)}, u32[]{:S(2)}) collective-permute-start(bf16[4,64,512]{2,1,0:T(8,128)(2,1)S(1)} %pad_maximum_fusion), channel_id=1, source_target_pairs={{0,16},{8,24},{1,17},{9,25},{2,18},{10,26},{3,19},{11,27},{4,20},{... | collective-permute-start | bytes 786440 | tf_op jit(solution)/shard_map/ppermute | solution.py:109
  19.7 3.4 %collective-permute-start.7 = (bf16[4,64,512]{2,1,0:T(8,128)(2,1)S(1)}, bf16[4,64,512]{2,1,0:T(8,128)(2,1)S(1)}, u32[]{:S(2)}, u32[]{:S(2)}) collective-permute-start(bf16[4,64,512]{2,1,0:T(8,128)(2,1)S(1)} %pad_maximum_fusion), channel_id=1, source_target_pairs={{0,8},{16,24},{1,9},{17,25},{2,10},{18,26},{3,11},{19,27},{4,12},{... | collective-permute-start | bytes 786440 | tf_op jit(solution)/shard_map/ppermute | solution.py:109
  23.2 2.8 %collective-permute-start.14 = (bf16[64,512]{1,0:T(8,128)(2,1)S(1)}, bf16[64,512]{1,0:T(8,128)(2,1)S(1)}, u32[]{:S(2)}, u32[]{:S(2)}) collective-permute-start(bf16[64,512]{1,0:T(8,128)(2,1)S(1)} %collective-permute-done.11), channel_id=1, source_target_pairs={{0,6},{1,7},{2,4},{3,5},{4,2},{5,3},{6,0},{7,1},{8,14},{9,15},{10,... | collective-permute-start | bytes 196616 | tf_op jit(solution)/shard_map/ppermute | solution.py:106
  26.0 1.7 %collective-permute-start.12 = (bf16[64,512]{1,0:T(8,128)(2,1)S(1)}, bf16[64,512]{1,0:T(8,128)(2,1)S(1)}, u32[]{:S(2)}, u32[]{:S(2)}) collective-permute-start(bf16[64,512]{1,0:T(8,128)(2,1)S(1)} %collective-permute-done.11), channel_id=1, source_target_pairs={{0,2},{1,3},{2,0},{3,1},{4,6},{5,7},{6,4},{7,5},{8,10},{9,11},{10,... | collective-permute-start | bytes 196616 | tf_op jit(solution)/shard_map/ppermute | solution.py:106
  27.6 1.7 %collective-permute-done.14 = bf16[64,512]{1,0:T(8,128)(2,1)S(1)} collective-permute-done((bf16[64,512]{1,0:T(8,128)(2,1)S(1)}, bf16[64,512]{1,0:T(8,128)(2,1)S(1)}, u32[]{:S(2)}, u32[]{:S(2)}) %collective-permute-start.14) | collective-permute-done | bytes 65568 | tf_op jit(solution)/shard_map/ppermute | solution.py:106
  29.3 2.1 %collective-permute-done.13 = bf16[64,512]{1,0:T(8,128)(2,1)S(1)} collective-permute-done((bf16[64,512]{1,0:T(8,128)(2,1)S(1)}, bf16[64,512]{1,0:T(8,128)(2,1)S(1)}, u32[]{:S(2)}, u32[]{:S(2)}) %collective-permute-start.13) | collective-permute-done | bytes 65568 | tf_op jit(solution)/shard_map/ppermute | solution.py:106
  31.4 0.5 %collective-permute-done.12 = bf16[64,512]{1,0:T(8,128)(2,1)S(1)} collective-permute-done((bf16[64,512]{1,0:T(8,128)(2,1)S(1)}, bf16[64,512]{1,0:T(8,128)(2,1)S(1)}, u32[]{:S(2)}, u32[]{:S(2)}) %collective-permute-start.12) | collective-permute-done | bytes 65568 | tf_op jit(solution)/shard_map/ppermute | solution.py:106
  31.9 0.1 collective-permute-start.15
  32.0 0.5 %collective-permute-start.10 = (bf16[4,64,512]{2,1,0:T(8,128)(2,1)S(1)}, bf16[4,64,512]{2,1,0:T(8,128)(2,1)S(1)}, u32[]{:S(2)}, u32[]{:S(2)}) collective-permute-start(bf16[4,64,512]{2,1,0:T(8,128)(2,1)S(1)} %collective-permute-done.9.refs_6_), channel_id=1, source_target_pairs={{0,1},{1,0},{2,3},{3,2},{4,5},{5,4},{6,7},{7,6},{8,9},{9,8},{10,11... | collective-permute-start | bytes 786440 | tf_op jit(solution)/shard_map/ppermute | solution.py:106
  32.5 0.1 collective-permute-start.8
  32.6 0.4 %collective-permute-start.4 = (bf16[2,64,768]{2,1,0:T(8,128)(2,1)S(1)}, bf16[2,64,768]{2,1,0:T(8,128)(2,1)S(1)}, u32[]{:S(2)}, u32[]{:S(2)}) collective-permute-start(bf16[2,64,768]{2,1,0:T(8,128)(2,1)S(1)} %pad_maximum_fusion.2.refs_0_), channel_id=1, source_target_pairs={{0,1},{1,0},{2,3},{3,2},{4,5},{5,4},{6,7},{7,6},{8,9},{9,8},{10,11... | collective-permute-start | bytes 589832 | tf_op jit(solution)/shard_map/ppermute | solution.py:106
  33.0 2.7 %collective-permute-done.5.refs_2_ = bf16[2,64,768]{2,1,0:T(8,128)(2,1)S(1)} collective-permute-done((bf16[2,64,768]{2,1,0:T(8,128)(2,1)S(1)}, bf16[2,64,768]{2,1,0:T(8,128)(2,1)S(1)}, u32[]{:S(2)}, u32[]{:S(2)}) %collective-permute-start.5) | collective-permute-done | bytes 196640 | tf_op jit(solution)/shard_map/ppermute | solution.py:106
  35.7 1.4 %collective-permute-done.6.refs_3_ = bf16[2,64,768]{2,1,0:T(8,128)(2,1)S(1)} collective-permute-done((bf16[2,64,768]{2,1,0:T(8,128)(2,1)S(1)}, bf16[2,64,768]{2,1,0:T(8,128)(2,1)S(1)}, u32[]{:S(2)}, u32[]{:S(2)}) %collective-permute-start.6) | collective-permute-done | bytes 196640 | tf_op jit(solution)/shard_map/ppermute | solution.py:106
  37.1 0.9 %chain.1 = bf16[64,768]{1,0:T(8,128)(2,1)} custom-call(bf16[64,512]{1,0:T(8,128)(2,1)S(1)} %dense_rows.1.own_ref, bf16[2,64,768]{2,1,0:T(8,128)(2,1)S(1)} %pad_maximum_fusion.2.refs_0_, bf16[2,64,768]{2,1,0:T(8,128)(2,1)S(1)} %collective-permute-done.4.refs_1_, bf16[2,64,768]{2,1,0:T(8,128)(2,1)S(1)} %collective-permute-done.5.refs_2_, ...), custom_call_target="tpu_custom_call" | custom-call | tf_op jit(solution)/shard_map/chain/pallas_call | solution.py:90
  (15 shorter events, 0.1 us)
Async XLA Ops:
  0.0 11.6 %copy-start = (bf16[64,768]{1,0:T(8,128)(2,1)S(1)}, bf16[64,768]{1,0:T(8,128)(2,1)}, u32[]{:S(2)}) copy-start(bf16[64,768]{1,0:T(8,128)(2,1)} %param.5) | copy-start | bytes 294916
  1.3 12.5 %collective-permute-start.2 = (bf16[64,512]{1,0:T(8,128)(2,1)S(1)}, bf16[64,512]{1,0:T(8,128)(2,1)S(1)}, u32[]{:S(2)}, u32[]{:S(2)}) collective-permute-start(bf16[64,512]{1,0:T(8,128)(2,1)S(1)} %dense_rows.1.own_ref), channel_id=1, source_target_pairs={{0,6},{1,7},{2,4},{3,5},{4,2},{5,3},{6,0},{7,1},{8,14},{9,15},{10,... | collective-permute-start | bytes 196616 | tf_op jit(solution)/shard_map/ppermute | solution.py:106
  6.4 7.4 %collective-permute-start.1 = (bf16[64,512]{1,0:T(8,128)(2,1)S(1)}, bf16[64,512]{1,0:T(8,128)(2,1)S(1)}, u32[]{:S(2)}, u32[]{:S(2)}) collective-permute-start(bf16[64,512]{1,0:T(8,128)(2,1)S(1)} %dense_rows.1.own_ref), channel_id=1, source_target_pairs={{0,4},{1,5},{2,6},{3,7},{4,0},{5,1},{6,2},{7,3},{8,12},{9,13},{10,... | collective-permute-start | bytes 196616 | tf_op jit(solution)/shard_map/ppermute | solution.py:106
  6.4 7.4 %collective-permute-start = (bf16[64,512]{1,0:T(8,128)(2,1)S(1)}, bf16[64,512]{1,0:T(8,128)(2,1)S(1)}, u32[]{:S(2)}, u32[]{:S(2)}) collective-permute-start(bf16[64,512]{1,0:T(8,128)(2,1)S(1)} %dense_rows.1.own_ref), channel_id=1, source_target_pairs={{0,2},{1,3},{2,0},{3,1},{4,6},{5,7},{6,4},{7,5},{8,10},{9,11},{10,... | collective-permute-start | bytes 196616 | tf_op jit(solution)/shard_map/ppermute | solution.py:106
  7.1 16.1 %collective-permute-start.11 = (bf16[64,512]{1,0:T(8,128)(2,1)S(1)}, bf16[64,512]{1,0:T(8,128)(2,1)S(1)}, u32[]{:S(2)}, u32[]{:S(2)}) collective-permute-start(bf16[64,512]{1,0:T(8,128)(2,1)S(1)} %dense_rows.1.own_ref), channel_id=1, source_target_pairs={{0,24},{8,16},{1,25},{9,17},{2,26},{10,18},{3,27},{11,19},{4,28},{... | collective-permute-start | bytes 196616 | tf_op jit(solution)/shard_map/ppermute | solution.py:109
  11.6 6.6 %collective-permute-start.3 = (bf16[1,64,768]{2,1,0:T(8,128)(2,1)S(1)}, bf16[1,64,768]{2,1,0:T(8,128)(2,1)S(1)}, u32[]{:S(2)}, u32[]{:S(2)}) collective-permute-start(bf16[1,64,768]{2,1,0:T(8,128)(2,1)S(1)} %bitcast.13), channel_id=1, source_target_pairs={{0,4},{1,5},{2,6},{3,7},{4,0},{5,1},{6,2},{7,3},{8,12},{9,13},{10,... | collective-permute-start | bytes 294920 | tf_op jit(solution)/shard_map/ppermute | solution.py:106
  18.3 13.8 %collective-permute-start.9 = (bf16[4,64,512]{2,1,0:T(8,128)(2,1)S(1)}, bf16[4,64,512]{2,1,0:T(8,128)(2,1)S(1)}, u32[]{:S(2)}, u32[]{:S(2)}) collective-permute-start(bf16[4,64,512]{2,1,0:T(8,128)(2,1)S(1)} %pad_maximum_fusion), channel_id=1, source_target_pairs={{0,16},{8,24},{1,17},{9,25},{2,18},{10,26},{3,19},{11,27},{4,20},{... | collective-permute-start | bytes 786440 | tf_op jit(solution)/shard_map/ppermute | solution.py:109
  19.7 12.8 %collective-permute-start.7 = (bf16[4,64,512]{2,1,0:T(8,128)(2,1)S(1)}, bf16[4,64,512]{2,1,0:T(8,128)(2,1)S(1)}, u32[]{:S(2)}, u32[]{:S(2)}) collective-permute-start(bf16[4,64,512]{2,1,0:T(8,128)(2,1)S(1)} %pad_maximum_fusion), channel_id=1, source_target_pairs={{0,8},{16,24},{1,9},{17,25},{2,10},{18,26},{3,11},{19,27},{4,12},{... | collective-permute-start | bytes 786440 | tf_op jit(solution)/shard_map/ppermute | solution.py:109
  23.2 6.1 %collective-permute-start.14 = (bf16[64,512]{1,0:T(8,128)(2,1)S(1)}, bf16[64,512]{1,0:T(8,128)(2,1)S(1)}, u32[]{:S(2)}, u32[]{:S(2)}) collective-permute-start(bf16[64,512]{1,0:T(8,128)(2,1)S(1)} %collective-permute-done.11), channel_id=1, source_target_pairs={{0,6},{1,7},{2,4},{3,5},{4,2},{5,3},{6,0},{7,1},{8,14},{9,15},{10,... | collective-permute-start | bytes 196616 | tf_op jit(solution)/shard_map/ppermute | solution.py:106
  26.0 5.4 %collective-permute-start.13 = (bf16[64,512]{1,0:T(8,128)(2,1)S(1)}, bf16[64,512]{1,0:T(8,128)(2,1)S(1)}, u32[]{:S(2)}, u32[]{:S(2)}) collective-permute-start(bf16[64,512]{1,0:T(8,128)(2,1)S(1)} %collective-permute-done.11), channel_id=1, source_target_pairs={{0,4},{1,5},{2,6},{3,7},{4,0},{5,1},{6,2},{7,3},{8,12},{9,13},{10,... | collective-permute-start | bytes 196616 | tf_op jit(solution)/shard_map/ppermute | solution.py:106
  26.0 5.9 %collective-permute-start.12 = (bf16[64,512]{1,0:T(8,128)(2,1)S(1)}, bf16[64,512]{1,0:T(8,128)(2,1)S(1)}, u32[]{:S(2)}, u32[]{:S(2)}) collective-permute-start(bf16[64,512]{1,0:T(8,128)(2,1)S(1)} %collective-permute-done.11), channel_id=1, source_target_pairs={{0,2},{1,3},{2,0},{3,1},{4,6},{5,7},{6,4},{7,5},{8,10},{9,11},{10,... | collective-permute-start | bytes 196616 | tf_op jit(solution)/shard_map/ppermute | solution.py:106
  29.3 6.4 %collective-permute-start.5 = (bf16[2,64,768]{2,1,0:T(8,128)(2,1)S(1)}, bf16[2,64,768]{2,1,0:T(8,128)(2,1)S(1)}, u32[]{:S(2)}, u32[]{:S(2)}) collective-permute-start(bf16[2,64,768]{2,1,0:T(8,128)(2,1)S(1)} %pad_maximum_fusion.2.refs_0_), channel_id=1, source_target_pairs={{0,2},{1,3},{2,0},{3,1},{4,6},{5,7},{6,4},{7,5},{8,10},{9,11},{10,... | collective-permute-start | bytes 589832 | tf_op jit(solution)/shard_map/ppermute | solution.py:106
  31.9 3.8 %collective-permute-start.15 = (bf16[4,64,512]{2,1,0:T(8,128)(2,1)S(1)}, bf16[4,64,512]{2,1,0:T(8,128)(2,1)S(1)}, u32[]{:S(2)}, u32[]{:S(2)}) collective-permute-start(bf16[4,64,512]{2,1,0:T(8,128)(2,1)S(1)} %pad_maximum_fusion.1.refs_8_), channel_id=1, source_target_pairs={{0,1},{1,0},{2,3},{3,2},{4,5},{5,4},{6,7},{7,6},{8,9},{9,8},{10,11... | collective-permute-start | bytes 786440 | tf_op jit(solution)/shard_map/ppermute | solution.py:106
  32.0 5.1 %collective-permute-start.10 = (bf16[4,64,512]{2,1,0:T(8,128)(2,1)S(1)}, bf16[4,64,512]{2,1,0:T(8,128)(2,1)S(1)}, u32[]{:S(2)}, u32[]{:S(2)}) collective-permute-start(bf16[4,64,512]{2,1,0:T(8,128)(2,1)S(1)} %collective-permute-done.9.refs_6_), channel_id=1, source_target_pairs={{0,1},{1,0},{2,3},{3,2},{4,5},{5,4},{6,7},{7,6},{8,9},{9,8},{10,11... | collective-permute-start | bytes 786440 | tf_op jit(solution)/shard_map/ppermute | solution.py:106
  32.5 4.6 %collective-permute-start.8 = (bf16[4,64,512]{2,1,0:T(8,128)(2,1)S(1)}, bf16[4,64,512]{2,1,0:T(8,128)(2,1)S(1)}, u32[]{:S(2)}, u32[]{:S(2)}) collective-permute-start(bf16[4,64,512]{2,1,0:T(8,128)(2,1)S(1)} %collective-permute-done.7.refs_4_), channel_id=1, source_target_pairs={{0,1},{1,0},{2,3},{3,2},{4,5},{5,4},{6,7},{7,6},{8,9},{9,8},{10,11... | collective-permute-start | bytes 786440 | tf_op jit(solution)/shard_map/ppermute | solution.py:106
  32.6 3.1 %collective-permute-start.4 = (bf16[2,64,768]{2,1,0:T(8,128)(2,1)S(1)}, bf16[2,64,768]{2,1,0:T(8,128)(2,1)S(1)}, u32[]{:S(2)}, u32[]{:S(2)}) collective-permute-start(bf16[2,64,768]{2,1,0:T(8,128)(2,1)S(1)} %pad_maximum_fusion.2.refs_0_), channel_id=1, source_target_pairs={{0,1},{1,0},{2,3},{3,2},{4,5},{5,4},{6,7},{7,6},{8,9},{9,8},{10,11... | collective-permute-start | bytes 589832 | tf_op jit(solution)/shard_map/ppermute | solution.py:106
  35.7 1.4 %collective-permute-start.6 = (bf16[2,64,768]{2,1,0:T(8,128)(2,1)S(1)}, bf16[2,64,768]{2,1,0:T(8,128)(2,1)S(1)}, u32[]{:S(2)}, u32[]{:S(2)}) collective-permute-start(bf16[2,64,768]{2,1,0:T(8,128)(2,1)S(1)} %collective-permute-done.5.refs_2_), channel_id=1, source_target_pairs={{0,1},{1,0},{2,3},{3,2},{4,5},{5,4},{6,7},{7,6},{8,9},{9,8},{10,11... | collective-permute-start | bytes 589832 | tf_op jit(solution)/shard_map/ppermute | solution.py:106

commit v11 on v2

v11 whole, which is shorter than its diff:
```python
import functools

import jax
import jax.numpy as jnp
from jax import lax
from jax.experimental import pallas as pl
from jax.experimental.pallas import tpu as pltpu
from jax.sharding import PartitionSpec as P


def dense_rows_kernel(cols_ref, live_ref, tiles_ref, degrees_ref, features_ref, rows_ref):
    row_count, slots, tile_size = tiles_ref.shape
    nodes = row_count * lax.axis_size("shard")
    blocks = nodes // tile_size
    share = rows_ref.shape[1] - nodes
    if share:
        shares = features_ref.shape[1] // share
        first = pl.multiple_of(lax.rem(lax.axis_index("section"), shares) * share, 128)
        rows_ref[:, nodes:] = features_ref[:, pl.ds(first, share)]
    block_row = lax.axis_index("shard") * row_count // tile_size
    live = live_ref[0, block_row]
    wide = row_count * slots
    slot = lax.rem(lax.broadcasted_iota(jnp.int32, (1, wide), 1), slots)
    column = jnp.full((1, wide), -1, jnp.int32)
    for k in range(slots):
        column = jnp.where(slot == k, jnp.where(k < live, cols_ref[0, block_row, k], -1), column)
    owner = lax.div(lax.broadcasted_iota(jnp.int32, (row_count, wide), 1), slots)
    mine = lax.broadcasted_iota(jnp.int32, (row_count, wide), 0) == owner
    column = jnp.where(mine, jnp.broadcast_to(column, (row_count, wide)), -1)
    tiles = tiles_ref[...].reshape(wide, tile_size)
    degree = jnp.broadcast_to(degrees_ref[...].astype(jnp.float32), (row_count, row_count))
    diagonal = lax.broadcasted_iota(jnp.int32, (row_count, row_count), 0) == lax.broadcasted_iota(
        jnp.int32, (row_count, row_count), 1
    )
    scale = lax.rsqrt(jnp.sum(jnp.where(diagonal, degree, 0.0), axis=1, keepdims=True))
    for b in range(blocks):
        pick = (column == b).astype(jnp.bfloat16)
        summed = jnp.dot(pick, tiles, preferred_element_type=jnp.float32)
        rows_ref[:, b * tile_size : (b + 1) * tile_size] = (summed * scale).astype(jnp.bfloat16)


def dense_rows(tile_cols, live_tiles, tile_rows, degrees, features, share):
    row_count = tile_rows.shape[0]
    nodes = row_count * lax.axis_size("shard")
    return pl.pallas_call(
        dense_rows_kernel,
        out_shape=pltpu.VMEM((row_count, nodes + share), jnp.bfloat16),
        in_specs=[
            pl.BlockSpec(memory_space=pltpu.SMEM),
            pl.BlockSpec(memory_space=pltpu.SMEM),
            pl.BlockSpec(memory_space=pltpu.VMEM),
            pl.BlockSpec(memory_space=pltpu.VMEM),
            pl.BlockSpec(memory_space=pltpu.VMEM),
        ],
        out_specs=pl.BlockSpec(memory_space=pltpu.VMEM),
        name="dense_rows",
    )(tile_cols, live_tiles, tile_rows, degrees, features)


def chain_kernel(nodes, own_ref, *refs):
    pair_refs, out_ref, halves = refs[:-2], refs[-2], refs[-1]
    row_count = own_ref.shape[0]
    share = own_ref.shape[1] - nodes
    sections, chips = len(pair_refs) // 2, pair_refs[0].shape[0]
    section, shard = lax.axis_index("section"), lax.axis_index("shard")
    chip, first_core = lax.div(shard, 2), lax.rem(shard, 2) == 0

    def times(mask, columns):
        left, right = [], []
        for piece in range(chips):
            source = lax.bitwise_xor(chip, piece)
            left.append(halves[:, pl.ds(pl.multiple_of(source * 2 * row_count, 128), 2 * row_count)])
            here, there = pair_refs[2 * mask][piece, :, columns], pair_refs[2 * mask + 1][piece, :, columns]
            right += [jnp.where(first_core, here, there), jnp.where(first_core, there, here)]
        left, right = jnp.concatenate(left, axis=1), jnp.concatenate(right, axis=0)
        both = jnp.dot(left, right, preferred_element_type=jnp.float32)
        return both[:row_count] + both[row_count:]

    halves[:row_count] = own_ref[:, :nodes]
    halves[row_count:] = jnp.zeros((row_count, nodes), jnp.bfloat16)
    for at in range(sections):

        @pl.when(section == at)
        def _(at=at):
            for earlier in reversed(range(at)):
                product = times(at ^ earlier, slice(0, nodes))
                high = product.astype(jnp.bfloat16)
                halves[:row_count] = high
                halves[row_count:] = (product - high.astype(jnp.float32)).astype(jnp.bfloat16)
            for giver in range(out_ref.shape[1] // share):
                product = times(at ^ giver, slice(nodes, nodes + share))
                out_ref[:, giver * share : (giver + 1) * share] = product.astype(jnp.bfloat16)


def chain(own, pairs, nodes, width):
    row_count = own.shape[0]
    return pl.pallas_call(
        functools.partial(chain_kernel, nodes),
        out_shape=jax.ShapeDtypeStruct((row_count, width), jnp.bfloat16),
        in_specs=[pl.BlockSpec(memory_space=pltpu.VMEM)] * (1 + len(pairs)),
        out_specs=pl.BlockSpec(memory_space=pltpu.VMEM),
        scratch_shapes=[pltpu.VMEM((2 * row_count, nodes), jnp.bfloat16)],
        compiler_params=pltpu.CompilerParams(vmem_limit_bytes=32 * 1024 * 1024),
        name="chain",
    )(own, *pairs)


def by_products(own, nodes, width):
    sections, shards = lax.axis_size("section"), lax.axis_size("shard")

    def along_shard(value, mask):
        return lax.ppermute(value, "shard", [(i, i ^ mask) for i in range(shards)])

    def along_section(value, mask):
        return lax.ppermute(value, "section", [(i, i ^ mask) for i in range(sections)])

    def along_z(value):
        return jnp.stack([value] + [along_shard(value, 2 * mask) for mask in range(1, shards // 2)])

    ahead = {mask: along_section(own, mask) for mask in range(1, sections) if mask & (mask - 1)}
    mine, ahead = lax.optimization_barrier((along_z(own), ahead))
    gathered = [mine]
    for mask in range(1, sections):
        gathered.append(along_z(ahead[mask]) if mask in ahead else along_section(mine, mask))
    pairs = []
    for here in gathered:
        pairs += [here, along_shard(here, 1)]
    return chain(own, pairs, nodes, width)


def by_hops(features, own):
    sections = lax.axis_size("section")
    part = features.shape[1] // sections
    piece = lax.dynamic_slice_in_dim(features, lax.axis_index("section") * part, part, axis=1)
    relations = lax.all_gather(own, "section", axis=0, tiled=False)
    pieces = []
    for hop in range(sections):
        slab = lax.all_gather(piece, "shard", axis=0, tiled=True)
        piece = jnp.dot(relations[hop], slab, preferred_element_type=jnp.float32).astype(jnp.bfloat16)
        pieces.append(piece)
    mine = lax.all_to_all(jnp.stack(pieces), "section", split_axis=0, concat_axis=0, tiled=True)
    return jnp.swapaxes(mine, 0, 1).reshape(features.shape)


def per_device(features, tile_cols, live_tiles, tile_values, degrees):
    row_count, width = features.shape
    sections, shards = lax.axis_size("section"), lax.axis_size("shard")
    nodes = row_count * shards
    doubles = shards >= 2 and shards & (shards - 1) == 0 and sections & (sections - 1) == 0
    products = doubles and nodes <= width and width % (sections - 1) == 0
    share = width // (sections - 1) if products else 0
    own = dense_rows(tile_cols, live_tiles, tile_values[0], degrees, features, share)
    out = by_products(own, nodes, width) if products else by_hops(features, own)
    return out[None]


def solution(mesh):
    in_specs = (
        P("shard", None),
        P("section", None, None),
        P("section", None),
        P("section", "shard", None, None),
        P("section", "shard"),
    )
    out_specs = P("section", "shard", None)
    return jax.shard_map(
        per_device, mesh=mesh, in_specs=in_specs, out_specs=out_specs, check_vma=False
    )
```

time: 79.3 us -> 32.3 us (0.41)
  blocking collectives: 75.3 us -> 0 us
  starting transfers between devices: 0 us -> 16.4 us
  waiting for transfers between devices: 0 us -> 13.3 us
  local copies, waits for them, and re-layouts: 0.98 us -> 0 us
    all_gather x5 -> x0, blocking collectives: 67.8 us -> none  [the longest x4 57.1 us: per_device(): slab = lax.all_gather(piece, 'shard', axis=0, tiled=True)]
    ppermute x0 -> x13, starting transfers between devices: none -> 16.4 us  [the longest x10 10.8 us: along_shard(): return lax.ppermute(value, 'shard', [(i, i ^ mask) for i in range(shards)])]
    ppermute x0 -> x13, waiting for transfers between devices: none -> 13.3 us  [the longest x10 13.3 us: along_shard(): return lax.ppermute(value, 'shard', [(i, i ^ mask) for i in range(shards)])]
    all_to_all x1 -> x0, blocking collectives: 7.55 us -> none  [per_device(): lax.all_to_all(jnp.stack(pieces), 'section', split_axis=0, concat_axis=0,...]
    pallas_call x1 -> x2, Pallas kernels: 1.98 us -> 2.27 us  [the longest x1 1.33 us: dense_rows(): pl.pallas_call(dense_rows_kernel, out_shape=pltpu.VMEM((row_count, nodes...]
  transfers between devices with their start and end apart: 0 -> 13, of which waited for: 0 -> 7; matrix products, arithmetic and copies ran while one was open for 0% -> 0% of each run, Pallas kernels for 0% -> 0%
where the time goes in v11:
time: 32.3 us; the launch traced here: 32.1 us
  starting transfers between devices  16.4 us (51%)
  waiting for transfers between devices  13.3 us (41%)
  Pallas kernels  2.27 us (7%)
    ppermute x10, waiting for transfers between devices, along_shard(): return lax.ppermute(value, 'shard', [(i, i ^ mask) for i in range(shards)])  13.3 us
    ppermute x10, starting transfers between devices, along_shard(): return lax.ppermute(value, 'shard', [(i, i ^ mask) for i in range(shards)])  10.8 us
    ppermute x3, starting transfers between devices, along_section(): lax.ppermute(value, 'section', [(i, i ^ mask) for i in range(sections)])  5.64 us
    pallas_call x1, Pallas kernels, dense_rows(): pl.pallas_call(dense_rows_kernel, out_shape=pltpu.VMEM((row_count, nodes...  1.33 us
    pallas_call x1, Pallas kernels, chain(): pl.pallas_call(functools.partial(chain_kernel, nodes), out_shape=jax.Shap...  0.94 us
  transfers between devices with their start and end apart: 13, of which 7 were waited for; matrix products, arithmetic and copies ran while one was open for 0% of the time, Pallas kernels for 0%

profile of v11, /device:TPU:0, one launch (start us, length us, event | category | flops | bytes accessed | tf_op | source)
XLA Modules:
  0.0 32.1 jit_solution(15144564117660453614)
XLA Ops:
  0.0 1.3 %dense_rows.1.own_ref = bf16[64,768]{1,0:T(8,128)(2,1)S(1)} custom-call(s32[1,4,16]{2,1,0:T(4,128)} %cols_ref.1, s32[1,4]{1,0:T(1,128)} %live_ref.1, bf16[64,16,128]{2,1,0:T(8,128)(2,1)} %bitcast.11, s32[1,64]{1,0:T(1,128)} %degrees_ref.1, bf16[64,768]{1,0:T(8,128)(2,1)} %features_ref.1), custom_call_target="tpu_custom_call" | custom-call | tf_op jit(solution)/shard_map/dense_rows/pallas_call | solution.py:45
  1.3 5.1 %collective-permute-start.2 = (bf16[64,768]{1,0:T(8,128)(2,1)S(1)}, bf16[64,768]{1,0:T(8,128)(2,1)S(1)}, u32[]{:S(2)}, u32[]{:S(2)}) collective-permute-start(bf16[64,768]{1,0:T(8,128)(2,1)S(1)} %dense_rows.1.own_ref), channel_id=1, source_target_pairs={{0,6},{1,7},{2,4},{3,5},{4,2},{5,3},{6,0},{7,1},{8,14},{9,15},{10,... | collective-permute-start | bytes 294920 | tf_op jit(solution)/shard_map/ppermute | solution.py:112
  6.5 0.0 collective-permute-start.1
  6.5 0.6 %collective-permute-start = (bf16[64,768]{1,0:T(8,128)(2,1)S(1)}, bf16[64,768]{1,0:T(8,128)(2,1)S(1)}, u32[]{:S(2)}, u32[]{:S(2)}) collective-permute-start(bf16[64,768]{1,0:T(8,128)(2,1)S(1)} %dense_rows.1.own_ref), channel_id=1, source_target_pairs={{0,2},{1,3},{2,0},{3,1},{4,6},{5,7},{6,4},{7,5},{8,10},{9,11},{10,... | collective-permute-start | bytes 294920 | tf_op jit(solution)/shard_map/ppermute | solution.py:112
  7.1 2.6 %collective-permute-start.3 = (bf16[64,768]{1,0:T(8,128)(2,1)S(1)}, bf16[64,768]{1,0:T(8,128)(2,1)S(1)}, u32[]{:S(2)}, u32[]{:S(2)}) collective-permute-start(bf16[64,768]{1,0:T(8,128)(2,1)S(1)} %dense_rows.1.own_ref), channel_id=1, source_target_pairs={{0,24},{8,16},{16,8},{24,0},{1,25},{9,17},{17,9},{25,1},{2,26},{10... | collective-permute-start | bytes 294920 | tf_op jit(solution)/shard_map/ppermute | solution.py:115
  9.7 0.5 %collective-permute-done.2 = bf16[64,768]{1,0:T(8,128)(2,1)S(1)} collective-permute-done((bf16[64,768]{1,0:T(8,128)(2,1)S(1)}, bf16[64,768]{1,0:T(8,128)(2,1)S(1)}, u32[]{:S(2)}, u32[]{:S(2)}) %collective-permute-start.2) | collective-permute-done | bytes 98336 | tf_op jit(solution)/shard_map/ppermute | solution.py:112
  10.1 4.6 %collective-permute-done.1 = bf16[64,768]{1,0:T(8,128)(2,1)S(1)} collective-permute-done((bf16[64,768]{1,0:T(8,128)(2,1)S(1)}, bf16[64,768]{1,0:T(8,128)(2,1)S(1)}, u32[]{:S(2)}, u32[]{:S(2)}) %collective-permute-start.1) | collective-permute-done | bytes 98336 | tf_op jit(solution)/shard_map/ppermute | solution.py:112
  14.7 0.0 collective-permute-done
  14.7 0.1 pad_maximum_fusion.refs_0_
  14.8 1.6 %collective-permute-start.7 = (bf16[4,64,768]{2,1,0:T(8,128)(2,1)S(1)}, bf16[4,64,768]{2,1,0:T(8,128)(2,1)S(1)}, u32[]{:S(2)}, u32[]{:S(2)}) collective-permute-start(bf16[4,64,768]{2,1,0:T(8,128)(2,1)S(1)} %pad_maximum_fusion.refs_0_), channel_id=1, source_target_pairs={{0,16},{8,24},{16,0},{24,8},{1,17},{9,25},{17,1},{25,9},{2,18},{10... | collective-permute-start | bytes 1179656 | tf_op jit(solution)/shard_map/ppermute | solution.py:115
  16.4 1.5 %collective-permute-start.5 = (bf16[4,64,768]{2,1,0:T(8,128)(2,1)S(1)}, bf16[4,64,768]{2,1,0:T(8,128)(2,1)S(1)}, u32[]{:S(2)}, u32[]{:S(2)}) collective-permute-start(bf16[4,64,768]{2,1,0:T(8,128)(2,1)S(1)} %pad_maximum_fusion.refs_0_), channel_id=1, source_target_pairs={{0,8},{8,0},{16,24},{24,16},{1,9},{9,1},{17,25},{25,17},{2,10},{10... | collective-permute-start | bytes 1179656 | tf_op jit(solution)/shard_map/ppermute | solution.py:115
  17.9 2.5 %collective-permute-start.11 = (bf16[64,768]{1,0:T(8,128)(2,1)S(1)}, bf16[64,768]{1,0:T(8,128)(2,1)S(1)}, u32[]{:S(2)}, u32[]{:S(2)}) collective-permute-start(bf16[64,768]{1,0:T(8,128)(2,1)S(1)} %collective-permute-done.3), channel_id=1, source_target_pairs={{0,6},{1,7},{2,4},{3,5},{4,2},{5,3},{6,0},{7,1},{8,14},{9,15},{10,... | collective-permute-start | bytes 294920 | tf_op jit(solution)/shard_map/ppermute | solution.py:112
  20.4 1.9 %collective-permute-start.9 = (bf16[64,768]{1,0:T(8,128)(2,1)S(1)}, bf16[64,768]{1,0:T(8,128)(2,1)S(1)}, u32[]{:S(2)}, u32[]{:S(2)}) collective-permute-start(bf16[64,768]{1,0:T(8,128)(2,1)S(1)} %collective-permute-done.3), channel_id=1, source_target_pairs={{0,2},{1,3},{2,0},{3,1},{4,6},{5,7},{6,4},{7,5},{8,10},{9,11},{10,... | collective-permute-start | bytes 294920 | tf_op jit(solution)/shard_map/ppermute | solution.py:112
  22.3 3.1 %collective-permute-done.11 = bf16[64,768]{1,0:T(8,128)(2,1)S(1)} collective-permute-done((bf16[64,768]{1,0:T(8,128)(2,1)S(1)}, bf16[64,768]{1,0:T(8,128)(2,1)S(1)}, u32[]{:S(2)}, u32[]{:S(2)}) %collective-permute-start.11) | collective-permute-done | bytes 98336 | tf_op jit(solution)/shard_map/ppermute | solution.py:112
  25.3 2.9 %collective-permute-done.10 = bf16[64,768]{1,0:T(8,128)(2,1)S(1)} collective-permute-done((bf16[64,768]{1,0:T(8,128)(2,1)S(1)}, bf16[64,768]{1,0:T(8,128)(2,1)S(1)}, u32[]{:S(2)}, u32[]{:S(2)}) %collective-permute-start.10) | collective-permute-done | bytes 98336 | tf_op jit(solution)/shard_map/ppermute | solution.py:112
  28.2 0.1 pad_maximum_fusion.1.refs_6_
  28.3 0.1 collective-permute-start.12
  28.4 0.5 %collective-permute-start.8 = (bf16[4,64,768]{2,1,0:T(8,128)(2,1)S(1)}, bf16[4,64,768]{2,1,0:T(8,128)(2,1)S(1)}, u32[]{:S(2)}, u32[]{:S(2)}) collective-permute-start(bf16[4,64,768]{2,1,0:T(8,128)(2,1)S(1)} %collective-permute-done.7.refs_4_), channel_id=1, source_target_pairs={{0,1},{1,0},{2,3},{3,2},{4,5},{5,4},{6,7},{7,6},{8,9},{9,8},{10,11... | collective-permute-start | bytes 1179656 | tf_op jit(solution)/shard_map/ppermute | solution.py:112
  28.9 0.1 collective-permute-start.6
  28.9 0.0 collective-permute-done.4.refs_1_
  29.0 1.1 %collective-permute-done.12.refs_7_ = bf16[4,64,768]{2,1,0:T(8,128)(2,1)S(1)} collective-permute-done((bf16[4,64,768]{2,1,0:T(8,128)(2,1)S(1)}, bf16[4,64,768]{2,1,0:T(8,128)(2,1)S(1)}, u32[]{:S(2)}, u32[]{:S(2)}) %collective-permute-start.12) | collective-permute-done | bytes 393248 | tf_op jit(solution)/shard_map/ppermute | solution.py:112
  30.1 0.6 %collective-permute-done.8.refs_5_ = bf16[4,64,768]{2,1,0:T(8,128)(2,1)S(1)} collective-permute-done((bf16[4,64,768]{2,1,0:T(8,128)(2,1)S(1)}, bf16[4,64,768]{2,1,0:T(8,128)(2,1)S(1)}, u32[]{:S(2)}, u32[]{:S(2)}) %collective-permute-start.8) | collective-permute-done | bytes 393248 | tf_op jit(solution)/shard_map/ppermute | solution.py:112
  30.6 0.6 %collective-permute-done.6.refs_3_ = bf16[4,64,768]{2,1,0:T(8,128)(2,1)S(1)} collective-permute-done((bf16[4,64,768]{2,1,0:T(8,128)(2,1)S(1)}, bf16[4,64,768]{2,1,0:T(8,128)(2,1)S(1)}, u32[]{:S(2)}, u32[]{:S(2)}) %collective-permute-start.6) | collective-permute-done | bytes 393248 | tf_op jit(solution)/shard_map/ppermute | solution.py:112
  31.2 0.9 %chain.1 = bf16[64,768]{1,0:T(8,128)(2,1)} custom-call(bf16[64,768]{1,0:T(8,128)(2,1)S(1)} %dense_rows.1.own_ref, bf16[4,64,768]{2,1,0:T(8,128)(2,1)S(1)} %pad_maximum_fusion.refs_0_, bf16[4,64,768]{2,1,0:T(8,128)(2,1)S(1)} %collective-permute-done.4.refs_1_, bf16[4,64,768]{2,1,0:T(8,128)(2,1)S(1)} %collective-permute-done.5.refs_2_, ...), custom_call_target="tpu_custom_call" | custom-call | tf_op jit(solution)/shard_map/chain/pallas_call | solution.py:97
  (6 shorter events, 0.0 us)
Async XLA Ops:
  1.3 8.8 %collective-permute-start.2 = (bf16[64,768]{1,0:T(8,128)(2,1)S(1)}, bf16[64,768]{1,0:T(8,128)(2,1)S(1)}, u32[]{:S(2)}, u32[]{:S(2)}) collective-permute-start(bf16[64,768]{1,0:T(8,128)(2,1)S(1)} %dense_rows.1.own_ref), channel_id=1, source_target_pairs={{0,6},{1,7},{2,4},{3,5},{4,2},{5,3},{6,0},{7,1},{8,14},{9,15},{10,... | collective-permute-start | bytes 294920 | tf_op jit(solution)/shard_map/ppermute | solution.py:112
  6.5 8.3 %collective-permute-start.1 = (bf16[64,768]{1,0:T(8,128)(2,1)S(1)}, bf16[64,768]{1,0:T(8,128)(2,1)S(1)}, u32[]{:S(2)}, u32[]{:S(2)}) collective-permute-start(bf16[64,768]{1,0:T(8,128)(2,1)S(1)} %dense_rows.1.own_ref), channel_id=1, source_target_pairs={{0,4},{1,5},{2,6},{3,7},{4,0},{5,1},{6,2},{7,3},{8,12},{9,13},{10,... | collective-permute-start | bytes 294920 | tf_op jit(solution)/shard_map/ppermute | solution.py:112
  6.5 8.3 %collective-permute-start = (bf16[64,768]{1,0:T(8,128)(2,1)S(1)}, bf16[64,768]{1,0:T(8,128)(2,1)S(1)}, u32[]{:S(2)}, u32[]{:S(2)}) collective-permute-start(bf16[64,768]{1,0:T(8,128)(2,1)S(1)} %dense_rows.1.own_ref), channel_id=1, source_target_pairs={{0,2},{1,3},{2,0},{3,1},{4,6},{5,7},{6,4},{7,5},{8,10},{9,11},{10,... | collective-permute-start | bytes 294920 | tf_op jit(solution)/shard_map/ppermute | solution.py:112
  7.1 7.7 %collective-permute-start.3 = (bf16[64,768]{1,0:T(8,128)(2,1)S(1)}, bf16[64,768]{1,0:T(8,128)(2,1)S(1)}, u32[]{:S(2)}, u32[]{:S(2)}) collective-permute-start(bf16[64,768]{1,0:T(8,128)(2,1)S(1)} %dense_rows.1.own_ref), channel_id=1, source_target_pairs={{0,24},{8,16},{16,8},{24,0},{1,25},{9,17},{17,9},{25,1},{2,26},{10... | collective-permute-start | bytes 294920 | tf_op jit(solution)/shard_map/ppermute | solution.py:115
  14.8 13.6 %collective-permute-start.7 = (bf16[4,64,768]{2,1,0:T(8,128)(2,1)S(1)}, bf16[4,64,768]{2,1,0:T(8,128)(2,1)S(1)}, u32[]{:S(2)}, u32[]{:S(2)}) collective-permute-start(bf16[4,64,768]{2,1,0:T(8,128)(2,1)S(1)} %pad_maximum_fusion.refs_0_), channel_id=1, source_target_pairs={{0,16},{8,24},{16,0},{24,8},{1,17},{9,25},{17,1},{25,9},{2,18},{10... | collective-permute-start | bytes 1179656 | tf_op jit(solution)/shard_map/ppermute | solution.py:115
  16.4 12.5 %collective-permute-start.5 = (bf16[4,64,768]{2,1,0:T(8,128)(2,1)S(1)}, bf16[4,64,768]{2,1,0:T(8,128)(2,1)S(1)}, u32[]{:S(2)}, u32[]{:S(2)}) collective-permute-start(bf16[4,64,768]{2,1,0:T(8,128)(2,1)S(1)} %pad_maximum_fusion.refs_0_), channel_id=1, source_target_pairs={{0,8},{8,0},{16,24},{24,16},{1,9},{9,1},{17,25},{25,17},{2,10},{10... | collective-permute-start | bytes 1179656 | tf_op jit(solution)/shard_map/ppermute | solution.py:115
  17.9 7.5 %collective-permute-start.11 = (bf16[64,768]{1,0:T(8,128)(2,1)S(1)}, bf16[64,768]{1,0:T(8,128)(2,1)S(1)}, u32[]{:S(2)}, u32[]{:S(2)}) collective-permute-start(bf16[64,768]{1,0:T(8,128)(2,1)S(1)} %collective-permute-done.3), channel_id=1, source_target_pairs={{0,6},{1,7},{2,4},{3,5},{4,2},{5,3},{6,0},{7,1},{8,14},{9,15},{10,... | collective-permute-start | bytes 294920 | tf_op jit(solution)/shard_map/ppermute | solution.py:112
  20.4 7.8 %collective-permute-start.10 = (bf16[64,768]{1,0:T(8,128)(2,1)S(1)}, bf16[64,768]{1,0:T(8,128)(2,1)S(1)}, u32[]{:S(2)}, u32[]{:S(2)}) collective-permute-start(bf16[64,768]{1,0:T(8,128)(2,1)S(1)} %collective-permute-done.3), channel_id=1, source_target_pairs={{0,4},{1,5},{2,6},{3,7},{4,0},{5,1},{6,2},{7,3},{8,12},{9,13},{10,... | collective-permute-start | bytes 294920 | tf_op jit(solution)/shard_map/ppermute | solution.py:112
  20.4 7.8 %collective-permute-start.9 = (bf16[64,768]{1,0:T(8,128)(2,1)S(1)}, bf16[64,768]{1,0:T(8,128)(2,1)S(1)}, u32[]{:S(2)}, u32[]{:S(2)}) collective-permute-start(bf16[64,768]{1,0:T(8,128)(2,1)S(1)} %collective-permute-done.3), channel_id=1, source_target_pairs={{0,2},{1,3},{2,0},{3,1},{4,6},{5,7},{6,4},{7,5},{8,10},{9,11},{10,... | collective-permute-start | bytes 294920 | tf_op jit(solution)/shard_map/ppermute | solution.py:112
  25.3 3.6 %collective-permute-start.4 = (bf16[4,64,768]{2,1,0:T(8,128)(2,1)S(1)}, bf16[4,64,768]{2,1,0:T(8,128)(2,1)S(1)}, u32[]{:S(2)}, u32[]{:S(2)}) collective-permute-start(bf16[4,64,768]{2,1,0:T(8,128)(2,1)S(1)} %pad_maximum_fusion.refs_0_), channel_id=1, source_target_pairs={{0,1},{1,0},{2,3},{3,2},{4,5},{5,4},{6,7},{7,6},{8,9},{9,8},{10,11... | collective-permute-start | bytes 1179656 | tf_op jit(solution)/shard_map/ppermute | solution.py:112
  28.3 1.8 %collective-permute-start.12 = (bf16[4,64,768]{2,1,0:T(8,128)(2,1)S(1)}, bf16[4,64,768]{2,1,0:T(8,128)(2,1)S(1)}, u32[]{:S(2)}, u32[]{:S(2)}) collective-permute-start(bf16[4,64,768]{2,1,0:T(8,128)(2,1)S(1)} %pad_maximum_fusion.1.refs_6_), channel_id=1, source_target_pairs={{0,1},{1,0},{2,3},{3,2},{4,5},{5,4},{6,7},{7,6},{8,9},{9,8},{10,11... | collective-permute-start | bytes 1179656 | tf_op jit(solution)/shard_map/ppermute | solution.py:112
  28.4 2.3 %collective-permute-start.8 = (bf16[4,64,768]{2,1,0:T(8,128)(2,1)S(1)}, bf16[4,64,768]{2,1,0:T(8,128)(2,1)S(1)}, u32[]{:S(2)}, u32[]{:S(2)}) collective-permute-start(bf16[4,64,768]{2,1,0:T(8,128)(2,1)S(1)} %collective-permute-done.7.refs_4_), channel_id=1, source_target_pairs={{0,1},{1,0},{2,3},{3,2},{4,5},{5,4},{6,7},{7,6},{8,9},{9,8},{10,11... | collective-permute-start | bytes 1179656 | tf_op jit(solution)/shard_map/ppermute | solution.py:112
  28.9 2.3 %collective-permute-start.6 = (bf16[4,64,768]{2,1,0:T(8,128)(2,1)S(1)}, bf16[4,64,768]{2,1,0:T(8,128)(2,1)S(1)}, u32[]{:S(2)}, u32[]{:S(2)}) collective-permute-start(bf16[4,64,768]{2,1,0:T(8,128)(2,1)S(1)} %collective-permute-done.5.refs_2_), channel_id=1, source_target_pairs={{0,1},{1,0},{2,3},{3,2},{4,5},{5,4},{6,7},{7,6},{8,9},{9,8},{10,11... | collective-permute-start | bytes 1179656 | tf_op jit(solution)/shard_map/ppermute | solution.py:112

commit v12 on v11

--- a/solution.py
+++ b/solution.py
@@ -57,52 +57,87 @@
     )(tile_cols, live_tiles, tile_rows, degrees, features)
 
 
-def chain_kernel(nodes, own_ref, *refs):
-    pair_refs, out_ref, halves = refs[:-2], refs[-2], refs[-1]
-    row_count = own_ref.shape[0]
-    share = own_ref.shape[1] - nodes
-    sections, chips = len(pair_refs) // 2, pair_refs[0].shape[0]
-    section, shard = lax.axis_index("section"), lax.axis_index("shard")
+def split_chain(section):
+    masks = [section ^ earlier for earlier in reversed(range(section))]
+    count = next((i for i, mask in enumerate(masks) if mask & (mask - 1)), len(masks))
+    return masks[:count], masks[count:]
+
+
+def times(halves, pair_refs, mask, columns):
+    row_count = halves.shape[0] // 2
+    shard = lax.axis_index("shard")
     chip, first_core = lax.div(shard, 2), lax.rem(shard, 2) == 0
-
-    def times(mask, columns):
-        left, right = [], []
-        for piece in range(chips):
-            source = lax.bitwise_xor(chip, piece)
-            left.append(halves[:, pl.ds(pl.multiple_of(source * 2 * row_count, 128), 2 * row_count)])
-            here, there = pair_refs[2 * mask][piece, :, columns], pair_refs[2 * mask + 1][piece, :, columns]
-            right += [jnp.where(first_core, here, there), jnp.where(first_core, there, here)]
-        left, right = jnp.concatenate(left, axis=1), jnp.concatenate(right, axis=0)
-        both = jnp.dot(left, right, preferred_element_type=jnp.float32)
-        return both[:row_count] + both[row_count:]
-
+    here_ref, there_ref = pair_refs[mask]
+    left, right = [], []
+    for piece in range(here_ref.shape[0]):
+        source = lax.bitwise_xor(chip, piece)
+        left.append(halves[:, pl.ds(pl.multiple_of(source * 2 * row_count, 128), 2 * row_count)])
+        here, there = here_ref[piece, :, columns], there_ref[piece, :, columns]
+        right += [jnp.where(first_core, here, there), jnp.where(first_core, there, here)]
+    left, right = jnp.concatenate(left, axis=1), jnp.concatenate(right, axis=0)
+    both = jnp.dot(left, right, preferred_element_type=jnp.float32)
+    return both[:row_count] + both[row_count:]
+
+
+def multiply_through(halves, pair_refs, masks):
+    row_count, nodes = halves.shape[0] // 2, halves.shape[1]
+    for mask in masks:
+        product = times(halves, pair_refs, mask, slice(0, nodes))
+        high = product.astype(jnp.bfloat16)
+        halves[:row_count] = high
+        halves[row_count:] = (product - high.astype(jnp.float32)).astype(jnp.bfloat16)
+
+
+def first_kernel(masks, sections, own_ref, *refs):
+    pair_refs, halves = dict(zip(masks, zip(refs[:-1:2], refs[1:-1:2]))), refs[-1]
+    row_count, nodes = own_ref.shape[0], halves.shape[1]
     halves[:row_count] = own_ref[:, :nodes]
     halves[row_count:] = jnp.zeros((row_count, nodes), jnp.bfloat16)
     for at in range(sections):
-
-        @pl.when(section == at)
+        near, _ = split_chain(at)
+        if near:
+            pl.when(lax.axis_index("section") == at)(functools.partial(multiply_through, halves, pair_refs, near))
+
+
+def second_kernel(sections, first_ref, *refs):
+    pair_refs, out_ref, halves = list(zip(refs[:-2:2], refs[1:-2:2])), refs[-2], refs[-1]
+    nodes = halves.shape[1]
+    share = pair_refs[0][0].shape[2] - nodes
+    halves[...] = first_ref[...]
+    for at in range(sections):
+
+        @pl.when(lax.axis_index("section") == at)
         def _(at=at):
-            for earlier in reversed(range(at)):
-                product = times(at ^ earlier, slice(0, nodes))
-                high = product.astype(jnp.bfloat16)
-                halves[:row_count] = high
-                halves[row_count:] = (product - high.astype(jnp.float32)).astype(jnp.bfloat16)
+            multiply_through(halves, pair_refs, split_chain(at)[1])
             for giver in range(out_ref.shape[1] // share):
-                product = times(at ^ giver, slice(nodes, nodes + share))
+                product = times(halves, pair_refs, at ^ giver, slice(nodes, nodes + share))
                 out_ref[:, giver * share : (giver + 1) * share] = product.astype(jnp.bfloat16)
 
 
-def chain(own, pairs, nodes, width):
-    row_count = own.shape[0]
+def first_products(own, pairs, nodes, sections):
+    masks = [mask for mask in range(1, sections) if not mask & (mask - 1)]
+    operands = [array for mask in masks for array in pairs[mask]]
     return pl.pallas_call(
-        functools.partial(chain_kernel, nodes),
-        out_shape=jax.ShapeDtypeStruct((row_count, width), jnp.bfloat16),
-        in_specs=[pl.BlockSpec(memory_space=pltpu.VMEM)] * (1 + len(pairs)),
+        functools.partial(first_kernel, masks, sections),
+        out_shape=pltpu.VMEM((2 * own.shape[0], nodes), jnp.bfloat16),
+        in_specs=[pl.BlockSpec(memory_space=pltpu.VMEM)] * (1 + len(operands)),
         out_specs=pl.BlockSpec(memory_space=pltpu.VMEM),
-        scratch_shapes=[pltpu.VMEM((2 * row_count, nodes), jnp.bfloat16)],
         compiler_params=pltpu.CompilerParams(vmem_limit_bytes=32 * 1024 * 1024),
-        name="chain",
-    )(own, *pairs)
+        name="first_products",
+    )(own, *operands)
+
+
+def second_products(first, pairs, width, sections):
+    operands = [array for pair in pairs for array in pair]
+    return pl.pallas_call(
+        functools.partial(second_kernel, sections),
+        out_shape=jax.ShapeDtypeStruct((first.shape[0] // 2, width), jnp.bfloat16),
+        in_specs=[pl.BlockSpec(memory_space=pltpu.VMEM)] * (1 + len(operands)),
+        out_specs=pl.BlockSpec(memory_space=pltpu.VMEM),
+        scratch_shapes=[pltpu.VMEM(first.shape, jnp.bfloat16)],
+        compiler_params=pltpu.CompilerParams(vmem_limit_bytes=32 * 1024 * 1024),
+        name="second_products",
+    )(first, *operands)
 
 
 def by_products(own, nodes, width):
@@ -122,10 +157,9 @@
     gathered = [mine]
     for mask in range(1, sections):
         gathered.append(along_z(ahead[mask]) if mask in ahead else along_section(mine, mask))
-    pairs = []
-    for here in gathered:
-        pairs += [here, along_shard(here, 1)]
-    return chain(own, pairs, nodes, width)
+    pairs = [(here, along_shard(here, 1)) for here in gathered]
+    first = first_products(own, pairs, nodes, sections)
+    return second_products(first, pairs, width, sections)
 
 
 def by_hops(features, own):

time: 32.3 us -> 31.2 us (0.966)
  waiting for transfers between devices: 13.3 us -> 12.2 us
    ppermute x10, waiting for transfers between devices: 13.3 us -> 11.7 us  [along_shard(): return lax.ppermute(value, 'shard', [(i, i ^ mask) for i in range(shards)])]
    ppermute x3, waiting for transfers between devices: 0.01 us -> 0.42 us  [along_section(): lax.ppermute(value, 'section', [(i, i ^ mask) for i in range(sections)])]
    pallas_call x1 -> x2, Pallas kernels: 0.94 us -> 0.96 us  [the longest x1 0.94 us: second_products(): pl.pallas_call(functools.partial(second_kernel, sections), out_shape=jax....]
  transfers between devices with their start and end apart: 13 -> 13, of which waited for: 7 -> 6; matrix products, arithmetic and copies ran while one was open for 0% -> 0% of each run, Pallas kernels for 0% -> 0%
where the time goes in v12:
time: 31.2 us; the launch traced here: 31 us
  starting transfers between devices  16.4 us (53%)
  waiting for transfers between devices  12.2 us (39%)
  Pallas kernels  2.29 us (7%)
    ppermute x10, waiting for transfers between devices, along_shard(): return lax.ppermute(value, 'shard', [(i, i ^ mask) for i in range(shards)])  11.7 us
    ppermute x10, starting transfers between devices, along_shard(): return lax.ppermute(value, 'shard', [(i, i ^ mask) for i in range(shards)])  10.7 us
    ppermute x3, starting transfers between devices, along_section(): lax.ppermute(value, 'section', [(i, i ^ mask) for i in range(sections)])  5.64 us
    pallas_call x1, Pallas kernels, dense_rows(): pl.pallas_call(dense_rows_kernel, out_shape=pltpu.VMEM((row_count, nodes...  1.33 us
    pallas_call x1, Pallas kernels, second_products(): pl.pallas_call(functools.partial(second_kernel, sections), out_shape=jax....  0.94 us
  transfers between devices with their start and end apart: 13, of which 6 were waited for; matrix products, arithmetic and copies ran while one was open for 0% of the time, Pallas kernels for 0%

profile of v12, /device:TPU:0, one launch (start us, length us, event | category | flops | bytes accessed | tf_op | source)
XLA Modules:
  0.0 31.0 jit_solution(7830789606235849362)
XLA Ops:
  0.0 1.3 %dense_rows.1.own_ref = bf16[64,768]{1,0:T(8,128)(2,1)S(1)} custom-call(s32[1,4,16]{2,1,0:T(4,128)} %cols_ref.1, s32[1,4]{1,0:T(1,128)} %live_ref.1, bf16[64,16,128]{2,1,0:T(8,128)(2,1)} %bitcast.11, s32[1,64]{1,0:T(1,128)} %degrees_ref.1, bf16[64,768]{1,0:T(8,128)(2,1)} %features_ref.1), custom_call_target="tpu_custom_call" | custom-call | tf_op jit(solution)/shard_map/dense_rows/pallas_call | solution.py:45
  1.3 5.1 %collective-permute-start.2 = (bf16[64,768]{1,0:T(8,128)(2,1)S(1)}, bf16[64,768]{1,0:T(8,128)(2,1)S(1)}, u32[]{:S(2)}, u32[]{:S(2)}) collective-permute-start(bf16[64,768]{1,0:T(8,128)(2,1)S(1)} %dense_rows.1.own_ref), channel_id=1, source_target_pairs={{0,6},{1,7},{2,4},{3,5},{4,2},{5,3},{6,0},{7,1},{8,14},{9,15},{10,... | collective-permute-start | bytes 294920 | tf_op jit(solution)/shard_map/ppermute | solution.py:147
  6.5 0.0 collective-permute-start.1
  6.5 0.6 %collective-permute-start = (bf16[64,768]{1,0:T(8,128)(2,1)S(1)}, bf16[64,768]{1,0:T(8,128)(2,1)S(1)}, u32[]{:S(2)}, u32[]{:S(2)}) collective-permute-start(bf16[64,768]{1,0:T(8,128)(2,1)S(1)} %dense_rows.1.own_ref), channel_id=1, source_target_pairs={{0,2},{1,3},{2,0},{3,1},{4,6},{5,7},{6,4},{7,5},{8,10},{9,11},{10,... | collective-permute-start | bytes 294920 | tf_op jit(solution)/shard_map/ppermute | solution.py:147
  7.1 2.6 %collective-permute-start.3 = (bf16[64,768]{1,0:T(8,128)(2,1)S(1)}, bf16[64,768]{1,0:T(8,128)(2,1)S(1)}, u32[]{:S(2)}, u32[]{:S(2)}) collective-permute-start(bf16[64,768]{1,0:T(8,128)(2,1)S(1)} %dense_rows.1.own_ref), channel_id=1, source_target_pairs={{0,24},{8,16},{16,8},{24,0},{1,25},{9,17},{17,9},{25,1},{2,26},{10... | collective-permute-start | bytes 294920 | tf_op jit(solution)/shard_map/ppermute | solution.py:150
  9.7 0.5 %collective-permute-done.2 = bf16[64,768]{1,0:T(8,128)(2,1)S(1)} collective-permute-done((bf16[64,768]{1,0:T(8,128)(2,1)S(1)}, bf16[64,768]{1,0:T(8,128)(2,1)S(1)}, u32[]{:S(2)}, u32[]{:S(2)}) %collective-permute-start.2) | collective-permute-done | bytes 98336 | tf_op jit(solution)/shard_map/ppermute | solution.py:147
  10.1 4.6 %collective-permute-done.1 = bf16[64,768]{1,0:T(8,128)(2,1)S(1)} collective-permute-done((bf16[64,768]{1,0:T(8,128)(2,1)S(1)}, bf16[64,768]{1,0:T(8,128)(2,1)S(1)}, u32[]{:S(2)}, u32[]{:S(2)}) %collective-permute-start.1) | collective-permute-done | bytes 98336 | tf_op jit(solution)/shard_map/ppermute | solution.py:147
  14.7 0.0 collective-permute-done
  14.7 0.1 pad_maximum_fusion.refs_0_
  14.8 0.0 collective-permute-done.3
  14.8 1.6 %collective-permute-start.6 = (bf16[4,64,768]{2,1,0:T(8,128)(2,1)S(1)}, bf16[4,64,768]{2,1,0:T(8,128)(2,1)S(1)}, u32[]{:S(2)}, u32[]{:S(2)}) collective-permute-start(bf16[4,64,768]{2,1,0:T(8,128)(2,1)S(1)} %pad_maximum_fusion.refs_0_), channel_id=1, source_target_pairs={{0,16},{8,24},{16,0},{24,8},{1,17},{9,25},{17,1},{25,9},{2,18},{10... | collective-permute-start | bytes 1179656 | tf_op jit(solution)/shard_map/ppermute | solution.py:150
  16.4 1.5 %collective-permute-start.4 = (bf16[4,64,768]{2,1,0:T(8,128)(2,1)S(1)}, bf16[4,64,768]{2,1,0:T(8,128)(2,1)S(1)}, u32[]{:S(2)}, u32[]{:S(2)}) collective-permute-start(bf16[4,64,768]{2,1,0:T(8,128)(2,1)S(1)} %pad_maximum_fusion.refs_0_), channel_id=1, source_target_pairs={{0,8},{8,0},{16,24},{24,16},{1,9},{9,1},{17,25},{25,17},{2,10},{10... | collective-permute-start | bytes 1179656 | tf_op jit(solution)/shard_map/ppermute | solution.py:150
  17.9 2.5 %collective-permute-start.11 = (bf16[64,768]{1,0:T(8,128)(2,1)S(1)}, bf16[64,768]{1,0:T(8,128)(2,1)S(1)}, u32[]{:S(2)}, u32[]{:S(2)}) collective-permute-start(bf16[64,768]{1,0:T(8,128)(2,1)S(1)} %collective-permute-done.3), channel_id=1, source_target_pairs={{0,6},{1,7},{2,4},{3,5},{4,2},{5,3},{6,0},{7,1},{8,14},{9,15},{10,... | collective-permute-start | bytes 294920 | tf_op jit(solution)/shard_map/ppermute | solution.py:147
  20.4 0.0 collective-permute-start.10
  20.4 1.9 %collective-permute-start.9 = (bf16[64,768]{1,0:T(8,128)(2,1)S(1)}, bf16[64,768]{1,0:T(8,128)(2,1)S(1)}, u32[]{:S(2)}, u32[]{:S(2)}) collective-permute-start(bf16[64,768]{1,0:T(8,128)(2,1)S(1)} %collective-permute-done.3), channel_id=1, source_target_pairs={{0,2},{1,3},{2,0},{3,1},{4,6},{5,7},{6,4},{7,5},{8,10},{9,11},{10,... | collective-permute-start | bytes 294920 | tf_op jit(solution)/shard_map/ppermute | solution.py:147
  22.3 3.1 %collective-permute-done.11 = bf16[64,768]{1,0:T(8,128)(2,1)S(1)} collective-permute-done((bf16[64,768]{1,0:T(8,128)(2,1)S(1)}, bf16[64,768]{1,0:T(8,128)(2,1)S(1)}, u32[]{:S(2)}, u32[]{:S(2)}) %collective-permute-start.11) | collective-permute-done | bytes 98336 | tf_op jit(solution)/shard_map/ppermute | solution.py:147
  25.3 0.5 %collective-permute-start.7 = (bf16[4,64,768]{2,1,0:T(8,128)(2,1)S(1)}, bf16[4,64,768]{2,1,0:T(8,128)(2,1)S(1)}, u32[]{:S(2)}, u32[]{:S(2)}) collective-permute-start(bf16[4,64,768]{2,1,0:T(8,128)(2,1)S(1)} %collective-permute-done.6.refs_2_.refs_4_), channel_id=1, source_target_pairs={{0,1},{1,0},{2,3},{3,2},{4,5},{5,4},{6,7},{7,6},{8,9},{9,8},{10,11... | collective-permute-start | bytes 1179656 | tf_op jit(solution)/shard_map/ppermute | solution.py:147
  25.8 0.4 %collective-permute-done.4.refs_0_.refs_2_ = bf16[4,64,768]{2,1,0:T(8,128)(2,1)S(1)} collective-permute-done((bf16[4,64,768]{2,1,0:T(8,128)(2,1)S(1)}, bf16[4,64,768]{2,1,0:T(8,128)(2,1)S(1)}, u32[]{:S(2)}, u32[]{:S(2)}) %collective-permute-start.4) | collective-permute-done | bytes 393248 | tf_op jit(solution)/shard_map/ppermute | solution.py:150
  26.3 2.0 %collective-permute-done.10 = bf16[64,768]{1,0:T(8,128)(2,1)S(1)} collective-permute-done((bf16[64,768]{1,0:T(8,128)(2,1)S(1)}, bf16[64,768]{1,0:T(8,128)(2,1)S(1)}, u32[]{:S(2)}, u32[]{:S(2)}) %collective-permute-start.10) | collective-permute-done | bytes 98336 | tf_op jit(solution)/shard_map/ppermute | solution.py:147
  28.2 0.1 pad_maximum_fusion.1.refs_6_
  28.3 0.1 collective-permute-start.12
  28.4 0.0 collective-permute-done.5.refs_1_.refs_3_
  28.4 1.6 %collective-permute-done.12.refs_7_ = bf16[4,64,768]{2,1,0:T(8,128)(2,1)S(1)} collective-permute-done((bf16[4,64,768]{2,1,0:T(8,128)(2,1)S(1)}, bf16[4,64,768]{2,1,0:T(8,128)(2,1)S(1)}, u32[]{:S(2)}, u32[]{:S(2)}) %collective-permute-start.12) | collective-permute-done | bytes 393248 | tf_op jit(solution)/shard_map/ppermute | solution.py:147
  30.1 0.9 %second_products.1 = bf16[64,768]{1,0:T(8,128)(2,1)} custom-call(bf16[128,512]{1,0:T(8,128)(2,1)S(1)} %first_products.1.first_ref, bf16[4,64,768]{2,1,0:T(8,128)(2,1)S(1)} %pad_maximum_fusion.refs_0_, bf16[4,64,768]{2,1,0:T(8,128)(2,1)S(1)} %collective-permute-done.8.refs_1_, bf16[4,64,768]{2,1,0:T(8,128)(2,1)S(1)} %collective-permute-done.4.refs_0_.refs_2_, ...), custom_call_target="tpu_custom_call" | custom-call | tf_op jit(solution)/shard_map/second_products/pallas_call | solution.py:132
  (7 shorter events, 0.0 us)
Async XLA Ops:
  1.3 8.8 %collective-permute-start.2 = (bf16[64,768]{1,0:T(8,128)(2,1)S(1)}, bf16[64,768]{1,0:T(8,128)(2,1)S(1)}, u32[]{:S(2)}, u32[]{:S(2)}) collective-permute-start(bf16[64,768]{1,0:T(8,128)(2,1)S(1)} %dense_rows.1.own_ref), channel_id=1, source_target_pairs={{0,6},{1,7},{2,4},{3,5},{4,2},{5,3},{6,0},{7,1},{8,14},{9,15},{10,... | collective-permute-start | bytes 294920 | tf_op jit(solution)/shard_map/ppermute | solution.py:147
  6.5 8.3 %collective-permute-start.1 = (bf16[64,768]{1,0:T(8,128)(2,1)S(1)}, bf16[64,768]{1,0:T(8,128)(2,1)S(1)}, u32[]{:S(2)}, u32[]{:S(2)}) collective-permute-start(bf16[64,768]{1,0:T(8,128)(2,1)S(1)} %dense_rows.1.own_ref), channel_id=1, source_target_pairs={{0,4},{1,5},{2,6},{3,7},{4,0},{5,1},{6,2},{7,3},{8,12},{9,13},{10,... | collective-permute-start | bytes 294920 | tf_op jit(solution)/shard_map/ppermute | solution.py:147
  6.5 8.3 %collective-permute-start = (bf16[64,768]{1,0:T(8,128)(2,1)S(1)}, bf16[64,768]{1,0:T(8,128)(2,1)S(1)}, u32[]{:S(2)}, u32[]{:S(2)}) collective-permute-start(bf16[64,768]{1,0:T(8,128)(2,1)S(1)} %dense_rows.1.own_ref), channel_id=1, source_target_pairs={{0,2},{1,3},{2,0},{3,1},{4,6},{5,7},{6,4},{7,5},{8,10},{9,11},{10,... | collective-permute-start | bytes 294920 | tf_op jit(solution)/shard_map/ppermute | solution.py:147
  7.1 7.7 %collective-permute-start.3 = (bf16[64,768]{1,0:T(8,128)(2,1)S(1)}, bf16[64,768]{1,0:T(8,128)(2,1)S(1)}, u32[]{:S(2)}, u32[]{:S(2)}) collective-permute-start(bf16[64,768]{1,0:T(8,128)(2,1)S(1)} %dense_rows.1.own_ref), channel_id=1, source_target_pairs={{0,24},{8,16},{16,8},{24,0},{1,25},{9,17},{17,9},{25,1},{2,26},{10... | collective-permute-start | bytes 294920 | tf_op jit(solution)/shard_map/ppermute | solution.py:150
  14.8 10.5 %collective-permute-start.6 = (bf16[4,64,768]{2,1,0:T(8,128)(2,1)S(1)}, bf16[4,64,768]{2,1,0:T(8,128)(2,1)S(1)}, u32[]{:S(2)}, u32[]{:S(2)}) collective-permute-start(bf16[4,64,768]{2,1,0:T(8,128)(2,1)S(1)} %pad_maximum_fusion.refs_0_), channel_id=1, source_target_pairs={{0,16},{8,24},{16,0},{24,8},{1,17},{9,25},{17,1},{25,9},{2,18},{10... | collective-permute-start | bytes 1179656 | tf_op jit(solution)/shard_map/ppermute | solution.py:150
  16.4 9.9 %collective-permute-start.4 = (bf16[4,64,768]{2,1,0:T(8,128)(2,1)S(1)}, bf16[4,64,768]{2,1,0:T(8,128)(2,1)S(1)}, u32[]{:S(2)}, u32[]{:S(2)}) collective-permute-start(bf16[4,64,768]{2,1,0:T(8,128)(2,1)S(1)} %pad_maximum_fusion.refs_0_), channel_id=1, source_target_pairs={{0,8},{8,0},{16,24},{24,16},{1,9},{9,1},{17,25},{25,17},{2,10},{10... | collective-permute-start | bytes 1179656 | tf_op jit(solution)/shard_map/ppermute | solution.py:150
  17.9 7.5 %collective-permute-start.11 = (bf16[64,768]{1,0:T(8,128)(2,1)S(1)}, bf16[64,768]{1,0:T(8,128)(2,1)S(1)}, u32[]{:S(2)}, u32[]{:S(2)}) collective-permute-start(bf16[64,768]{1,0:T(8,128)(2,1)S(1)} %collective-permute-done.3), channel_id=1, source_target_pairs={{0,6},{1,7},{2,4},{3,5},{4,2},{5,3},{6,0},{7,1},{8,14},{9,15},{10,... | collective-permute-start | bytes 294920 | tf_op jit(solution)/shard_map/ppermute | solution.py:147
  20.4 7.8 %collective-permute-start.10 = (bf16[64,768]{1,0:T(8,128)(2,1)S(1)}, bf16[64,768]{1,0:T(8,128)(2,1)S(1)}, u32[]{:S(2)}, u32[]{:S(2)}) collective-permute-start(bf16[64,768]{1,0:T(8,128)(2,1)S(1)} %collective-permute-done.3), channel_id=1, source_target_pairs={{0,4},{1,5},{2,6},{3,7},{4,0},{5,1},{6,2},{7,3},{8,12},{9,13},{10,... | collective-permute-start | bytes 294920 | tf_op jit(solution)/shard_map/ppermute | solution.py:147
  20.4 7.8 %collective-permute-start.9 = (bf16[64,768]{1,0:T(8,128)(2,1)S(1)}, bf16[64,768]{1,0:T(8,128)(2,1)S(1)}, u32[]{:S(2)}, u32[]{:S(2)}) collective-permute-start(bf16[64,768]{1,0:T(8,128)(2,1)S(1)} %collective-permute-done.3), channel_id=1, source_target_pairs={{0,2},{1,3},{2,0},{3,1},{4,6},{5,7},{6,4},{7,5},{8,10},{9,11},{10,... | collective-permute-start | bytes 294920 | tf_op jit(solution)/shard_map/ppermute | solution.py:147
  25.3 3.1 %collective-permute-start.8 = (bf16[4,64,768]{2,1,0:T(8,128)(2,1)S(1)}, bf16[4,64,768]{2,1,0:T(8,128)(2,1)S(1)}, u32[]{:S(2)}, u32[]{:S(2)}) collective-permute-start(bf16[4,64,768]{2,1,0:T(8,128)(2,1)S(1)} %pad_maximum_fusion.refs_0_), channel_id=1, source_target_pairs={{0,1},{1,0},{2,3},{3,2},{4,5},{5,4},{6,7},{7,6},{8,9},{9,8},{10,11... | collective-permute-start | bytes 1179656 | tf_op jit(solution)/shard_map/ppermute | solution.py:147
  25.3 3.0 %collective-permute-start.7 = (bf16[4,64,768]{2,1,0:T(8,128)(2,1)S(1)}, bf16[4,64,768]{2,1,0:T(8,128)(2,1)S(1)}, u32[]{:S(2)}, u32[]{:S(2)}) collective-permute-start(bf16[4,64,768]{2,1,0:T(8,128)(2,1)S(1)} %collective-permute-done.6.refs_2_.refs_4_), channel_id=1, source_target_pairs={{0,1},{1,0},{2,3},{3,2},{4,5},{5,4},{6,7},{7,6},{8,9},{9,8},{10,11... | collective-permute-start | bytes 1179656 | tf_op jit(solution)/shard_map/ppermute | solution.py:147
  26.3 2.1 %collective-permute-start.5 = (bf16[4,64,768]{2,1,0:T(8,128)(2,1)S(1)}, bf16[4,64,768]{2,1,0:T(8,128)(2,1)S(1)}, u32[]{:S(2)}, u32[]{:S(2)}) collective-permute-start(bf16[4,64,768]{2,1,0:T(8,128)(2,1)S(1)} %collective-permute-done.4.refs_0_.refs_2_), channel_id=1, source_target_pairs={{0,1},{1,0},{2,3},{3,2},{4,5},{5,4},{6,7},{7,6},{8,9},{9,8},{10,11... | collective-permute-start | bytes 1179656 | tf_op jit(solution)/shard_map/ppermute | solution.py:147
  28.3 1.8 %collective-permute-start.12 = (bf16[4,64,768]{2,1,0:T(8,128)(2,1)S(1)}, bf16[4,64,768]{2,1,0:T(8,128)(2,1)S(1)}, u32[]{:S(2)}, u32[]{:S(2)}) collective-permute-start(bf16[4,64,768]{2,1,0:T(8,128)(2,1)S(1)} %pad_maximum_fusion.1.refs_6_), channel_id=1, source_target_pairs={{0,1},{1,0},{2,3},{3,2},{4,5},{5,4},{6,7},{7,6},{8,9},{9,8},{10,11... | collective-permute-start | bytes 1179656 | tf_op jit(solution)/shard_map/ppermute | solution.py:147

commit v13 on v12

--- a/solution.py
+++ b/solution.py
@@ -69,8 +69,9 @@
     chip, first_core = lax.div(shard, 2), lax.rem(shard, 2) == 0
     here_ref, there_ref = pair_refs[mask]
     left, right = [], []
-    for piece in range(here_ref.shape[0]):
-        source = lax.bitwise_xor(chip, piece)
+    chips = here_ref.shape[0]
+    for piece in range(chips):
+        source = lax.rem(chip - piece + chips, chips)
         left.append(halves[:, pl.ds(pl.multiple_of(source * 2 * row_count, 128), 2 * row_count)])
         here, there = here_ref[piece, :, columns], there_ref[piece, :, columns]
         right += [jnp.where(first_core, here, there), jnp.where(first_core, there, here)]
@@ -143,21 +144,22 @@
 def by_products(own, nodes, width):
     sections, shards = lax.axis_size("section"), lax.axis_size("shard")
 
-    def along_shard(value, mask):
-        return lax.ppermute(value, "shard", [(i, i ^ mask) for i in range(shards)])
+    def across_cores(value):
+        return lax.ppermute(value, "shard", [(i, i ^ 1) for i in range(shards)])
 
     def along_section(value, mask):
         return lax.ppermute(value, "section", [(i, i ^ mask) for i in range(sections)])
 
     def along_z(value):
-        return jnp.stack([value] + [along_shard(value, 2 * mask) for mask in range(1, shards // 2)])
+        turns = [[(i, (i + 2 * back) % shards) for i in range(shards)] for back in range(1, shards // 2)]
+        return jnp.stack([value] + [lax.ppermute(value, "shard", turn) for turn in turns])
 
     ahead = {mask: along_section(own, mask) for mask in range(1, sections) if mask & (mask - 1)}
     mine, ahead = lax.optimization_barrier((along_z(own), ahead))
     gathered = [mine]
     for mask in range(1, sections):
         gathered.append(along_z(ahead[mask]) if mask in ahead else along_section(mine, mask))
-    pairs = [(here, along_shard(here, 1)) for here in gathered]
+    pairs = [(here, across_cores(here)) for here in gathered]
     first = first_products(own, pairs, nodes, sections)
     return second_products(first, pairs, width, sections)
 
@@ -180,8 +182,8 @@
     row_count, width = features.shape
     sections, shards = lax.axis_size("section"), lax.axis_size("shard")
     nodes = row_count * shards
-    doubles = shards >= 2 and shards & (shards - 1) == 0 and sections & (sections - 1) == 0
-    products = doubles and nodes <= width and width % (sections - 1) == 0
+    pairs = shards % 2 == 0 and sections > 1 and sections & (sections - 1) == 0
+    products = pairs and nodes <= width and width % (sections - 1) == 0
     share = width // (sections - 1) if products else 0
     own = dense_rows(tile_cols, live_tiles, tile_values[0], degrees, features, share)
     out = by_products(own, nodes, width) if products else by_hops(features, own)

time: 31.2 us -> 31.5 us (level)
  waiting for transfers between devices: 12.2 us -> 12.9 us
  starting transfers between devices: 16.4 us -> 16 us
    ppermute x3, waiting for transfers between devices: 0.42 us -> 3.83 us  [along_section(): lax.ppermute(value, 'section', [(i, i ^ mask) for i in range(sections)])]
    ppermute x10, waiting for transfers between devices: 11.7 us -> 9.05 us  [the longest x6 7.38 us: along_z(): lax.ppermute(value, 'shard', turn)]
  transfers between devices with their start and end apart: 13 -> 13, of which waited for: 6 -> 7; matrix products, arithmetic and copies ran while one was open for 0% -> 0% of each run, Pallas kernels for 0% -> 0%
where the time goes in v13:
time: 31.5 us; the launch traced here: 31.3 us
  starting transfers between devices  16 us (51%)
  waiting for transfers between devices  12.9 us (41%)
  Pallas kernels  2.28 us (7%)
    ppermute x6, starting transfers between devices, along_z(): lax.ppermute(value, 'shard', turn)  10.4 us
    ppermute x6, waiting for transfers between devices, along_z(): lax.ppermute(value, 'shard', turn)  7.38 us
    ppermute x3, starting transfers between devices, along_section(): lax.ppermute(value, 'section', [(i, i ^ mask) for i in range(sections)])  5.51 us
    ppermute x3, waiting for transfers between devices, along_section(): lax.ppermute(value, 'section', [(i, i ^ mask) for i in range(sections)])  3.83 us
    ppermute x4, waiting for transfers between devices, across_cores(): return lax.ppermute(value, 'shard', [(i, i ^ 1) for i in range(shards)])  1.67 us
    pallas_call x1, Pallas kernels, dense_rows(): pl.pallas_call(dense_rows_kernel, out_shape=pltpu.VMEM((row_count, nodes...  1.33 us
    pallas_call x1, Pallas kernels, second_products(): pl.pallas_call(functools.partial(second_kernel, sections), out_shape=jax....  0.94 us
  transfers between devices with their start and end apart: 13, of which 7 were waited for; matrix products, arithmetic and copies ran while one was open for 0% of the time, Pallas kernels for 0%

profile of v13, /device:TPU:0, one launch (start us, length us, event | category | flops | bytes accessed | tf_op | source)
XLA Modules:
  0.0 31.3 jit_solution(4844446466822535603)
XLA Ops:
  0.0 1.3 %dense_rows.1.own_ref = bf16[64,768]{1,0:T(8,128)(2,1)S(1)} custom-call(s32[1,4,16]{2,1,0:T(4,128)} %cols_ref.1, s32[1,4]{1,0:T(1,128)} %live_ref.1, bf16[64,16,128]{2,1,0:T(8,128)(2,1)} %bitcast.11, s32[1,64]{1,0:T(1,128)} %degrees_ref.1, bf16[64,768]{1,0:T(8,128)(2,1)} %features_ref.1), custom_call_target="tpu_custom_call" | custom-call | tf_op jit(solution)/shard_map/dense_rows/pallas_call | solution.py:45
  1.3 5.1 %collective-permute-start.2 = (bf16[64,768]{1,0:T(8,128)(2,1)S(1)}, bf16[64,768]{1,0:T(8,128)(2,1)S(1)}, u32[]{:S(2)}, u32[]{:S(2)}) collective-permute-start(bf16[64,768]{1,0:T(8,128)(2,1)S(1)} %dense_rows.1.own_ref), channel_id=1, source_target_pairs={{0,6},{1,7},{2,0},{3,1},{4,2},{5,3},{6,4},{7,5},{8,14},{9,15},{10,... | collective-permute-start | bytes 294920 | tf_op jit(solution)/shard_map/ppermute | solution.py:155
  6.5 1.0 %collective-permute-start = (bf16[64,768]{1,0:T(8,128)(2,1)S(1)}, bf16[64,768]{1,0:T(8,128)(2,1)S(1)}, u32[]{:S(2)}, u32[]{:S(2)}) collective-permute-start(bf16[64,768]{1,0:T(8,128)(2,1)S(1)} %dense_rows.1.own_ref), channel_id=1, source_target_pairs={{0,2},{1,3},{2,4},{3,5},{4,6},{5,7},{6,0},{7,1},{8,10},{9,11},{10,... | collective-permute-start | bytes 294920 | tf_op jit(solution)/shard_map/ppermute | solution.py:155
  7.5 2.4 %collective-permute-start.3 = (bf16[64,768]{1,0:T(8,128)(2,1)S(1)}, bf16[64,768]{1,0:T(8,128)(2,1)S(1)}, u32[]{:S(2)}, u32[]{:S(2)}) collective-permute-start(bf16[64,768]{1,0:T(8,128)(2,1)S(1)} %dense_rows.1.own_ref), channel_id=1, source_target_pairs={{0,24},{8,16},{16,8},{24,0},{1,25},{9,17},{17,9},{25,1},{2,26},{10... | collective-permute-start | bytes 294920 | tf_op jit(solution)/shard_map/ppermute | solution.py:151
  9.9 0.0 collective-permute-done.2
  9.9 5.3 %collective-permute-done.1 = bf16[64,768]{1,0:T(8,128)(2,1)S(1)} collective-permute-done((bf16[64,768]{1,0:T(8,128)(2,1)S(1)}, bf16[64,768]{1,0:T(8,128)(2,1)S(1)}, u32[]{:S(2)}, u32[]{:S(2)}) %collective-permute-start.1) | collective-permute-done | bytes 98336 | tf_op jit(solution)/shard_map/ppermute | solution.py:155
  15.2 0.0 collective-permute-done
  15.2 0.1 pad_maximum_fusion.refs_0_
  15.3 0.0 collective-permute-done.3
  15.3 1.6 %collective-permute-start.6 = (bf16[4,64,768]{2,1,0:T(8,128)(2,1)S(1)}, bf16[4,64,768]{2,1,0:T(8,128)(2,1)S(1)}, u32[]{:S(2)}, u32[]{:S(2)}) collective-permute-start(bf16[4,64,768]{2,1,0:T(8,128)(2,1)S(1)} %pad_maximum_fusion.refs_0_), channel_id=1, source_target_pairs={{0,16},{8,24},{16,0},{24,8},{1,17},{9,25},{17,1},{25,9},{2,18},{10... | collective-permute-start | bytes 1179656 | tf_op jit(solution)/shard_map/ppermute | solution.py:151
  16.9 1.5 %collective-permute-start.4 = (bf16[4,64,768]{2,1,0:T(8,128)(2,1)S(1)}, bf16[4,64,768]{2,1,0:T(8,128)(2,1)S(1)}, u32[]{:S(2)}, u32[]{:S(2)}) collective-permute-start(bf16[4,64,768]{2,1,0:T(8,128)(2,1)S(1)} %pad_maximum_fusion.refs_0_), channel_id=1, source_target_pairs={{0,8},{8,0},{16,24},{24,16},{1,9},{9,1},{17,25},{25,17},{2,10},{10... | collective-permute-start | bytes 1179656 | tf_op jit(solution)/shard_map/ppermute | solution.py:151
  18.3 1.9 %collective-permute-start.11 = (bf16[64,768]{1,0:T(8,128)(2,1)S(1)}, bf16[64,768]{1,0:T(8,128)(2,1)S(1)}, u32[]{:S(2)}, u32[]{:S(2)}) collective-permute-start(bf16[64,768]{1,0:T(8,128)(2,1)S(1)} %collective-permute-done.3), channel_id=1, source_target_pairs={{0,6},{1,7},{2,0},{3,1},{4,2},{5,3},{6,4},{7,5},{8,14},{9,15},{10,... | collective-permute-start | bytes 294920 | tf_op jit(solution)/shard_map/ppermute | solution.py:155
  20.3 0.3 %collective-permute-start.10 = (bf16[64,768]{1,0:T(8,128)(2,1)S(1)}, bf16[64,768]{1,0:T(8,128)(2,1)S(1)}, u32[]{:S(2)}, u32[]{:S(2)}) collective-permute-start(bf16[64,768]{1,0:T(8,128)(2,1)S(1)} %collective-permute-done.3), channel_id=1, source_target_pairs={{0,4},{1,5},{2,6},{3,7},{4,0},{5,1},{6,2},{7,3},{8,12},{9,13},{10,... | collective-permute-start | bytes 294920 | tf_op jit(solution)/shard_map/ppermute | solution.py:155
  20.6 2.0 %collective-permute-start.9 = (bf16[64,768]{1,0:T(8,128)(2,1)S(1)}, bf16[64,768]{1,0:T(8,128)(2,1)S(1)}, u32[]{:S(2)}, u32[]{:S(2)}) collective-permute-start(bf16[64,768]{1,0:T(8,128)(2,1)S(1)} %collective-permute-done.3), channel_id=1, source_target_pairs={{0,2},{1,3},{2,4},{3,5},{4,6},{5,7},{6,0},{7,1},{8,10},{9,11},{10,... | collective-permute-start | bytes 294920 | tf_op jit(solution)/shard_map/ppermute | solution.py:155
  22.6 0.7 %collective-permute-done.11 = bf16[64,768]{1,0:T(8,128)(2,1)S(1)} collective-permute-done((bf16[64,768]{1,0:T(8,128)(2,1)S(1)}, bf16[64,768]{1,0:T(8,128)(2,1)S(1)}, u32[]{:S(2)}, u32[]{:S(2)}) %collective-permute-start.11) | collective-permute-done | bytes 98336 | tf_op jit(solution)/shard_map/ppermute | solution.py:155
  23.3 0.0 collective-permute-start.8
  23.3 2.6 %collective-permute-done.6.refs_2_.refs_4_ = bf16[4,64,768]{2,1,0:T(8,128)(2,1)S(1)} collective-permute-done((bf16[4,64,768]{2,1,0:T(8,128)(2,1)S(1)}, bf16[4,64,768]{2,1,0:T(8,128)(2,1)S(1)}, u32[]{:S(2)}, u32[]{:S(2)}) %collective-permute-start.6) | collective-permute-done | bytes 393248 | tf_op jit(solution)/shard_map/ppermute | solution.py:151
  25.9 1.3 %collective-permute-done.4.refs_0_.refs_2_ = bf16[4,64,768]{2,1,0:T(8,128)(2,1)S(1)} collective-permute-done((bf16[4,64,768]{2,1,0:T(8,128)(2,1)S(1)}, bf16[4,64,768]{2,1,0:T(8,128)(2,1)S(1)}, u32[]{:S(2)}, u32[]{:S(2)}) %collective-permute-start.4) | collective-permute-done | bytes 393248 | tf_op jit(solution)/shard_map/ppermute | solution.py:151
  27.1 1.4 %collective-permute-done.10 = bf16[64,768]{1,0:T(8,128)(2,1)S(1)} collective-permute-done((bf16[64,768]{1,0:T(8,128)(2,1)S(1)}, bf16[64,768]{1,0:T(8,128)(2,1)S(1)}, u32[]{:S(2)}, u32[]{:S(2)}) %collective-permute-start.10) | collective-permute-done | bytes 98336 | tf_op jit(solution)/shard_map/ppermute | solution.py:155
  28.6 0.1 pad_maximum_fusion.1.refs_6_
  28.6 0.1 collective-permute-start.12
  28.7 0.1 collective-permute-done.5.refs_1_.refs_3_
  28.9 1.5 %collective-permute-done.12.refs_7_ = bf16[4,64,768]{2,1,0:T(8,128)(2,1)S(1)} collective-permute-done((bf16[4,64,768]{2,1,0:T(8,128)(2,1)S(1)}, bf16[4,64,768]{2,1,0:T(8,128)(2,1)S(1)}, u32[]{:S(2)}, u32[]{:S(2)}) %collective-permute-start.12) | collective-permute-done | bytes 393248 | tf_op jit(solution)/shard_map/ppermute | solution.py:148
  30.4 0.9 %second_products.1 = bf16[64,768]{1,0:T(8,128)(2,1)} custom-call(bf16[128,512]{1,0:T(8,128)(2,1)S(1)} %first_products.1.first_ref, bf16[4,64,768]{2,1,0:T(8,128)(2,1)S(1)} %pad_maximum_fusion.refs_0_, bf16[4,64,768]{2,1,0:T(8,128)(2,1)S(1)} %collective-permute-done.8.refs_1_, bf16[4,64,768]{2,1,0:T(8,128)(2,1)S(1)} %collective-permute-done.4.refs_0_.refs_2_, ...), custom_call_target="tpu_custom_call" | custom-call | tf_op jit(solution)/shard_map/second_products/pallas_call | solution.py:133
  (7 shorter events, 0.0 us)
Async XLA Ops:
  1.3 8.6 %collective-permute-start.2 = (bf16[64,768]{1,0:T(8,128)(2,1)S(1)}, bf16[64,768]{1,0:T(8,128)(2,1)S(1)}, u32[]{:S(2)}, u32[]{:S(2)}) collective-permute-start(bf16[64,768]{1,0:T(8,128)(2,1)S(1)} %dense_rows.1.own_ref), channel_id=1, source_target_pairs={{0,6},{1,7},{2,0},{3,1},{4,2},{5,3},{6,4},{7,5},{8,14},{9,15},{10,... | collective-permute-start | bytes 294920 | tf_op jit(solution)/shard_map/ppermute | solution.py:155
  6.5 8.7 %collective-permute-start.1 = (bf16[64,768]{1,0:T(8,128)(2,1)S(1)}, bf16[64,768]{1,0:T(8,128)(2,1)S(1)}, u32[]{:S(2)}, u32[]{:S(2)}) collective-permute-start(bf16[64,768]{1,0:T(8,128)(2,1)S(1)} %dense_rows.1.own_ref), channel_id=1, source_target_pairs={{0,4},{1,5},{2,6},{3,7},{4,0},{5,1},{6,2},{7,3},{8,12},{9,13},{10,... | collective-permute-start | bytes 294920 | tf_op jit(solution)/shard_map/ppermute | solution.py:155
  6.5 8.7 %collective-permute-start = (bf16[64,768]{1,0:T(8,128)(2,1)S(1)}, bf16[64,768]{1,0:T(8,128)(2,1)S(1)}, u32[]{:S(2)}, u32[]{:S(2)}) collective-permute-start(bf16[64,768]{1,0:T(8,128)(2,1)S(1)} %dense_rows.1.own_ref), channel_id=1, source_target_pairs={{0,2},{1,3},{2,4},{3,5},{4,6},{5,7},{6,0},{7,1},{8,10},{9,11},{10,... | collective-permute-start | bytes 294920 | tf_op jit(solution)/shard_map/ppermute | solution.py:155
  7.5 7.8 %collective-permute-start.3 = (bf16[64,768]{1,0:T(8,128)(2,1)S(1)}, bf16[64,768]{1,0:T(8,128)(2,1)S(1)}, u32[]{:S(2)}, u32[]{:S(2)}) collective-permute-start(bf16[64,768]{1,0:T(8,128)(2,1)S(1)} %dense_rows.1.own_ref), channel_id=1, source_target_pairs={{0,24},{8,16},{16,8},{24,0},{1,25},{9,17},{17,9},{25,1},{2,26},{10... | collective-permute-start | bytes 294920 | tf_op jit(solution)/shard_map/ppermute | solution.py:151
  15.3 10.6 %collective-permute-start.6 = (bf16[4,64,768]{2,1,0:T(8,128)(2,1)S(1)}, bf16[4,64,768]{2,1,0:T(8,128)(2,1)S(1)}, u32[]{:S(2)}, u32[]{:S(2)}) collective-permute-start(bf16[4,64,768]{2,1,0:T(8,128)(2,1)S(1)} %pad_maximum_fusion.refs_0_), channel_id=1, source_target_pairs={{0,16},{8,24},{16,0},{24,8},{1,17},{9,25},{17,1},{25,9},{2,18},{10... | collective-permute-start | bytes 1179656 | tf_op jit(solution)/shard_map/ppermute | solution.py:151
  16.9 10.3 %collective-permute-start.4 = (bf16[4,64,768]{2,1,0:T(8,128)(2,1)S(1)}, bf16[4,64,768]{2,1,0:T(8,128)(2,1)S(1)}, u32[]{:S(2)}, u32[]{:S(2)}) collective-permute-start(bf16[4,64,768]{2,1,0:T(8,128)(2,1)S(1)} %pad_maximum_fusion.refs_0_), channel_id=1, source_target_pairs={{0,8},{8,0},{16,24},{24,16},{1,9},{9,1},{17,25},{25,17},{2,10},{10... | collective-permute-start | bytes 1179656 | tf_op jit(solution)/shard_map/ppermute | solution.py:151
  18.3 5.0 %collective-permute-start.11 = (bf16[64,768]{1,0:T(8,128)(2,1)S(1)}, bf16[64,768]{1,0:T(8,128)(2,1)S(1)}, u32[]{:S(2)}, u32[]{:S(2)}) collective-permute-start(bf16[64,768]{1,0:T(8,128)(2,1)S(1)} %collective-permute-done.3), channel_id=1, source_target_pairs={{0,6},{1,7},{2,0},{3,1},{4,2},{5,3},{6,4},{7,5},{8,14},{9,15},{10,... | collective-permute-start | bytes 294920 | tf_op jit(solution)/shard_map/ppermute | solution.py:155
  20.3 8.3 %collective-permute-start.10 = (bf16[64,768]{1,0:T(8,128)(2,1)S(1)}, bf16[64,768]{1,0:T(8,128)(2,1)S(1)}, u32[]{:S(2)}, u32[]{:S(2)}) collective-permute-start(bf16[64,768]{1,0:T(8,128)(2,1)S(1)} %collective-permute-done.3), channel_id=1, source_target_pairs={{0,4},{1,5},{2,6},{3,7},{4,0},{5,1},{6,2},{7,3},{8,12},{9,13},{10,... | collective-permute-start | bytes 294920 | tf_op jit(solution)/shard_map/ppermute | solution.py:155
  20.6 7.9 %collective-permute-start.9 = (bf16[64,768]{1,0:T(8,128)(2,1)S(1)}, bf16[64,768]{1,0:T(8,128)(2,1)S(1)}, u32[]{:S(2)}, u32[]{:S(2)}) collective-permute-start(bf16[64,768]{1,0:T(8,128)(2,1)S(1)} %collective-permute-done.3), channel_id=1, source_target_pairs={{0,2},{1,3},{2,4},{3,5},{4,6},{5,7},{6,0},{7,1},{8,10},{9,11},{10,... | collective-permute-start | bytes 294920 | tf_op jit(solution)/shard_map/ppermute | solution.py:155
  23.3 5.6 %collective-permute-start.8 = (bf16[4,64,768]{2,1,0:T(8,128)(2,1)S(1)}, bf16[4,64,768]{2,1,0:T(8,128)(2,1)S(1)}, u32[]{:S(2)}, u32[]{:S(2)}) collective-permute-start(bf16[4,64,768]{2,1,0:T(8,128)(2,1)S(1)} %pad_maximum_fusion.refs_0_), channel_id=1, source_target_pairs={{0,1},{1,0},{2,3},{3,2},{4,5},{5,4},{6,7},{7,6},{8,9},{9,8},{10,11... | collective-permute-start | bytes 1179656 | tf_op jit(solution)/shard_map/ppermute | solution.py:148
  25.9 2.8 %collective-permute-start.7 = (bf16[4,64,768]{2,1,0:T(8,128)(2,1)S(1)}, bf16[4,64,768]{2,1,0:T(8,128)(2,1)S(1)}, u32[]{:S(2)}, u32[]{:S(2)}) collective-permute-start(bf16[4,64,768]{2,1,0:T(8,128)(2,1)S(1)} %collective-permute-done.6.refs_2_.refs_4_), channel_id=1, source_target_pairs={{0,1},{1,0},{2,3},{3,2},{4,5},{5,4},{6,7},{7,6},{8,9},{9,8},{10,11... | collective-permute-start | bytes 1179656 | tf_op jit(solution)/shard_map/ppermute | solution.py:148
  27.1 1.7 %collective-permute-start.5 = (bf16[4,64,768]{2,1,0:T(8,128)(2,1)S(1)}, bf16[4,64,768]{2,1,0:T(8,128)(2,1)S(1)}, u32[]{:S(2)}, u32[]{:S(2)}) collective-permute-start(bf16[4,64,768]{2,1,0:T(8,128)(2,1)S(1)} %collective-permute-done.4.refs_0_.refs_2_), channel_id=1, source_target_pairs={{0,1},{1,0},{2,3},{3,2},{4,5},{5,4},{6,7},{7,6},{8,9},{9,8},{10,11... | collective-permute-start | bytes 1179656 | tf_op jit(solution)/shard_map/ppermute | solution.py:148
  28.6 1.8 %collective-permute-start.12 = (bf16[4,64,768]{2,1,0:T(8,128)(2,1)S(1)}, bf16[4,64,768]{2,1,0:T(8,128)(2,1)S(1)}, u32[]{:S(2)}, u32[]{:S(2)}) collective-permute-start(bf16[4,64,768]{2,1,0:T(8,128)(2,1)S(1)} %pad_maximum_fusion.1.refs_6_), channel_id=1, source_target_pairs={{0,1},{1,0},{2,3},{3,2},{4,5},{5,4},{6,7},{7,6},{8,9},{9,8},{10,11... | collective-permute-start | bytes 1179656 | tf_op jit(solution)/shard_map/ppermute | solution.py:148

commit v14 on v12

--- a/solution.py
+++ b/solution.py
@@ -143,21 +143,32 @@
 def by_products(own, nodes, width):
     sections, shards = lax.axis_size("section"), lax.axis_size("shard")
 
-    def along_shard(value, mask):
-        return lax.ppermute(value, "shard", [(i, i ^ mask) for i in range(shards)])
+    def move(value, mask, to_section, to_shard):
+        pairs = []
+        for section in range(sections):
+            if section ^ mask != sections - 1:
+                pairs += [(section * shards + i, to_section(section) * shards + to_shard(i)) for i in range(shards)]
+        return lax.ppermute(value, ("section", "shard"), pairs)
+
+    def same(index):
+        return index
 
     def along_section(value, mask):
-        return lax.ppermute(value, "section", [(i, i ^ mask) for i in range(sections)])
-
-    def along_z(value):
-        return jnp.stack([value] + [along_shard(value, 2 * mask) for mask in range(1, shards // 2)])
+        return move(value, 0, lambda section: section ^ mask, same)
+
+    def across_cores(value, mask):
+        return move(value, mask, same, lambda i: i ^ 1)
+
+    def along_z(value, mask):
+        steps = range(2, shards, 2)
+        return jnp.stack([value] + [move(value, mask, same, lambda i, step=step: i ^ step) for step in steps])
 
     ahead = {mask: along_section(own, mask) for mask in range(1, sections) if mask & (mask - 1)}
-    mine, ahead = lax.optimization_barrier((along_z(own), ahead))
+    mine, ahead = lax.optimization_barrier((along_z(own, 0), ahead))
     gathered = [mine]
     for mask in range(1, sections):
-        gathered.append(along_z(ahead[mask]) if mask in ahead else along_section(mine, mask))
-    pairs = [(here, along_shard(here, 1)) for here in gathered]
+        gathered.append(along_z(ahead[mask], mask) if mask in ahead else along_section(mine, mask))
+    pairs = [(here, across_cores(here, mask)) for mask, here in enumerate(gathered)]
     first = first_products(own, pairs, nodes, sections)
     return second_products(first, pairs, width, sections)
 

time: 31.2 us -> 45.3 us (1.45)
  the two profiles are of different devices: /device:TPU:0 before, /device:TPU:27 now
where the time goes in v14:
time: 45.3 us; the launch traced here: 44.9 us
  starting transfers between devices  37.9 us (84%)
  waiting for transfers between devices  4.12 us (9%)
  Pallas kernels  2.55 us (6%)
    ppermute x13, starting transfers between devices, move(): return lax.ppermute(value, ('section', 'shard'), pairs)  37.9 us
    ppermute x13, waiting for transfers between devices, move(): return lax.ppermute(value, ('section', 'shard'), pairs)  4.12 us
    pallas_call x1, Pallas kernels, dense_rows(): pl.pallas_call(dense_rows_kernel, out_shape=pltpu.VMEM((row_count, nodes...  1.34 us
    pallas_call x1, Pallas kernels, second_products(): pl.pallas_call(functools.partial(second_kernel, sections), out_shape=jax....  0.94 us
  transfers between devices with their start and end apart: 13, of which 4 were waited for; matrix products, arithmetic and copies ran while one was open for 0% of the time, Pallas kernels for 1%

profile of v14, /device:TPU:27, one launch (start us, length us, event | category | flops | bytes accessed | tf_op | source)
XLA Modules:
  0.0 44.9 jit_solution(8619421858096806770)
XLA Ops:
  0.0 1.3 %dense_rows.1.own_ref = bf16[64,768]{1,0:T(8,128)(2,1)S(1)} custom-call(s32[1,4,16]{2,1,0:T(4,128)} %cols_ref.1, s32[1,4]{1,0:T(1,128)} %live_ref.1, bf16[64,16,128]{2,1,0:T(8,128)(2,1)} %bitcast.11, s32[1,64]{1,0:T(1,128)} %degrees_ref.1, bf16[64,768]{1,0:T(8,128)(2,1)} %features_ref.1), custom_call_target="tpu_custom_call" | custom-call | tf_op jit(solution)/shard_map/dense_rows/pallas_call | solution.py:45
  1.3 1.9 %collective-permute-start.2 = (bf16[64,768]{1,0:T(8,128)(2,1)S(1)}, bf16[64,768]{1,0:T(8,128)(2,1)S(1)}, u32[]{:S(2)}, u32[]{:S(2)}) collective-permute-start(bf16[64,768]{1,0:T(8,128)(2,1)S(1)} %dense_rows.1.own_ref), channel_id=1, source_target_pairs={{0,6},{1,7},{2,4},{3,5},{4,2},{5,3},{6,0},{7,1},{8,14},{9,15},{10,... | collective-permute-start | bytes 294920 | tf_op jit(solution)/shard_map/ppermute | solution.py:151
  3.3 3.2 %collective-permute-start.1 = (bf16[64,768]{1,0:T(8,128)(2,1)S(1)}, bf16[64,768]{1,0:T(8,128)(2,1)S(1)}, u32[]{:S(2)}, u32[]{:S(2)}) collective-permute-start(bf16[64,768]{1,0:T(8,128)(2,1)S(1)} %dense_rows.1.own_ref), channel_id=1, source_target_pairs={{0,4},{1,5},{2,6},{3,7},{4,0},{5,1},{6,2},{7,3},{8,12},{9,13},{10,... | collective-permute-start | bytes 294920 | tf_op jit(solution)/shard_map/ppermute | solution.py:151
  6.5 4.1 %collective-permute-start = (bf16[64,768]{1,0:T(8,128)(2,1)S(1)}, bf16[64,768]{1,0:T(8,128)(2,1)S(1)}, u32[]{:S(2)}, u32[]{:S(2)}) collective-permute-start(bf16[64,768]{1,0:T(8,128)(2,1)S(1)} %dense_rows.1.own_ref), channel_id=1, source_target_pairs={{0,2},{1,3},{2,0},{3,1},{4,6},{5,7},{6,4},{7,5},{8,10},{9,11},{10,... | collective-permute-start | bytes 294920 | tf_op jit(solution)/shard_map/ppermute | solution.py:151
  10.6 3.1 %collective-permute-start.3 = (bf16[64,768]{1,0:T(8,128)(2,1)S(1)}, bf16[64,768]{1,0:T(8,128)(2,1)S(1)}, u32[]{:S(2)}, u32[]{:S(2)}) collective-permute-start(bf16[64,768]{1,0:T(8,128)(2,1)S(1)} %dense_rows.1.own_ref), channel_id=1, source_target_pairs={{0,24},{1,25},{2,26},{3,27},{4,28},{5,29},{6,30},{7,31},{8,16},{9,... | collective-permute-start | bytes 294920 | tf_op jit(solution)/shard_map/ppermute | solution.py:151
  13.8 0.5 %collective-permute-done.1 = bf16[64,768]{1,0:T(8,128)(2,1)S(1)} collective-permute-done((bf16[64,768]{1,0:T(8,128)(2,1)S(1)}, bf16[64,768]{1,0:T(8,128)(2,1)S(1)}, u32[]{:S(2)}, u32[]{:S(2)}) %collective-permute-start.1) | collective-permute-done | bytes 98336 | tf_op jit(solution)/shard_map/ppermute | solution.py:151
  14.3 1.3 %collective-permute-done = bf16[64,768]{1,0:T(8,128)(2,1)S(1)} collective-permute-done((bf16[64,768]{1,0:T(8,128)(2,1)S(1)}, bf16[64,768]{1,0:T(8,128)(2,1)S(1)}, u32[]{:S(2)}, u32[]{:S(2)}) %collective-permute-start) | collective-permute-done | bytes 98336 | tf_op jit(solution)/shard_map/ppermute | solution.py:151
  15.6 0.1 pad_maximum_fusion.refs_0_
  15.6 1.3 %collective-permute-done.3 = bf16[64,768]{1,0:T(8,128)(2,1)S(1)} collective-permute-done((bf16[64,768]{1,0:T(8,128)(2,1)S(1)}, bf16[64,768]{1,0:T(8,128)(2,1)S(1)}, u32[]{:S(2)}, u32[]{:S(2)}) %collective-permute-start.3) | collective-permute-done | bytes 98336 | tf_op jit(solution)/shard_map/ppermute | solution.py:151
  16.9 1.3 %collective-permute-start.6 = (bf16[4,64,768]{2,1,0:T(8,128)(2,1)S(1)}, bf16[4,64,768]{2,1,0:T(8,128)(2,1)S(1)}, u32[]{:S(2)}, u32[]{:S(2)}) collective-permute-start(bf16[4,64,768]{2,1,0:T(8,128)(2,1)S(1)} %pad_maximum_fusion.refs_0_), channel_id=1, source_target_pairs={{0,16},{1,17},{2,18},{3,19},{4,20},{5,21},{6,22},{7,23},{8,24},{9,... | collective-permute-start | bytes 1179656 | tf_op jit(solution)/shard_map/ppermute | solution.py:151
  18.2 4.0 %collective-permute-start.4 = (bf16[4,64,768]{2,1,0:T(8,128)(2,1)S(1)}, bf16[4,64,768]{2,1,0:T(8,128)(2,1)S(1)}, u32[]{:S(2)}, u32[]{:S(2)}) collective-permute-start(bf16[4,64,768]{2,1,0:T(8,128)(2,1)S(1)} %pad_maximum_fusion.refs_0_), channel_id=1, source_target_pairs={{0,8},{1,9},{2,10},{3,11},{4,12},{5,13},{6,14},{7,15},{8,0},{9,1},... | collective-permute-start | bytes 1179656 | tf_op jit(solution)/shard_map/ppermute | solution.py:151
  22.2 1.9 %collective-permute-start.11 = (bf16[64,768]{1,0:T(8,128)(2,1)S(1)}, bf16[64,768]{1,0:T(8,128)(2,1)S(1)}, u32[]{:S(2)}, u32[]{:S(2)}) collective-permute-start(bf16[64,768]{1,0:T(8,128)(2,1)S(1)} %collective-permute-done.3), channel_id=1, source_target_pairs={{8,14},{9,15},{10,12},{11,13},{12,10},{13,11},{14,8},{15,9},{16,22... | collective-permute-start | bytes 294920 | tf_op jit(solution)/shard_map/ppermute | solution.py:151
  24.1 3.1 %collective-permute-start.10 = (bf16[64,768]{1,0:T(8,128)(2,1)S(1)}, bf16[64,768]{1,0:T(8,128)(2,1)S(1)}, u32[]{:S(2)}, u32[]{:S(2)}) collective-permute-start(bf16[64,768]{1,0:T(8,128)(2,1)S(1)} %collective-permute-done.3), channel_id=1, source_target_pairs={{8,12},{9,13},{10,14},{11,15},{12,8},{13,9},{14,10},{15,11},{16,20... | collective-permute-start | bytes 294920 | tf_op jit(solution)/shard_map/ppermute | solution.py:151
  27.2 4.3 %collective-permute-start.9 = (bf16[64,768]{1,0:T(8,128)(2,1)S(1)}, bf16[64,768]{1,0:T(8,128)(2,1)S(1)}, u32[]{:S(2)}, u32[]{:S(2)}) collective-permute-start(bf16[64,768]{1,0:T(8,128)(2,1)S(1)} %collective-permute-done.3), channel_id=1, source_target_pairs={{8,10},{9,11},{10,8},{11,9},{12,14},{13,15},{14,12},{15,13},{16,18... | collective-permute-start | bytes 294920 | tf_op jit(solution)/shard_map/ppermute | solution.py:151
  31.5 0.0 collective-permute-done.11
  31.5 6.0 %collective-permute-start.8 = (bf16[4,64,768]{2,1,0:T(8,128)(2,1)S(1)}, bf16[4,64,768]{2,1,0:T(8,128)(2,1)S(1)}, u32[]{:S(2)}, u32[]{:S(2)}) collective-permute-start(bf16[4,64,768]{2,1,0:T(8,128)(2,1)S(1)} %pad_maximum_fusion.refs_0_), channel_id=1, source_target_pairs={{0,1},{1,0},{2,3},{3,2},{4,5},{5,4},{6,7},{7,6},{8,9},{9,8},{10,11... | collective-permute-start | bytes 1179656 | tf_op jit(solution)/shard_map/ppermute | solution.py:151
  37.5 0.0 collective-permute-done.6.refs_2_.refs_4_
  37.5 0.7 %collective-permute-start.7 = (bf16[4,64,768]{2,1,0:T(8,128)(2,1)S(1)}, bf16[4,64,768]{2,1,0:T(8,128)(2,1)S(1)}, u32[]{:S(2)}, u32[]{:S(2)}) collective-permute-start(bf16[4,64,768]{2,1,0:T(8,128)(2,1)S(1)} %collective-permute-done.6.refs_2_.refs_4_), channel_id=1, source_target_pairs={{0,1},{1,0},{2,3},{3,2},{4,5},{5,4},{6,7},{7,6},{16,17},{17,16},{1... | collective-permute-start | bytes 1179656 | tf_op jit(solution)/shard_map/ppermute | solution.py:151
  38.2 1.9 %collective-permute-start.5 = (bf16[4,64,768]{2,1,0:T(8,128)(2,1)S(1)}, bf16[4,64,768]{2,1,0:T(8,128)(2,1)S(1)}, u32[]{:S(2)}, u32[]{:S(2)}) collective-permute-start(bf16[4,64,768]{2,1,0:T(8,128)(2,1)S(1)} %collective-permute-done.4.refs_0_.refs_2_), channel_id=1, source_target_pairs={{0,1},{1,0},{2,3},{3,2},{4,5},{5,4},{6,7},{7,6},{8,9},{9,8},{10,11... | collective-permute-start | bytes 1179656 | tf_op jit(solution)/shard_map/ppermute | solution.py:151
  40.2 0.1 pad_maximum_fusion.1.refs_6_
  40.2 2.4 %collective-permute-start.12 = (bf16[4,64,768]{2,1,0:T(8,128)(2,1)S(1)}, bf16[4,64,768]{2,1,0:T(8,128)(2,1)S(1)}, u32[]{:S(2)}, u32[]{:S(2)}) collective-permute-start(bf16[4,64,768]{2,1,0:T(8,128)(2,1)S(1)} %pad_maximum_fusion.1.refs_6_), channel_id=1, source_target_pairs={{8,9},{9,8},{10,11},{11,10},{12,13},{13,12},{14,15},{15,14},{16,17... | collective-permute-start | bytes 1179656 | tf_op jit(solution)/shard_map/ppermute | solution.py:151
  42.7 0.3 first_products.1.first_ref
  42.9 1.0 %collective-permute-done.12.refs_7_ = bf16[4,64,768]{2,1,0:T(8,128)(2,1)S(1)} collective-permute-done((bf16[4,64,768]{2,1,0:T(8,128)(2,1)S(1)}, bf16[4,64,768]{2,1,0:T(8,128)(2,1)S(1)}, u32[]{:S(2)}, u32[]{:S(2)}) %collective-permute-start.12) | collective-permute-done | bytes 393248 | tf_op jit(solution)/shard_map/ppermute | solution.py:151
  44.0 0.9 %second_products.1 = bf16[64,768]{1,0:T(8,128)(2,1)} custom-call(bf16[128,512]{1,0:T(8,128)(2,1)S(1)} %first_products.1.first_ref, bf16[4,64,768]{2,1,0:T(8,128)(2,1)S(1)} %pad_maximum_fusion.refs_0_, bf16[4,64,768]{2,1,0:T(8,128)(2,1)S(1)} %collective-permute-done.8.refs_1_, bf16[4,64,768]{2,1,0:T(8,128)(2,1)S(1)} %collective-permute-done.4.refs_0_.refs_2_, ...), custom_call_target="tpu_custom_call" | custom-call | tf_op jit(solution)/shard_map/second_products/pallas_call | solution.py:132
  (7 shorter events, 0.0 us)
Async XLA Ops:
  1.3 12.4 %collective-permute-start.2 = (bf16[64,768]{1,0:T(8,128)(2,1)S(1)}, bf16[64,768]{1,0:T(8,128)(2,1)S(1)}, u32[]{:S(2)}, u32[]{:S(2)}) collective-permute-start(bf16[64,768]{1,0:T(8,128)(2,1)S(1)} %dense_rows.1.own_ref), channel_id=1, source_target_pairs={{0,6},{1,7},{2,4},{3,5},{4,2},{5,3},{6,0},{7,1},{8,14},{9,15},{10,... | collective-permute-start | bytes 294920 | tf_op jit(solution)/shard_map/ppermute | solution.py:151
  3.3 11.0 %collective-permute-start.1 = (bf16[64,768]{1,0:T(8,128)(2,1)S(1)}, bf16[64,768]{1,0:T(8,128)(2,1)S(1)}, u32[]{:S(2)}, u32[]{:S(2)}) collective-permute-start(bf16[64,768]{1,0:T(8,128)(2,1)S(1)} %dense_rows.1.own_ref), channel_id=1, source_target_pairs={{0,4},{1,5},{2,6},{3,7},{4,0},{5,1},{6,2},{7,3},{8,12},{9,13},{10,... | collective-permute-start | bytes 294920 | tf_op jit(solution)/shard_map/ppermute | solution.py:151
  6.5 9.1 %collective-permute-start = (bf16[64,768]{1,0:T(8,128)(2,1)S(1)}, bf16[64,768]{1,0:T(8,128)(2,1)S(1)}, u32[]{:S(2)}, u32[]{:S(2)}) collective-permute-start(bf16[64,768]{1,0:T(8,128)(2,1)S(1)} %dense_rows.1.own_ref), channel_id=1, source_target_pairs={{0,2},{1,3},{2,0},{3,1},{4,6},{5,7},{6,4},{7,5},{8,10},{9,11},{10,... | collective-permute-start | bytes 294920 | tf_op jit(solution)/shard_map/ppermute | solution.py:151
  10.6 6.3 %collective-permute-start.3 = (bf16[64,768]{1,0:T(8,128)(2,1)S(1)}, bf16[64,768]{1,0:T(8,128)(2,1)S(1)}, u32[]{:S(2)}, u32[]{:S(2)}) collective-permute-start(bf16[64,768]{1,0:T(8,128)(2,1)S(1)} %dense_rows.1.own_ref), channel_id=1, source_target_pairs={{0,24},{1,25},{2,26},{3,27},{4,28},{5,29},{6,30},{7,31},{8,16},{9,... | collective-permute-start | bytes 294920 | tf_op jit(solution)/shard_map/ppermute | solution.py:151
  16.9 20.6 %collective-permute-start.6 = (bf16[4,64,768]{2,1,0:T(8,128)(2,1)S(1)}, bf16[4,64,768]{2,1,0:T(8,128)(2,1)S(1)}, u32[]{:S(2)}, u32[]{:S(2)}) collective-permute-start(bf16[4,64,768]{2,1,0:T(8,128)(2,1)S(1)} %pad_maximum_fusion.refs_0_), channel_id=1, source_target_pairs={{0,16},{1,17},{2,18},{3,19},{4,20},{5,21},{6,22},{7,23},{8,24},{9,... | collective-permute-start | bytes 1179656 | tf_op jit(solution)/shard_map/ppermute | solution.py:151
  18.2 20.0 %collective-permute-start.4 = (bf16[4,64,768]{2,1,0:T(8,128)(2,1)S(1)}, bf16[4,64,768]{2,1,0:T(8,128)(2,1)S(1)}, u32[]{:S(2)}, u32[]{:S(2)}) collective-permute-start(bf16[4,64,768]{2,1,0:T(8,128)(2,1)S(1)} %pad_maximum_fusion.refs_0_), channel_id=1, source_target_pairs={{0,8},{1,9},{2,10},{3,11},{4,12},{5,13},{6,14},{7,15},{8,0},{9,1},... | collective-permute-start | bytes 1179656 | tf_op jit(solution)/shard_map/ppermute | solution.py:151
  22.2 9.3 %collective-permute-start.11 = (bf16[64,768]{1,0:T(8,128)(2,1)S(1)}, bf16[64,768]{1,0:T(8,128)(2,1)S(1)}, u32[]{:S(2)}, u32[]{:S(2)}) collective-permute-start(bf16[64,768]{1,0:T(8,128)(2,1)S(1)} %collective-permute-done.3), channel_id=1, source_target_pairs={{8,14},{9,15},{10,12},{11,13},{12,10},{13,11},{14,8},{15,9},{16,22... | collective-permute-start | bytes 294920 | tf_op jit(solution)/shard_map/ppermute | solution.py:151
  24.1 16.0 %collective-permute-start.10 = (bf16[64,768]{1,0:T(8,128)(2,1)S(1)}, bf16[64,768]{1,0:T(8,128)(2,1)S(1)}, u32[]{:S(2)}, u32[]{:S(2)}) collective-permute-start(bf16[64,768]{1,0:T(8,128)(2,1)S(1)} %collective-permute-done.3), channel_id=1, source_target_pairs={{8,12},{9,13},{10,14},{11,15},{12,8},{13,9},{14,10},{15,11},{16,20... | collective-permute-start | bytes 294920 | tf_op jit(solution)/shard_map/ppermute | solution.py:151
  27.2 12.9 %collective-permute-start.9 = (bf16[64,768]{1,0:T(8,128)(2,1)S(1)}, bf16[64,768]{1,0:T(8,128)(2,1)S(1)}, u32[]{:S(2)}, u32[]{:S(2)}) collective-permute-start(bf16[64,768]{1,0:T(8,128)(2,1)S(1)} %collective-permute-done.3), channel_id=1, source_target_pairs={{8,10},{9,11},{10,8},{11,9},{12,14},{13,15},{14,12},{15,13},{16,18... | collective-permute-start | bytes 294920 | tf_op jit(solution)/shard_map/ppermute | solution.py:151
  31.5 11.4 %collective-permute-start.8 = (bf16[4,64,768]{2,1,0:T(8,128)(2,1)S(1)}, bf16[4,64,768]{2,1,0:T(8,128)(2,1)S(1)}, u32[]{:S(2)}, u32[]{:S(2)}) collective-permute-start(bf16[4,64,768]{2,1,0:T(8,128)(2,1)S(1)} %pad_maximum_fusion.refs_0_), channel_id=1, source_target_pairs={{0,1},{1,0},{2,3},{3,2},{4,5},{5,4},{6,7},{7,6},{8,9},{9,8},{10,11... | collective-permute-start | bytes 1179656 | tf_op jit(solution)/shard_map/ppermute | solution.py:151
  37.5 5.1 %collective-permute-start.7 = (bf16[4,64,768]{2,1,0:T(8,128)(2,1)S(1)}, bf16[4,64,768]{2,1,0:T(8,128)(2,1)S(1)}, u32[]{:S(2)}, u32[]{:S(2)}) collective-permute-start(bf16[4,64,768]{2,1,0:T(8,128)(2,1)S(1)} %collective-permute-done.6.refs_2_.refs_4_), channel_id=1, source_target_pairs={{0,1},{1,0},{2,3},{3,2},{4,5},{5,4},{6,7},{7,6},{16,17},{17,16},{1... | collective-permute-start | bytes 1179656 | tf_op jit(solution)/shard_map/ppermute | solution.py:151
  38.2 4.4 %collective-permute-start.5 = (bf16[4,64,768]{2,1,0:T(8,128)(2,1)S(1)}, bf16[4,64,768]{2,1,0:T(8,128)(2,1)S(1)}, u32[]{:S(2)}, u32[]{:S(2)}) collective-permute-start(bf16[4,64,768]{2,1,0:T(8,128)(2,1)S(1)} %collective-permute-done.4.refs_0_.refs_2_), channel_id=1, source_target_pairs={{0,1},{1,0},{2,3},{3,2},{4,5},{5,4},{6,7},{7,6},{8,9},{9,8},{10,11... | collective-permute-start | bytes 1179656 | tf_op jit(solution)/shard_map/ppermute | solution.py:151
  40.2 3.7 %collective-permute-start.12 = (bf16[4,64,768]{2,1,0:T(8,128)(2,1)S(1)}, bf16[4,64,768]{2,1,0:T(8,128)(2,1)S(1)}, u32[]{:S(2)}, u32[]{:S(2)}) collective-permute-start(bf16[4,64,768]{2,1,0:T(8,128)(2,1)S(1)} %pad_maximum_fusion.1.refs_6_), channel_id=1, source_target_pairs={{8,9},{9,8},{10,11},{11,10},{12,13},{13,12},{14,15},{15,14},{16,17... | collective-permute-start | bytes 1179656 | tf_op jit(solution)/shard_map/ppermute | solution.py:151

commit v15 on v12

--- a/solution.py
+++ b/solution.py
@@ -8,15 +8,10 @@
 from jax.sharding import PartitionSpec as P
 
 
-def dense_rows_kernel(cols_ref, live_ref, tiles_ref, degrees_ref, features_ref, rows_ref):
+def dense_rows_kernel(cols_ref, live_ref, tiles_ref, degrees_ref, features_ref, rows_ref, *sent_refs):
     row_count, slots, tile_size = tiles_ref.shape
-    nodes = row_count * lax.axis_size("shard")
+    nodes = rows_ref.shape[1]
     blocks = nodes // tile_size
-    share = rows_ref.shape[1] - nodes
-    if share:
-        shares = features_ref.shape[1] // share
-        first = pl.multiple_of(lax.rem(lax.axis_index("section"), shares) * share, 128)
-        rows_ref[:, nodes:] = features_ref[:, pl.ds(first, share)]
     block_row = lax.axis_index("shard") * row_count // tile_size
     live = live_ref[0, block_row]
     wide = row_count * slots
@@ -37,14 +32,29 @@
         pick = (column == b).astype(jnp.bfloat16)
         summed = jnp.dot(pick, tiles, preferred_element_type=jnp.float32)
         rows_ref[:, b * tile_size : (b + 1) * tile_size] = (summed * scale).astype(jnp.bfloat16)
-
-
-def dense_rows(tile_cols, live_tiles, tile_rows, degrees, features, share):
+    for sent_ref in sent_refs:
+        sections, section = lax.axis_size("section"), lax.axis_index("section")
+        bulk, share = sent_ref.shape[1], sent_ref.shape[1] - nodes
+        shares = (features_ref.shape[1] - bulk) // share
+
+        @pl.when(section == sections - 1)
+        def _():
+            sent_ref[...] = features_ref[:, :bulk]
+
+        @pl.when(section < sections - 1)
+        def _():
+            first = pl.multiple_of(bulk + jnp.minimum(section, shares - 1) * share, 128)
+            sent_ref[:, :nodes] = rows_ref[...]
+            sent_ref[:, nodes:] = features_ref[:, pl.ds(first, share)]
+
+
+def dense_rows(tile_cols, live_tiles, tile_rows, degrees, features, sent_width):
     row_count = tile_rows.shape[0]
     nodes = row_count * lax.axis_size("shard")
+    widths = [nodes, sent_width] if sent_width else [nodes]
     return pl.pallas_call(
         dense_rows_kernel,
-        out_shape=pltpu.VMEM((row_count, nodes + share), jnp.bfloat16),
+        out_shape=[pltpu.VMEM((row_count, columns), jnp.bfloat16) for columns in widths],
         in_specs=[
             pl.BlockSpec(memory_space=pltpu.SMEM),
             pl.BlockSpec(memory_space=pltpu.SMEM),
@@ -52,7 +62,7 @@
             pl.BlockSpec(memory_space=pltpu.VMEM),
             pl.BlockSpec(memory_space=pltpu.VMEM),
         ],
-        out_specs=pl.BlockSpec(memory_space=pltpu.VMEM),
+        out_specs=[pl.BlockSpec(memory_space=pltpu.VMEM)] * len(widths),
         name="dense_rows",
     )(tile_cols, live_tiles, tile_rows, degrees, features)
 
@@ -91,7 +101,7 @@
 def first_kernel(masks, sections, own_ref, *refs):
     pair_refs, halves = dict(zip(masks, zip(refs[:-1:2], refs[1:-1:2]))), refs[-1]
     row_count, nodes = own_ref.shape[0], halves.shape[1]
-    halves[:row_count] = own_ref[:, :nodes]
+    halves[:row_count] = own_ref[...]
     halves[row_count:] = jnp.zeros((row_count, nodes), jnp.bfloat16)
     for at in range(sections):
         near, _ = split_chain(at)
@@ -101,17 +111,20 @@
 
 def second_kernel(sections, first_ref, *refs):
     pair_refs, out_ref, halves = list(zip(refs[:-2:2], refs[1:-2:2])), refs[-2], refs[-1]
-    nodes = halves.shape[1]
-    share = pair_refs[0][0].shape[2] - nodes
+    nodes, bulk = halves.shape[1], pair_refs[0][0].shape[2]
+    share = bulk - nodes
     halves[...] = first_ref[...]
     for at in range(sections):
 
         @pl.when(lax.axis_index("section") == at)
         def _(at=at):
             multiply_through(halves, pair_refs, split_chain(at)[1])
-            for giver in range(out_ref.shape[1] // share):
-                product = times(halves, pair_refs, at ^ giver, slice(nodes, nodes + share))
-                out_ref[:, giver * share : (giver + 1) * share] = product.astype(jnp.bfloat16)
+            product = times(halves, pair_refs, at ^ (sections - 1), slice(0, bulk))
+            out_ref[:, :bulk] = product.astype(jnp.bfloat16)
+            for giver in range((out_ref.shape[1] - bulk) // share):
+                product = times(halves, pair_refs, at ^ giver, slice(nodes, bulk))
+                first = bulk + giver * share
+                out_ref[:, first : first + share] = product.astype(jnp.bfloat16)
 
 
 def first_products(own, pairs, nodes, sections):
@@ -140,7 +153,7 @@
     )(first, *operands)
 
 
-def by_products(own, nodes, width):
+def by_products(own, sent, width):
     sections, shards = lax.axis_size("section"), lax.axis_size("shard")
 
     def along_shard(value, mask):
@@ -152,13 +165,13 @@
     def along_z(value):
         return jnp.stack([value] + [along_shard(value, 2 * mask) for mask in range(1, shards // 2)])
 
-    ahead = {mask: along_section(own, mask) for mask in range(1, sections) if mask & (mask - 1)}
-    mine, ahead = lax.optimization_barrier((along_z(own), ahead))
+    ahead = {mask: along_section(sent, mask) for mask in range(1, sections) if mask & (mask - 1)}
+    mine, ahead = lax.optimization_barrier((along_z(sent), ahead))
     gathered = [mine]
     for mask in range(1, sections):
         gathered.append(along_z(ahead[mask]) if mask in ahead else along_section(mine, mask))
     pairs = [(here, along_shard(here, 1)) for here in gathered]
-    first = first_products(own, pairs, nodes, sections)
+    first = first_products(own, pairs, own.shape[1], sections)
     return second_products(first, pairs, width, sections)
 
 
@@ -180,12 +193,14 @@
     row_count, width = features.shape
     sections, shards = lax.axis_size("section"), lax.axis_size("shard")
     nodes = row_count * shards
-    doubles = shards >= 2 and shards & (shards - 1) == 0 and sections & (sections - 1) == 0
-    products = doubles and nodes <= width and width % (sections - 1) == 0
-    share = width // (sections - 1) if products else 0
-    own = dense_rows(tile_cols, live_tiles, tile_values[0], degrees, features, share)
-    out = by_products(own, nodes, width) if products else by_hops(features, own)
-    return out[None]
+    sent_width = pl.cdiv((sections - 1) * nodes + width, sections * 128) * 128
+    even = shards >= 2 and shards & (shards - 1) == 0 and sections > 1 and sections & (sections - 1) == 0
+    parts = nodes < sent_width < width and (width - sent_width) % (sent_width - nodes) == 0
+    if even and parts:
+        own, sent = dense_rows(tile_cols, live_tiles, tile_values[0], degrees, features, sent_width)
+        return by_products(own, sent, width)[None]
+    (own,) = dense_rows(tile_cols, live_tiles, tile_values[0], degrees, features, 0)
+    return by_hops(features, own)[None]
 
 
 def solution(mesh):

time: 31.2 us -> 28.8 us (0.923)
  waiting for transfers between devices: 12.2 us -> 9.66 us
    ppermute x10, waiting for transfers between devices: 11.7 us -> 9.65 us  [along_shard(): return lax.ppermute(value, 'shard', [(i, i ^ mask) for i in range(shards)])]
    ppermute x3, waiting for transfers between devices: 0.42 us -> 0.01 us  [along_section(): lax.ppermute(value, 'section', [(i, i ^ mask) for i in range(sections)])]
  transfers between devices with their start and end apart: 13 -> 13, of which waited for: 6 -> 4; matrix products, arithmetic and copies ran while one was open for 0% -> 0% of each run, Pallas kernels for 0% -> 0%
where the time goes in v15:
time: 28.8 us; the launch traced here: 28.6 us
  starting transfers between devices  16.4 us (57%)
  waiting for transfers between devices  9.66 us (34%)
  Pallas kernels  2.33 us (8%)
    ppermute x10, starting transfers between devices, along_shard(): return lax.ppermute(value, 'shard', [(i, i ^ mask) for i in range(shards)])  10.8 us
    ppermute x10, waiting for transfers between devices, along_shard(): return lax.ppermute(value, 'shard', [(i, i ^ mask) for i in range(shards)])  9.65 us
    ppermute x3, starting transfers between devices, along_section(): lax.ppermute(value, 'section', [(i, i ^ mask) for i in range(sections)])  5.65 us
    pallas_call x1, Pallas kernels, dense_rows(): pl.pallas_call(dense_rows_kernel, out_shape=[pltpu.VMEM((row_count, colum...  1.33 us
    pallas_call x1, Pallas kernels, second_products(): pl.pallas_call(functools.partial(second_kernel, sections), out_shape=jax....  0.97 us
  transfers between devices with their start and end apart: 13, of which 4 were waited for; matrix products, arithmetic and copies ran while one was open for 0% of the time, Pallas kernels for 0%

profile of v15, /device:TPU:0, one launch (start us, length us, event | category | flops | bytes accessed | tf_op | source)
XLA Modules:
  0.0 28.6 jit_solution(11730389938427863733)
XLA Ops:
  0.0 1.3 %dense_rows.1 = (bf16[64,512]{1,0:T(8,128)(2,1)S(1)}, bf16[64,640]{1,0:T(8,128)(2,1)S(1)}) custom-call(s32[1,4,16]{2,1,0:T(4,128)} %cols_ref.1, s32[1,4]{1,0:T(1,128)} %live_ref.1, bf16[64,16,128]{2,1,0:T(8,128)(2,1)} %bitcast.11, s32[1,64]{1,0:T(1,128)} %degrees_ref.1, bf16[64,768]{1,0:T(8,128)(2,1)} %features_ref.1), custom_call_target="tpu_custom_call" | custom-call | tf_op jit(solution)/shard_map/dense_rows/pallas_call | solution.py:55
  1.3 5.1 %collective-permute-start.2 = (bf16[64,640]{1,0:T(8,128)(2,1)S(1)}, bf16[64,640]{1,0:T(8,128)(2,1)S(1)}, u32[]{:S(2)}, u32[]{:S(2)}) collective-permute-start(bf16[64,640]{1,0:T(8,128)(2,1)S(1)} %get-tuple-element.10), channel_id=1, source_target_pairs={{0,6},{1,7},{2,4},{3,5},{4,2},{5,3},{6,0},{7,1},{8,14},{9,15},{10,... | collective-permute-start | bytes 245768 | tf_op jit(solution)/shard_map/ppermute | solution.py:160
  6.5 0.0 collective-permute-start.1
  6.5 0.6 %collective-permute-start = (bf16[64,640]{1,0:T(8,128)(2,1)S(1)}, bf16[64,640]{1,0:T(8,128)(2,1)S(1)}, u32[]{:S(2)}, u32[]{:S(2)}) collective-permute-start(bf16[64,640]{1,0:T(8,128)(2,1)S(1)} %get-tuple-element.10), channel_id=1, source_target_pairs={{0,2},{1,3},{2,0},{3,1},{4,6},{5,7},{6,4},{7,5},{8,10},{9,11},{10,... | collective-permute-start | bytes 245768 | tf_op jit(solution)/shard_map/ppermute | solution.py:160
  7.1 2.6 %collective-permute-start.3 = (bf16[64,640]{1,0:T(8,128)(2,1)S(1)}, bf16[64,640]{1,0:T(8,128)(2,1)S(1)}, u32[]{:S(2)}, u32[]{:S(2)}) collective-permute-start(bf16[64,640]{1,0:T(8,128)(2,1)S(1)} %get-tuple-element.10), channel_id=1, source_target_pairs={{0,24},{8,16},{16,8},{24,0},{1,25},{9,17},{17,9},{25,1},{2,26},{10... | collective-permute-start | bytes 245768 | tf_op jit(solution)/shard_map/ppermute | solution.py:163
  9.7 0.0 collective-permute-done.2
  9.7 3.6 %collective-permute-done.1 = bf16[64,640]{1,0:T(8,128)(2,1)S(1)} collective-permute-done((bf16[64,640]{1,0:T(8,128)(2,1)S(1)}, bf16[64,640]{1,0:T(8,128)(2,1)S(1)}, u32[]{:S(2)}, u32[]{:S(2)}) %collective-permute-start.1) | collective-permute-done | bytes 81952 | tf_op jit(solution)/shard_map/ppermute | solution.py:160
  13.3 0.0 collective-permute-done
  13.3 0.1 pad_maximum_fusion.refs_0_
  13.4 0.0 collective-permute-done.3
  13.4 1.6 %collective-permute-start.6 = (bf16[4,64,640]{2,1,0:T(8,128)(2,1)S(1)}, bf16[4,64,640]{2,1,0:T(8,128)(2,1)S(1)}, u32[]{:S(2)}, u32[]{:S(2)}) collective-permute-start(bf16[4,64,640]{2,1,0:T(8,128)(2,1)S(1)} %pad_maximum_fusion.refs_0_), channel_id=1, source_target_pairs={{0,16},{8,24},{16,0},{24,8},{1,17},{9,25},{17,1},{25,9},{2,18},{10... | collective-permute-start | bytes 983048 | tf_op jit(solution)/shard_map/ppermute | solution.py:163
  15.0 1.5 %collective-permute-start.4 = (bf16[4,64,640]{2,1,0:T(8,128)(2,1)S(1)}, bf16[4,64,640]{2,1,0:T(8,128)(2,1)S(1)}, u32[]{:S(2)}, u32[]{:S(2)}) collective-permute-start(bf16[4,64,640]{2,1,0:T(8,128)(2,1)S(1)} %pad_maximum_fusion.refs_0_), channel_id=1, source_target_pairs={{0,8},{8,0},{16,24},{24,16},{1,9},{9,1},{17,25},{25,17},{2,10},{10... | collective-permute-start | bytes 983048 | tf_op jit(solution)/shard_map/ppermute | solution.py:163
  16.5 2.7 %collective-permute-start.11 = (bf16[64,640]{1,0:T(8,128)(2,1)S(1)}, bf16[64,640]{1,0:T(8,128)(2,1)S(1)}, u32[]{:S(2)}, u32[]{:S(2)}) collective-permute-start(bf16[64,640]{1,0:T(8,128)(2,1)S(1)} %collective-permute-done.3), channel_id=1, source_target_pairs={{0,6},{1,7},{2,4},{3,5},{4,2},{5,3},{6,0},{7,1},{8,14},{9,15},{10,... | collective-permute-start | bytes 245768 | tf_op jit(solution)/shard_map/ppermute | solution.py:160
  19.2 0.0 collective-permute-start.10
  19.2 1.7 %collective-permute-start.9 = (bf16[64,640]{1,0:T(8,128)(2,1)S(1)}, bf16[64,640]{1,0:T(8,128)(2,1)S(1)}, u32[]{:S(2)}, u32[]{:S(2)}) collective-permute-start(bf16[64,640]{1,0:T(8,128)(2,1)S(1)} %collective-permute-done.3), channel_id=1, source_target_pairs={{0,2},{1,3},{2,0},{3,1},{4,6},{5,7},{6,4},{7,5},{8,10},{9,11},{10,... | collective-permute-start | bytes 245768 | tf_op jit(solution)/shard_map/ppermute | solution.py:160
  20.8 2.5 %collective-permute-done.11 = bf16[64,640]{1,0:T(8,128)(2,1)S(1)} collective-permute-done((bf16[64,640]{1,0:T(8,128)(2,1)S(1)}, bf16[64,640]{1,0:T(8,128)(2,1)S(1)}, u32[]{:S(2)}, u32[]{:S(2)}) %collective-permute-start.11) | collective-permute-done | bytes 81952 | tf_op jit(solution)/shard_map/ppermute | solution.py:160
  23.4 0.0 collective-permute-start.8
  23.4 0.5 %collective-permute-start.7 = (bf16[4,64,640]{2,1,0:T(8,128)(2,1)S(1)}, bf16[4,64,640]{2,1,0:T(8,128)(2,1)S(1)}, u32[]{:S(2)}, u32[]{:S(2)}) collective-permute-start(bf16[4,64,640]{2,1,0:T(8,128)(2,1)S(1)} %collective-permute-done.6.refs_2_.refs_4_), channel_id=1, source_target_pairs={{0,1},{1,0},{2,3},{3,2},{4,5},{5,4},{6,7},{7,6},{8,9},{9,8},{10,11... | collective-permute-start | bytes 983048 | tf_op jit(solution)/shard_map/ppermute | solution.py:160
  23.9 0.1 collective-permute-start.5
  24.0 1.9 %collective-permute-done.10 = bf16[64,640]{1,0:T(8,128)(2,1)S(1)} collective-permute-done((bf16[64,640]{1,0:T(8,128)(2,1)S(1)}, bf16[64,640]{1,0:T(8,128)(2,1)S(1)}, u32[]{:S(2)}, u32[]{:S(2)}) %collective-permute-start.10) | collective-permute-done | bytes 81952 | tf_op jit(solution)/shard_map/ppermute | solution.py:160
  25.9 0.1 pad_maximum_fusion.1.refs_6_
  25.9 0.1 collective-permute-start.12
  26.1 1.6 %collective-permute-done.12.refs_7_ = bf16[4,64,640]{2,1,0:T(8,128)(2,1)S(1)} collective-permute-done((bf16[4,64,640]{2,1,0:T(8,128)(2,1)S(1)}, bf16[4,64,640]{2,1,0:T(8,128)(2,1)S(1)}, u32[]{:S(2)}, u32[]{:S(2)}) %collective-permute-start.12) | collective-permute-done | bytes 327712 | tf_op jit(solution)/shard_map/ppermute | solution.py:160
  27.6 1.0 %second_products.1 = bf16[64,768]{1,0:T(8,128)(2,1)} custom-call(bf16[128,512]{1,0:T(8,128)(2,1)S(1)} %first_products.1.first_ref, bf16[4,64,640]{2,1,0:T(8,128)(2,1)S(1)} %pad_maximum_fusion.refs_0_, bf16[4,64,640]{2,1,0:T(8,128)(2,1)S(1)} %collective-permute-done.8.refs_1_, bf16[4,64,640]{2,1,0:T(8,128)(2,1)S(1)} %collective-permute-done.4.refs_0_.refs_2_, ...), custom_call_target="tpu_custom_call" | custom-call | tf_op jit(solution)/shard_map/second_products/pallas_call | solution.py:145
  (7 shorter events, 0.0 us)
Async XLA Ops:
  1.3 8.3 %collective-permute-start.2 = (bf16[64,640]{1,0:T(8,128)(2,1)S(1)}, bf16[64,640]{1,0:T(8,128)(2,1)S(1)}, u32[]{:S(2)}, u32[]{:S(2)}) collective-permute-start(bf16[64,640]{1,0:T(8,128)(2,1)S(1)} %get-tuple-element.10), channel_id=1, source_target_pairs={{0,6},{1,7},{2,4},{3,5},{4,2},{5,3},{6,0},{7,1},{8,14},{9,15},{10,... | collective-permute-start | bytes 245768 | tf_op jit(solution)/shard_map/ppermute | solution.py:160
  6.5 6.9 %collective-permute-start.1 = (bf16[64,640]{1,0:T(8,128)(2,1)S(1)}, bf16[64,640]{1,0:T(8,128)(2,1)S(1)}, u32[]{:S(2)}, u32[]{:S(2)}) collective-permute-start(bf16[64,640]{1,0:T(8,128)(2,1)S(1)} %get-tuple-element.10), channel_id=1, source_target_pairs={{0,4},{1,5},{2,6},{3,7},{4,0},{5,1},{6,2},{7,3},{8,12},{9,13},{10,... | collective-permute-start | bytes 245768 | tf_op jit(solution)/shard_map/ppermute | solution.py:160
  6.5 6.9 %collective-permute-start = (bf16[64,640]{1,0:T(8,128)(2,1)S(1)}, bf16[64,640]{1,0:T(8,128)(2,1)S(1)}, u32[]{:S(2)}, u32[]{:S(2)}) collective-permute-start(bf16[64,640]{1,0:T(8,128)(2,1)S(1)} %get-tuple-element.10), channel_id=1, source_target_pairs={{0,2},{1,3},{2,0},{3,1},{4,6},{5,7},{6,4},{7,5},{8,10},{9,11},{10,... | collective-permute-start | bytes 245768 | tf_op jit(solution)/shard_map/ppermute | solution.py:160
  7.1 6.3 %collective-permute-start.3 = (bf16[64,640]{1,0:T(8,128)(2,1)S(1)}, bf16[64,640]{1,0:T(8,128)(2,1)S(1)}, u32[]{:S(2)}, u32[]{:S(2)}) collective-permute-start(bf16[64,640]{1,0:T(8,128)(2,1)S(1)} %get-tuple-element.10), channel_id=1, source_target_pairs={{0,24},{8,16},{16,8},{24,0},{1,25},{9,17},{17,9},{25,1},{2,26},{10... | collective-permute-start | bytes 245768 | tf_op jit(solution)/shard_map/ppermute | solution.py:163
  13.4 10.0 %collective-permute-start.6 = (bf16[4,64,640]{2,1,0:T(8,128)(2,1)S(1)}, bf16[4,64,640]{2,1,0:T(8,128)(2,1)S(1)}, u32[]{:S(2)}, u32[]{:S(2)}) collective-permute-start(bf16[4,64,640]{2,1,0:T(8,128)(2,1)S(1)} %pad_maximum_fusion.refs_0_), channel_id=1, source_target_pairs={{0,16},{8,24},{16,0},{24,8},{1,17},{9,25},{17,1},{25,9},{2,18},{10... | collective-permute-start | bytes 983048 | tf_op jit(solution)/shard_map/ppermute | solution.py:163
  15.0 8.9 %collective-permute-start.4 = (bf16[4,64,640]{2,1,0:T(8,128)(2,1)S(1)}, bf16[4,64,640]{2,1,0:T(8,128)(2,1)S(1)}, u32[]{:S(2)}, u32[]{:S(2)}) collective-permute-start(bf16[4,64,640]{2,1,0:T(8,128)(2,1)S(1)} %pad_maximum_fusion.refs_0_), channel_id=1, source_target_pairs={{0,8},{8,0},{16,24},{24,16},{1,9},{9,1},{17,25},{25,17},{2,10},{10... | collective-permute-start | bytes 983048 | tf_op jit(solution)/shard_map/ppermute | solution.py:163
  16.5 6.9 %collective-permute-start.11 = (bf16[64,640]{1,0:T(8,128)(2,1)S(1)}, bf16[64,640]{1,0:T(8,128)(2,1)S(1)}, u32[]{:S(2)}, u32[]{:S(2)}) collective-permute-start(bf16[64,640]{1,0:T(8,128)(2,1)S(1)} %collective-permute-done.3), channel_id=1, source_target_pairs={{0,6},{1,7},{2,4},{3,5},{4,2},{5,3},{6,0},{7,1},{8,14},{9,15},{10,... | collective-permute-start | bytes 245768 | tf_op jit(solution)/shard_map/ppermute | solution.py:160
  19.2 6.7 %collective-permute-start.10 = (bf16[64,640]{1,0:T(8,128)(2,1)S(1)}, bf16[64,640]{1,0:T(8,128)(2,1)S(1)}, u32[]{:S(2)}, u32[]{:S(2)}) collective-permute-start(bf16[64,640]{1,0:T(8,128)(2,1)S(1)} %collective-permute-done.3), channel_id=1, source_target_pairs={{0,4},{1,5},{2,6},{3,7},{4,0},{5,1},{6,2},{7,3},{8,12},{9,13},{10,... | collective-permute-start | bytes 245768 | tf_op jit(solution)/shard_map/ppermute | solution.py:160
  19.2 6.7 %collective-permute-start.9 = (bf16[64,640]{1,0:T(8,128)(2,1)S(1)}, bf16[64,640]{1,0:T(8,128)(2,1)S(1)}, u32[]{:S(2)}, u32[]{:S(2)}) collective-permute-start(bf16[64,640]{1,0:T(8,128)(2,1)S(1)} %collective-permute-done.3), channel_id=1, source_target_pairs={{0,2},{1,3},{2,0},{3,1},{4,6},{5,7},{6,4},{7,5},{8,10},{9,11},{10,... | collective-permute-start | bytes 245768 | tf_op jit(solution)/shard_map/ppermute | solution.py:160
  23.4 2.7 %collective-permute-start.8 = (bf16[4,64,640]{2,1,0:T(8,128)(2,1)S(1)}, bf16[4,64,640]{2,1,0:T(8,128)(2,1)S(1)}, u32[]{:S(2)}, u32[]{:S(2)}) collective-permute-start(bf16[4,64,640]{2,1,0:T(8,128)(2,1)S(1)} %pad_maximum_fusion.refs_0_), channel_id=1, source_target_pairs={{0,1},{1,0},{2,3},{3,2},{4,5},{5,4},{6,7},{7,6},{8,9},{9,8},{10,11... | collective-permute-start | bytes 983048 | tf_op jit(solution)/shard_map/ppermute | solution.py:160
  23.4 2.6 %collective-permute-start.7 = (bf16[4,64,640]{2,1,0:T(8,128)(2,1)S(1)}, bf16[4,64,640]{2,1,0:T(8,128)(2,1)S(1)}, u32[]{:S(2)}, u32[]{:S(2)}) collective-permute-start(bf16[4,64,640]{2,1,0:T(8,128)(2,1)S(1)} %collective-permute-done.6.refs_2_.refs_4_), channel_id=1, source_target_pairs={{0,1},{1,0},{2,3},{3,2},{4,5},{5,4},{6,7},{7,6},{8,9},{9,8},{10,11... | collective-permute-start | bytes 983048 | tf_op jit(solution)/shard_map/ppermute | solution.py:160
  23.9 2.1 %collective-permute-start.5 = (bf16[4,64,640]{2,1,0:T(8,128)(2,1)S(1)}, bf16[4,64,640]{2,1,0:T(8,128)(2,1)S(1)}, u32[]{:S(2)}, u32[]{:S(2)}) collective-permute-start(bf16[4,64,640]{2,1,0:T(8,128)(2,1)S(1)} %collective-permute-done.4.refs_0_.refs_2_), channel_id=1, source_target_pairs={{0,1},{1,0},{2,3},{3,2},{4,5},{5,4},{6,7},{7,6},{8,9},{9,8},{10,11... | collective-permute-start | bytes 983048 | tf_op jit(solution)/shard_map/ppermute | solution.py:160
  25.9 1.7 %collective-permute-start.12 = (bf16[4,64,640]{2,1,0:T(8,128)(2,1)S(1)}, bf16[4,64,640]{2,1,0:T(8,128)(2,1)S(1)}, u32[]{:S(2)}, u32[]{:S(2)}) collective-permute-start(bf16[4,64,640]{2,1,0:T(8,128)(2,1)S(1)} %pad_maximum_fusion.1.refs_6_), channel_id=1, source_target_pairs={{0,1},{1,0},{2,3},{3,2},{4,5},{5,4},{6,7},{7,6},{8,9},{9,8},{10,11... | collective-permute-start | bytes 983048 | tf_op jit(solution)/shard_map/ppermute | solution.py:160

commit v16 on v15

--- a/solution.py
+++ b/solution.py
@@ -73,66 +73,79 @@
     return masks[:count], masks[count:]
 
 
-def times(halves, pair_refs, mask, columns):
+def times(halves, pieces, mask, columns):
     row_count = halves.shape[0] // 2
     shard = lax.axis_index("shard")
     chip, first_core = lax.div(shard, 2), lax.rem(shard, 2) == 0
-    here_ref, there_ref = pair_refs[mask]
     left, right = [], []
-    for piece in range(here_ref.shape[0]):
+    for piece, (here_ref, there_ref) in enumerate(pieces[mask]):
         source = lax.bitwise_xor(chip, piece)
         left.append(halves[:, pl.ds(pl.multiple_of(source * 2 * row_count, 128), 2 * row_count)])
-        here, there = here_ref[piece, :, columns], there_ref[piece, :, columns]
+        here, there = here_ref[:, columns], there_ref[:, columns]
         right += [jnp.where(first_core, here, there), jnp.where(first_core, there, here)]
     left, right = jnp.concatenate(left, axis=1), jnp.concatenate(right, axis=0)
     both = jnp.dot(left, right, preferred_element_type=jnp.float32)
     return both[:row_count] + both[row_count:]
 
 
-def multiply_through(halves, pair_refs, masks):
+def pieces_of(refs, kinds):
+    pieces, at = {}, 0
+    for mask, count in kinds:
+        here, there = refs[at : at + count], refs[at + count : at + 2 * count]
+        if count == 1:
+            here, there = ([ref.at[piece] for piece in range(ref.shape[0])] for ref in (here[0], there[0]))
+        pieces[mask], at = list(zip(here, there)), at + 2 * count
+    return pieces
+
+
+def multiply_through(halves, pieces, masks):
     row_count, nodes = halves.shape[0] // 2, halves.shape[1]
     for mask in masks:
-        product = times(halves, pair_refs, mask, slice(0, nodes))
+        product = times(halves, pieces, mask, slice(0, nodes))
         high = product.astype(jnp.bfloat16)
         halves[:row_count] = high
         halves[row_count:] = (product - high.astype(jnp.float32)).astype(jnp.bfloat16)
 
 
-def first_kernel(masks, sections, own_ref, *refs):
-    pair_refs, halves = dict(zip(masks, zip(refs[:-1:2], refs[1:-1:2]))), refs[-1]
+def first_kernel(kinds, sections, own_ref, *refs):
+    pieces, halves = pieces_of(refs[:-1], kinds), refs[-1]
     row_count, nodes = own_ref.shape[0], halves.shape[1]
     halves[:row_count] = own_ref[...]
     halves[row_count:] = jnp.zeros((row_count, nodes), jnp.bfloat16)
     for at in range(sections):
         near, _ = split_chain(at)
         if near:
-            pl.when(lax.axis_index("section") == at)(functools.partial(multiply_through, halves, pair_refs, near))
-
-
-def second_kernel(sections, first_ref, *refs):
-    pair_refs, out_ref, halves = list(zip(refs[:-2:2], refs[1:-2:2])), refs[-2], refs[-1]
-    nodes, bulk = halves.shape[1], pair_refs[0][0].shape[2]
+            pl.when(lax.axis_index("section") == at)(functools.partial(multiply_through, halves, pieces, near))
+
+
+def second_kernel(kinds, sections, first_ref, *refs):
+    pieces, out_ref, halves = pieces_of(refs[:-2], kinds), refs[-2], refs[-1]
+    nodes, bulk = halves.shape[1], refs[0].shape[-1]
     share = bulk - nodes
     halves[...] = first_ref[...]
     for at in range(sections):
 
         @pl.when(lax.axis_index("section") == at)
         def _(at=at):
-            multiply_through(halves, pair_refs, split_chain(at)[1])
-            product = times(halves, pair_refs, at ^ (sections - 1), slice(0, bulk))
+            multiply_through(halves, pieces, split_chain(at)[1])
+            product = times(halves, pieces, at ^ (sections - 1), slice(0, bulk))
             out_ref[:, :bulk] = product.astype(jnp.bfloat16)
             for giver in range((out_ref.shape[1] - bulk) // share):
-                product = times(halves, pair_refs, at ^ giver, slice(nodes, bulk))
+                product = times(halves, pieces, at ^ giver, slice(nodes, bulk))
                 first = bulk + giver * share
                 out_ref[:, first : first + share] = product.astype(jnp.bfloat16)
 
 
-def first_products(own, pairs, nodes, sections):
-    masks = [mask for mask in range(1, sections) if not mask & (mask - 1)]
-    operands = [array for mask in masks for array in pairs[mask]]
+def flat(arrived, masks):
+    kinds = [(mask, len(arrived[mask][0])) for mask in masks]
+    return kinds, [array for mask in masks for side in arrived[mask] for array in side]
+
+
+def first_products(own, arrived, sections):
+    kinds, operands = flat(arrived, [mask for mask in range(1, sections) if not mask & (mask - 1)])
     return pl.pallas_call(
-        functools.partial(first_kernel, masks, sections),
-        out_shape=pltpu.VMEM((2 * own.shape[0], nodes), jnp.bfloat16),
+        functools.partial(first_kernel, kinds, sections),
+        out_shape=pltpu.VMEM((2 * own.shape[0], own.shape[1]), jnp.bfloat16),
         in_specs=[pl.BlockSpec(memory_space=pltpu.VMEM)] * (1 + len(operands)),
         out_specs=pl.BlockSpec(memory_space=pltpu.VMEM),
         compiler_params=pltpu.CompilerParams(vmem_limit_bytes=32 * 1024 * 1024),
@@ -140,10 +153,10 @@
     )(own, *operands)
 
 
-def second_products(first, pairs, width, sections):
-    operands = [array for pair in pairs for array in pair]
+def second_products(first, arrived, width, sections):
+    kinds, operands = flat(arrived, list(range(sections)))
     return pl.pallas_call(
-        functools.partial(second_kernel, sections),
+        functools.partial(second_kernel, kinds, sections),
         out_shape=jax.ShapeDtypeStruct((first.shape[0] // 2, width), jnp.bfloat16),
         in_specs=[pl.BlockSpec(memory_space=pltpu.VMEM)] * (1 + len(operands)),
         out_specs=pl.BlockSpec(memory_space=pltpu.VMEM),
@@ -163,16 +176,16 @@
         return lax.ppermute(value, "section", [(i, i ^ mask) for i in range(sections)])
 
     def along_z(value):
-        return jnp.stack([value] + [along_shard(value, 2 * mask) for mask in range(1, shards // 2)])
+        return [value] + [along_shard(value, 2 * mask) for mask in range(1, shards // 2)]
 
     ahead = {mask: along_section(sent, mask) for mask in range(1, sections) if mask & (mask - 1)}
-    mine, ahead = lax.optimization_barrier((along_z(sent), ahead))
-    gathered = [mine]
+    mine, ahead = lax.optimization_barrier((jnp.stack(along_z(sent)), ahead))
+    arrived = [[mine]]
     for mask in range(1, sections):
-        gathered.append(along_z(ahead[mask]) if mask in ahead else along_section(mine, mask))
-    pairs = [(here, along_shard(here, 1)) for here in gathered]
-    first = first_products(own, pairs, own.shape[1], sections)
-    return second_products(first, pairs, width, sections)
+        arrived.append(along_z(ahead[mask]) if mask in ahead else [along_section(mine, mask)])
+    arrived = [(here, [along_shard(array, 1) for array in here]) for here in arrived]
+    first = first_products(own, arrived, sections)
+    return second_products(first, arrived, width, sections)
 
 
 def by_hops(features, own):

time: 28.8 us -> 38.8 us (1.35)
  waiting for transfers between devices: 9.66 us -> 21.8 us
  starting transfers between devices: 16.4 us -> 14.4 us
    ppermute x3, waiting for transfers between devices: 0.01 us -> 7.3 us  [along_section(): lax.ppermute(value, 'section', [(i, i ^ mask) for i in range(sections)])]
    ppermute x10 -> x13, waiting for transfers between devices: 9.65 us -> 14.5 us  [along_shard(): return lax.ppermute(value, 'shard', [(i, i ^ mask) for i in range(shards)])]
    ppermute x10 -> x13, starting transfers between devices: 10.8 us -> 8.75 us  [along_shard(): return lax.ppermute(value, 'shard', [(i, i ^ mask) for i in range(shards)])]
  transfers between devices with their start and end apart: 13 -> 16, of which waited for: 4 -> 9; matrix products, arithmetic and copies ran while one was open for 0% -> 0% of each run, Pallas kernels for 0% -> 0%
where the time goes in v16:
time: 38.8 us; the launch traced here: 38.6 us
  waiting for transfers between devices  21.8 us (56%)
  starting transfers between devices  14.4 us (37%)
  Pallas kernels  2.33 us (6%)
    ppermute x13, waiting for transfers between devices, along_shard(): return lax.ppermute(value, 'shard', [(i, i ^ mask) for i in range(shards)])  14.5 us
    ppermute x13, starting transfers between devices, along_shard(): return lax.ppermute(value, 'shard', [(i, i ^ mask) for i in range(shards)])  8.75 us
    ppermute x3, waiting for transfers between devices, along_section(): lax.ppermute(value, 'section', [(i, i ^ mask) for i in range(sections)])  7.3 us
    ppermute x3, starting transfers between devices, along_section(): lax.ppermute(value, 'section', [(i, i ^ mask) for i in range(sections)])  5.65 us
    pallas_call x1, Pallas kernels, dense_rows(): pl.pallas_call(dense_rows_kernel, out_shape=[pltpu.VMEM((row_count, colum...  1.33 us
    pallas_call x1, Pallas kernels, second_products(): pl.pallas_call(functools.partial(second_kernel, kinds, sections), out_sha...  0.98 us
  transfers between devices with their start and end apart: 16, of which 9 were waited for; matrix products, arithmetic and copies ran while one was open for 0% of the time, Pallas kernels for 0%

profile of v16, /device:TPU:0, one launch (start us, length us, event | category | flops | bytes accessed | tf_op | source)
XLA Modules:
  0.0 38.6 jit_solution(5632708404836560787)
XLA Ops:
  0.0 1.3 %dense_rows.1 = (bf16[64,512]{1,0:T(8,128)(2,1)S(1)}, bf16[64,640]{1,0:T(8,128)(2,1)S(1)}) custom-call(s32[1,4,16]{2,1,0:T(4,128)} %cols_ref.1, s32[1,4]{1,0:T(1,128)} %live_ref.1, bf16[64,16,128]{2,1,0:T(8,128)(2,1)} %bitcast.7, s32[1,64]{1,0:T(1,128)} %degrees_ref.1, bf16[64,768]{1,0:T(8,128)(2,1)} %features_ref.1), custom_call_target="tpu_custom_call" | custom-call | tf_op jit(solution)/shard_map/dense_rows/pallas_call | solution.py:55
  1.3 5.1 %collective-permute-start.2 = (bf16[64,640]{1,0:T(8,128)(2,1)S(1)}, bf16[64,640]{1,0:T(8,128)(2,1)S(1)}, u32[]{:S(2)}, u32[]{:S(2)}) collective-permute-start(bf16[64,640]{1,0:T(8,128)(2,1)S(1)} %get-tuple-element.10), channel_id=1, source_target_pairs={{0,6},{1,7},{2,4},{3,5},{4,2},{5,3},{6,0},{7,1},{8,14},{9,15},{10,... | collective-permute-start | bytes 245768 | tf_op jit(solution)/shard_map/ppermute | solution.py:173
  6.5 0.6 %collective-permute-start = (bf16[64,640]{1,0:T(8,128)(2,1)S(1)}, bf16[64,640]{1,0:T(8,128)(2,1)S(1)}, u32[]{:S(2)}, u32[]{:S(2)}) collective-permute-start(bf16[64,640]{1,0:T(8,128)(2,1)S(1)} %get-tuple-element.10), channel_id=1, source_target_pairs={{0,2},{1,3},{2,0},{3,1},{4,6},{5,7},{6,4},{7,5},{8,10},{9,11},{10,... | collective-permute-start | bytes 245768 | tf_op jit(solution)/shard_map/ppermute | solution.py:173
  7.1 2.6 %collective-permute-start.3 = (bf16[64,640]{1,0:T(8,128)(2,1)S(1)}, bf16[64,640]{1,0:T(8,128)(2,1)S(1)}, u32[]{:S(2)}, u32[]{:S(2)}) collective-permute-start(bf16[64,640]{1,0:T(8,128)(2,1)S(1)} %get-tuple-element.10), channel_id=1, source_target_pairs={{0,24},{8,16},{16,8},{24,0},{1,25},{9,17},{17,9},{25,1},{2,26},{10... | collective-permute-start | bytes 245768 | tf_op jit(solution)/shard_map/ppermute | solution.py:176
  9.7 0.0 collective-permute-done.2
  9.7 3.6 %collective-permute-done.1 = bf16[64,640]{1,0:T(8,128)(2,1)S(1)} collective-permute-done((bf16[64,640]{1,0:T(8,128)(2,1)S(1)}, bf16[64,640]{1,0:T(8,128)(2,1)S(1)}, u32[]{:S(2)}, u32[]{:S(2)}) %collective-permute-start.1) | collective-permute-done | bytes 81952 | tf_op jit(solution)/shard_map/ppermute | solution.py:173
  13.3 0.1 pad_maximum_fusion.refs_0_
  13.4 0.0 collective-permute-done.3.refs_6_
  13.4 1.6 %collective-permute-start.6 = (bf16[4,64,640]{2,1,0:T(8,128)(2,1)S(1)}, bf16[4,64,640]{2,1,0:T(8,128)(2,1)S(1)}, u32[]{:S(2)}, u32[]{:S(2)}) collective-permute-start(bf16[4,64,640]{2,1,0:T(8,128)(2,1)S(1)} %pad_maximum_fusion.refs_0_), channel_id=1, source_target_pairs={{0,16},{8,24},{16,0},{24,8},{1,17},{9,25},{17,1},{25,9},{2,18},{10... | collective-permute-start | bytes 983048 | tf_op jit(solution)/shard_map/ppermute | solution.py:176
  15.0 1.5 %collective-permute-start.4 = (bf16[4,64,640]{2,1,0:T(8,128)(2,1)S(1)}, bf16[4,64,640]{2,1,0:T(8,128)(2,1)S(1)}, u32[]{:S(2)}, u32[]{:S(2)}) collective-permute-start(bf16[4,64,640]{2,1,0:T(8,128)(2,1)S(1)} %pad_maximum_fusion.refs_0_), channel_id=1, source_target_pairs={{0,8},{8,0},{16,24},{24,16},{1,9},{9,1},{17,25},{25,17},{2,10},{10... | collective-permute-start | bytes 983048 | tf_op jit(solution)/shard_map/ppermute | solution.py:176
  16.5 5.9 %collective-permute-done.6.refs_2_.refs_4_ = bf16[4,64,640]{2,1,0:T(8,128)(2,1)S(1)} collective-permute-done((bf16[4,64,640]{2,1,0:T(8,128)(2,1)S(1)}, bf16[4,64,640]{2,1,0:T(8,128)(2,1)S(1)}, u32[]{:S(2)}, u32[]{:S(2)}) %collective-permute-start.6) | collective-permute-done | bytes 327712 | tf_op jit(solution)/shard_map/ppermute | solution.py:176
  22.4 1.4 %collective-permute-done.4.refs_0_.refs_2_ = bf16[4,64,640]{2,1,0:T(8,128)(2,1)S(1)} collective-permute-done((bf16[4,64,640]{2,1,0:T(8,128)(2,1)S(1)}, bf16[4,64,640]{2,1,0:T(8,128)(2,1)S(1)}, u32[]{:S(2)}, u32[]{:S(2)}) %collective-permute-start.4) | collective-permute-done | bytes 327712 | tf_op jit(solution)/shard_map/ppermute | solution.py:176
  23.8 0.5 %collective-permute-start.8 = (bf16[4,64,640]{2,1,0:T(8,128)(2,1)S(1)}, bf16[4,64,640]{2,1,0:T(8,128)(2,1)S(1)}, u32[]{:S(2)}, u32[]{:S(2)}) collective-permute-start(bf16[4,64,640]{2,1,0:T(8,128)(2,1)S(1)} %pad_maximum_fusion.refs_0_), channel_id=1, source_target_pairs={{0,1},{1,0},{2,3},{3,2},{4,5},{5,4},{6,7},{7,6},{8,9},{9,8},{10,11... | collective-permute-start | bytes 983048 | tf_op jit(solution)/shard_map/ppermute | solution.py:173
  24.3 1.9 %collective-permute-start.11 = (bf16[64,640]{1,0:T(8,128)(2,1)S(1)}, bf16[64,640]{1,0:T(8,128)(2,1)S(1)}, u32[]{:S(2)}, u32[]{:S(2)}) collective-permute-start(bf16[64,640]{1,0:T(8,128)(2,1)S(1)} %collective-permute-done.3.refs_6_), channel_id=1, source_target_pairs={{0,6},{1,7},{2,4},{3,5},{4,2},{5,3},{6,0},{7,1},{8,14},{9,15},{10,... | collective-permute-start | bytes 245768 | tf_op jit(solution)/shard_map/ppermute | solution.py:173
  26.1 0.0 collective-permute-start.10
  26.2 5.2 %collective-permute-done.11.refs_9_ = bf16[64,640]{1,0:T(8,128)(2,1)S(1)} collective-permute-done((bf16[64,640]{1,0:T(8,128)(2,1)S(1)}, bf16[64,640]{1,0:T(8,128)(2,1)S(1)}, u32[]{:S(2)}, u32[]{:S(2)}) %collective-permute-start.11) | collective-permute-done | bytes 81952 | tf_op jit(solution)/shard_map/ppermute | solution.py:173
  31.4 2.6 %collective-permute-done.10.refs_8_ = bf16[64,640]{1,0:T(8,128)(2,1)S(1)} collective-permute-done((bf16[64,640]{1,0:T(8,128)(2,1)S(1)}, bf16[64,640]{1,0:T(8,128)(2,1)S(1)}, u32[]{:S(2)}, u32[]{:S(2)}) %collective-permute-start.10) | collective-permute-done | bytes 81952 | tf_op jit(solution)/shard_map/ppermute | solution.py:173
  34.0 1.8 %collective-permute-done.9.refs_7_ = bf16[64,640]{1,0:T(8,128)(2,1)S(1)} collective-permute-done((bf16[64,640]{1,0:T(8,128)(2,1)S(1)}, bf16[64,640]{1,0:T(8,128)(2,1)S(1)}, u32[]{:S(2)}, u32[]{:S(2)}) %collective-permute-start.9) | collective-permute-done | bytes 81952 | tf_op jit(solution)/shard_map/ppermute | solution.py:173
  35.8 0.5 %collective-permute-start.14 = (bf16[64,640]{1,0:T(8,128)(2,1)S(1)}, bf16[64,640]{1,0:T(8,128)(2,1)S(1)}, u32[]{:S(2)}, u32[]{:S(2)}) collective-permute-start(bf16[64,640]{1,0:T(8,128)(2,1)S(1)} %collective-permute-done.10.refs_8_), channel_id=1, source_target_pairs={{0,1},{1,0},{2,3},{3,2},{4,5},{5,4},{6,7},{7,6},{8,9},{9,8},{10,11... | collective-permute-start | bytes 245768 | tf_op jit(solution)/shard_map/ppermute | solution.py:173
  36.4 0.1 collective-permute-start.13
  36.5 0.7 %collective-permute-done.15.refs_13_ = bf16[64,640]{1,0:T(8,128)(2,1)S(1)} collective-permute-done((bf16[64,640]{1,0:T(8,128)(2,1)S(1)}, bf16[64,640]{1,0:T(8,128)(2,1)S(1)}, u32[]{:S(2)}, u32[]{:S(2)}) %collective-permute-start.15) | collective-permute-done | bytes 81952 | tf_op jit(solution)/shard_map/ppermute | solution.py:173
  37.1 0.2 collective-permute-done.14.refs_12_
  37.3 0.4 collective-permute-done.13.refs_11_
  37.6 1.0 %second_products.1 = bf16[64,768]{1,0:T(8,128)(2,1)} custom-call(bf16[128,512]{1,0:T(8,128)(2,1)S(1)} %first_products.1.first_ref, bf16[4,64,640]{2,1,0:T(8,128)(2,1)S(1)} %pad_maximum_fusion.refs_0_, bf16[4,64,640]{2,1,0:T(8,128)(2,1)S(1)} %collective-permute-done.8.refs_1_, bf16[4,64,640]{2,1,0:T(8,128)(2,1)S(1)} %collective-permute-done.4.refs_0_.refs_2_, ...), custom_call_target="tpu_custom_call" | custom-call | tf_op jit(solution)/shard_map/second_products/pallas_call | solution.py:158
  (12 shorter events, 0.0 us)
Async XLA Ops:
  1.3 8.3 %collective-permute-start.2 = (bf16[64,640]{1,0:T(8,128)(2,1)S(1)}, bf16[64,640]{1,0:T(8,128)(2,1)S(1)}, u32[]{:S(2)}, u32[]{:S(2)}) collective-permute-start(bf16[64,640]{1,0:T(8,128)(2,1)S(1)} %get-tuple-element.10), channel_id=1, source_target_pairs={{0,6},{1,7},{2,4},{3,5},{4,2},{5,3},{6,0},{7,1},{8,14},{9,15},{10,... | collective-permute-start | bytes 245768 | tf_op jit(solution)/shard_map/ppermute | solution.py:173
  6.5 6.9 %collective-permute-start.1 = (bf16[64,640]{1,0:T(8,128)(2,1)S(1)}, bf16[64,640]{1,0:T(8,128)(2,1)S(1)}, u32[]{:S(2)}, u32[]{:S(2)}) collective-permute-start(bf16[64,640]{1,0:T(8,128)(2,1)S(1)} %get-tuple-element.10), channel_id=1, source_target_pairs={{0,4},{1,5},{2,6},{3,7},{4,0},{5,1},{6,2},{7,3},{8,12},{9,13},{10,... | collective-permute-start | bytes 245768 | tf_op jit(solution)/shard_map/ppermute | solution.py:173
  6.5 6.9 %collective-permute-start = (bf16[64,640]{1,0:T(8,128)(2,1)S(1)}, bf16[64,640]{1,0:T(8,128)(2,1)S(1)}, u32[]{:S(2)}, u32[]{:S(2)}) collective-permute-start(bf16[64,640]{1,0:T(8,128)(2,1)S(1)} %get-tuple-element.10), channel_id=1, source_target_pairs={{0,2},{1,3},{2,0},{3,1},{4,6},{5,7},{6,4},{7,5},{8,10},{9,11},{10,... | collective-permute-start | bytes 245768 | tf_op jit(solution)/shard_map/ppermute | solution.py:173
  7.1 6.3 %collective-permute-start.3 = (bf16[64,640]{1,0:T(8,128)(2,1)S(1)}, bf16[64,640]{1,0:T(8,128)(2,1)S(1)}, u32[]{:S(2)}, u32[]{:S(2)}) collective-permute-start(bf16[64,640]{1,0:T(8,128)(2,1)S(1)} %get-tuple-element.10), channel_id=1, source_target_pairs={{0,24},{8,16},{16,8},{24,0},{1,25},{9,17},{17,9},{25,1},{2,26},{10... | collective-permute-start | bytes 245768 | tf_op jit(solution)/shard_map/ppermute | solution.py:176
  13.4 9.0 %collective-permute-start.6 = (bf16[4,64,640]{2,1,0:T(8,128)(2,1)S(1)}, bf16[4,64,640]{2,1,0:T(8,128)(2,1)S(1)}, u32[]{:S(2)}, u32[]{:S(2)}) collective-permute-start(bf16[4,64,640]{2,1,0:T(8,128)(2,1)S(1)} %pad_maximum_fusion.refs_0_), channel_id=1, source_target_pairs={{0,16},{8,24},{16,0},{24,8},{1,17},{9,25},{17,1},{25,9},{2,18},{10... | collective-permute-start | bytes 983048 | tf_op jit(solution)/shard_map/ppermute | solution.py:176
  15.0 8.8 %collective-permute-start.4 = (bf16[4,64,640]{2,1,0:T(8,128)(2,1)S(1)}, bf16[4,64,640]{2,1,0:T(8,128)(2,1)S(1)}, u32[]{:S(2)}, u32[]{:S(2)}) collective-permute-start(bf16[4,64,640]{2,1,0:T(8,128)(2,1)S(1)} %pad_maximum_fusion.refs_0_), channel_id=1, source_target_pairs={{0,8},{8,0},{16,24},{24,16},{1,9},{9,1},{17,25},{25,17},{2,10},{10... | collective-permute-start | bytes 983048 | tf_op jit(solution)/shard_map/ppermute | solution.py:176
  22.4 13.5 %collective-permute-start.7 = (bf16[4,64,640]{2,1,0:T(8,128)(2,1)S(1)}, bf16[4,64,640]{2,1,0:T(8,128)(2,1)S(1)}, u32[]{:S(2)}, u32[]{:S(2)}) collective-permute-start(bf16[4,64,640]{2,1,0:T(8,128)(2,1)S(1)} %collective-permute-done.6.refs_2_.refs_4_), channel_id=1, source_target_pairs={{0,1},{1,0},{2,3},{3,2},{4,5},{5,4},{6,7},{7,6},{8,9},{9,8},{10,11... | collective-permute-start | bytes 983048 | tf_op jit(solution)/shard_map/ppermute | solution.py:173
  23.8 12.6 %collective-permute-start.5 = (bf16[4,64,640]{2,1,0:T(8,128)(2,1)S(1)}, bf16[4,64,640]{2,1,0:T(8,128)(2,1)S(1)}, u32[]{:S(2)}, u32[]{:S(2)}) collective-permute-start(bf16[4,64,640]{2,1,0:T(8,128)(2,1)S(1)} %collective-permute-done.4.refs_0_.refs_2_), channel_id=1, source_target_pairs={{0,1},{1,0},{2,3},{3,2},{4,5},{5,4},{6,7},{7,6},{8,9},{9,8},{10,11... | collective-permute-start | bytes 983048 | tf_op jit(solution)/shard_map/ppermute | solution.py:173
  23.8 13.9 %collective-permute-start.8 = (bf16[4,64,640]{2,1,0:T(8,128)(2,1)S(1)}, bf16[4,64,640]{2,1,0:T(8,128)(2,1)S(1)}, u32[]{:S(2)}, u32[]{:S(2)}) collective-permute-start(bf16[4,64,640]{2,1,0:T(8,128)(2,1)S(1)} %pad_maximum_fusion.refs_0_), channel_id=1, source_target_pairs={{0,1},{1,0},{2,3},{3,2},{4,5},{5,4},{6,7},{7,6},{8,9},{9,8},{10,11... | collective-permute-start | bytes 983048 | tf_op jit(solution)/shard_map/ppermute | solution.py:173
  24.3 7.1 %collective-permute-start.11 = (bf16[64,640]{1,0:T(8,128)(2,1)S(1)}, bf16[64,640]{1,0:T(8,128)(2,1)S(1)}, u32[]{:S(2)}, u32[]{:S(2)}) collective-permute-start(bf16[64,640]{1,0:T(8,128)(2,1)S(1)} %collective-permute-done.3.refs_6_), channel_id=1, source_target_pairs={{0,6},{1,7},{2,4},{3,5},{4,2},{5,3},{6,0},{7,1},{8,14},{9,15},{10,... | collective-permute-start | bytes 245768 | tf_op jit(solution)/shard_map/ppermute | solution.py:173
  26.1 7.9 %collective-permute-start.10 = (bf16[64,640]{1,0:T(8,128)(2,1)S(1)}, bf16[64,640]{1,0:T(8,128)(2,1)S(1)}, u32[]{:S(2)}, u32[]{:S(2)}) collective-permute-start(bf16[64,640]{1,0:T(8,128)(2,1)S(1)} %collective-permute-done.3.refs_6_), channel_id=1, source_target_pairs={{0,4},{1,5},{2,6},{3,7},{4,0},{5,1},{6,2},{7,3},{8,12},{9,13},{10,... | collective-permute-start | bytes 245768 | tf_op jit(solution)/shard_map/ppermute | solution.py:173
  31.4 4.4 %collective-permute-start.9 = (bf16[64,640]{1,0:T(8,128)(2,1)S(1)}, bf16[64,640]{1,0:T(8,128)(2,1)S(1)}, u32[]{:S(2)}, u32[]{:S(2)}) collective-permute-start(bf16[64,640]{1,0:T(8,128)(2,1)S(1)} %collective-permute-done.3.refs_6_), channel_id=1, source_target_pairs={{0,2},{1,3},{2,0},{3,1},{4,6},{5,7},{6,4},{7,5},{8,10},{9,11},{10,... | collective-permute-start | bytes 245768 | tf_op jit(solution)/shard_map/ppermute | solution.py:173
  34.0 2.4 %collective-permute-start.12 = (bf16[64,640]{1,0:T(8,128)(2,1)S(1)}, bf16[64,640]{1,0:T(8,128)(2,1)S(1)}, u32[]{:S(2)}, u32[]{:S(2)}) collective-permute-start(bf16[64,640]{1,0:T(8,128)(2,1)S(1)} %collective-permute-done.3.refs_6_), channel_id=1, source_target_pairs={{0,1},{1,0},{2,3},{3,2},{4,5},{5,4},{6,7},{7,6},{8,9},{9,8},{10,11... | collective-permute-start | bytes 245768 | tf_op jit(solution)/shard_map/ppermute | solution.py:173
  35.8 1.3 %collective-permute-start.15 = (bf16[64,640]{1,0:T(8,128)(2,1)S(1)}, bf16[64,640]{1,0:T(8,128)(2,1)S(1)}, u32[]{:S(2)}, u32[]{:S(2)}) collective-permute-start(bf16[64,640]{1,0:T(8,128)(2,1)S(1)} %collective-permute-done.11.refs_9_), channel_id=1, source_target_pairs={{0,1},{1,0},{2,3},{3,2},{4,5},{5,4},{6,7},{7,6},{8,9},{9,8},{10,11... | collective-permute-start | bytes 245768 | tf_op jit(solution)/shard_map/ppermute | solution.py:173
  35.8 1.4 %collective-permute-start.14 = (bf16[64,640]{1,0:T(8,128)(2,1)S(1)}, bf16[64,640]{1,0:T(8,128)(2,1)S(1)}, u32[]{:S(2)}, u32[]{:S(2)}) collective-permute-start(bf16[64,640]{1,0:T(8,128)(2,1)S(1)} %collective-permute-done.10.refs_8_), channel_id=1, source_target_pairs={{0,1},{1,0},{2,3},{3,2},{4,5},{5,4},{6,7},{7,6},{8,9},{9,8},{10,11... | collective-permute-start | bytes 245768 | tf_op jit(solution)/shard_map/ppermute | solution.py:173
  36.4 1.3 %collective-permute-start.13 = (bf16[64,640]{1,0:T(8,128)(2,1)S(1)}, bf16[64,640]{1,0:T(8,128)(2,1)S(1)}, u32[]{:S(2)}, u32[]{:S(2)}) collective-permute-start(bf16[64,640]{1,0:T(8,128)(2,1)S(1)} %collective-permute-done.9.refs_7_), channel_id=1, source_target_pairs={{0,1},{1,0},{2,3},{3,2},{4,5},{5,4},{6,7},{7,6},{8,9},{9,8},{10,11... | collective-permute-start | bytes 245768 | tf_op jit(solution)/shard_map/ppermute | solution.py:173

commit v17 on v15

--- a/solution.py
+++ b/solution.py
@@ -34,27 +34,26 @@
         rows_ref[:, b * tile_size : (b + 1) * tile_size] = (summed * scale).astype(jnp.bfloat16)
     for sent_ref in sent_refs:
         sections, section = lax.axis_size("section"), lax.axis_index("section")
-        bulk, share = sent_ref.shape[1], sent_ref.shape[1] - nodes
-        shares = (features_ref.shape[1] - bulk) // share
-
-        @pl.when(section == sections - 1)
-        def _():
-            sent_ref[...] = features_ref[:, :bulk]
-
-        @pl.when(section < sections - 1)
-        def _():
-            first = pl.multiple_of(bulk + jnp.minimum(section, shares - 1) * share, 128)
-            sent_ref[:, :nodes] = rows_ref[...]
-            sent_ref[:, nodes:] = features_ref[:, pl.ds(first, share)]
-
-
-def dense_rows(tile_cols, live_tiles, tile_rows, degrees, features, sent_width):
+        part = sent_ref.shape[0] - blocks * row_count
+        for at in range(sections):
+
+            @pl.when(section == at)
+            def _(at=at):
+                source = features_ref if at == sections - 1 else rows_ref
+                for b in range(blocks):
+                    rows = slice(b * row_count, (b + 1) * row_count)
+                    sent_ref[rows] = source[:, b * tile_size : (b + 1) * tile_size]
+                column, row = nodes + at * part // row_count * tile_size, at * part % row_count
+                sent_ref[blocks * row_count :] = features_ref[row : row + part, column : column + tile_size]
+
+
+def dense_rows(tile_cols, live_tiles, tile_rows, degrees, features, sent_rows):
     row_count = tile_rows.shape[0]
     nodes = row_count * lax.axis_size("shard")
-    widths = [nodes, sent_width] if sent_width else [nodes]
+    shapes = [(row_count, nodes)] + ([(sent_rows, tile_rows.shape[2])] if sent_rows else [])
     return pl.pallas_call(
         dense_rows_kernel,
-        out_shape=[pltpu.VMEM((row_count, columns), jnp.bfloat16) for columns in widths],
+        out_shape=[pltpu.VMEM(shape, jnp.bfloat16) for shape in shapes],
         in_specs=[
             pl.BlockSpec(memory_space=pltpu.SMEM),
             pl.BlockSpec(memory_space=pltpu.SMEM),
@@ -62,7 +61,7 @@
             pl.BlockSpec(memory_space=pltpu.VMEM),
             pl.BlockSpec(memory_space=pltpu.VMEM),
         ],
-        out_specs=[pl.BlockSpec(memory_space=pltpu.VMEM)] * len(widths),
+        out_specs=[pl.BlockSpec(memory_space=pltpu.VMEM)] * len(shapes),
         name="dense_rows",
     )(tile_cols, live_tiles, tile_rows, degrees, features)
 
@@ -73,26 +72,37 @@
     return masks[:count], masks[count:]
 
 
-def times(halves, pair_refs, mask, columns):
+def gathered_rows(pair_refs, mask, first, count):
+    first_core = lax.rem(lax.axis_index("shard"), 2) == 0
+    here_ref, there_ref = pair_refs[mask]
+    found = []
+    for piece in range(here_ref.shape[0]):
+        here, there = here_ref[piece, first : first + count], there_ref[piece, first : first + count]
+        found += [jnp.where(first_core, here, there), jnp.where(first_core, there, here)]
+    return found
+
+
+def times(halves, matrix):
     row_count = halves.shape[0] // 2
-    shard = lax.axis_index("shard")
-    chip, first_core = lax.div(shard, 2), lax.rem(shard, 2) == 0
-    here_ref, there_ref = pair_refs[mask]
-    left, right = [], []
-    for piece in range(here_ref.shape[0]):
+    chip, chips = lax.div(lax.axis_index("shard"), 2), len(matrix[0]) // 2
+    left = []
+    for piece in range(chips):
         source = lax.bitwise_xor(chip, piece)
         left.append(halves[:, pl.ds(pl.multiple_of(source * 2 * row_count, 128), 2 * row_count)])
-        here, there = here_ref[piece, :, columns], there_ref[piece, :, columns]
-        right += [jnp.where(first_core, here, there), jnp.where(first_core, there, here)]
-    left, right = jnp.concatenate(left, axis=1), jnp.concatenate(right, axis=0)
+    left = jnp.concatenate(left, axis=1)
+    right = jnp.concatenate([jnp.concatenate(tile, axis=0) for tile in matrix], axis=1)
     both = jnp.dot(left, right, preferred_element_type=jnp.float32)
     return both[:row_count] + both[row_count:]
 
 
+def stacked_tiles(pair_refs, mask, row_count, tiles):
+    return [gathered_rows(pair_refs, mask, tile * row_count, row_count) for tile in range(tiles)]
+
+
 def multiply_through(halves, pair_refs, masks):
-    row_count, nodes = halves.shape[0] // 2, halves.shape[1]
+    row_count, tiles = halves.shape[0] // 2, halves.shape[1] // 128
     for mask in masks:
-        product = times(halves, pair_refs, mask, slice(0, nodes))
+        product = times(halves, stacked_tiles(pair_refs, mask, row_count, tiles))
         high = product.astype(jnp.bfloat16)
         halves[:row_count] = high
         halves[row_count:] = (product - high.astype(jnp.float32)).astype(jnp.bfloat16)
@@ -111,20 +121,25 @@
 
 def second_kernel(sections, first_ref, *refs):
     pair_refs, out_ref, halves = list(zip(refs[:-2:2], refs[1:-2:2])), refs[-2], refs[-1]
-    nodes, bulk = halves.shape[1], pair_refs[0][0].shape[2]
-    share = bulk - nodes
+    row_count, nodes = halves.shape[0] // 2, halves.shape[1]
+    tiles = nodes // 128
+    stacked = tiles * row_count
+    part = pair_refs[0][0].shape[1] - stacked
     halves[...] = first_ref[...]
     for at in range(sections):
 
         @pl.when(lax.axis_index("section") == at)
         def _(at=at):
             multiply_through(halves, pair_refs, split_chain(at)[1])
-            product = times(halves, pair_refs, at ^ (sections - 1), slice(0, bulk))
-            out_ref[:, :bulk] = product.astype(jnp.bfloat16)
-            for giver in range((out_ref.shape[1] - bulk) // share):
-                product = times(halves, pair_refs, at ^ giver, slice(nodes, bulk))
-                first = bulk + giver * share
-                out_ref[:, first : first + share] = product.astype(jnp.bfloat16)
+            bulk = stacked_tiles(pair_refs, at ^ (sections - 1), row_count, tiles)
+            out_ref[:, :nodes] = times(halves, bulk).astype(jnp.bfloat16)
+            parts = [gathered_rows(pair_refs, at ^ giver, stacked, part) for giver in range(sections)]
+            each = row_count // part
+            rest = [
+                [jnp.concatenate(rows, axis=0) for rows in zip(*parts[tile : tile + each])]
+                for tile in range(0, sections, each)
+            ]
+            out_ref[:, nodes:] = times(halves, rest).astype(jnp.bfloat16)
 
 
 def first_products(own, pairs, nodes, sections):
@@ -193,11 +208,14 @@
     row_count, width = features.shape
     sections, shards = lax.axis_size("section"), lax.axis_size("shard")
     nodes = row_count * shards
-    sent_width = pl.cdiv((sections - 1) * nodes + width, sections * 128) * 128
+    tile_size = tile_values.shape[3]
+    part = max(width - nodes, 0) // tile_size * row_count // sections
+    sent_rows = nodes // tile_size * row_count + part
     even = shards >= 2 and shards & (shards - 1) == 0 and sections > 1 and sections & (sections - 1) == 0
-    parts = nodes < sent_width < width and (width - sent_width) % (sent_width - nodes) == 0
-    if even and parts:
-        own, sent = dense_rows(tile_cols, live_tiles, tile_values[0], degrees, features, sent_width)
+    parts = part >= 16 and part % 16 == 0 and row_count % part == 0 and tile_size == 128
+    whole = part * sections * tile_size == (width - nodes) * row_count
+    if even and parts and whole:
+        own, sent = dense_rows(tile_cols, live_tiles, tile_values[0], degrees, features, sent_rows)
         return by_products(own, sent, width)[None]
     (own,) = dense_rows(tile_cols, live_tiles, tile_values[0], degrees, features, 0)
     return by_hops(features, own)[None]

time: 28.8 us -> 27.6 us (0.958)
  waiting for transfers between devices: 9.66 us -> 8.54 us
    ppermute x10, waiting for transfers between devices: 9.65 us -> 8.54 us  [along_shard(): return lax.ppermute(value, 'shard', [(i, i ^ mask) for i in range(shards)])]
where the time goes in v17:
time: 27.6 us; the launch traced here: 27.5 us
  starting transfers between devices  16.5 us (60%)
  waiting for transfers between devices  8.54 us (31%)
  Pallas kernels  2.32 us (8%)
    ppermute x10, starting transfers between devices, along_shard(): return lax.ppermute(value, 'shard', [(i, i ^ mask) for i in range(shards)])  10.8 us
    ppermute x10, waiting for transfers between devices, along_shard(): return lax.ppermute(value, 'shard', [(i, i ^ mask) for i in range(shards)])  8.54 us
    ppermute x3, starting transfers between devices, along_section(): lax.ppermute(value, 'section', [(i, i ^ mask) for i in range(sections)])  5.68 us
    pallas_call x1, Pallas kernels, dense_rows(): pl.pallas_call(dense_rows_kernel, out_shape=[pltpu.VMEM(shape, jnp.bfloat...  1.34 us
    pallas_call x1, Pallas kernels, second_products(): pl.pallas_call(functools.partial(second_kernel, sections), out_shape=jax....  0.96 us
  transfers between devices with their start and end apart: 13, of which 4 were waited for; matrix products, arithmetic and copies ran while one was open for 0% of the time, Pallas kernels for 0%

profile of v17, /device:TPU:0, one launch (start us, length us, event | category | flops | bytes accessed | tf_op | source)
XLA Modules:
  0.0 27.5 jit_solution(3626195125890551398)
XLA Ops:
  0.0 1.3 %dense_rows.1 = (bf16[64,512]{1,0:T(8,128)(2,1)S(1)}, bf16[288,128]{1,0:T(8,128)(2,1)S(1)}) custom-call(s32[1,4,16]{2,1,0:T(4,128)} %cols_ref.1, s32[1,4]{1,0:T(1,128)} %live_ref.1, bf16[64,16,128]{2,1,0:T(8,128)(2,1)} %bitcast.11, s32[1,64]{1,0:T(1,128)} %degrees_ref.1, bf16[64,768]{1,0:T(8,128)(2,1)} %features_ref.1), custom_call_target="tpu_custom_call" | custom-call | tf_op jit(solution)/shard_map/dense_rows/pallas_call | solution.py:54
  1.3 5.1 %collective-permute-start.2 = (bf16[288,128]{1,0:T(8,128)(2,1)S(1)}, bf16[288,128]{1,0:T(8,128)(2,1)S(1)}, u32[]{:S(2)}, u32[]{:S(2)}) collective-permute-start(bf16[288,128]{1,0:T(8,128)(2,1)S(1)} %get-tuple-element.10), channel_id=1, source_target_pairs={{0,6},{1,7},{2,4},{3,5},{4,2},{5,3},{6,0},{7,1},{8,14},{9,15},{10,... | collective-permute-start | bytes 221192 | tf_op jit(solution)/shard_map/ppermute | solution.py:175
  6.5 0.0 collective-permute-start.1
  6.5 0.6 %collective-permute-start = (bf16[288,128]{1,0:T(8,128)(2,1)S(1)}, bf16[288,128]{1,0:T(8,128)(2,1)S(1)}, u32[]{:S(2)}, u32[]{:S(2)}) collective-permute-start(bf16[288,128]{1,0:T(8,128)(2,1)S(1)} %get-tuple-element.10), channel_id=1, source_target_pairs={{0,2},{1,3},{2,0},{3,1},{4,6},{5,7},{6,4},{7,5},{8,10},{9,11},{10,... | collective-permute-start | bytes 221192 | tf_op jit(solution)/shard_map/ppermute | solution.py:175
  7.1 2.6 %collective-permute-start.3 = (bf16[288,128]{1,0:T(8,128)(2,1)S(1)}, bf16[288,128]{1,0:T(8,128)(2,1)S(1)}, u32[]{:S(2)}, u32[]{:S(2)}) collective-permute-start(bf16[288,128]{1,0:T(8,128)(2,1)S(1)} %get-tuple-element.10), channel_id=1, source_target_pairs={{0,24},{8,16},{16,8},{24,0},{1,25},{9,17},{17,9},{25,1},{2,26},{10... | collective-permute-start | bytes 221192 | tf_op jit(solution)/shard_map/ppermute | solution.py:178
  9.7 0.0 collective-permute-done.2
  9.7 3.0 %collective-permute-done.1 = bf16[288,128]{1,0:T(8,128)(2,1)S(1)} collective-permute-done((bf16[288,128]{1,0:T(8,128)(2,1)S(1)}, bf16[288,128]{1,0:T(8,128)(2,1)S(1)}, u32[]{:S(2)}, u32[]{:S(2)}) %collective-permute-start.1) | collective-permute-done | bytes 73760 | tf_op jit(solution)/shard_map/ppermute | solution.py:175
  12.7 0.0 collective-permute-done
  12.7 0.0 collective-permute-done.3
  12.7 1.6 %collective-permute-start.6 = (bf16[4,288,128]{2,1,0:T(8,128)(2,1)S(1)}, bf16[4,288,128]{2,1,0:T(8,128)(2,1)S(1)}, u32[]{:S(2)}, u32[]{:S(2)}) collective-permute-start(bf16[4,288,128]{2,1,0:T(8,128)(2,1)S(1)} %pad_maximum_fusion.refs_0_), channel_id=1, source_target_pairs={{0,16},{8,24},{16,0},{24,8},{1,17},{9,25},{17,1},{25,9},{2,18},{10... | collective-permute-start | bytes 884744 | tf_op jit(solution)/shard_map/ppermute | solution.py:178
  14.3 1.5 %collective-permute-start.4 = (bf16[4,288,128]{2,1,0:T(8,128)(2,1)S(1)}, bf16[4,288,128]{2,1,0:T(8,128)(2,1)S(1)}, u32[]{:S(2)}, u32[]{:S(2)}) collective-permute-start(bf16[4,288,128]{2,1,0:T(8,128)(2,1)S(1)} %pad_maximum_fusion.refs_0_), channel_id=1, source_target_pairs={{0,8},{8,0},{16,24},{24,16},{1,9},{9,1},{17,25},{25,17},{2,10},{10... | collective-permute-start | bytes 884744 | tf_op jit(solution)/shard_map/ppermute | solution.py:178
  15.8 3.3 %collective-permute-start.11 = (bf16[288,128]{1,0:T(8,128)(2,1)S(1)}, bf16[288,128]{1,0:T(8,128)(2,1)S(1)}, u32[]{:S(2)}, u32[]{:S(2)}) collective-permute-start(bf16[288,128]{1,0:T(8,128)(2,1)S(1)} %collective-permute-done.3), channel_id=1, source_target_pairs={{0,6},{1,7},{2,4},{3,5},{4,2},{5,3},{6,0},{7,1},{8,14},{9,15},{10,... | collective-permute-start | bytes 221192 | tf_op jit(solution)/shard_map/ppermute | solution.py:175
  19.1 0.0 collective-permute-start.10
  19.1 1.1 %collective-permute-start.9 = (bf16[288,128]{1,0:T(8,128)(2,1)S(1)}, bf16[288,128]{1,0:T(8,128)(2,1)S(1)}, u32[]{:S(2)}, u32[]{:S(2)}) collective-permute-start(bf16[288,128]{1,0:T(8,128)(2,1)S(1)} %collective-permute-done.3), channel_id=1, source_target_pairs={{0,2},{1,3},{2,0},{3,1},{4,6},{5,7},{6,4},{7,5},{8,10},{9,11},{10,... | collective-permute-start | bytes 221192 | tf_op jit(solution)/shard_map/ppermute | solution.py:175
  20.2 2.3 %collective-permute-done.11 = bf16[288,128]{1,0:T(8,128)(2,1)S(1)} collective-permute-done((bf16[288,128]{1,0:T(8,128)(2,1)S(1)}, bf16[288,128]{1,0:T(8,128)(2,1)S(1)}, u32[]{:S(2)}, u32[]{:S(2)}) %collective-permute-start.11) | collective-permute-done | bytes 73760 | tf_op jit(solution)/shard_map/ppermute | solution.py:175
  22.5 0.0 collective-permute-start.8
  22.5 0.5 %collective-permute-start.7 = (bf16[4,288,128]{2,1,0:T(8,128)(2,1)S(1)}, bf16[4,288,128]{2,1,0:T(8,128)(2,1)S(1)}, u32[]{:S(2)}, u32[]{:S(2)}) collective-permute-start(bf16[4,288,128]{2,1,0:T(8,128)(2,1)S(1)} %collective-permute-done.6.refs_2_.refs_4_), channel_id=1, source_target_pairs={{0,1},{1,0},{2,3},{3,2},{4,5},{5,4},{6,7},{7,6},{8,9},{9,8},{10,11... | collective-permute-start | bytes 884744 | tf_op jit(solution)/shard_map/ppermute | solution.py:175
  23.0 0.1 collective-permute-start.5
  23.1 1.8 %collective-permute-done.10 = bf16[288,128]{1,0:T(8,128)(2,1)S(1)} collective-permute-done((bf16[288,128]{1,0:T(8,128)(2,1)S(1)}, bf16[288,128]{1,0:T(8,128)(2,1)S(1)}, u32[]{:S(2)}, u32[]{:S(2)}) %collective-permute-start.10) | collective-permute-done | bytes 73760 | tf_op jit(solution)/shard_map/ppermute | solution.py:175
  24.8 0.0 collective-permute-done.9
  24.9 0.1 collective-permute-start.12
  25.0 0.0 collective-permute-done.7.refs_3_.refs_5_
  25.0 1.5 %collective-permute-done.12.refs_7_ = bf16[4,288,128]{2,1,0:T(8,128)(2,1)S(1)} collective-permute-done((bf16[4,288,128]{2,1,0:T(8,128)(2,1)S(1)}, bf16[4,288,128]{2,1,0:T(8,128)(2,1)S(1)}, u32[]{:S(2)}, u32[]{:S(2)}) %collective-permute-start.12) | collective-permute-done | bytes 294944 | tf_op jit(solution)/shard_map/ppermute | solution.py:175
  26.5 1.0 %second_products.1 = bf16[64,768]{1,0:T(8,128)(2,1)} custom-call(bf16[128,512]{1,0:T(8,128)(2,1)S(1)} %first_products.1.first_ref, bf16[4,288,128]{2,1,0:T(8,128)(2,1)S(1)} %pad_maximum_fusion.refs_0_, bf16[4,288,128]{2,1,0:T(8,128)(2,1)S(1)} %collective-permute-done.8.refs_1_, bf16[4,288,128]{2,1,0:T(8,128)(2,1)S(1)} %collective-permute-done.4.refs_0_.refs_2_, ...), custom_call_target="tpu_custom_call" | custom-call | tf_op jit(solution)/shard_map/second_products/pallas_call | solution.py:160
  (7 shorter events, 0.1 us)
Async XLA Ops:
  1.3 8.4 %collective-permute-start.2 = (bf16[288,128]{1,0:T(8,128)(2,1)S(1)}, bf16[288,128]{1,0:T(8,128)(2,1)S(1)}, u32[]{:S(2)}, u32[]{:S(2)}) collective-permute-start(bf16[288,128]{1,0:T(8,128)(2,1)S(1)} %get-tuple-element.10), channel_id=1, source_target_pairs={{0,6},{1,7},{2,4},{3,5},{4,2},{5,3},{6,0},{7,1},{8,14},{9,15},{10,... | collective-permute-start | bytes 221192 | tf_op jit(solution)/shard_map/ppermute | solution.py:175
  6.5 6.2 %collective-permute-start.1 = (bf16[288,128]{1,0:T(8,128)(2,1)S(1)}, bf16[288,128]{1,0:T(8,128)(2,1)S(1)}, u32[]{:S(2)}, u32[]{:S(2)}) collective-permute-start(bf16[288,128]{1,0:T(8,128)(2,1)S(1)} %get-tuple-element.10), channel_id=1, source_target_pairs={{0,4},{1,5},{2,6},{3,7},{4,0},{5,1},{6,2},{7,3},{8,12},{9,13},{10,... | collective-permute-start | bytes 221192 | tf_op jit(solution)/shard_map/ppermute | solution.py:175
  6.5 6.2 %collective-permute-start = (bf16[288,128]{1,0:T(8,128)(2,1)S(1)}, bf16[288,128]{1,0:T(8,128)(2,1)S(1)}, u32[]{:S(2)}, u32[]{:S(2)}) collective-permute-start(bf16[288,128]{1,0:T(8,128)(2,1)S(1)} %get-tuple-element.10), channel_id=1, source_target_pairs={{0,2},{1,3},{2,0},{3,1},{4,6},{5,7},{6,4},{7,5},{8,10},{9,11},{10,... | collective-permute-start | bytes 221192 | tf_op jit(solution)/shard_map/ppermute | solution.py:175
  7.1 5.6 %collective-permute-start.3 = (bf16[288,128]{1,0:T(8,128)(2,1)S(1)}, bf16[288,128]{1,0:T(8,128)(2,1)S(1)}, u32[]{:S(2)}, u32[]{:S(2)}) collective-permute-start(bf16[288,128]{1,0:T(8,128)(2,1)S(1)} %get-tuple-element.10), channel_id=1, source_target_pairs={{0,24},{8,16},{16,8},{24,0},{1,25},{9,17},{17,9},{25,1},{2,26},{10... | collective-permute-start | bytes 221192 | tf_op jit(solution)/shard_map/ppermute | solution.py:178
  12.7 9.8 %collective-permute-start.6 = (bf16[4,288,128]{2,1,0:T(8,128)(2,1)S(1)}, bf16[4,288,128]{2,1,0:T(8,128)(2,1)S(1)}, u32[]{:S(2)}, u32[]{:S(2)}) collective-permute-start(bf16[4,288,128]{2,1,0:T(8,128)(2,1)S(1)} %pad_maximum_fusion.refs_0_), channel_id=1, source_target_pairs={{0,16},{8,24},{16,0},{24,8},{1,17},{9,25},{17,1},{25,9},{2,18},{10... | collective-permute-start | bytes 884744 | tf_op jit(solution)/shard_map/ppermute | solution.py:178
  14.3 8.7 %collective-permute-start.4 = (bf16[4,288,128]{2,1,0:T(8,128)(2,1)S(1)}, bf16[4,288,128]{2,1,0:T(8,128)(2,1)S(1)}, u32[]{:S(2)}, u32[]{:S(2)}) collective-permute-start(bf16[4,288,128]{2,1,0:T(8,128)(2,1)S(1)} %pad_maximum_fusion.refs_0_), channel_id=1, source_target_pairs={{0,8},{8,0},{16,24},{24,16},{1,9},{9,1},{17,25},{25,17},{2,10},{10... | collective-permute-start | bytes 884744 | tf_op jit(solution)/shard_map/ppermute | solution.py:178
  15.8 6.7 %collective-permute-start.11 = (bf16[288,128]{1,0:T(8,128)(2,1)S(1)}, bf16[288,128]{1,0:T(8,128)(2,1)S(1)}, u32[]{:S(2)}, u32[]{:S(2)}) collective-permute-start(bf16[288,128]{1,0:T(8,128)(2,1)S(1)} %collective-permute-done.3), channel_id=1, source_target_pairs={{0,6},{1,7},{2,4},{3,5},{4,2},{5,3},{6,0},{7,1},{8,14},{9,15},{10,... | collective-permute-start | bytes 221192 | tf_op jit(solution)/shard_map/ppermute | solution.py:175
  19.1 5.7 %collective-permute-start.10 = (bf16[288,128]{1,0:T(8,128)(2,1)S(1)}, bf16[288,128]{1,0:T(8,128)(2,1)S(1)}, u32[]{:S(2)}, u32[]{:S(2)}) collective-permute-start(bf16[288,128]{1,0:T(8,128)(2,1)S(1)} %collective-permute-done.3), channel_id=1, source_target_pairs={{0,4},{1,5},{2,6},{3,7},{4,0},{5,1},{6,2},{7,3},{8,12},{9,13},{10,... | collective-permute-start | bytes 221192 | tf_op jit(solution)/shard_map/ppermute | solution.py:175
  19.1 5.7 %collective-permute-start.9 = (bf16[288,128]{1,0:T(8,128)(2,1)S(1)}, bf16[288,128]{1,0:T(8,128)(2,1)S(1)}, u32[]{:S(2)}, u32[]{:S(2)}) collective-permute-start(bf16[288,128]{1,0:T(8,128)(2,1)S(1)} %collective-permute-done.3), channel_id=1, source_target_pairs={{0,2},{1,3},{2,0},{3,1},{4,6},{5,7},{6,4},{7,5},{8,10},{9,11},{10,... | collective-permute-start | bytes 221192 | tf_op jit(solution)/shard_map/ppermute | solution.py:175
  22.5 2.5 %collective-permute-start.8 = (bf16[4,288,128]{2,1,0:T(8,128)(2,1)S(1)}, bf16[4,288,128]{2,1,0:T(8,128)(2,1)S(1)}, u32[]{:S(2)}, u32[]{:S(2)}) collective-permute-start(bf16[4,288,128]{2,1,0:T(8,128)(2,1)S(1)} %pad_maximum_fusion.refs_0_), channel_id=1, source_target_pairs={{0,1},{1,0},{2,3},{3,2},{4,5},{5,4},{6,7},{7,6},{8,9},{9,8},{10,11... | collective-permute-start | bytes 884744 | tf_op jit(solution)/shard_map/ppermute | solution.py:175
  22.5 2.5 %collective-permute-start.7 = (bf16[4,288,128]{2,1,0:T(8,128)(2,1)S(1)}, bf16[4,288,128]{2,1,0:T(8,128)(2,1)S(1)}, u32[]{:S(2)}, u32[]{:S(2)}) collective-permute-start(bf16[4,288,128]{2,1,0:T(8,128)(2,1)S(1)} %collective-permute-done.6.refs_2_.refs_4_), channel_id=1, source_target_pairs={{0,1},{1,0},{2,3},{3,2},{4,5},{5,4},{6,7},{7,6},{8,9},{9,8},{10,11... | collective-permute-start | bytes 884744 | tf_op jit(solution)/shard_map/ppermute | solution.py:175
  23.0 2.0 %collective-permute-start.5 = (bf16[4,288,128]{2,1,0:T(8,128)(2,1)S(1)}, bf16[4,288,128]{2,1,0:T(8,128)(2,1)S(1)}, u32[]{:S(2)}, u32[]{:S(2)}) collective-permute-start(bf16[4,288,128]{2,1,0:T(8,128)(2,1)S(1)} %collective-permute-done.4.refs_0_.refs_2_), channel_id=1, source_target_pairs={{0,1},{1,0},{2,3},{3,2},{4,5},{5,4},{6,7},{7,6},{8,9},{9,8},{10,11... | collective-permute-start | bytes 884744 | tf_op jit(solution)/shard_map/ppermute | solution.py:175
  24.9 1.6 %collective-permute-start.12 = (bf16[4,288,128]{2,1,0:T(8,128)(2,1)S(1)}, bf16[4,288,128]{2,1,0:T(8,128)(2,1)S(1)}, u32[]{:S(2)}, u32[]{:S(2)}) collective-permute-start(bf16[4,288,128]{2,1,0:T(8,128)(2,1)S(1)} %pad_maximum_fusion.1.refs_6_), channel_id=1, source_target_pairs={{0,1},{1,0},{2,3},{3,2},{4,5},{5,4},{6,7},{7,6},{8,9},{9,8},{10,11... | collective-permute-start | bytes 884744 | tf_op jit(solution)/shard_map/ppermute | solution.py:175

commit v18 on v17

--- a/solution.py
+++ b/solution.py
@@ -28,10 +28,13 @@
         jnp.int32, (row_count, row_count), 1
     )
     scale = lax.rsqrt(jnp.sum(jnp.where(diagonal, degree, 0.0), axis=1, keepdims=True))
-    for b in range(blocks):
-        pick = (column == b).astype(jnp.bfloat16)
+    for start in range(0, blocks, 4):
+        group = range(start, min(start + 4, blocks))
+        pick = jnp.concatenate([(column == b).astype(jnp.bfloat16) for b in group], axis=0)
         summed = jnp.dot(pick, tiles, preferred_element_type=jnp.float32)
-        rows_ref[:, b * tile_size : (b + 1) * tile_size] = (summed * scale).astype(jnp.bfloat16)
+        for at, b in enumerate(group):
+            block = summed[at * row_count : (at + 1) * row_count] * scale
+            rows_ref[:, b * tile_size : (b + 1) * tile_size] = block.astype(jnp.bfloat16)
     for sent_ref in sent_refs:
         sections, section = lax.axis_size("section"), lax.axis_index("section")
         part = sent_ref.shape[0] - blocks * row_count

time: 27.6 us -> 27.6 us (level)
  no operation moved by 1% of the time
where the time goes in v18:
time: 27.6 us; the launch traced here: 27.5 us
  starting transfers between devices  16.5 us (60%)
  waiting for transfers between devices  8.54 us (31%)
  Pallas kernels  2.3 us (8%)
    ppermute x10, starting transfers between devices, along_shard(): return lax.ppermute(value, 'shard', [(i, i ^ mask) for i in range(shards)])  10.8 us
    ppermute x10, waiting for transfers between devices, along_shard(): return lax.ppermute(value, 'shard', [(i, i ^ mask) for i in range(shards)])  8.54 us
    ppermute x3, starting transfers between devices, along_section(): lax.ppermute(value, 'section', [(i, i ^ mask) for i in range(sections)])  5.68 us
    pallas_call x1, Pallas kernels, dense_rows(): pl.pallas_call(dense_rows_kernel, out_shape=[pltpu.VMEM(shape, jnp.bfloat...  1.32 us
    pallas_call x1, Pallas kernels, second_products(): pl.pallas_call(functools.partial(second_kernel, sections), out_shape=jax....  0.95 us
  transfers between devices with their start and end apart: 13, of which 4 were waited for; matrix products, arithmetic and copies ran while one was open for 0% of the time, Pallas kernels for 0%

profile of v18, /device:TPU:0, one launch (start us, length us, event | category | flops | bytes accessed | tf_op | source)
XLA Modules:
  0.0 27.5 jit_solution(15454462538807971955)
XLA Ops:
  0.0 1.3 %dense_rows.1 = (bf16[64,512]{1,0:T(8,128)(2,1)S(1)}, bf16[288,128]{1,0:T(8,128)(2,1)S(1)}) custom-call(s32[1,4,16]{2,1,0:T(4,128)} %cols_ref.1, s32[1,4]{1,0:T(1,128)} %live_ref.1, bf16[64,16,128]{2,1,0:T(8,128)(2,1)} %bitcast.11, s32[1,64]{1,0:T(1,128)} %degrees_ref.1, bf16[64,768]{1,0:T(8,128)(2,1)} %features_ref.1), custom_call_target="tpu_custom_call" | custom-call | tf_op jit(solution)/shard_map/dense_rows/pallas_call | solution.py:57
  1.3 5.1 %collective-permute-start.2 = (bf16[288,128]{1,0:T(8,128)(2,1)S(1)}, bf16[288,128]{1,0:T(8,128)(2,1)S(1)}, u32[]{:S(2)}, u32[]{:S(2)}) collective-permute-start(bf16[288,128]{1,0:T(8,128)(2,1)S(1)} %get-tuple-element.10), channel_id=1, source_target_pairs={{0,6},{1,7},{2,4},{3,5},{4,2},{5,3},{6,0},{7,1},{8,14},{9,15},{10,... | collective-permute-start | bytes 221192 | tf_op jit(solution)/shard_map/ppermute | solution.py:178
  6.4 0.0 collective-permute-start.1
  6.4 0.6 %collective-permute-start = (bf16[288,128]{1,0:T(8,128)(2,1)S(1)}, bf16[288,128]{1,0:T(8,128)(2,1)S(1)}, u32[]{:S(2)}, u32[]{:S(2)}) collective-permute-start(bf16[288,128]{1,0:T(8,128)(2,1)S(1)} %get-tuple-element.10), channel_id=1, source_target_pairs={{0,2},{1,3},{2,0},{3,1},{4,6},{5,7},{6,4},{7,5},{8,10},{9,11},{10,... | collective-permute-start | bytes 221192 | tf_op jit(solution)/shard_map/ppermute | solution.py:178
  7.1 2.6 %collective-permute-start.3 = (bf16[288,128]{1,0:T(8,128)(2,1)S(1)}, bf16[288,128]{1,0:T(8,128)(2,1)S(1)}, u32[]{:S(2)}, u32[]{:S(2)}) collective-permute-start(bf16[288,128]{1,0:T(8,128)(2,1)S(1)} %get-tuple-element.10), channel_id=1, source_target_pairs={{0,24},{8,16},{16,8},{24,0},{1,25},{9,17},{17,9},{25,1},{2,26},{10... | collective-permute-start | bytes 221192 | tf_op jit(solution)/shard_map/ppermute | solution.py:181
  9.7 0.0 collective-permute-done.2
  9.7 3.0 %collective-permute-done.1 = bf16[288,128]{1,0:T(8,128)(2,1)S(1)} collective-permute-done((bf16[288,128]{1,0:T(8,128)(2,1)S(1)}, bf16[288,128]{1,0:T(8,128)(2,1)S(1)}, u32[]{:S(2)}, u32[]{:S(2)}) %collective-permute-start.1) | collective-permute-done | bytes 73760 | tf_op jit(solution)/shard_map/ppermute | solution.py:178
  12.7 1.6 %collective-permute-start.6 = (bf16[4,288,128]{2,1,0:T(8,128)(2,1)S(1)}, bf16[4,288,128]{2,1,0:T(8,128)(2,1)S(1)}, u32[]{:S(2)}, u32[]{:S(2)}) collective-permute-start(bf16[4,288,128]{2,1,0:T(8,128)(2,1)S(1)} %pad_maximum_fusion.refs_0_), channel_id=1, source_target_pairs={{0,16},{8,24},{16,0},{24,8},{1,17},{9,25},{17,1},{25,9},{2,18},{10... | collective-permute-start | bytes 884744 | tf_op jit(solution)/shard_map/ppermute | solution.py:181
  14.3 1.5 %collective-permute-start.4 = (bf16[4,288,128]{2,1,0:T(8,128)(2,1)S(1)}, bf16[4,288,128]{2,1,0:T(8,128)(2,1)S(1)}, u32[]{:S(2)}, u32[]{:S(2)}) collective-permute-start(bf16[4,288,128]{2,1,0:T(8,128)(2,1)S(1)} %pad_maximum_fusion.refs_0_), channel_id=1, source_target_pairs={{0,8},{8,0},{16,24},{24,16},{1,9},{9,1},{17,25},{25,17},{2,10},{10... | collective-permute-start | bytes 884744 | tf_op jit(solution)/shard_map/ppermute | solution.py:181
  15.8 3.3 %collective-permute-start.11 = (bf16[288,128]{1,0:T(8,128)(2,1)S(1)}, bf16[288,128]{1,0:T(8,128)(2,1)S(1)}, u32[]{:S(2)}, u32[]{:S(2)}) collective-permute-start(bf16[288,128]{1,0:T(8,128)(2,1)S(1)} %collective-permute-done.3), channel_id=1, source_target_pairs={{0,6},{1,7},{2,4},{3,5},{4,2},{5,3},{6,0},{7,1},{8,14},{9,15},{10,... | collective-permute-start | bytes 221192 | tf_op jit(solution)/shard_map/ppermute | solution.py:178
  19.1 1.1 %collective-permute-start.9 = (bf16[288,128]{1,0:T(8,128)(2,1)S(1)}, bf16[288,128]{1,0:T(8,128)(2,1)S(1)}, u32[]{:S(2)}, u32[]{:S(2)}) collective-permute-start(bf16[288,128]{1,0:T(8,128)(2,1)S(1)} %collective-permute-done.3), channel_id=1, source_target_pairs={{0,2},{1,3},{2,0},{3,1},{4,6},{5,7},{6,4},{7,5},{8,10},{9,11},{10,... | collective-permute-start | bytes 221192 | tf_op jit(solution)/shard_map/ppermute | solution.py:178
  20.2 2.3 %collective-permute-done.11 = bf16[288,128]{1,0:T(8,128)(2,1)S(1)} collective-permute-done((bf16[288,128]{1,0:T(8,128)(2,1)S(1)}, bf16[288,128]{1,0:T(8,128)(2,1)S(1)}, u32[]{:S(2)}, u32[]{:S(2)}) %collective-permute-start.11) | collective-permute-done | bytes 73760 | tf_op jit(solution)/shard_map/ppermute | solution.py:178
  22.5 0.0 collective-permute-done.6.refs_2_.refs_4_
  22.5 0.5 %collective-permute-start.7 = (bf16[4,288,128]{2,1,0:T(8,128)(2,1)S(1)}, bf16[4,288,128]{2,1,0:T(8,128)(2,1)S(1)}, u32[]{:S(2)}, u32[]{:S(2)}) collective-permute-start(bf16[4,288,128]{2,1,0:T(8,128)(2,1)S(1)} %collective-permute-done.6.refs_2_.refs_4_), channel_id=1, source_target_pairs={{0,1},{1,0},{2,3},{3,2},{4,5},{5,4},{6,7},{7,6},{8,9},{9,8},{10,11... | collective-permute-start | bytes 884744 | tf_op jit(solution)/shard_map/ppermute | solution.py:178
  23.0 0.0 collective-permute-done.4.refs_0_.refs_2_
  23.0 0.1 collective-permute-start.5
  23.1 1.7 %collective-permute-done.10 = bf16[288,128]{1,0:T(8,128)(2,1)S(1)} collective-permute-done((bf16[288,128]{1,0:T(8,128)(2,1)S(1)}, bf16[288,128]{1,0:T(8,128)(2,1)S(1)}, u32[]{:S(2)}, u32[]{:S(2)}) %collective-permute-start.10) | collective-permute-done | bytes 73760 | tf_op jit(solution)/shard_map/ppermute | solution.py:178
  24.8 0.0 collective-permute-done.9
  24.9 0.1 collective-permute-start.12
  24.9 0.0 collective-permute-done.7.refs_3_.refs_5_
  25.0 0.0 collective-permute-done.5.refs_1_.refs_3_
  25.0 0.0 collective-permute-done.8.refs_1_
  25.0 1.5 %collective-permute-done.12.refs_7_ = bf16[4,288,128]{2,1,0:T(8,128)(2,1)S(1)} collective-permute-done((bf16[4,288,128]{2,1,0:T(8,128)(2,1)S(1)}, bf16[4,288,128]{2,1,0:T(8,128)(2,1)S(1)}, u32[]{:S(2)}, u32[]{:S(2)}) %collective-permute-start.12) | collective-permute-done | bytes 294944 | tf_op jit(solution)/shard_map/ppermute | solution.py:178
  26.5 1.0 %second_products.1 = bf16[64,768]{1,0:T(8,128)(2,1)} custom-call(bf16[128,512]{1,0:T(8,128)(2,1)S(1)} %first_products.1.first_ref, bf16[4,288,128]{2,1,0:T(8,128)(2,1)S(1)} %pad_maximum_fusion.refs_0_, bf16[4,288,128]{2,1,0:T(8,128)(2,1)S(1)} %collective-permute-done.8.refs_1_, bf16[4,288,128]{2,1,0:T(8,128)(2,1)S(1)} %collective-permute-done.4.refs_0_.refs_2_, ...), custom_call_target="tpu_custom_call" | custom-call | tf_op jit(solution)/shard_map/second_products/pallas_call | solution.py:163
  (7 shorter events, 0.1 us)
Async XLA Ops:
  1.3 8.4 %collective-permute-start.2 = (bf16[288,128]{1,0:T(8,128)(2,1)S(1)}, bf16[288,128]{1,0:T(8,128)(2,1)S(1)}, u32[]{:S(2)}, u32[]{:S(2)}) collective-permute-start(bf16[288,128]{1,0:T(8,128)(2,1)S(1)} %get-tuple-element.10), channel_id=1, source_target_pairs={{0,6},{1,7},{2,4},{3,5},{4,2},{5,3},{6,0},{7,1},{8,14},{9,15},{10,... | collective-permute-start | bytes 221192 | tf_op jit(solution)/shard_map/ppermute | solution.py:178
  6.4 6.2 %collective-permute-start.1 = (bf16[288,128]{1,0:T(8,128)(2,1)S(1)}, bf16[288,128]{1,0:T(8,128)(2,1)S(1)}, u32[]{:S(2)}, u32[]{:S(2)}) collective-permute-start(bf16[288,128]{1,0:T(8,128)(2,1)S(1)} %get-tuple-element.10), channel_id=1, source_target_pairs={{0,4},{1,5},{2,6},{3,7},{4,0},{5,1},{6,2},{7,3},{8,12},{9,13},{10,... | collective-permute-start | bytes 221192 | tf_op jit(solution)/shard_map/ppermute | solution.py:178
  6.4 6.2 %collective-permute-start = (bf16[288,128]{1,0:T(8,128)(2,1)S(1)}, bf16[288,128]{1,0:T(8,128)(2,1)S(1)}, u32[]{:S(2)}, u32[]{:S(2)}) collective-permute-start(bf16[288,128]{1,0:T(8,128)(2,1)S(1)} %get-tuple-element.10), channel_id=1, source_target_pairs={{0,2},{1,3},{2,0},{3,1},{4,6},{5,7},{6,4},{7,5},{8,10},{9,11},{10,... | collective-permute-start | bytes 221192 | tf_op jit(solution)/shard_map/ppermute | solution.py:178
  7.1 5.6 %collective-permute-start.3 = (bf16[288,128]{1,0:T(8,128)(2,1)S(1)}, bf16[288,128]{1,0:T(8,128)(2,1)S(1)}, u32[]{:S(2)}, u32[]{:S(2)}) collective-permute-start(bf16[288,128]{1,0:T(8,128)(2,1)S(1)} %get-tuple-element.10), channel_id=1, source_target_pairs={{0,24},{8,16},{16,8},{24,0},{1,25},{9,17},{17,9},{25,1},{2,26},{10... | collective-permute-start | bytes 221192 | tf_op jit(solution)/shard_map/ppermute | solution.py:181
  12.7 9.8 %collective-permute-start.6 = (bf16[4,288,128]{2,1,0:T(8,128)(2,1)S(1)}, bf16[4,288,128]{2,1,0:T(8,128)(2,1)S(1)}, u32[]{:S(2)}, u32[]{:S(2)}) collective-permute-start(bf16[4,288,128]{2,1,0:T(8,128)(2,1)S(1)} %pad_maximum_fusion.refs_0_), channel_id=1, source_target_pairs={{0,16},{8,24},{16,0},{24,8},{1,17},{9,25},{17,1},{25,9},{2,18},{10... | collective-permute-start | bytes 884744 | tf_op jit(solution)/shard_map/ppermute | solution.py:181
  14.3 8.7 %collective-permute-start.4 = (bf16[4,288,128]{2,1,0:T(8,128)(2,1)S(1)}, bf16[4,288,128]{2,1,0:T(8,128)(2,1)S(1)}, u32[]{:S(2)}, u32[]{:S(2)}) collective-permute-start(bf16[4,288,128]{2,1,0:T(8,128)(2,1)S(1)} %pad_maximum_fusion.refs_0_), channel_id=1, source_target_pairs={{0,8},{8,0},{16,24},{24,16},{1,9},{9,1},{17,25},{25,17},{2,10},{10... | collective-permute-start | bytes 884744 | tf_op jit(solution)/shard_map/ppermute | solution.py:181
  15.8 6.7 %collective-permute-start.11 = (bf16[288,128]{1,0:T(8,128)(2,1)S(1)}, bf16[288,128]{1,0:T(8,128)(2,1)S(1)}, u32[]{:S(2)}, u32[]{:S(2)}) collective-permute-start(bf16[288,128]{1,0:T(8,128)(2,1)S(1)} %collective-permute-done.3), channel_id=1, source_target_pairs={{0,6},{1,7},{2,4},{3,5},{4,2},{5,3},{6,0},{7,1},{8,14},{9,15},{10,... | collective-permute-start | bytes 221192 | tf_op jit(solution)/shard_map/ppermute | solution.py:178
  19.1 5.7 %collective-permute-start.10 = (bf16[288,128]{1,0:T(8,128)(2,1)S(1)}, bf16[288,128]{1,0:T(8,128)(2,1)S(1)}, u32[]{:S(2)}, u32[]{:S(2)}) collective-permute-start(bf16[288,128]{1,0:T(8,128)(2,1)S(1)} %collective-permute-done.3), channel_id=1, source_target_pairs={{0,4},{1,5},{2,6},{3,7},{4,0},{5,1},{6,2},{7,3},{8,12},{9,13},{10,... | collective-permute-start | bytes 221192 | tf_op jit(solution)/shard_map/ppermute | solution.py:178
  19.1 5.7 %collective-permute-start.9 = (bf16[288,128]{1,0:T(8,128)(2,1)S(1)}, bf16[288,128]{1,0:T(8,128)(2,1)S(1)}, u32[]{:S(2)}, u32[]{:S(2)}) collective-permute-start(bf16[288,128]{1,0:T(8,128)(2,1)S(1)} %collective-permute-done.3), channel_id=1, source_target_pairs={{0,2},{1,3},{2,0},{3,1},{4,6},{5,7},{6,4},{7,5},{8,10},{9,11},{10,... | collective-permute-start | bytes 221192 | tf_op jit(solution)/shard_map/ppermute | solution.py:178
  22.5 2.5 %collective-permute-start.8 = (bf16[4,288,128]{2,1,0:T(8,128)(2,1)S(1)}, bf16[4,288,128]{2,1,0:T(8,128)(2,1)S(1)}, u32[]{:S(2)}, u32[]{:S(2)}) collective-permute-start(bf16[4,288,128]{2,1,0:T(8,128)(2,1)S(1)} %pad_maximum_fusion.refs_0_), channel_id=1, source_target_pairs={{0,1},{1,0},{2,3},{3,2},{4,5},{5,4},{6,7},{7,6},{8,9},{9,8},{10,11... | collective-permute-start | bytes 884744 | tf_op jit(solution)/shard_map/ppermute | solution.py:178
  22.5 2.5 %collective-permute-start.7 = (bf16[4,288,128]{2,1,0:T(8,128)(2,1)S(1)}, bf16[4,288,128]{2,1,0:T(8,128)(2,1)S(1)}, u32[]{:S(2)}, u32[]{:S(2)}) collective-permute-start(bf16[4,288,128]{2,1,0:T(8,128)(2,1)S(1)} %collective-permute-done.6.refs_2_.refs_4_), channel_id=1, source_target_pairs={{0,1},{1,0},{2,3},{3,2},{4,5},{5,4},{6,7},{7,6},{8,9},{9,8},{10,11... | collective-permute-start | bytes 884744 | tf_op jit(solution)/shard_map/ppermute | solution.py:178
  23.0 2.0 %collective-permute-start.5 = (bf16[4,288,128]{2,1,0:T(8,128)(2,1)S(1)}, bf16[4,288,128]{2,1,0:T(8,128)(2,1)S(1)}, u32[]{:S(2)}, u32[]{:S(2)}) collective-permute-start(bf16[4,288,128]{2,1,0:T(8,128)(2,1)S(1)} %collective-permute-done.4.refs_0_.refs_2_), channel_id=1, source_target_pairs={{0,1},{1,0},{2,3},{3,2},{4,5},{5,4},{6,7},{7,6},{8,9},{9,8},{10,11... | collective-permute-start | bytes 884744 | tf_op jit(solution)/shard_map/ppermute | solution.py:178
  24.9 1.6 %collective-permute-start.12 = (bf16[4,288,128]{2,1,0:T(8,128)(2,1)S(1)}, bf16[4,288,128]{2,1,0:T(8,128)(2,1)S(1)}, u32[]{:S(2)}, u32[]{:S(2)}) collective-permute-start(bf16[4,288,128]{2,1,0:T(8,128)(2,1)S(1)} %pad_maximum_fusion.1.refs_6_), channel_id=1, source_target_pairs={{0,1},{1,0},{2,3},{3,2},{4,5},{5,4},{6,7},{7,6},{8,9},{9,8},{10,11... | collective-permute-start | bytes 884744 | tf_op jit(solution)/shard_map/ppermute | solution.py:178

commit v19 on v17

--- a/solution.py
+++ b/solution.py
@@ -74,12 +74,12 @@
 
 def gathered_rows(pair_refs, mask, first, count):
     first_core = lax.rem(lax.axis_index("shard"), 2) == 0
-    here_ref, there_ref = pair_refs[mask]
-    found = []
-    for piece in range(here_ref.shape[0]):
-        here, there = here_ref[piece, first : first + count], there_ref[piece, first : first + count]
-        found += [jnp.where(first_core, here, there), jnp.where(first_core, there, here)]
-    return found
+    found = {}
+    for here_ref, there_ref, order in pair_refs[mask]:
+        for piece, source in enumerate(order):
+            here, there = here_ref[piece, first : first + count], there_ref[piece, first : first + count]
+            found[source] = [jnp.where(first_core, here, there), jnp.where(first_core, there, here)]
+    return [rows for source in sorted(found) for rows in found[source]]
 
 
 def times(halves, matrix):
@@ -95,6 +95,11 @@
     return both[:row_count] + both[row_count:]
 
 
+def by_mask(refs, orders):
+    refs = iter(refs)
+    return {mask: [(next(refs), next(refs), order) for order in groups] for mask, groups in orders}
+
+
 def stacked_tiles(pair_refs, mask, row_count, tiles):
     return [gathered_rows(pair_refs, mask, tile * row_count, row_count) for tile in range(tiles)]
 
@@ -108,8 +113,8 @@
         halves[row_count:] = (product - high.astype(jnp.float32)).astype(jnp.bfloat16)
 
 
-def first_kernel(masks, sections, own_ref, *refs):
-    pair_refs, halves = dict(zip(masks, zip(refs[:-1:2], refs[1:-1:2]))), refs[-1]
+def first_kernel(orders, sections, own_ref, *refs):
+    pair_refs, halves = by_mask(refs[:-1], orders), refs[-1]
     row_count, nodes = own_ref.shape[0], halves.shape[1]
     halves[:row_count] = own_ref[...]
     halves[row_count:] = jnp.zeros((row_count, nodes), jnp.bfloat16)
@@ -119,12 +124,12 @@
             pl.when(lax.axis_index("section") == at)(functools.partial(multiply_through, halves, pair_refs, near))
 
 
-def second_kernel(sections, first_ref, *refs):
-    pair_refs, out_ref, halves = list(zip(refs[:-2:2], refs[1:-2:2])), refs[-2], refs[-1]
+def second_kernel(orders, sections, first_ref, *refs):
+    pair_refs, out_ref, halves = by_mask(refs[:-2], orders), refs[-2], refs[-1]
     row_count, nodes = halves.shape[0] // 2, halves.shape[1]
     tiles = nodes // 128
     stacked = tiles * row_count
-    part = pair_refs[0][0].shape[1] - stacked
+    part = refs[0].shape[1] - stacked
     halves[...] = first_ref[...]
     for at in range(sections):
 
@@ -142,11 +147,15 @@
             out_ref[:, nodes:] = times(halves, rest).astype(jnp.bfloat16)
 
 
+def flat(pairs, masks):
+    orders = [(mask, [order for order, _ in pairs[mask]]) for mask in masks]
+    return orders, [array for mask in masks for _, pair in pairs[mask] for array in pair]
+
+
 def first_products(own, pairs, nodes, sections):
-    masks = [mask for mask in range(1, sections) if not mask & (mask - 1)]
-    operands = [array for mask in masks for array in pairs[mask]]
+    orders, operands = flat(pairs, [mask for mask in range(1, sections) if not mask & (mask - 1)])
     return pl.pallas_call(
-        functools.partial(first_kernel, masks, sections),
+        functools.partial(first_kernel, orders, sections),
         out_shape=pltpu.VMEM((2 * own.shape[0], nodes), jnp.bfloat16),
         in_specs=[pl.BlockSpec(memory_space=pltpu.VMEM)] * (1 + len(operands)),
         out_specs=pl.BlockSpec(memory_space=pltpu.VMEM),
@@ -156,9 +165,9 @@
 
 
 def second_products(first, pairs, width, sections):
-    operands = [array for pair in pairs for array in pair]
+    orders, operands = flat(pairs, list(range(sections)))
     return pl.pallas_call(
-        functools.partial(second_kernel, sections),
+        functools.partial(second_kernel, orders, sections),
         out_shape=jax.ShapeDtypeStruct((first.shape[0] // 2, width), jnp.bfloat16),
         in_specs=[pl.BlockSpec(memory_space=pltpu.VMEM)] * (1 + len(operands)),
         out_specs=pl.BlockSpec(memory_space=pltpu.VMEM),
@@ -177,15 +186,23 @@
     def along_section(value, mask):
         return lax.ppermute(value, "section", [(i, i ^ mask) for i in range(sections)])
 
-    def along_z(value):
-        return jnp.stack([value] + [along_shard(value, 2 * mask) for mask in range(1, shards // 2)])
+    def along_z(value, groups):
+        came = [value] + [along_shard(value, 2 * mask) for mask in range(1, shards // 2)]
+        return [jnp.stack([came[mask] for mask in order]) for order in groups]
+
+    whole = [list(range(shards // 2))]
+    last_first = [0] + whole[0][:0:-1]
+    in_two = [last_first[: shards // 4], last_first[shards // 4 :]]
 
     ahead = {mask: along_section(sent, mask) for mask in range(1, sections) if mask & (mask - 1)}
-    mine, ahead = lax.optimization_barrier((along_z(sent), ahead))
-    gathered = [mine]
+    mine, ahead = lax.optimization_barrier((along_z(sent, whole)[0], ahead))
+    arrived = [(whole, [mine])]
     for mask in range(1, sections):
-        gathered.append(along_z(ahead[mask]) if mask in ahead else along_section(mine, mask))
-    pairs = [(here, along_shard(here, 1)) for here in gathered]
+        if mask in ahead:
+            arrived.append((in_two, along_z(ahead[mask], in_two)))
+        else:
+            arrived.append((whole, [along_section(mine, mask)]))
+    pairs = [[(order, (here, along_shard(here, 1))) for order, here in zip(*group)] for group in arrived]
     first = first_products(own, pairs, own.shape[1], sections)
     return second_products(first, pairs, width, sections)
 
@@ -211,7 +228,7 @@
     tile_size = tile_values.shape[3]
     part = max(width - nodes, 0) // tile_size * row_count // sections
     sent_rows = nodes // tile_size * row_count + part
-    even = shards >= 2 and shards & (shards - 1) == 0 and sections > 1 and sections & (sections - 1) == 0
+    even = shards >= 4 and shards & (shards - 1) == 0 and sections > 1 and sections & (sections - 1) == 0
     parts = part >= 16 and part % 16 == 0 and row_count % part == 0 and tile_size == 128
     whole = part * sections * tile_size == (width - nodes) * row_count
     if even and parts and whole:

time: 27.6 us -> 27.3 us (0.989)
  waiting for transfers between devices: 8.54 us -> 7.71 us
  starting transfers between devices: 16.5 us -> 17 us
    ppermute x10 -> x11, waiting for transfers between devices: 8.54 us -> 7.7 us  [along_shard(): return lax.ppermute(value, 'shard', [(i, i ^ mask) for i in range(shards)])]
    ppermute x10 -> x11, starting transfers between devices: 10.8 us -> 11.3 us  [along_shard(): return lax.ppermute(value, 'shard', [(i, i ^ mask) for i in range(shards)])]
  transfers between devices with their start and end apart: 13 -> 14, of which waited for: 4 -> 5; matrix products, arithmetic and copies ran while one was open for 0% -> 0% of each run, Pallas kernels for 0% -> 0%
where the time goes in v19:
time: 27.3 us; the launch traced here: 27.1 us
  starting transfers between devices  17 us (62%)
  waiting for transfers between devices  7.71 us (28%)
  Pallas kernels  2.31 us (8%)
    ppermute x11, starting transfers between devices, along_shard(): return lax.ppermute(value, 'shard', [(i, i ^ mask) for i in range(shards)])  11.3 us
    ppermute x11, waiting for transfers between devices, along_shard(): return lax.ppermute(value, 'shard', [(i, i ^ mask) for i in range(shards)])  7.7 us
    ppermute x3, starting transfers between devices, along_section(): lax.ppermute(value, 'section', [(i, i ^ mask) for i in range(sections)])  5.68 us
    pallas_call x1, Pallas kernels, dense_rows(): pl.pallas_call(dense_rows_kernel, out_shape=[pltpu.VMEM(shape, jnp.bfloat...  1.34 us
    pallas_call x1, Pallas kernels, second_products(): pl.pallas_call(functools.partial(second_kernel, orders, sections), out_sh...  0.96 us
  transfers between devices with their start and end apart: 14, of which 5 were waited for; matrix products, arithmetic and copies ran while one was open for 0% of the time, Pallas kernels for 0%

profile of v19, /device:TPU:0, one launch (start us, length us, event | category | flops | bytes accessed | tf_op | source)
XLA Modules:
  0.0 27.1 jit_solution(6932210882100051446)
XLA Ops:
  0.0 1.3 %dense_rows.1 = (bf16[64,512]{1,0:T(8,128)(2,1)S(1)}, bf16[288,128]{1,0:T(8,128)(2,1)S(1)}) custom-call(s32[1,4,16]{2,1,0:T(4,128)} %cols_ref.1, s32[1,4]{1,0:T(1,128)} %live_ref.1, bf16[64,16,128]{2,1,0:T(8,128)(2,1)} %bitcast.11, s32[1,64]{1,0:T(1,128)} %degrees_ref.1, bf16[64,768]{1,0:T(8,128)(2,1)} %features_ref.1), custom_call_target="tpu_custom_call" | custom-call | tf_op jit(solution)/shard_map/dense_rows/pallas_call | solution.py:54
  1.3 5.1 %collective-permute-start.2 = (bf16[288,128]{1,0:T(8,128)(2,1)S(1)}, bf16[288,128]{1,0:T(8,128)(2,1)S(1)}, u32[]{:S(2)}, u32[]{:S(2)}) collective-permute-start(bf16[288,128]{1,0:T(8,128)(2,1)S(1)} %get-tuple-element.10), channel_id=1, source_target_pairs={{0,6},{1,7},{2,4},{3,5},{4,2},{5,3},{6,0},{7,1},{8,14},{9,15},{10,... | collective-permute-start | bytes 221192 | tf_op jit(solution)/shard_map/ppermute | solution.py:184
  6.5 0.6 %collective-permute-start = (bf16[288,128]{1,0:T(8,128)(2,1)S(1)}, bf16[288,128]{1,0:T(8,128)(2,1)S(1)}, u32[]{:S(2)}, u32[]{:S(2)}) collective-permute-start(bf16[288,128]{1,0:T(8,128)(2,1)S(1)} %get-tuple-element.10), channel_id=1, source_target_pairs={{0,2},{1,3},{2,0},{3,1},{4,6},{5,7},{6,4},{7,5},{8,10},{9,11},{10,... | collective-permute-start | bytes 221192 | tf_op jit(solution)/shard_map/ppermute | solution.py:184
  7.1 2.6 %collective-permute-start.3 = (bf16[288,128]{1,0:T(8,128)(2,1)S(1)}, bf16[288,128]{1,0:T(8,128)(2,1)S(1)}, u32[]{:S(2)}, u32[]{:S(2)}) collective-permute-start(bf16[288,128]{1,0:T(8,128)(2,1)S(1)} %get-tuple-element.10), channel_id=1, source_target_pairs={{0,24},{8,16},{16,8},{24,0},{1,25},{9,17},{17,9},{25,1},{2,26},{10... | collective-permute-start | bytes 221192 | tf_op jit(solution)/shard_map/ppermute | solution.py:187
  9.7 0.0 collective-permute-done.2
  9.7 3.0 %collective-permute-done.1 = bf16[288,128]{1,0:T(8,128)(2,1)S(1)} collective-permute-done((bf16[288,128]{1,0:T(8,128)(2,1)S(1)}, bf16[288,128]{1,0:T(8,128)(2,1)S(1)}, u32[]{:S(2)}, u32[]{:S(2)}) %collective-permute-start.1) | collective-permute-done | bytes 73760 | tf_op jit(solution)/shard_map/ppermute | solution.py:184
  12.7 0.0 collective-permute-done
  12.7 0.0 collective-permute-done.3
  12.7 1.6 %collective-permute-start.6 = (bf16[4,288,128]{2,1,0:T(8,128)(2,1)S(1)}, bf16[4,288,128]{2,1,0:T(8,128)(2,1)S(1)}, u32[]{:S(2)}, u32[]{:S(2)}) collective-permute-start(bf16[4,288,128]{2,1,0:T(8,128)(2,1)S(1)} %pad_maximum_fusion.refs_0_), channel_id=1, source_target_pairs={{0,16},{8,24},{16,0},{24,8},{1,17},{9,25},{17,1},{25,9},{2,18},{10... | collective-permute-start | bytes 884744 | tf_op jit(solution)/shard_map/ppermute | solution.py:187
  14.3 1.5 %collective-permute-start.4 = (bf16[4,288,128]{2,1,0:T(8,128)(2,1)S(1)}, bf16[4,288,128]{2,1,0:T(8,128)(2,1)S(1)}, u32[]{:S(2)}, u32[]{:S(2)}) collective-permute-start(bf16[4,288,128]{2,1,0:T(8,128)(2,1)S(1)} %pad_maximum_fusion.refs_0_), channel_id=1, source_target_pairs={{0,8},{8,0},{16,24},{24,16},{1,9},{9,1},{17,25},{25,17},{2,10},{10... | collective-permute-start | bytes 884744 | tf_op jit(solution)/shard_map/ppermute | solution.py:187
  15.8 3.3 %collective-permute-start.9 = (bf16[288,128]{1,0:T(8,128)(2,1)S(1)}, bf16[288,128]{1,0:T(8,128)(2,1)S(1)}, u32[]{:S(2)}, u32[]{:S(2)}) collective-permute-start(bf16[288,128]{1,0:T(8,128)(2,1)S(1)} %collective-permute-done.3), channel_id=1, source_target_pairs={{0,6},{1,7},{2,4},{3,5},{4,2},{5,3},{6,0},{7,1},{8,14},{9,15},{10,... | collective-permute-start | bytes 221192 | tf_op jit(solution)/shard_map/ppermute | solution.py:184
  19.1 0.0 collective-permute-start.12
  19.1 1.1 %collective-permute-start.11 = (bf16[288,128]{1,0:T(8,128)(2,1)S(1)}, bf16[288,128]{1,0:T(8,128)(2,1)S(1)}, u32[]{:S(2)}, u32[]{:S(2)}) collective-permute-start(bf16[288,128]{1,0:T(8,128)(2,1)S(1)} %collective-permute-done.3), channel_id=1, source_target_pairs={{0,4},{1,5},{2,6},{3,7},{4,0},{5,1},{6,2},{7,3},{8,12},{9,13},{10,... | collective-permute-start | bytes 221192 | tf_op jit(solution)/shard_map/ppermute | solution.py:184
  20.2 2.4 %collective-permute-done.9 = bf16[288,128]{1,0:T(8,128)(2,1)S(1)} collective-permute-done((bf16[288,128]{1,0:T(8,128)(2,1)S(1)}, bf16[288,128]{1,0:T(8,128)(2,1)S(1)}, u32[]{:S(2)}, u32[]{:S(2)}) %collective-permute-start.9) | collective-permute-done | bytes 73760 | tf_op jit(solution)/shard_map/ppermute | solution.py:184
  22.6 0.0 collective-permute-start.8
  22.6 0.0 collective-permute-done.6.refs_2_.refs_4_
  22.6 0.5 %collective-permute-start.7 = (bf16[4,288,128]{2,1,0:T(8,128)(2,1)S(1)}, bf16[4,288,128]{2,1,0:T(8,128)(2,1)S(1)}, u32[]{:S(2)}, u32[]{:S(2)}) collective-permute-start(bf16[4,288,128]{2,1,0:T(8,128)(2,1)S(1)} %collective-permute-done.6.refs_2_.refs_4_), channel_id=1, source_target_pairs={{0,1},{1,0},{2,3},{3,2},{4,5},{5,4},{6,7},{7,6},{8,9},{9,8},{10,11... | collective-permute-start | bytes 884744 | tf_op jit(solution)/shard_map/ppermute | solution.py:184
  23.1 0.0 collective-permute-done.4.refs_0_.refs_2_
  23.1 0.1 collective-permute-start.5
  23.2 1.4 %collective-permute-done.12 = bf16[288,128]{1,0:T(8,128)(2,1)S(1)} collective-permute-done((bf16[288,128]{1,0:T(8,128)(2,1)S(1)}, bf16[288,128]{1,0:T(8,128)(2,1)S(1)}, u32[]{:S(2)}, u32[]{:S(2)}) %collective-permute-start.12) | collective-permute-done | bytes 73760 | tf_op jit(solution)/shard_map/ppermute | solution.py:184
  24.6 0.6 %collective-permute-start.13 = (bf16[2,288,128]{2,1,0:T(8,128)(2,1)S(1)}, bf16[2,288,128]{2,1,0:T(8,128)(2,1)S(1)}, u32[]{:S(2)}, u32[]{:S(2)}) collective-permute-start(bf16[2,288,128]{2,1,0:T(8,128)(2,1)S(1)} %pad_maximum_fusion.2.refs_8_), channel_id=1, source_target_pairs={{0,1},{1,0},{2,3},{3,2},{4,5},{5,4},{6,7},{7,6},{8,9},{9,8},{10,11... | collective-permute-start | bytes 442376 | tf_op jit(solution)/shard_map/ppermute | solution.py:184
  25.2 0.7 %collective-permute-done.10.refs_7_ = bf16[2,288,128]{2,1,0:T(8,128)(2,1)S(1)} collective-permute-done((bf16[2,288,128]{2,1,0:T(8,128)(2,1)S(1)}, bf16[2,288,128]{2,1,0:T(8,128)(2,1)S(1)}, u32[]{:S(2)}, u32[]{:S(2)}) %collective-permute-start.10) | collective-permute-done | bytes 147488 | tf_op jit(solution)/shard_map/ppermute | solution.py:184
  25.9 0.2 collective-permute-done.13.refs_9_
  26.2 1.0 %second_products.1 = bf16[64,768]{1,0:T(8,128)(2,1)} custom-call(bf16[128,512]{1,0:T(8,128)(2,1)S(1)} %first_products.1.first_ref, bf16[4,288,128]{2,1,0:T(8,128)(2,1)S(1)} %pad_maximum_fusion.refs_0_, bf16[4,288,128]{2,1,0:T(8,128)(2,1)S(1)} %collective-permute-done.8.refs_1_, bf16[4,288,128]{2,1,0:T(8,128)(2,1)S(1)} %collective-permute-done.4.refs_0_.refs_2_, ...), custom_call_target="tpu_custom_call" | custom-call | tf_op jit(solution)/shard_map/second_products/pallas_call | solution.py:169
  (10 shorter events, 0.1 us)
Async XLA Ops:
  1.3 8.4 %collective-permute-start.2 = (bf16[288,128]{1,0:T(8,128)(2,1)S(1)}, bf16[288,128]{1,0:T(8,128)(2,1)S(1)}, u32[]{:S(2)}, u32[]{:S(2)}) collective-permute-start(bf16[288,128]{1,0:T(8,128)(2,1)S(1)} %get-tuple-element.10), channel_id=1, source_target_pairs={{0,6},{1,7},{2,4},{3,5},{4,2},{5,3},{6,0},{7,1},{8,14},{9,15},{10,... | collective-permute-start | bytes 221192 | tf_op jit(solution)/shard_map/ppermute | solution.py:184
  6.5 6.2 %collective-permute-start.1 = (bf16[288,128]{1,0:T(8,128)(2,1)S(1)}, bf16[288,128]{1,0:T(8,128)(2,1)S(1)}, u32[]{:S(2)}, u32[]{:S(2)}) collective-permute-start(bf16[288,128]{1,0:T(8,128)(2,1)S(1)} %get-tuple-element.10), channel_id=1, source_target_pairs={{0,4},{1,5},{2,6},{3,7},{4,0},{5,1},{6,2},{7,3},{8,12},{9,13},{10,... | collective-permute-start | bytes 221192 | tf_op jit(solution)/shard_map/ppermute | solution.py:184
  6.5 6.2 %collective-permute-start = (bf16[288,128]{1,0:T(8,128)(2,1)S(1)}, bf16[288,128]{1,0:T(8,128)(2,1)S(1)}, u32[]{:S(2)}, u32[]{:S(2)}) collective-permute-start(bf16[288,128]{1,0:T(8,128)(2,1)S(1)} %get-tuple-element.10), channel_id=1, source_target_pairs={{0,2},{1,3},{2,0},{3,1},{4,6},{5,7},{6,4},{7,5},{8,10},{9,11},{10,... | collective-permute-start | bytes 221192 | tf_op jit(solution)/shard_map/ppermute | solution.py:184
  7.1 5.6 %collective-permute-start.3 = (bf16[288,128]{1,0:T(8,128)(2,1)S(1)}, bf16[288,128]{1,0:T(8,128)(2,1)S(1)}, u32[]{:S(2)}, u32[]{:S(2)}) collective-permute-start(bf16[288,128]{1,0:T(8,128)(2,1)S(1)} %get-tuple-element.10), channel_id=1, source_target_pairs={{0,24},{8,16},{16,8},{24,0},{1,25},{9,17},{17,9},{25,1},{2,26},{10... | collective-permute-start | bytes 221192 | tf_op jit(solution)/shard_map/ppermute | solution.py:187
  12.7 9.9 %collective-permute-start.6 = (bf16[4,288,128]{2,1,0:T(8,128)(2,1)S(1)}, bf16[4,288,128]{2,1,0:T(8,128)(2,1)S(1)}, u32[]{:S(2)}, u32[]{:S(2)}) collective-permute-start(bf16[4,288,128]{2,1,0:T(8,128)(2,1)S(1)} %pad_maximum_fusion.refs_0_), channel_id=1, source_target_pairs={{0,16},{8,24},{16,0},{24,8},{1,17},{9,25},{17,1},{25,9},{2,18},{10... | collective-permute-start | bytes 884744 | tf_op jit(solution)/shard_map/ppermute | solution.py:187
  14.3 8.8 %collective-permute-start.4 = (bf16[4,288,128]{2,1,0:T(8,128)(2,1)S(1)}, bf16[4,288,128]{2,1,0:T(8,128)(2,1)S(1)}, u32[]{:S(2)}, u32[]{:S(2)}) collective-permute-start(bf16[4,288,128]{2,1,0:T(8,128)(2,1)S(1)} %pad_maximum_fusion.refs_0_), channel_id=1, source_target_pairs={{0,8},{8,0},{16,24},{24,16},{1,9},{9,1},{17,25},{25,17},{2,10},{10... | collective-permute-start | bytes 884744 | tf_op jit(solution)/shard_map/ppermute | solution.py:187
  15.8 6.8 %collective-permute-start.9 = (bf16[288,128]{1,0:T(8,128)(2,1)S(1)}, bf16[288,128]{1,0:T(8,128)(2,1)S(1)}, u32[]{:S(2)}, u32[]{:S(2)}) collective-permute-start(bf16[288,128]{1,0:T(8,128)(2,1)S(1)} %collective-permute-done.3), channel_id=1, source_target_pairs={{0,6},{1,7},{2,4},{3,5},{4,2},{5,3},{6,0},{7,1},{8,14},{9,15},{10,... | collective-permute-start | bytes 221192 | tf_op jit(solution)/shard_map/ppermute | solution.py:184
  19.1 5.4 %collective-permute-start.12 = (bf16[288,128]{1,0:T(8,128)(2,1)S(1)}, bf16[288,128]{1,0:T(8,128)(2,1)S(1)}, u32[]{:S(2)}, u32[]{:S(2)}) collective-permute-start(bf16[288,128]{1,0:T(8,128)(2,1)S(1)} %collective-permute-done.3), channel_id=1, source_target_pairs={{0,2},{1,3},{2,0},{3,1},{4,6},{5,7},{6,4},{7,5},{8,10},{9,11},{10,... | collective-permute-start | bytes 221192 | tf_op jit(solution)/shard_map/ppermute | solution.py:184
  19.1 5.4 %collective-permute-start.11 = (bf16[288,128]{1,0:T(8,128)(2,1)S(1)}, bf16[288,128]{1,0:T(8,128)(2,1)S(1)}, u32[]{:S(2)}, u32[]{:S(2)}) collective-permute-start(bf16[288,128]{1,0:T(8,128)(2,1)S(1)} %collective-permute-done.3), channel_id=1, source_target_pairs={{0,4},{1,5},{2,6},{3,7},{4,0},{5,1},{6,2},{7,3},{8,12},{9,13},{10,... | collective-permute-start | bytes 221192 | tf_op jit(solution)/shard_map/ppermute | solution.py:184
  22.6 3.6 %collective-permute-start.8 = (bf16[4,288,128]{2,1,0:T(8,128)(2,1)S(1)}, bf16[4,288,128]{2,1,0:T(8,128)(2,1)S(1)}, u32[]{:S(2)}, u32[]{:S(2)}) collective-permute-start(bf16[4,288,128]{2,1,0:T(8,128)(2,1)S(1)} %pad_maximum_fusion.refs_0_), channel_id=1, source_target_pairs={{0,1},{1,0},{2,3},{3,2},{4,5},{5,4},{6,7},{7,6},{8,9},{9,8},{10,11... | collective-permute-start | bytes 884744 | tf_op jit(solution)/shard_map/ppermute | solution.py:184
  22.6 2.6 %collective-permute-start.7 = (bf16[4,288,128]{2,1,0:T(8,128)(2,1)S(1)}, bf16[4,288,128]{2,1,0:T(8,128)(2,1)S(1)}, u32[]{:S(2)}, u32[]{:S(2)}) collective-permute-start(bf16[4,288,128]{2,1,0:T(8,128)(2,1)S(1)} %collective-permute-done.6.refs_2_.refs_4_), channel_id=1, source_target_pairs={{0,1},{1,0},{2,3},{3,2},{4,5},{5,4},{6,7},{7,6},{8,9},{9,8},{10,11... | collective-permute-start | bytes 884744 | tf_op jit(solution)/shard_map/ppermute | solution.py:184
  23.1 2.0 %collective-permute-start.5 = (bf16[4,288,128]{2,1,0:T(8,128)(2,1)S(1)}, bf16[4,288,128]{2,1,0:T(8,128)(2,1)S(1)}, u32[]{:S(2)}, u32[]{:S(2)}) collective-permute-start(bf16[4,288,128]{2,1,0:T(8,128)(2,1)S(1)} %collective-permute-done.4.refs_0_.refs_2_), channel_id=1, source_target_pairs={{0,1},{1,0},{2,3},{3,2},{4,5},{5,4},{6,7},{7,6},{8,9},{9,8},{10,11... | collective-permute-start | bytes 884744 | tf_op jit(solution)/shard_map/ppermute | solution.py:184
  24.5 1.4 %collective-permute-start.10 = (bf16[2,288,128]{2,1,0:T(8,128)(2,1)S(1)}, bf16[2,288,128]{2,1,0:T(8,128)(2,1)S(1)}, u32[]{:S(2)}, u32[]{:S(2)}) collective-permute-start(bf16[2,288,128]{2,1,0:T(8,128)(2,1)S(1)} %pad_maximum_fusion.1.refs_6_), channel_id=1, source_target_pairs={{0,1},{1,0},{2,3},{3,2},{4,5},{5,4},{6,7},{7,6},{8,9},{9,8},{10,11... | collective-permute-start | bytes 442376 | tf_op jit(solution)/shard_map/ppermute | solution.py:184
  24.6 1.6 %collective-permute-start.13 = (bf16[2,288,128]{2,1,0:T(8,128)(2,1)S(1)}, bf16[2,288,128]{2,1,0:T(8,128)(2,1)S(1)}, u32[]{:S(2)}, u32[]{:S(2)}) collective-permute-start(bf16[2,288,128]{2,1,0:T(8,128)(2,1)S(1)} %pad_maximum_fusion.2.refs_8_), channel_id=1, source_target_pairs={{0,1},{1,0},{2,3},{3,2},{4,5},{5,4},{6,7},{7,6},{8,9},{9,8},{10,11... | collective-permute-start | bytes 442376 | tf_op jit(solution)/shard_map/ppermute | solution.py:184

commit v20 on v19

--- a/solution.py
+++ b/solution.py
@@ -8,7 +8,10 @@
 from jax.sharding import PartitionSpec as P
 
 
-def dense_rows_kernel(cols_ref, live_ref, tiles_ref, degrees_ref, features_ref, rows_ref, *sent_refs):
+def dense_rows_kernel(cols_ref, live_ref, tiles_ref, degrees_ref, features_ref, rows_ref, *rest):
+    *sent_refs, arrived, arrival = rest
+    copy = pltpu.make_async_copy(tiles_ref, arrived, arrival)
+    copy.start()
     row_count, slots, tile_size = tiles_ref.shape
     nodes = rows_ref.shape[1]
     blocks = nodes // tile_size
@@ -22,12 +25,13 @@
     owner = lax.div(lax.broadcasted_iota(jnp.int32, (row_count, wide), 1), slots)
     mine = lax.broadcasted_iota(jnp.int32, (row_count, wide), 0) == owner
     column = jnp.where(mine, jnp.broadcast_to(column, (row_count, wide)), -1)
-    tiles = tiles_ref[...].reshape(wide, tile_size)
     degree = jnp.broadcast_to(degrees_ref[...].astype(jnp.float32), (row_count, row_count))
     diagonal = lax.broadcasted_iota(jnp.int32, (row_count, row_count), 0) == lax.broadcasted_iota(
         jnp.int32, (row_count, row_count), 1
     )
     scale = lax.rsqrt(jnp.sum(jnp.where(diagonal, degree, 0.0), axis=1, keepdims=True))
+    copy.wait()
+    tiles = arrived[...].reshape(wide, tile_size)
     for b in range(blocks):
         pick = (column == b).astype(jnp.bfloat16)
         summed = jnp.dot(pick, tiles, preferred_element_type=jnp.float32)
@@ -57,11 +61,12 @@
         in_specs=[
             pl.BlockSpec(memory_space=pltpu.SMEM),
             pl.BlockSpec(memory_space=pltpu.SMEM),
-            pl.BlockSpec(memory_space=pltpu.VMEM),
+            pl.BlockSpec(memory_space=pl.ANY),
             pl.BlockSpec(memory_space=pltpu.VMEM),
             pl.BlockSpec(memory_space=pltpu.VMEM),
         ],
         out_specs=[pl.BlockSpec(memory_space=pltpu.VMEM)] * len(shapes),
+        scratch_shapes=[pltpu.VMEM(tile_rows.shape, tile_rows.dtype), pltpu.SemaphoreType.DMA],
         name="dense_rows",
     )(tile_cols, live_tiles, tile_rows, degrees, features)
 

time: 27.3 us -> 28.2 us (1.033)
  Pallas kernels: 2.31 us -> 3.19 us
    pallas_call x1, Pallas kernels: 1.34 us -> 2.22 us  [dense_rows(): pl.pallas_call(dense_rows_kernel, out_shape=[pltpu.VMEM(shape, jnp.bfloat...]
where the time goes in v20:
time: 28.2 us; the launch traced here: 28 us
  starting transfers between devices  17 us (60%)
  waiting for transfers between devices  7.71 us (27%)
  Pallas kernels  3.19 us (11%)
    ppermute x11, starting transfers between devices, along_shard(): return lax.ppermute(value, 'shard', [(i, i ^ mask) for i in range(shards)])  11.3 us
    ppermute x11, waiting for transfers between devices, along_shard(): return lax.ppermute(value, 'shard', [(i, i ^ mask) for i in range(shards)])  7.7 us
    ppermute x3, starting transfers between devices, along_section(): lax.ppermute(value, 'section', [(i, i ^ mask) for i in range(sections)])  5.68 us
    pallas_call x1, Pallas kernels, dense_rows(): pl.pallas_call(dense_rows_kernel, out_shape=[pltpu.VMEM(shape, jnp.bfloat...  2.22 us
    pallas_call x1, Pallas kernels, second_products(): pl.pallas_call(functools.partial(second_kernel, orders, sections), out_sh...  0.95 us
  transfers between devices with their start and end apart: 14, of which 5 were waited for; matrix products, arithmetic and copies ran while one was open for 0% of the time, Pallas kernels for 0%

profile of v20, /device:TPU:0, one launch (start us, length us, event | category | flops | bytes accessed | tf_op | source)
XLA Modules:
  0.0 28.0 jit_solution(5828368823040308332)
XLA Ops:
  0.0 2.2 %dense_rows.1 = (bf16[64,512]{1,0:T(8,128)(2,1)S(1)}, bf16[288,128]{1,0:T(8,128)(2,1)S(1)}) custom-call(s32[1,4,16]{2,1,0:T(4,128)} %cols_ref.1, s32[1,4]{1,0:T(1,128)} %live_ref.1, bf16[64,16,128]{2,1,0:T(8,128)(2,1)} %bitcast.11, s32[1,64]{1,0:T(1,128)} %degrees_ref.1, bf16[64,768]{1,0:T(8,128)(2,1)} %features_ref.1), custom_call_target="tpu_custom_call" | custom-call | tf_op jit(solution)/shard_map/dense_rows/pallas_call | solution.py:58
  2.2 5.1 %collective-permute-start.2 = (bf16[288,128]{1,0:T(8,128)(2,1)S(1)}, bf16[288,128]{1,0:T(8,128)(2,1)S(1)}, u32[]{:S(2)}, u32[]{:S(2)}) collective-permute-start(bf16[288,128]{1,0:T(8,128)(2,1)S(1)} %get-tuple-element.10), channel_id=1, source_target_pairs={{0,6},{1,7},{2,4},{3,5},{4,2},{5,3},{6,0},{7,1},{8,14},{9,15},{10,... | collective-permute-start | bytes 221192 | tf_op jit(solution)/shard_map/ppermute | solution.py:189
  7.3 0.0 collective-permute-start.1
  7.3 0.6 %collective-permute-start = (bf16[288,128]{1,0:T(8,128)(2,1)S(1)}, bf16[288,128]{1,0:T(8,128)(2,1)S(1)}, u32[]{:S(2)}, u32[]{:S(2)}) collective-permute-start(bf16[288,128]{1,0:T(8,128)(2,1)S(1)} %get-tuple-element.10), channel_id=1, source_target_pairs={{0,2},{1,3},{2,0},{3,1},{4,6},{5,7},{6,4},{7,5},{8,10},{9,11},{10,... | collective-permute-start | bytes 221192 | tf_op jit(solution)/shard_map/ppermute | solution.py:189
  8.0 2.6 %collective-permute-start.3 = (bf16[288,128]{1,0:T(8,128)(2,1)S(1)}, bf16[288,128]{1,0:T(8,128)(2,1)S(1)}, u32[]{:S(2)}, u32[]{:S(2)}) collective-permute-start(bf16[288,128]{1,0:T(8,128)(2,1)S(1)} %get-tuple-element.10), channel_id=1, source_target_pairs={{0,24},{8,16},{16,8},{24,0},{1,25},{9,17},{17,9},{25,1},{2,26},{10... | collective-permute-start | bytes 221192 | tf_op jit(solution)/shard_map/ppermute | solution.py:192
  10.6 0.0 collective-permute-done.2
  10.6 3.0 %collective-permute-done.1 = bf16[288,128]{1,0:T(8,128)(2,1)S(1)} collective-permute-done((bf16[288,128]{1,0:T(8,128)(2,1)S(1)}, bf16[288,128]{1,0:T(8,128)(2,1)S(1)}, u32[]{:S(2)}, u32[]{:S(2)}) %collective-permute-start.1) | collective-permute-done | bytes 73760 | tf_op jit(solution)/shard_map/ppermute | solution.py:189
  13.6 1.6 %collective-permute-start.6 = (bf16[4,288,128]{2,1,0:T(8,128)(2,1)S(1)}, bf16[4,288,128]{2,1,0:T(8,128)(2,1)S(1)}, u32[]{:S(2)}, u32[]{:S(2)}) collective-permute-start(bf16[4,288,128]{2,1,0:T(8,128)(2,1)S(1)} %pad_maximum_fusion.refs_0_), channel_id=1, source_target_pairs={{0,16},{8,24},{16,0},{24,8},{1,17},{9,25},{17,1},{25,9},{2,18},{10... | collective-permute-start | bytes 884744 | tf_op jit(solution)/shard_map/ppermute | solution.py:192
  15.2 1.5 %collective-permute-start.4 = (bf16[4,288,128]{2,1,0:T(8,128)(2,1)S(1)}, bf16[4,288,128]{2,1,0:T(8,128)(2,1)S(1)}, u32[]{:S(2)}, u32[]{:S(2)}) collective-permute-start(bf16[4,288,128]{2,1,0:T(8,128)(2,1)S(1)} %pad_maximum_fusion.refs_0_), channel_id=1, source_target_pairs={{0,8},{8,0},{16,24},{24,16},{1,9},{9,1},{17,25},{25,17},{2,10},{10... | collective-permute-start | bytes 884744 | tf_op jit(solution)/shard_map/ppermute | solution.py:192
  16.7 3.3 %collective-permute-start.9 = (bf16[288,128]{1,0:T(8,128)(2,1)S(1)}, bf16[288,128]{1,0:T(8,128)(2,1)S(1)}, u32[]{:S(2)}, u32[]{:S(2)}) collective-permute-start(bf16[288,128]{1,0:T(8,128)(2,1)S(1)} %collective-permute-done.3), channel_id=1, source_target_pairs={{0,6},{1,7},{2,4},{3,5},{4,2},{5,3},{6,0},{7,1},{8,14},{9,15},{10,... | collective-permute-start | bytes 221192 | tf_op jit(solution)/shard_map/ppermute | solution.py:189
  20.0 0.0 collective-permute-start.12
  20.0 1.1 %collective-permute-start.11 = (bf16[288,128]{1,0:T(8,128)(2,1)S(1)}, bf16[288,128]{1,0:T(8,128)(2,1)S(1)}, u32[]{:S(2)}, u32[]{:S(2)}) collective-permute-start(bf16[288,128]{1,0:T(8,128)(2,1)S(1)} %collective-permute-done.3), channel_id=1, source_target_pairs={{0,4},{1,5},{2,6},{3,7},{4,0},{5,1},{6,2},{7,3},{8,12},{9,13},{10,... | collective-permute-start | bytes 221192 | tf_op jit(solution)/shard_map/ppermute | solution.py:189
  21.1 2.4 %collective-permute-done.9 = bf16[288,128]{1,0:T(8,128)(2,1)S(1)} collective-permute-done((bf16[288,128]{1,0:T(8,128)(2,1)S(1)}, bf16[288,128]{1,0:T(8,128)(2,1)S(1)}, u32[]{:S(2)}, u32[]{:S(2)}) %collective-permute-start.9) | collective-permute-done | bytes 73760 | tf_op jit(solution)/shard_map/ppermute | solution.py:189
  23.5 0.0 collective-permute-done.6.refs_2_.refs_4_
  23.5 0.5 %collective-permute-start.7 = (bf16[4,288,128]{2,1,0:T(8,128)(2,1)S(1)}, bf16[4,288,128]{2,1,0:T(8,128)(2,1)S(1)}, u32[]{:S(2)}, u32[]{:S(2)}) collective-permute-start(bf16[4,288,128]{2,1,0:T(8,128)(2,1)S(1)} %collective-permute-done.6.refs_2_.refs_4_), channel_id=1, source_target_pairs={{0,1},{1,0},{2,3},{3,2},{4,5},{5,4},{6,7},{7,6},{8,9},{9,8},{10,11... | collective-permute-start | bytes 884744 | tf_op jit(solution)/shard_map/ppermute | solution.py:189
  24.0 0.0 collective-permute-done.4.refs_0_.refs_2_
  24.0 0.1 collective-permute-start.5
  24.1 1.3 %collective-permute-done.12 = bf16[288,128]{1,0:T(8,128)(2,1)S(1)} collective-permute-done((bf16[288,128]{1,0:T(8,128)(2,1)S(1)}, bf16[288,128]{1,0:T(8,128)(2,1)S(1)}, u32[]{:S(2)}, u32[]{:S(2)}) %collective-permute-start.12) | collective-permute-done | bytes 73760 | tf_op jit(solution)/shard_map/ppermute | solution.py:189
  25.5 0.6 %collective-permute-start.13 = (bf16[2,288,128]{2,1,0:T(8,128)(2,1)S(1)}, bf16[2,288,128]{2,1,0:T(8,128)(2,1)S(1)}, u32[]{:S(2)}, u32[]{:S(2)}) collective-permute-start(bf16[2,288,128]{2,1,0:T(8,128)(2,1)S(1)} %pad_maximum_fusion.2.refs_8_), channel_id=1, source_target_pairs={{0,1},{1,0},{2,3},{3,2},{4,5},{5,4},{6,7},{7,6},{8,9},{9,8},{10,11... | collective-permute-start | bytes 442376 | tf_op jit(solution)/shard_map/ppermute | solution.py:189
  26.0 0.0 collective-permute-done.7.refs_3_.refs_5_
  26.0 0.0 collective-permute-done.5.refs_1_.refs_3_
  26.1 0.7 %collective-permute-done.10.refs_7_ = bf16[2,288,128]{2,1,0:T(8,128)(2,1)S(1)} collective-permute-done((bf16[2,288,128]{2,1,0:T(8,128)(2,1)S(1)}, bf16[2,288,128]{2,1,0:T(8,128)(2,1)S(1)}, u32[]{:S(2)}, u32[]{:S(2)}) %collective-permute-start.10) | collective-permute-done | bytes 147488 | tf_op jit(solution)/shard_map/ppermute | solution.py:189
  26.8 0.2 collective-permute-done.13.refs_9_
  27.0 1.0 %second_products.1 = bf16[64,768]{1,0:T(8,128)(2,1)} custom-call(bf16[128,512]{1,0:T(8,128)(2,1)S(1)} %first_products.1.first_ref, bf16[4,288,128]{2,1,0:T(8,128)(2,1)S(1)} %pad_maximum_fusion.refs_0_, bf16[4,288,128]{2,1,0:T(8,128)(2,1)S(1)} %collective-permute-done.8.refs_1_, bf16[4,288,128]{2,1,0:T(8,128)(2,1)S(1)} %collective-permute-done.4.refs_0_.refs_2_, ...), custom_call_target="tpu_custom_call" | custom-call | tf_op jit(solution)/shard_map/second_products/pallas_call | solution.py:174
  (10 shorter events, 0.1 us)
Async XLA Ops:
  2.2 8.4 %collective-permute-start.2 = (bf16[288,128]{1,0:T(8,128)(2,1)S(1)}, bf16[288,128]{1,0:T(8,128)(2,1)S(1)}, u32[]{:S(2)}, u32[]{:S(2)}) collective-permute-start(bf16[288,128]{1,0:T(8,128)(2,1)S(1)} %get-tuple-element.10), channel_id=1, source_target_pairs={{0,6},{1,7},{2,4},{3,5},{4,2},{5,3},{6,0},{7,1},{8,14},{9,15},{10,... | collective-permute-start | bytes 221192 | tf_op jit(solution)/shard_map/ppermute | solution.py:189
  7.3 6.2 %collective-permute-start.1 = (bf16[288,128]{1,0:T(8,128)(2,1)S(1)}, bf16[288,128]{1,0:T(8,128)(2,1)S(1)}, u32[]{:S(2)}, u32[]{:S(2)}) collective-permute-start(bf16[288,128]{1,0:T(8,128)(2,1)S(1)} %get-tuple-element.10), channel_id=1, source_target_pairs={{0,4},{1,5},{2,6},{3,7},{4,0},{5,1},{6,2},{7,3},{8,12},{9,13},{10,... | collective-permute-start | bytes 221192 | tf_op jit(solution)/shard_map/ppermute | solution.py:189
  7.3 6.2 %collective-permute-start = (bf16[288,128]{1,0:T(8,128)(2,1)S(1)}, bf16[288,128]{1,0:T(8,128)(2,1)S(1)}, u32[]{:S(2)}, u32[]{:S(2)}) collective-permute-start(bf16[288,128]{1,0:T(8,128)(2,1)S(1)} %get-tuple-element.10), channel_id=1, source_target_pairs={{0,2},{1,3},{2,0},{3,1},{4,6},{5,7},{6,4},{7,5},{8,10},{9,11},{10,... | collective-permute-start | bytes 221192 | tf_op jit(solution)/shard_map/ppermute | solution.py:189
  8.0 5.6 %collective-permute-start.3 = (bf16[288,128]{1,0:T(8,128)(2,1)S(1)}, bf16[288,128]{1,0:T(8,128)(2,1)S(1)}, u32[]{:S(2)}, u32[]{:S(2)}) collective-permute-start(bf16[288,128]{1,0:T(8,128)(2,1)S(1)} %get-tuple-element.10), channel_id=1, source_target_pairs={{0,24},{8,16},{16,8},{24,0},{1,25},{9,17},{17,9},{25,1},{2,26},{10... | collective-permute-start | bytes 221192 | tf_op jit(solution)/shard_map/ppermute | solution.py:192
  13.6 9.9 %collective-permute-start.6 = (bf16[4,288,128]{2,1,0:T(8,128)(2,1)S(1)}, bf16[4,288,128]{2,1,0:T(8,128)(2,1)S(1)}, u32[]{:S(2)}, u32[]{:S(2)}) collective-permute-start(bf16[4,288,128]{2,1,0:T(8,128)(2,1)S(1)} %pad_maximum_fusion.refs_0_), channel_id=1, source_target_pairs={{0,16},{8,24},{16,0},{24,8},{1,17},{9,25},{17,1},{25,9},{2,18},{10... | collective-permute-start | bytes 884744 | tf_op jit(solution)/shard_map/ppermute | solution.py:192
  15.2 8.8 %collective-permute-start.4 = (bf16[4,288,128]{2,1,0:T(8,128)(2,1)S(1)}, bf16[4,288,128]{2,1,0:T(8,128)(2,1)S(1)}, u32[]{:S(2)}, u32[]{:S(2)}) collective-permute-start(bf16[4,288,128]{2,1,0:T(8,128)(2,1)S(1)} %pad_maximum_fusion.refs_0_), channel_id=1, source_target_pairs={{0,8},{8,0},{16,24},{24,16},{1,9},{9,1},{17,25},{25,17},{2,10},{10... | collective-permute-start | bytes 884744 | tf_op jit(solution)/shard_map/ppermute | solution.py:192
  16.7 6.8 %collective-permute-start.9 = (bf16[288,128]{1,0:T(8,128)(2,1)S(1)}, bf16[288,128]{1,0:T(8,128)(2,1)S(1)}, u32[]{:S(2)}, u32[]{:S(2)}) collective-permute-start(bf16[288,128]{1,0:T(8,128)(2,1)S(1)} %collective-permute-done.3), channel_id=1, source_target_pairs={{0,6},{1,7},{2,4},{3,5},{4,2},{5,3},{6,0},{7,1},{8,14},{9,15},{10,... | collective-permute-start | bytes 221192 | tf_op jit(solution)/shard_map/ppermute | solution.py:189
  20.0 5.4 %collective-permute-start.12 = (bf16[288,128]{1,0:T(8,128)(2,1)S(1)}, bf16[288,128]{1,0:T(8,128)(2,1)S(1)}, u32[]{:S(2)}, u32[]{:S(2)}) collective-permute-start(bf16[288,128]{1,0:T(8,128)(2,1)S(1)} %collective-permute-done.3), channel_id=1, source_target_pairs={{0,2},{1,3},{2,0},{3,1},{4,6},{5,7},{6,4},{7,5},{8,10},{9,11},{10,... | collective-permute-start | bytes 221192 | tf_op jit(solution)/shard_map/ppermute | solution.py:189
  20.0 5.4 %collective-permute-start.11 = (bf16[288,128]{1,0:T(8,128)(2,1)S(1)}, bf16[288,128]{1,0:T(8,128)(2,1)S(1)}, u32[]{:S(2)}, u32[]{:S(2)}) collective-permute-start(bf16[288,128]{1,0:T(8,128)(2,1)S(1)} %collective-permute-done.3), channel_id=1, source_target_pairs={{0,4},{1,5},{2,6},{3,7},{4,0},{5,1},{6,2},{7,3},{8,12},{9,13},{10,... | collective-permute-start | bytes 221192 | tf_op jit(solution)/shard_map/ppermute | solution.py:189
  23.5 3.6 %collective-permute-start.8 = (bf16[4,288,128]{2,1,0:T(8,128)(2,1)S(1)}, bf16[4,288,128]{2,1,0:T(8,128)(2,1)S(1)}, u32[]{:S(2)}, u32[]{:S(2)}) collective-permute-start(bf16[4,288,128]{2,1,0:T(8,128)(2,1)S(1)} %pad_maximum_fusion.refs_0_), channel_id=1, source_target_pairs={{0,1},{1,0},{2,3},{3,2},{4,5},{5,4},{6,7},{7,6},{8,9},{9,8},{10,11... | collective-permute-start | bytes 884744 | tf_op jit(solution)/shard_map/ppermute | solution.py:189
  23.5 2.6 %collective-permute-start.7 = (bf16[4,288,128]{2,1,0:T(8,128)(2,1)S(1)}, bf16[4,288,128]{2,1,0:T(8,128)(2,1)S(1)}, u32[]{:S(2)}, u32[]{:S(2)}) collective-permute-start(bf16[4,288,128]{2,1,0:T(8,128)(2,1)S(1)} %collective-permute-done.6.refs_2_.refs_4_), channel_id=1, source_target_pairs={{0,1},{1,0},{2,3},{3,2},{4,5},{5,4},{6,7},{7,6},{8,9},{9,8},{10,11... | collective-permute-start | bytes 884744 | tf_op jit(solution)/shard_map/ppermute | solution.py:189
  24.0 2.0 %collective-permute-start.5 = (bf16[4,288,128]{2,1,0:T(8,128)(2,1)S(1)}, bf16[4,288,128]{2,1,0:T(8,128)(2,1)S(1)}, u32[]{:S(2)}, u32[]{:S(2)}) collective-permute-start(bf16[4,288,128]{2,1,0:T(8,128)(2,1)S(1)} %collective-permute-done.4.refs_0_.refs_2_), channel_id=1, source_target_pairs={{0,1},{1,0},{2,3},{3,2},{4,5},{5,4},{6,7},{7,6},{8,9},{9,8},{10,11... | collective-permute-start | bytes 884744 | tf_op jit(solution)/shard_map/ppermute | solution.py:189
  25.4 1.4 %collective-permute-start.10 = (bf16[2,288,128]{2,1,0:T(8,128)(2,1)S(1)}, bf16[2,288,128]{2,1,0:T(8,128)(2,1)S(1)}, u32[]{:S(2)}, u32[]{:S(2)}) collective-permute-start(bf16[2,288,128]{2,1,0:T(8,128)(2,1)S(1)} %pad_maximum_fusion.1.refs_6_), channel_id=1, source_target_pairs={{0,1},{1,0},{2,3},{3,2},{4,5},{5,4},{6,7},{7,6},{8,9},{9,8},{10,11... | collective-permute-start | bytes 442376 | tf_op jit(solution)/shard_map/ppermute | solution.py:189
  25.5 1.6 %collective-permute-start.13 = (bf16[2,288,128]{2,1,0:T(8,128)(2,1)S(1)}, bf16[2,288,128]{2,1,0:T(8,128)(2,1)S(1)}, u32[]{:S(2)}, u32[]{:S(2)}) collective-permute-start(bf16[2,288,128]{2,1,0:T(8,128)(2,1)S(1)} %pad_maximum_fusion.2.refs_8_), channel_id=1, source_target_pairs={{0,1},{1,0},{2,3},{3,2},{4,5},{5,4},{6,7},{7,6},{8,9},{9,8},{10,11... | collective-permute-start | bytes 442376 | tf_op jit(solution)/shard_map/ppermute | solution.py:189

commit v21 on v19

--- a/solution.py
+++ b/solution.py
@@ -87,7 +87,7 @@
     chip, chips = lax.div(lax.axis_index("shard"), 2), len(matrix[0]) // 2
     left = []
     for piece in range(chips):
-        source = lax.bitwise_xor(chip, piece)
+        source = lax.rem(chip - piece + chips, chips)
         left.append(halves[:, pl.ds(pl.multiple_of(source * 2 * row_count, 128), 2 * row_count)])
     left = jnp.concatenate(left, axis=1)
     right = jnp.concatenate([jnp.concatenate(tile, axis=0) for tile in matrix], axis=1)
@@ -187,8 +187,9 @@
         return lax.ppermute(value, "section", [(i, i ^ mask) for i in range(sections)])
 
     def along_z(value, groups):
-        came = [value] + [along_shard(value, 2 * mask) for mask in range(1, shards // 2)]
-        return [jnp.stack([came[mask] for mask in order]) for order in groups]
+        turns = [[(i, (i + 2 * back) % shards) for i in range(shards)] for back in range(1, shards // 2)]
+        came = [value] + [lax.ppermute(value, "shard", turn) for turn in turns]
+        return [jnp.stack([came[back] for back in order]) for order in groups]
 
     whole = [list(range(shards // 2))]
     last_first = [0] + whole[0][:0:-1]

time: 27.3 us -> 28.6 us (1.048)
  waiting for transfers between devices: 7.71 us -> 10.3 us
  starting transfers between devices: 17 us -> 15.7 us
    ppermute x11 -> x5, starting transfers between devices: 11.3 us -> 0.08 us  [along_shard(): return lax.ppermute(value, 'shard', [(i, i ^ mask) for i in range(shards)])]
    ppermute x0 -> x6, starting transfers between devices: none -> 10.1 us  [along_z(): came = [value] + [lax.ppermute(value, 'shard', turn) for turn in turns]]
    ppermute x0 -> x6, waiting for transfers between devices: none -> 7.18 us  [along_z(): came = [value] + [lax.ppermute(value, 'shard', turn) for turn in turns]]
    ppermute x11 -> x5, waiting for transfers between devices: 7.7 us -> 1.31 us  [along_shard(): return lax.ppermute(value, 'shard', [(i, i ^ mask) for i in range(shards)])]
    ppermute x3, waiting for transfers between devices: 0.01 us -> 1.84 us  [along_section(): lax.ppermute(value, 'section', [(i, i ^ mask) for i in range(sections)])]
  transfers between devices with their start and end apart: 14 -> 14, of which waited for: 5 -> 7; matrix products, arithmetic and copies ran while one was open for 0% -> 0% of each run, Pallas kernels for 0% -> 0%
where the time goes in v21:
time: 28.6 us; the launch traced here: 28.5 us
  starting transfers between devices  15.7 us (55%)
  waiting for transfers between devices  10.3 us (36%)
  Pallas kernels  2.32 us (8%)
    ppermute x6, starting transfers between devices, along_z(): came = [value] + [lax.ppermute(value, 'shard', turn) for turn in turns]  10.1 us
    ppermute x6, waiting for transfers between devices, along_z(): came = [value] + [lax.ppermute(value, 'shard', turn) for turn in turns]  7.18 us
    ppermute x3, starting transfers between devices, along_section(): lax.ppermute(value, 'section', [(i, i ^ mask) for i in range(sections)])  5.53 us
    ppermute x3, waiting for transfers between devices, along_section(): lax.ppermute(value, 'section', [(i, i ^ mask) for i in range(sections)])  1.84 us
    pallas_call x1, Pallas kernels, dense_rows(): pl.pallas_call(dense_rows_kernel, out_shape=[pltpu.VMEM(shape, jnp.bfloat...  1.34 us
    ppermute x5, waiting for transfers between devices, along_shard(): return lax.ppermute(value, 'shard', [(i, i ^ mask) for i in range(shards)])  1.31 us
    pallas_call x1, Pallas kernels, second_products(): pl.pallas_call(functools.partial(second_kernel, orders, sections), out_sh...  0.96 us
  transfers between devices with their start and end apart: 14, of which 7 were waited for; matrix products, arithmetic and copies ran while one was open for 0% of the time, Pallas kernels for 0%

profile of v21, /device:TPU:0, one launch (start us, length us, event | category | flops | bytes accessed | tf_op | source)
XLA Modules:
  0.0 28.5 jit_solution(17402137405435644374)
XLA Ops:
  0.0 1.3 %dense_rows.1 = (bf16[64,512]{1,0:T(8,128)(2,1)S(1)}, bf16[288,128]{1,0:T(8,128)(2,1)S(1)}) custom-call(s32[1,4,16]{2,1,0:T(4,128)} %cols_ref.1, s32[1,4]{1,0:T(1,128)} %live_ref.1, bf16[64,16,128]{2,1,0:T(8,128)(2,1)} %bitcast.11, s32[1,64]{1,0:T(1,128)} %degrees_ref.1, bf16[64,768]{1,0:T(8,128)(2,1)} %features_ref.1), custom_call_target="tpu_custom_call" | custom-call | tf_op jit(solution)/shard_map/dense_rows/pallas_call | solution.py:54
  1.3 5.1 %collective-permute-start.2 = (bf16[288,128]{1,0:T(8,128)(2,1)S(1)}, bf16[288,128]{1,0:T(8,128)(2,1)S(1)}, u32[]{:S(2)}, u32[]{:S(2)}) collective-permute-start(bf16[288,128]{1,0:T(8,128)(2,1)S(1)} %get-tuple-element.10), channel_id=1, source_target_pairs={{0,6},{1,7},{2,0},{3,1},{4,2},{5,3},{6,4},{7,5},{8,14},{9,15},{10,... | collective-permute-start | bytes 221192 | tf_op jit(solution)/shard_map/ppermute | solution.py:191
  6.4 0.0 collective-permute-start.1
  6.5 1.0 %collective-permute-start = (bf16[288,128]{1,0:T(8,128)(2,1)S(1)}, bf16[288,128]{1,0:T(8,128)(2,1)S(1)}, u32[]{:S(2)}, u32[]{:S(2)}) collective-permute-start(bf16[288,128]{1,0:T(8,128)(2,1)S(1)} %get-tuple-element.10), channel_id=1, source_target_pairs={{0,2},{1,3},{2,4},{3,5},{4,6},{5,7},{6,0},{7,1},{8,10},{9,11},{10,... | collective-permute-start | bytes 221192 | tf_op jit(solution)/shard_map/ppermute | solution.py:191
  7.5 2.5 %collective-permute-start.3 = (bf16[288,128]{1,0:T(8,128)(2,1)S(1)}, bf16[288,128]{1,0:T(8,128)(2,1)S(1)}, u32[]{:S(2)}, u32[]{:S(2)}) collective-permute-start(bf16[288,128]{1,0:T(8,128)(2,1)S(1)} %get-tuple-element.10), channel_id=1, source_target_pairs={{0,24},{8,16},{16,8},{24,0},{1,25},{9,17},{17,9},{25,1},{2,26},{10... | collective-permute-start | bytes 221192 | tf_op jit(solution)/shard_map/ppermute | solution.py:187
  9.9 3.5 %collective-permute-done.1 = bf16[288,128]{1,0:T(8,128)(2,1)S(1)} collective-permute-done((bf16[288,128]{1,0:T(8,128)(2,1)S(1)}, bf16[288,128]{1,0:T(8,128)(2,1)S(1)}, u32[]{:S(2)}, u32[]{:S(2)}) %collective-permute-start.1) | collective-permute-done | bytes 73760 | tf_op jit(solution)/shard_map/ppermute | solution.py:191
  13.5 1.6 %collective-permute-start.6 = (bf16[4,288,128]{2,1,0:T(8,128)(2,1)S(1)}, bf16[4,288,128]{2,1,0:T(8,128)(2,1)S(1)}, u32[]{:S(2)}, u32[]{:S(2)}) collective-permute-start(bf16[4,288,128]{2,1,0:T(8,128)(2,1)S(1)} %pad_maximum_fusion.refs_0_), channel_id=1, source_target_pairs={{0,16},{8,24},{16,0},{24,8},{1,17},{9,25},{17,1},{25,9},{2,18},{10... | collective-permute-start | bytes 884744 | tf_op jit(solution)/shard_map/ppermute | solution.py:187
  15.1 1.5 %collective-permute-start.4 = (bf16[4,288,128]{2,1,0:T(8,128)(2,1)S(1)}, bf16[4,288,128]{2,1,0:T(8,128)(2,1)S(1)}, u32[]{:S(2)}, u32[]{:S(2)}) collective-permute-start(bf16[4,288,128]{2,1,0:T(8,128)(2,1)S(1)} %pad_maximum_fusion.refs_0_), channel_id=1, source_target_pairs={{0,8},{8,0},{16,24},{24,16},{1,9},{9,1},{17,25},{25,17},{2,10},{10... | collective-permute-start | bytes 884744 | tf_op jit(solution)/shard_map/ppermute | solution.py:187
  16.6 2.0 %collective-permute-start.9 = (bf16[288,128]{1,0:T(8,128)(2,1)S(1)}, bf16[288,128]{1,0:T(8,128)(2,1)S(1)}, u32[]{:S(2)}, u32[]{:S(2)}) collective-permute-start(bf16[288,128]{1,0:T(8,128)(2,1)S(1)} %collective-permute-done.3), channel_id=1, source_target_pairs={{0,6},{1,7},{2,0},{3,1},{4,2},{5,3},{6,4},{7,5},{8,14},{9,15},{10,... | collective-permute-start | bytes 221192 | tf_op jit(solution)/shard_map/ppermute | solution.py:191
  18.6 0.0 collective-permute-start.12
  18.6 1.9 %collective-permute-start.11 = (bf16[288,128]{1,0:T(8,128)(2,1)S(1)}, bf16[288,128]{1,0:T(8,128)(2,1)S(1)}, u32[]{:S(2)}, u32[]{:S(2)}) collective-permute-start(bf16[288,128]{1,0:T(8,128)(2,1)S(1)} %collective-permute-done.3), channel_id=1, source_target_pairs={{0,4},{1,5},{2,6},{3,7},{4,0},{5,1},{6,2},{7,3},{8,12},{9,13},{10,... | collective-permute-start | bytes 221192 | tf_op jit(solution)/shard_map/ppermute | solution.py:191
  20.5 1.3 %collective-permute-done.9 = bf16[288,128]{1,0:T(8,128)(2,1)S(1)} collective-permute-done((bf16[288,128]{1,0:T(8,128)(2,1)S(1)}, bf16[288,128]{1,0:T(8,128)(2,1)S(1)}, u32[]{:S(2)}, u32[]{:S(2)}) %collective-permute-start.9) | collective-permute-done | bytes 73760 | tf_op jit(solution)/shard_map/ppermute | solution.py:191
  21.8 0.6 %collective-permute-done.6.refs_2_.refs_4_ = bf16[4,288,128]{2,1,0:T(8,128)(2,1)S(1)} collective-permute-done((bf16[4,288,128]{2,1,0:T(8,128)(2,1)S(1)}, bf16[4,288,128]{2,1,0:T(8,128)(2,1)S(1)}, u32[]{:S(2)}, u32[]{:S(2)}) %collective-permute-start.6) | collective-permute-done | bytes 294944 | tf_op jit(solution)/shard_map/ppermute | solution.py:187
  22.4 0.0 collective-permute-start.7
  22.4 1.2 %collective-permute-done.4.refs_0_.refs_2_ = bf16[4,288,128]{2,1,0:T(8,128)(2,1)S(1)} collective-permute-done((bf16[4,288,128]{2,1,0:T(8,128)(2,1)S(1)}, bf16[4,288,128]{2,1,0:T(8,128)(2,1)S(1)}, u32[]{:S(2)}, u32[]{:S(2)}) %collective-permute-start.4) | collective-permute-done | bytes 294944 | tf_op jit(solution)/shard_map/ppermute | solution.py:187
  23.7 0.0 collective-permute-start.5
  23.7 1.1 %collective-permute-done.12 = bf16[288,128]{1,0:T(8,128)(2,1)S(1)} collective-permute-done((bf16[288,128]{1,0:T(8,128)(2,1)S(1)}, bf16[288,128]{1,0:T(8,128)(2,1)S(1)}, u32[]{:S(2)}, u32[]{:S(2)}) %collective-permute-start.12) | collective-permute-done | bytes 73760 | tf_op jit(solution)/shard_map/ppermute | solution.py:191
  24.8 1.2 %collective-permute-done.11 = bf16[288,128]{1,0:T(8,128)(2,1)S(1)} collective-permute-done((bf16[288,128]{1,0:T(8,128)(2,1)S(1)}, bf16[288,128]{1,0:T(8,128)(2,1)S(1)}, u32[]{:S(2)}, u32[]{:S(2)}) %collective-permute-start.11) | collective-permute-done | bytes 73760 | tf_op jit(solution)/shard_map/ppermute | solution.py:191
  26.1 0.1 collective-permute-start.13
  26.1 0.0 collective-permute-done.7.refs_3_.refs_5_
  26.2 0.0 collective-permute-done.10.refs_7_
  26.2 1.3 %collective-permute-done.13.refs_9_ = bf16[2,288,128]{2,1,0:T(8,128)(2,1)S(1)} collective-permute-done((bf16[2,288,128]{2,1,0:T(8,128)(2,1)S(1)}, bf16[2,288,128]{2,1,0:T(8,128)(2,1)S(1)}, u32[]{:S(2)}, u32[]{:S(2)}) %collective-permute-start.13) | collective-permute-done | bytes 147488 | tf_op jit(solution)/shard_map/ppermute | solution.py:184
  27.5 0.0 collective-permute-done.8.refs_1_
  27.5 1.0 %second_products.1 = bf16[64,768]{1,0:T(8,128)(2,1)} custom-call(bf16[128,512]{1,0:T(8,128)(2,1)S(1)} %first_products.1.first_ref, bf16[4,288,128]{2,1,0:T(8,128)(2,1)S(1)} %pad_maximum_fusion.refs_0_, bf16[4,288,128]{2,1,0:T(8,128)(2,1)S(1)} %collective-permute-done.8.refs_1_, bf16[4,288,128]{2,1,0:T(8,128)(2,1)S(1)} %collective-permute-done.4.refs_0_.refs_2_, ...), custom_call_target="tpu_custom_call" | custom-call | tf_op jit(solution)/shard_map/second_products/pallas_call | solution.py:169
  (10 shorter events, 0.1 us)
Async XLA Ops:
  1.3 8.6 %collective-permute-start.2 = (bf16[288,128]{1,0:T(8,128)(2,1)S(1)}, bf16[288,128]{1,0:T(8,128)(2,1)S(1)}, u32[]{:S(2)}, u32[]{:S(2)}) collective-permute-start(bf16[288,128]{1,0:T(8,128)(2,1)S(1)} %get-tuple-element.10), channel_id=1, source_target_pairs={{0,6},{1,7},{2,0},{3,1},{4,2},{5,3},{6,4},{7,5},{8,14},{9,15},{10,... | collective-permute-start | bytes 221192 | tf_op jit(solution)/shard_map/ppermute | solution.py:191
  6.4 7.0 %collective-permute-start.1 = (bf16[288,128]{1,0:T(8,128)(2,1)S(1)}, bf16[288,128]{1,0:T(8,128)(2,1)S(1)}, u32[]{:S(2)}, u32[]{:S(2)}) collective-permute-start(bf16[288,128]{1,0:T(8,128)(2,1)S(1)} %get-tuple-element.10), channel_id=1, source_target_pairs={{0,4},{1,5},{2,6},{3,7},{4,0},{5,1},{6,2},{7,3},{8,12},{9,13},{10,... | collective-permute-start | bytes 221192 | tf_op jit(solution)/shard_map/ppermute | solution.py:191
  6.5 7.0 %collective-permute-start = (bf16[288,128]{1,0:T(8,128)(2,1)S(1)}, bf16[288,128]{1,0:T(8,128)(2,1)S(1)}, u32[]{:S(2)}, u32[]{:S(2)}) collective-permute-start(bf16[288,128]{1,0:T(8,128)(2,1)S(1)} %get-tuple-element.10), channel_id=1, source_target_pairs={{0,2},{1,3},{2,4},{3,5},{4,6},{5,7},{6,0},{7,1},{8,10},{9,11},{10,... | collective-permute-start | bytes 221192 | tf_op jit(solution)/shard_map/ppermute | solution.py:191
  7.5 6.0 %collective-permute-start.3 = (bf16[288,128]{1,0:T(8,128)(2,1)S(1)}, bf16[288,128]{1,0:T(8,128)(2,1)S(1)}, u32[]{:S(2)}, u32[]{:S(2)}) collective-permute-start(bf16[288,128]{1,0:T(8,128)(2,1)S(1)} %get-tuple-element.10), channel_id=1, source_target_pairs={{0,24},{8,16},{16,8},{24,0},{1,25},{9,17},{17,9},{25,1},{2,26},{10... | collective-permute-start | bytes 221192 | tf_op jit(solution)/shard_map/ppermute | solution.py:187
  13.5 8.9 %collective-permute-start.6 = (bf16[4,288,128]{2,1,0:T(8,128)(2,1)S(1)}, bf16[4,288,128]{2,1,0:T(8,128)(2,1)S(1)}, u32[]{:S(2)}, u32[]{:S(2)}) collective-permute-start(bf16[4,288,128]{2,1,0:T(8,128)(2,1)S(1)} %pad_maximum_fusion.refs_0_), channel_id=1, source_target_pairs={{0,16},{8,24},{16,0},{24,8},{1,17},{9,25},{17,1},{25,9},{2,18},{10... | collective-permute-start | bytes 884744 | tf_op jit(solution)/shard_map/ppermute | solution.py:187
  15.1 8.6 %collective-permute-start.4 = (bf16[4,288,128]{2,1,0:T(8,128)(2,1)S(1)}, bf16[4,288,128]{2,1,0:T(8,128)(2,1)S(1)}, u32[]{:S(2)}, u32[]{:S(2)}) collective-permute-start(bf16[4,288,128]{2,1,0:T(8,128)(2,1)S(1)} %pad_maximum_fusion.refs_0_), channel_id=1, source_target_pairs={{0,8},{8,0},{16,24},{24,16},{1,9},{9,1},{17,25},{25,17},{2,10},{10... | collective-permute-start | bytes 884744 | tf_op jit(solution)/shard_map/ppermute | solution.py:187
  16.6 5.2 %collective-permute-start.9 = (bf16[288,128]{1,0:T(8,128)(2,1)S(1)}, bf16[288,128]{1,0:T(8,128)(2,1)S(1)}, u32[]{:S(2)}, u32[]{:S(2)}) collective-permute-start(bf16[288,128]{1,0:T(8,128)(2,1)S(1)} %collective-permute-done.3), channel_id=1, source_target_pairs={{0,6},{1,7},{2,0},{3,1},{4,2},{5,3},{6,4},{7,5},{8,14},{9,15},{10,... | collective-permute-start | bytes 221192 | tf_op jit(solution)/shard_map/ppermute | solution.py:191
  18.6 6.3 %collective-permute-start.12 = (bf16[288,128]{1,0:T(8,128)(2,1)S(1)}, bf16[288,128]{1,0:T(8,128)(2,1)S(1)}, u32[]{:S(2)}, u32[]{:S(2)}) collective-permute-start(bf16[288,128]{1,0:T(8,128)(2,1)S(1)} %collective-permute-done.3), channel_id=1, source_target_pairs={{0,2},{1,3},{2,4},{3,5},{4,6},{5,7},{6,0},{7,1},{8,10},{9,11},{10,... | collective-permute-start | bytes 221192 | tf_op jit(solution)/shard_map/ppermute | solution.py:191
  18.6 7.4 %collective-permute-start.11 = (bf16[288,128]{1,0:T(8,128)(2,1)S(1)}, bf16[288,128]{1,0:T(8,128)(2,1)S(1)}, u32[]{:S(2)}, u32[]{:S(2)}) collective-permute-start(bf16[288,128]{1,0:T(8,128)(2,1)S(1)} %collective-permute-done.3), channel_id=1, source_target_pairs={{0,4},{1,5},{2,6},{3,7},{4,0},{5,1},{6,2},{7,3},{8,12},{9,13},{10,... | collective-permute-start | bytes 221192 | tf_op jit(solution)/shard_map/ppermute | solution.py:191
  21.8 5.7 %collective-permute-start.8 = (bf16[4,288,128]{2,1,0:T(8,128)(2,1)S(1)}, bf16[4,288,128]{2,1,0:T(8,128)(2,1)S(1)}, u32[]{:S(2)}, u32[]{:S(2)}) collective-permute-start(bf16[4,288,128]{2,1,0:T(8,128)(2,1)S(1)} %pad_maximum_fusion.refs_0_), channel_id=1, source_target_pairs={{0,1},{1,0},{2,3},{3,2},{4,5},{5,4},{6,7},{7,6},{8,9},{9,8},{10,11... | collective-permute-start | bytes 884744 | tf_op jit(solution)/shard_map/ppermute | solution.py:184
  22.4 3.7 %collective-permute-start.7 = (bf16[4,288,128]{2,1,0:T(8,128)(2,1)S(1)}, bf16[4,288,128]{2,1,0:T(8,128)(2,1)S(1)}, u32[]{:S(2)}, u32[]{:S(2)}) collective-permute-start(bf16[4,288,128]{2,1,0:T(8,128)(2,1)S(1)} %collective-permute-done.6.refs_2_.refs_4_), channel_id=1, source_target_pairs={{0,1},{1,0},{2,3},{3,2},{4,5},{5,4},{6,7},{7,6},{8,9},{9,8},{10,11... | collective-permute-start | bytes 884744 | tf_op jit(solution)/shard_map/ppermute | solution.py:184
  23.7 2.5 %collective-permute-start.5 = (bf16[4,288,128]{2,1,0:T(8,128)(2,1)S(1)}, bf16[4,288,128]{2,1,0:T(8,128)(2,1)S(1)}, u32[]{:S(2)}, u32[]{:S(2)}) collective-permute-start(bf16[4,288,128]{2,1,0:T(8,128)(2,1)S(1)} %collective-permute-done.4.refs_0_.refs_2_), channel_id=1, source_target_pairs={{0,1},{1,0},{2,3},{3,2},{4,5},{5,4},{6,7},{7,6},{8,9},{9,8},{10,11... | collective-permute-start | bytes 884744 | tf_op jit(solution)/shard_map/ppermute | solution.py:184
  24.8 1.4 %collective-permute-start.10 = (bf16[2,288,128]{2,1,0:T(8,128)(2,1)S(1)}, bf16[2,288,128]{2,1,0:T(8,128)(2,1)S(1)}, u32[]{:S(2)}, u32[]{:S(2)}) collective-permute-start(bf16[2,288,128]{2,1,0:T(8,128)(2,1)S(1)} %pad_maximum_fusion.1.refs_6_), channel_id=1, source_target_pairs={{0,1},{1,0},{2,3},{3,2},{4,5},{5,4},{6,7},{7,6},{8,9},{9,8},{10,11... | collective-permute-start | bytes 442376 | tf_op jit(solution)/shard_map/ppermute | solution.py:184
  26.1 1.4 %collective-permute-start.13 = (bf16[2,288,128]{2,1,0:T(8,128)(2,1)S(1)}, bf16[2,288,128]{2,1,0:T(8,128)(2,1)S(1)}, u32[]{:S(2)}, u32[]{:S(2)}) collective-permute-start(bf16[2,288,128]{2,1,0:T(8,128)(2,1)S(1)} %pad_maximum_fusion.2.refs_8_), channel_id=1, source_target_pairs={{0,1},{1,0},{2,3},{3,2},{4,5},{5,4},{6,7},{7,6},{8,9},{9,8},{10,11... | collective-permute-start | bytes 442376 | tf_op jit(solution)/shard_map/ppermute | solution.py:184

commit v22 on v19

--- a/solution.py
+++ b/solution.py
@@ -192,7 +192,7 @@
 
     whole = [list(range(shards // 2))]
     last_first = [0] + whole[0][:0:-1]
-    in_two = [last_first[: shards // 4], last_first[shards // 4 :]]
+    in_two = [last_first[:-1], last_first[-1:]]
 
     ahead = {mask: along_section(sent, mask) for mask in range(1, sections) if mask & (mask - 1)}
     mine, ahead = lax.optimization_barrier((along_z(sent, whole)[0], ahead))

time: 27.3 us -> 31.1 us (1.14)
  waiting for transfers between devices: 7.71 us -> 12.7 us
  starting transfers between devices: 17 us -> 15.8 us
    ppermute x3, waiting for transfers between devices: 0.01 us -> 3.44 us  [along_section(): lax.ppermute(value, 'section', [(i, i ^ mask) for i in range(sections)])]
    ppermute x11, waiting for transfers between devices: 7.7 us -> 9.22 us  [along_shard(): return lax.ppermute(value, 'shard', [(i, i ^ mask) for i in range(shards)])]
    ppermute x11, starting transfers between devices: 11.3 us -> 10.2 us  [along_shard(): return lax.ppermute(value, 'shard', [(i, i ^ mask) for i in range(shards)])]
  transfers between devices with their start and end apart: 14 -> 14, of which waited for: 5 -> 6; matrix products, arithmetic and copies ran while one was open for 0% -> 0% of each run, Pallas kernels for 0% -> 0%
where the time goes in v22:
time: 31.1 us; the launch traced here: 31 us
  starting transfers between devices  15.8 us (51%)
  waiting for transfers between devices  12.7 us (41%)
  Pallas kernels  2.33 us (7%)
    ppermute x11, starting transfers between devices, along_shard(): return lax.ppermute(value, 'shard', [(i, i ^ mask) for i in range(shards)])  10.2 us
    ppermute x11, waiting for transfers between devices, along_shard(): return lax.ppermute(value, 'shard', [(i, i ^ mask) for i in range(shards)])  9.22 us
    ppermute x3, starting transfers between devices, along_section(): lax.ppermute(value, 'section', [(i, i ^ mask) for i in range(sections)])  5.68 us
    ppermute x3, waiting for transfers between devices, along_section(): lax.ppermute(value, 'section', [(i, i ^ mask) for i in range(sections)])  3.44 us
    pallas_call x1, Pallas kernels, dense_rows(): pl.pallas_call(dense_rows_kernel, out_shape=[pltpu.VMEM(shape, jnp.bfloat...  1.34 us
    pallas_call x1, Pallas kernels, second_products(): pl.pallas_call(functools.partial(second_kernel, orders, sections), out_sh...  0.97 us
  transfers between devices with their start and end apart: 14, of which 6 were waited for; matrix products, arithmetic and copies ran while one was open for 0% of the time, Pallas kernels for 0%

profile of v22, /device:TPU:0, one launch (start us, length us, event | category | flops | bytes accessed | tf_op | source)
XLA Modules:
  0.0 31.0 jit_solution(3685505240554830457)
XLA Ops:
  0.0 1.3 %dense_rows.1 = (bf16[64,512]{1,0:T(8,128)(2,1)S(1)}, bf16[288,128]{1,0:T(8,128)(2,1)S(1)}) custom-call(s32[1,4,16]{2,1,0:T(4,128)} %cols_ref.1, s32[1,4]{1,0:T(1,128)} %live_ref.1, bf16[64,16,128]{2,1,0:T(8,128)(2,1)} %bitcast.13, s32[1,64]{1,0:T(1,128)} %degrees_ref.1, bf16[64,768]{1,0:T(8,128)(2,1)} %features_ref.1), custom_call_target="tpu_custom_call" | custom-call | tf_op jit(solution)/shard_map/dense_rows/pallas_call | solution.py:54
  1.3 5.1 %collective-permute-start.2 = (bf16[288,128]{1,0:T(8,128)(2,1)S(1)}, bf16[288,128]{1,0:T(8,128)(2,1)S(1)}, u32[]{:S(2)}, u32[]{:S(2)}) collective-permute-start(bf16[288,128]{1,0:T(8,128)(2,1)S(1)} %get-tuple-element.10), channel_id=1, source_target_pairs={{0,6},{1,7},{2,4},{3,5},{4,2},{5,3},{6,0},{7,1},{8,14},{9,15},{10,... | collective-permute-start | bytes 221192 | tf_op jit(solution)/shard_map/ppermute | solution.py:184
  6.5 0.0 collective-permute-start.1
  6.5 0.6 %collective-permute-start = (bf16[288,128]{1,0:T(8,128)(2,1)S(1)}, bf16[288,128]{1,0:T(8,128)(2,1)S(1)}, u32[]{:S(2)}, u32[]{:S(2)}) collective-permute-start(bf16[288,128]{1,0:T(8,128)(2,1)S(1)} %get-tuple-element.10), channel_id=1, source_target_pairs={{0,2},{1,3},{2,0},{3,1},{4,6},{5,7},{6,4},{7,5},{8,10},{9,11},{10,... | collective-permute-start | bytes 221192 | tf_op jit(solution)/shard_map/ppermute | solution.py:184
  7.1 2.6 %collective-permute-start.3 = (bf16[288,128]{1,0:T(8,128)(2,1)S(1)}, bf16[288,128]{1,0:T(8,128)(2,1)S(1)}, u32[]{:S(2)}, u32[]{:S(2)}) collective-permute-start(bf16[288,128]{1,0:T(8,128)(2,1)S(1)} %get-tuple-element.10), channel_id=1, source_target_pairs={{0,24},{8,16},{16,8},{24,0},{1,25},{9,17},{17,9},{25,1},{2,26},{10... | collective-permute-start | bytes 221192 | tf_op jit(solution)/shard_map/ppermute | solution.py:187
  9.7 0.0 collective-permute-done.2
  9.7 3.0 %collective-permute-done.1 = bf16[288,128]{1,0:T(8,128)(2,1)S(1)} collective-permute-done((bf16[288,128]{1,0:T(8,128)(2,1)S(1)}, bf16[288,128]{1,0:T(8,128)(2,1)S(1)}, u32[]{:S(2)}, u32[]{:S(2)}) %collective-permute-start.1) | collective-permute-done | bytes 73760 | tf_op jit(solution)/shard_map/ppermute | solution.py:184
  12.7 0.0 collective-permute-done
  12.7 0.0 collective-permute-done.3
  12.7 1.6 %collective-permute-start.6 = (bf16[4,288,128]{2,1,0:T(8,128)(2,1)S(1)}, bf16[4,288,128]{2,1,0:T(8,128)(2,1)S(1)}, u32[]{:S(2)}, u32[]{:S(2)}) collective-permute-start(bf16[4,288,128]{2,1,0:T(8,128)(2,1)S(1)} %pad_maximum_fusion.refs_0_), channel_id=1, source_target_pairs={{0,16},{8,24},{16,0},{24,8},{1,17},{9,25},{17,1},{25,9},{2,18},{10... | collective-permute-start | bytes 884744 | tf_op jit(solution)/shard_map/ppermute | solution.py:187
  14.3 1.5 %collective-permute-start.4 = (bf16[4,288,128]{2,1,0:T(8,128)(2,1)S(1)}, bf16[4,288,128]{2,1,0:T(8,128)(2,1)S(1)}, u32[]{:S(2)}, u32[]{:S(2)}) collective-permute-start(bf16[4,288,128]{2,1,0:T(8,128)(2,1)S(1)} %pad_maximum_fusion.refs_0_), channel_id=1, source_target_pairs={{0,8},{8,0},{16,24},{24,16},{1,9},{9,1},{17,25},{25,17},{2,10},{10... | collective-permute-start | bytes 884744 | tf_op jit(solution)/shard_map/ppermute | solution.py:187
  15.8 1.8 %collective-permute-start.10 = (bf16[288,128]{1,0:T(8,128)(2,1)S(1)}, bf16[288,128]{1,0:T(8,128)(2,1)S(1)}, u32[]{:S(2)}, u32[]{:S(2)}) collective-permute-start(bf16[288,128]{1,0:T(8,128)(2,1)S(1)} %collective-permute-done.3), channel_id=1, source_target_pairs={{0,4},{1,5},{2,6},{3,7},{4,0},{5,1},{6,2},{7,3},{8,12},{9,13},{10,... | collective-permute-start | bytes 221192 | tf_op jit(solution)/shard_map/ppermute | solution.py:184
  17.7 1.5 %collective-permute-start.9 = (bf16[288,128]{1,0:T(8,128)(2,1)S(1)}, bf16[288,128]{1,0:T(8,128)(2,1)S(1)}, u32[]{:S(2)}, u32[]{:S(2)}) collective-permute-start(bf16[288,128]{1,0:T(8,128)(2,1)S(1)} %collective-permute-done.3), channel_id=1, source_target_pairs={{0,6},{1,7},{2,4},{3,5},{4,2},{5,3},{6,0},{7,1},{8,14},{9,15},{10,... | collective-permute-start | bytes 221192 | tf_op jit(solution)/shard_map/ppermute | solution.py:184
  19.2 0.0 collective-permute-start.8
  19.2 2.0 %collective-permute-done.6.refs_2_.refs_4_ = bf16[4,288,128]{2,1,0:T(8,128)(2,1)S(1)} collective-permute-done((bf16[4,288,128]{2,1,0:T(8,128)(2,1)S(1)}, bf16[4,288,128]{2,1,0:T(8,128)(2,1)S(1)}, u32[]{:S(2)}, u32[]{:S(2)}) %collective-permute-start.6) | collective-permute-done | bytes 294944 | tf_op jit(solution)/shard_map/ppermute | solution.py:187
  21.2 1.5 %collective-permute-done.4.refs_0_.refs_2_ = bf16[4,288,128]{2,1,0:T(8,128)(2,1)S(1)} collective-permute-done((bf16[4,288,128]{2,1,0:T(8,128)(2,1)S(1)}, bf16[4,288,128]{2,1,0:T(8,128)(2,1)S(1)}, u32[]{:S(2)}, u32[]{:S(2)}) %collective-permute-start.4) | collective-permute-done | bytes 294944 | tf_op jit(solution)/shard_map/ppermute | solution.py:187
  22.6 0.0 collective-permute-start.5
  22.6 0.0 collective-permute-done.10
  22.6 1.3 %collective-permute-done.9 = bf16[288,128]{1,0:T(8,128)(2,1)S(1)} collective-permute-done((bf16[288,128]{1,0:T(8,128)(2,1)S(1)}, bf16[288,128]{1,0:T(8,128)(2,1)S(1)}, u32[]{:S(2)}, u32[]{:S(2)}) %collective-permute-start.9) | collective-permute-done | bytes 73760 | tf_op jit(solution)/shard_map/ppermute | solution.py:184
  23.9 0.1 collective-permute-start.11
  24.0 1.0 %collective-permute-start.12 = (bf16[288,128]{1,0:T(8,128)(2,1)S(1)}, bf16[288,128]{1,0:T(8,128)(2,1)S(1)}, u32[]{:S(2)}, u32[]{:S(2)}) collective-permute-start(bf16[288,128]{1,0:T(8,128)(2,1)S(1)} %collective-permute-done.3), channel_id=1, source_target_pairs={{0,2},{1,3},{2,0},{3,1},{4,6},{5,7},{6,4},{7,5},{8,10},{9,11},{10,... | collective-permute-start | bytes 221192 | tf_op jit(solution)/shard_map/ppermute | solution.py:184
  25.0 3.7 %collective-permute-done.12 = bf16[288,128]{1,0:T(8,128)(2,1)S(1)} collective-permute-done((bf16[288,128]{1,0:T(8,128)(2,1)S(1)}, bf16[288,128]{1,0:T(8,128)(2,1)S(1)}, u32[]{:S(2)}, u32[]{:S(2)}) %collective-permute-start.12) | collective-permute-done | bytes 73760 | tf_op jit(solution)/shard_map/ppermute | solution.py:184
  28.8 1.2 %collective-permute-done.13.refs_9_ = bf16[1,288,128]{2,1,0:T(8,128)(2,1)S(1)} collective-permute-done((bf16[1,288,128]{2,1,0:T(8,128)(2,1)S(1)}, bf16[1,288,128]{2,1,0:T(8,128)(2,1)S(1)}, u32[]{:S(2)}, u32[]{:S(2)}) %collective-permute-start.13) | collective-permute-done | bytes 73760 | tf_op jit(solution)/shard_map/ppermute | solution.py:184
  30.0 1.0 %second_products.1 = bf16[64,768]{1,0:T(8,128)(2,1)} custom-call(bf16[128,512]{1,0:T(8,128)(2,1)S(1)} %first_products.1.first_ref, bf16[4,288,128]{2,1,0:T(8,128)(2,1)S(1)} %pad_maximum_fusion.refs_0_, bf16[4,288,128]{2,1,0:T(8,128)(2,1)S(1)} %collective-permute-done.8.refs_1_, bf16[4,288,128]{2,1,0:T(8,128)(2,1)S(1)} %collective-permute-done.4.refs_0_.refs_2_, ...), custom_call_target="tpu_custom_call" | custom-call | tf_op jit(solution)/shard_map/second_products/pallas_call | solution.py:169
  (9 shorter events, 0.1 us)
Async XLA Ops:
  1.3 8.4 %collective-permute-start.2 = (bf16[288,128]{1,0:T(8,128)(2,1)S(1)}, bf16[288,128]{1,0:T(8,128)(2,1)S(1)}, u32[]{:S(2)}, u32[]{:S(2)}) collective-permute-start(bf16[288,128]{1,0:T(8,128)(2,1)S(1)} %get-tuple-element.10), channel_id=1, source_target_pairs={{0,6},{1,7},{2,4},{3,5},{4,2},{5,3},{6,0},{7,1},{8,14},{9,15},{10,... | collective-permute-start | bytes 221192 | tf_op jit(solution)/shard_map/ppermute | solution.py:184
  6.5 6.2 %collective-permute-start.1 = (bf16[288,128]{1,0:T(8,128)(2,1)S(1)}, bf16[288,128]{1,0:T(8,128)(2,1)S(1)}, u32[]{:S(2)}, u32[]{:S(2)}) collective-permute-start(bf16[288,128]{1,0:T(8,128)(2,1)S(1)} %get-tuple-element.10), channel_id=1, source_target_pairs={{0,4},{1,5},{2,6},{3,7},{4,0},{5,1},{6,2},{7,3},{8,12},{9,13},{10,... | collective-permute-start | bytes 221192 | tf_op jit(solution)/shard_map/ppermute | solution.py:184
  6.5 6.2 %collective-permute-start = (bf16[288,128]{1,0:T(8,128)(2,1)S(1)}, bf16[288,128]{1,0:T(8,128)(2,1)S(1)}, u32[]{:S(2)}, u32[]{:S(2)}) collective-permute-start(bf16[288,128]{1,0:T(8,128)(2,1)S(1)} %get-tuple-element.10), channel_id=1, source_target_pairs={{0,2},{1,3},{2,0},{3,1},{4,6},{5,7},{6,4},{7,5},{8,10},{9,11},{10,... | collective-permute-start | bytes 221192 | tf_op jit(solution)/shard_map/ppermute | solution.py:184
  7.1 5.6 %collective-permute-start.3 = (bf16[288,128]{1,0:T(8,128)(2,1)S(1)}, bf16[288,128]{1,0:T(8,128)(2,1)S(1)}, u32[]{:S(2)}, u32[]{:S(2)}) collective-permute-start(bf16[288,128]{1,0:T(8,128)(2,1)S(1)} %get-tuple-element.10), channel_id=1, source_target_pairs={{0,24},{8,16},{16,8},{24,0},{1,25},{9,17},{17,9},{25,1},{2,26},{10... | collective-permute-start | bytes 221192 | tf_op jit(solution)/shard_map/ppermute | solution.py:187
  12.7 8.4 %collective-permute-start.6 = (bf16[4,288,128]{2,1,0:T(8,128)(2,1)S(1)}, bf16[4,288,128]{2,1,0:T(8,128)(2,1)S(1)}, u32[]{:S(2)}, u32[]{:S(2)}) collective-permute-start(bf16[4,288,128]{2,1,0:T(8,128)(2,1)S(1)} %pad_maximum_fusion.refs_0_), channel_id=1, source_target_pairs={{0,16},{8,24},{16,0},{24,8},{1,17},{9,25},{17,1},{25,9},{2,18},{10... | collective-permute-start | bytes 884744 | tf_op jit(solution)/shard_map/ppermute | solution.py:187
  14.3 8.3 %collective-permute-start.4 = (bf16[4,288,128]{2,1,0:T(8,128)(2,1)S(1)}, bf16[4,288,128]{2,1,0:T(8,128)(2,1)S(1)}, u32[]{:S(2)}, u32[]{:S(2)}) collective-permute-start(bf16[4,288,128]{2,1,0:T(8,128)(2,1)S(1)} %pad_maximum_fusion.refs_0_), channel_id=1, source_target_pairs={{0,8},{8,0},{16,24},{24,16},{1,9},{9,1},{17,25},{25,17},{2,10},{10... | collective-permute-start | bytes 884744 | tf_op jit(solution)/shard_map/ppermute | solution.py:187
  15.8 6.8 %collective-permute-start.10 = (bf16[288,128]{1,0:T(8,128)(2,1)S(1)}, bf16[288,128]{1,0:T(8,128)(2,1)S(1)}, u32[]{:S(2)}, u32[]{:S(2)}) collective-permute-start(bf16[288,128]{1,0:T(8,128)(2,1)S(1)} %collective-permute-done.3), channel_id=1, source_target_pairs={{0,4},{1,5},{2,6},{3,7},{4,0},{5,1},{6,2},{7,3},{8,12},{9,13},{10,... | collective-permute-start | bytes 221192 | tf_op jit(solution)/shard_map/ppermute | solution.py:184
  17.7 6.3 %collective-permute-start.9 = (bf16[288,128]{1,0:T(8,128)(2,1)S(1)}, bf16[288,128]{1,0:T(8,128)(2,1)S(1)}, u32[]{:S(2)}, u32[]{:S(2)}) collective-permute-start(bf16[288,128]{1,0:T(8,128)(2,1)S(1)} %collective-permute-done.3), channel_id=1, source_target_pairs={{0,6},{1,7},{2,4},{3,5},{4,2},{5,3},{6,0},{7,1},{8,14},{9,15},{10,... | collective-permute-start | bytes 221192 | tf_op jit(solution)/shard_map/ppermute | solution.py:184
  19.2 10.8 %collective-permute-start.8 = (bf16[4,288,128]{2,1,0:T(8,128)(2,1)S(1)}, bf16[4,288,128]{2,1,0:T(8,128)(2,1)S(1)}, u32[]{:S(2)}, u32[]{:S(2)}) collective-permute-start(bf16[4,288,128]{2,1,0:T(8,128)(2,1)S(1)} %pad_maximum_fusion.refs_0_), channel_id=1, source_target_pairs={{0,1},{1,0},{2,3},{3,2},{4,5},{5,4},{6,7},{7,6},{8,9},{9,8},{10,11... | collective-permute-start | bytes 884744 | tf_op jit(solution)/shard_map/ppermute | solution.py:184
  21.2 7.6 %collective-permute-start.7 = (bf16[4,288,128]{2,1,0:T(8,128)(2,1)S(1)}, bf16[4,288,128]{2,1,0:T(8,128)(2,1)S(1)}, u32[]{:S(2)}, u32[]{:S(2)}) collective-permute-start(bf16[4,288,128]{2,1,0:T(8,128)(2,1)S(1)} %collective-permute-done.6.refs_2_.refs_4_), channel_id=1, source_target_pairs={{0,1},{1,0},{2,3},{3,2},{4,5},{5,4},{6,7},{7,6},{8,9},{9,8},{10,11... | collective-permute-start | bytes 884744 | tf_op jit(solution)/shard_map/ppermute | solution.py:184
  22.6 6.1 %collective-permute-start.5 = (bf16[4,288,128]{2,1,0:T(8,128)(2,1)S(1)}, bf16[4,288,128]{2,1,0:T(8,128)(2,1)S(1)}, u32[]{:S(2)}, u32[]{:S(2)}) collective-permute-start(bf16[4,288,128]{2,1,0:T(8,128)(2,1)S(1)} %collective-permute-done.4.refs_0_.refs_2_), channel_id=1, source_target_pairs={{0,1},{1,0},{2,3},{3,2},{4,5},{5,4},{6,7},{7,6},{8,9},{9,8},{10,11... | collective-permute-start | bytes 884744 | tf_op jit(solution)/shard_map/ppermute | solution.py:184
  23.9 6.0 %collective-permute-start.11 = (bf16[3,288,128]{2,1,0:T(8,128)(2,1)S(1)}, bf16[3,288,128]{2,1,0:T(8,128)(2,1)S(1)}, u32[]{:S(2)}, u32[]{:S(2)}) collective-permute-start(bf16[3,288,128]{2,1,0:T(8,128)(2,1)S(1)} %pad_maximum_fusion.1.refs_6_), channel_id=1, source_target_pairs={{0,1},{1,0},{2,3},{3,2},{4,5},{5,4},{6,7},{7,6},{8,9},{9,8},{10,11... | collective-permute-start | bytes 663560 | tf_op jit(solution)/shard_map/ppermute | solution.py:184
  24.0 4.7 %collective-permute-start.12 = (bf16[288,128]{1,0:T(8,128)(2,1)S(1)}, bf16[288,128]{1,0:T(8,128)(2,1)S(1)}, u32[]{:S(2)}, u32[]{:S(2)}) collective-permute-start(bf16[288,128]{1,0:T(8,128)(2,1)S(1)} %collective-permute-done.3), channel_id=1, source_target_pairs={{0,2},{1,3},{2,0},{3,1},{4,6},{5,7},{6,4},{7,5},{8,10},{9,11},{10,... | collective-permute-start | bytes 221192 | tf_op jit(solution)/shard_map/ppermute | solution.py:184
  28.7 1.3 %collective-permute-start.13 = (bf16[1,288,128]{2,1,0:T(8,128)(2,1)S(1)}, bf16[1,288,128]{2,1,0:T(8,128)(2,1)S(1)}, u32[]{:S(2)}, u32[]{:S(2)}) collective-permute-start(bf16[1,288,128]{2,1,0:T(8,128)(2,1)S(1)} %bitcast.10), channel_id=1, source_target_pairs={{0,1},{1,0},{2,3},{3,2},{4,5},{5,4},{6,7},{7,6},{8,9},{9,8},{10,11... | collective-permute-start | bytes 221192 | tf_op jit(solution)/shard_map/ppermute | solution.py:184

commit v23 on v19

--- a/solution.py
+++ b/solution.py
@@ -196,12 +196,13 @@
 
     ahead = {mask: along_section(sent, mask) for mask in range(1, sections) if mask & (mask - 1)}
     mine, ahead = lax.optimization_barrier((along_z(sent, whole)[0], ahead))
-    arrived = [(whole, [mine])]
-    for mask in range(1, sections):
+    arrived = {0: (whole, [mine])}
+    for mask in reversed(range(1, sections)):
         if mask in ahead:
-            arrived.append((in_two, along_z(ahead[mask], in_two)))
+            arrived[mask] = (in_two, along_z(ahead[mask], in_two))
         else:
-            arrived.append((whole, [along_section(mine, mask)]))
+            arrived[mask] = (whole, [along_section(mine, mask)])
+    arrived = [arrived[mask] for mask in range(sections)]
     pairs = [[(order, (here, along_shard(here, 1))) for order, here in zip(*group)] for group in arrived]
     first = first_products(own, pairs, own.shape[1], sections)
     return second_products(first, pairs, width, sections)

time: 27.3 us -> 27.3 us (level)
  no operation moved by 1% of the time
where the time goes in v23:
time: 27.3 us; the launch traced here: 27.1 us
  starting transfers between devices  17 us (62%)
  waiting for transfers between devices  7.71 us (28%)
  Pallas kernels  2.31 us (8%)
    ppermute x11, starting transfers between devices, along_shard(): return lax.ppermute(value, 'shard', [(i, i ^ mask) for i in range(shards)])  11.3 us
    ppermute x11, waiting for transfers between devices, along_shard(): return lax.ppermute(value, 'shard', [(i, i ^ mask) for i in range(shards)])  7.7 us
    ppermute x3, starting transfers between devices, along_section(): lax.ppermute(value, 'section', [(i, i ^ mask) for i in range(sections)])  5.68 us
    pallas_call x1, Pallas kernels, dense_rows(): pl.pallas_call(dense_rows_kernel, out_shape=[pltpu.VMEM(shape, jnp.bfloat...  1.34 us
    pallas_call x1, Pallas kernels, second_products(): pl.pallas_call(functools.partial(second_kernel, orders, sections), out_sh...  0.96 us
  transfers between devices with their start and end apart: 14, of which 5 were waited for; matrix products, arithmetic and copies ran while one was open for 0% of the time, Pallas kernels for 0%

profile of v23, /device:TPU:0, one launch (start us, length us, event | category | flops | bytes accessed | tf_op | source)
XLA Modules:
  0.0 27.1 jit_solution(6932210882100051446)
XLA Ops:
  0.0 1.3 %dense_rows.1 = (bf16[64,512]{1,0:T(8,128)(2,1)S(1)}, bf16[288,128]{1,0:T(8,128)(2,1)S(1)}) custom-call(s32[1,4,16]{2,1,0:T(4,128)} %cols_ref.1, s32[1,4]{1,0:T(1,128)} %live_ref.1, bf16[64,16,128]{2,1,0:T(8,128)(2,1)} %bitcast.11, s32[1,64]{1,0:T(1,128)} %degrees_ref.1, bf16[64,768]{1,0:T(8,128)(2,1)} %features_ref.1), custom_call_target="tpu_custom_call" | custom-call | tf_op jit(solution)/shard_map/dense_rows/pallas_call | solution.py:54
  1.3 5.1 %collective-permute-start.2 = (bf16[288,128]{1,0:T(8,128)(2,1)S(1)}, bf16[288,128]{1,0:T(8,128)(2,1)S(1)}, u32[]{:S(2)}, u32[]{:S(2)}) collective-permute-start(bf16[288,128]{1,0:T(8,128)(2,1)S(1)} %get-tuple-element.10), channel_id=1, source_target_pairs={{0,6},{1,7},{2,4},{3,5},{4,2},{5,3},{6,0},{7,1},{8,14},{9,15},{10,... | collective-permute-start | bytes 221192 | tf_op jit(solution)/shard_map/ppermute | solution.py:184
  6.5 0.6 %collective-permute-start = (bf16[288,128]{1,0:T(8,128)(2,1)S(1)}, bf16[288,128]{1,0:T(8,128)(2,1)S(1)}, u32[]{:S(2)}, u32[]{:S(2)}) collective-permute-start(bf16[288,128]{1,0:T(8,128)(2,1)S(1)} %get-tuple-element.10), channel_id=1, source_target_pairs={{0,2},{1,3},{2,0},{3,1},{4,6},{5,7},{6,4},{7,5},{8,10},{9,11},{10,... | collective-permute-start | bytes 221192 | tf_op jit(solution)/shard_map/ppermute | solution.py:184
  7.1 2.6 %collective-permute-start.3 = (bf16[288,128]{1,0:T(8,128)(2,1)S(1)}, bf16[288,128]{1,0:T(8,128)(2,1)S(1)}, u32[]{:S(2)}, u32[]{:S(2)}) collective-permute-start(bf16[288,128]{1,0:T(8,128)(2,1)S(1)} %get-tuple-element.10), channel_id=1, source_target_pairs={{0,24},{8,16},{16,8},{24,0},{1,25},{9,17},{17,9},{25,1},{2,26},{10... | collective-permute-start | bytes 221192 | tf_op jit(solution)/shard_map/ppermute | solution.py:187
  9.7 0.0 collective-permute-done.2
  9.7 3.0 %collective-permute-done.1 = bf16[288,128]{1,0:T(8,128)(2,1)S(1)} collective-permute-done((bf16[288,128]{1,0:T(8,128)(2,1)S(1)}, bf16[288,128]{1,0:T(8,128)(2,1)S(1)}, u32[]{:S(2)}, u32[]{:S(2)}) %collective-permute-start.1) | collective-permute-done | bytes 73760 | tf_op jit(solution)/shard_map/ppermute | solution.py:184
  12.7 0.0 collective-permute-done
  12.7 0.0 collective-permute-done.3
  12.7 1.6 %collective-permute-start.6 = (bf16[4,288,128]{2,1,0:T(8,128)(2,1)S(1)}, bf16[4,288,128]{2,1,0:T(8,128)(2,1)S(1)}, u32[]{:S(2)}, u32[]{:S(2)}) collective-permute-start(bf16[4,288,128]{2,1,0:T(8,128)(2,1)S(1)} %pad_maximum_fusion.refs_0_), channel_id=1, source_target_pairs={{0,16},{8,24},{16,0},{24,8},{1,17},{9,25},{17,1},{25,9},{2,18},{10... | collective-permute-start | bytes 884744 | tf_op jit(solution)/shard_map/ppermute | solution.py:187
  14.3 1.5 %collective-permute-start.4 = (bf16[4,288,128]{2,1,0:T(8,128)(2,1)S(1)}, bf16[4,288,128]{2,1,0:T(8,128)(2,1)S(1)}, u32[]{:S(2)}, u32[]{:S(2)}) collective-permute-start(bf16[4,288,128]{2,1,0:T(8,128)(2,1)S(1)} %pad_maximum_fusion.refs_0_), channel_id=1, source_target_pairs={{0,8},{8,0},{16,24},{24,16},{1,9},{9,1},{17,25},{25,17},{2,10},{10... | collective-permute-start | bytes 884744 | tf_op jit(solution)/shard_map/ppermute | solution.py:187
  15.8 3.3 %collective-permute-start.9 = (bf16[288,128]{1,0:T(8,128)(2,1)S(1)}, bf16[288,128]{1,0:T(8,128)(2,1)S(1)}, u32[]{:S(2)}, u32[]{:S(2)}) collective-permute-start(bf16[288,128]{1,0:T(8,128)(2,1)S(1)} %collective-permute-done.3), channel_id=1, source_target_pairs={{0,6},{1,7},{2,4},{3,5},{4,2},{5,3},{6,0},{7,1},{8,14},{9,15},{10,... | collective-permute-start | bytes 221192 | tf_op jit(solution)/shard_map/ppermute | solution.py:184
  19.1 0.0 collective-permute-start.12
  19.1 1.1 %collective-permute-start.11 = (bf16[288,128]{1,0:T(8,128)(2,1)S(1)}, bf16[288,128]{1,0:T(8,128)(2,1)S(1)}, u32[]{:S(2)}, u32[]{:S(2)}) collective-permute-start(bf16[288,128]{1,0:T(8,128)(2,1)S(1)} %collective-permute-done.3), channel_id=1, source_target_pairs={{0,4},{1,5},{2,6},{3,7},{4,0},{5,1},{6,2},{7,3},{8,12},{9,13},{10,... | collective-permute-start | bytes 221192 | tf_op jit(solution)/shard_map/ppermute | solution.py:184
  20.2 2.4 %collective-permute-done.9 = bf16[288,128]{1,0:T(8,128)(2,1)S(1)} collective-permute-done((bf16[288,128]{1,0:T(8,128)(2,1)S(1)}, bf16[288,128]{1,0:T(8,128)(2,1)S(1)}, u32[]{:S(2)}, u32[]{:S(2)}) %collective-permute-start.9) | collective-permute-done | bytes 73760 | tf_op jit(solution)/shard_map/ppermute | solution.py:184
  22.6 0.0 collective-permute-start.8
  22.6 0.0 collective-permute-done.6.refs_2_.refs_4_
  22.6 0.5 %collective-permute-start.7 = (bf16[4,288,128]{2,1,0:T(8,128)(2,1)S(1)}, bf16[4,288,128]{2,1,0:T(8,128)(2,1)S(1)}, u32[]{:S(2)}, u32[]{:S(2)}) collective-permute-start(bf16[4,288,128]{2,1,0:T(8,128)(2,1)S(1)} %collective-permute-done.6.refs_2_.refs_4_), channel_id=1, source_target_pairs={{0,1},{1,0},{2,3},{3,2},{4,5},{5,4},{6,7},{7,6},{8,9},{9,8},{10,11... | collective-permute-start | bytes 884744 | tf_op jit(solution)/shard_map/ppermute | solution.py:184
  23.1 0.0 collective-permute-done.4.refs_0_.refs_2_
  23.1 0.1 collective-permute-start.5
  23.2 1.4 %collective-permute-done.12 = bf16[288,128]{1,0:T(8,128)(2,1)S(1)} collective-permute-done((bf16[288,128]{1,0:T(8,128)(2,1)S(1)}, bf16[288,128]{1,0:T(8,128)(2,1)S(1)}, u32[]{:S(2)}, u32[]{:S(2)}) %collective-permute-start.12) | collective-permute-done | bytes 73760 | tf_op jit(solution)/shard_map/ppermute | solution.py:184
  24.6 0.6 %collective-permute-start.13 = (bf16[2,288,128]{2,1,0:T(8,128)(2,1)S(1)}, bf16[2,288,128]{2,1,0:T(8,128)(2,1)S(1)}, u32[]{:S(2)}, u32[]{:S(2)}) collective-permute-start(bf16[2,288,128]{2,1,0:T(8,128)(2,1)S(1)} %pad_maximum_fusion.2.refs_8_), channel_id=1, source_target_pairs={{0,1},{1,0},{2,3},{3,2},{4,5},{5,4},{6,7},{7,6},{8,9},{9,8},{10,11... | collective-permute-start | bytes 442376 | tf_op jit(solution)/shard_map/ppermute | solution.py:184
  25.2 0.7 %collective-permute-done.10.refs_7_ = bf16[2,288,128]{2,1,0:T(8,128)(2,1)S(1)} collective-permute-done((bf16[2,288,128]{2,1,0:T(8,128)(2,1)S(1)}, bf16[2,288,128]{2,1,0:T(8,128)(2,1)S(1)}, u32[]{:S(2)}, u32[]{:S(2)}) %collective-permute-start.10) | collective-permute-done | bytes 147488 | tf_op jit(solution)/shard_map/ppermute | solution.py:184
  25.9 0.2 collective-permute-done.13.refs_9_
  26.2 1.0 %second_products.1 = bf16[64,768]{1,0:T(8,128)(2,1)} custom-call(bf16[128,512]{1,0:T(8,128)(2,1)S(1)} %first_products.1.first_ref, bf16[4,288,128]{2,1,0:T(8,128)(2,1)S(1)} %pad_maximum_fusion.refs_0_, bf16[4,288,128]{2,1,0:T(8,128)(2,1)S(1)} %collective-permute-done.8.refs_1_, bf16[4,288,128]{2,1,0:T(8,128)(2,1)S(1)} %collective-permute-done.4.refs_0_.refs_2_, ...), custom_call_target="tpu_custom_call" | custom-call | tf_op jit(solution)/shard_map/second_products/pallas_call | solution.py:169
  (10 shorter events, 0.1 us)
Async XLA Ops:
  1.3 8.4 %collective-permute-start.2 = (bf16[288,128]{1,0:T(8,128)(2,1)S(1)}, bf16[288,128]{1,0:T(8,128)(2,1)S(1)}, u32[]{:S(2)}, u32[]{:S(2)}) collective-permute-start(bf16[288,128]{1,0:T(8,128)(2,1)S(1)} %get-tuple-element.10), channel_id=1, source_target_pairs={{0,6},{1,7},{2,4},{3,5},{4,2},{5,3},{6,0},{7,1},{8,14},{9,15},{10,... | collective-permute-start | bytes 221192 | tf_op jit(solution)/shard_map/ppermute | solution.py:184
  6.5 6.2 %collective-permute-start.1 = (bf16[288,128]{1,0:T(8,128)(2,1)S(1)}, bf16[288,128]{1,0:T(8,128)(2,1)S(1)}, u32[]{:S(2)}, u32[]{:S(2)}) collective-permute-start(bf16[288,128]{1,0:T(8,128)(2,1)S(1)} %get-tuple-element.10), channel_id=1, source_target_pairs={{0,4},{1,5},{2,6},{3,7},{4,0},{5,1},{6,2},{7,3},{8,12},{9,13},{10,... | collective-permute-start | bytes 221192 | tf_op jit(solution)/shard_map/ppermute | solution.py:184
  6.5 6.2 %collective-permute-start = (bf16[288,128]{1,0:T(8,128)(2,1)S(1)}, bf16[288,128]{1,0:T(8,128)(2,1)S(1)}, u32[]{:S(2)}, u32[]{:S(2)}) collective-permute-start(bf16[288,128]{1,0:T(8,128)(2,1)S(1)} %get-tuple-element.10), channel_id=1, source_target_pairs={{0,2},{1,3},{2,0},{3,1},{4,6},{5,7},{6,4},{7,5},{8,10},{9,11},{10,... | collective-permute-start | bytes 221192 | tf_op jit(solution)/shard_map/ppermute | solution.py:184
  7.1 5.6 %collective-permute-start.3 = (bf16[288,128]{1,0:T(8,128)(2,1)S(1)}, bf16[288,128]{1,0:T(8,128)(2,1)S(1)}, u32[]{:S(2)}, u32[]{:S(2)}) collective-permute-start(bf16[288,128]{1,0:T(8,128)(2,1)S(1)} %get-tuple-element.10), channel_id=1, source_target_pairs={{0,24},{8,16},{16,8},{24,0},{1,25},{9,17},{17,9},{25,1},{2,26},{10... | collective-permute-start | bytes 221192 | tf_op jit(solution)/shard_map/ppermute | solution.py:187
  12.7 9.9 %collective-permute-start.6 = (bf16[4,288,128]{2,1,0:T(8,128)(2,1)S(1)}, bf16[4,288,128]{2,1,0:T(8,128)(2,1)S(1)}, u32[]{:S(2)}, u32[]{:S(2)}) collective-permute-start(bf16[4,288,128]{2,1,0:T(8,128)(2,1)S(1)} %pad_maximum_fusion.refs_0_), channel_id=1, source_target_pairs={{0,16},{8,24},{16,0},{24,8},{1,17},{9,25},{17,1},{25,9},{2,18},{10... | collective-permute-start | bytes 884744 | tf_op jit(solution)/shard_map/ppermute | solution.py:187
  14.3 8.8 %collective-permute-start.4 = (bf16[4,288,128]{2,1,0:T(8,128)(2,1)S(1)}, bf16[4,288,128]{2,1,0:T(8,128)(2,1)S(1)}, u32[]{:S(2)}, u32[]{:S(2)}) collective-permute-start(bf16[4,288,128]{2,1,0:T(8,128)(2,1)S(1)} %pad_maximum_fusion.refs_0_), channel_id=1, source_target_pairs={{0,8},{8,0},{16,24},{24,16},{1,9},{9,1},{17,25},{25,17},{2,10},{10... | collective-permute-start | bytes 884744 | tf_op jit(solution)/shard_map/ppermute | solution.py:187
  15.8 6.8 %collective-permute-start.9 = (bf16[288,128]{1,0:T(8,128)(2,1)S(1)}, bf16[288,128]{1,0:T(8,128)(2,1)S(1)}, u32[]{:S(2)}, u32[]{:S(2)}) collective-permute-start(bf16[288,128]{1,0:T(8,128)(2,1)S(1)} %collective-permute-done.3), channel_id=1, source_target_pairs={{0,6},{1,7},{2,4},{3,5},{4,2},{5,3},{6,0},{7,1},{8,14},{9,15},{10,... | collective-permute-start | bytes 221192 | tf_op jit(solution)/shard_map/ppermute | solution.py:184
  19.1 5.4 %collective-permute-start.12 = (bf16[288,128]{1,0:T(8,128)(2,1)S(1)}, bf16[288,128]{1,0:T(8,128)(2,1)S(1)}, u32[]{:S(2)}, u32[]{:S(2)}) collective-permute-start(bf16[288,128]{1,0:T(8,128)(2,1)S(1)} %collective-permute-done.3), channel_id=1, source_target_pairs={{0,2},{1,3},{2,0},{3,1},{4,6},{5,7},{6,4},{7,5},{8,10},{9,11},{10,... | collective-permute-start | bytes 221192 | tf_op jit(solution)/shard_map/ppermute | solution.py:184
  19.1 5.4 %collective-permute-start.11 = (bf16[288,128]{1,0:T(8,128)(2,1)S(1)}, bf16[288,128]{1,0:T(8,128)(2,1)S(1)}, u32[]{:S(2)}, u32[]{:S(2)}) collective-permute-start(bf16[288,128]{1,0:T(8,128)(2,1)S(1)} %collective-permute-done.3), channel_id=1, source_target_pairs={{0,4},{1,5},{2,6},{3,7},{4,0},{5,1},{6,2},{7,3},{8,12},{9,13},{10,... | collective-permute-start | bytes 221192 | tf_op jit(solution)/shard_map/ppermute | solution.py:184
  22.6 3.6 %collective-permute-start.8 = (bf16[4,288,128]{2,1,0:T(8,128)(2,1)S(1)}, bf16[4,288,128]{2,1,0:T(8,128)(2,1)S(1)}, u32[]{:S(2)}, u32[]{:S(2)}) collective-permute-start(bf16[4,288,128]{2,1,0:T(8,128)(2,1)S(1)} %pad_maximum_fusion.refs_0_), channel_id=1, source_target_pairs={{0,1},{1,0},{2,3},{3,2},{4,5},{5,4},{6,7},{7,6},{8,9},{9,8},{10,11... | collective-permute-start | bytes 884744 | tf_op jit(solution)/shard_map/ppermute | solution.py:184
  22.6 2.6 %collective-permute-start.7 = (bf16[4,288,128]{2,1,0:T(8,128)(2,1)S(1)}, bf16[4,288,128]{2,1,0:T(8,128)(2,1)S(1)}, u32[]{:S(2)}, u32[]{:S(2)}) collective-permute-start(bf16[4,288,128]{2,1,0:T(8,128)(2,1)S(1)} %collective-permute-done.6.refs_2_.refs_4_), channel_id=1, source_target_pairs={{0,1},{1,0},{2,3},{3,2},{4,5},{5,4},{6,7},{7,6},{8,9},{9,8},{10,11... | collective-permute-start | bytes 884744 | tf_op jit(solution)/shard_map/ppermute | solution.py:184
  23.1 2.0 %collective-permute-start.5 = (bf16[4,288,128]{2,1,0:T(8,128)(2,1)S(1)}, bf16[4,288,128]{2,1,0:T(8,128)(2,1)S(1)}, u32[]{:S(2)}, u32[]{:S(2)}) collective-permute-start(bf16[4,288,128]{2,1,0:T(8,128)(2,1)S(1)} %collective-permute-done.4.refs_0_.refs_2_), channel_id=1, source_target_pairs={{0,1},{1,0},{2,3},{3,2},{4,5},{5,4},{6,7},{7,6},{8,9},{9,8},{10,11... | collective-permute-start | bytes 884744 | tf_op jit(solution)/shard_map/ppermute | solution.py:184
  24.5 1.4 %collective-permute-start.10 = (bf16[2,288,128]{2,1,0:T(8,128)(2,1)S(1)}, bf16[2,288,128]{2,1,0:T(8,128)(2,1)S(1)}, u32[]{:S(2)}, u32[]{:S(2)}) collective-permute-start(bf16[2,288,128]{2,1,0:T(8,128)(2,1)S(1)} %pad_maximum_fusion.1.refs_6_), channel_id=1, source_target_pairs={{0,1},{1,0},{2,3},{3,2},{4,5},{5,4},{6,7},{7,6},{8,9},{9,8},{10,11... | collective-permute-start | bytes 442376 | tf_op jit(solution)/shard_map/ppermute | solution.py:184
  24.6 1.6 %collective-permute-start.13 = (bf16[2,288,128]{2,1,0:T(8,128)(2,1)S(1)}, bf16[2,288,128]{2,1,0:T(8,128)(2,1)S(1)}, u32[]{:S(2)}, u32[]{:S(2)}) collective-permute-start(bf16[2,288,128]{2,1,0:T(8,128)(2,1)S(1)} %pad_maximum_fusion.2.refs_8_), channel_id=1, source_target_pairs={{0,1},{1,0},{2,3},{3,2},{4,5},{5,4},{6,7},{7,6},{8,9},{9,8},{10,11... | collective-permute-start | bytes 442376 | tf_op jit(solution)/shard_map/ppermute | solution.py:184
